TPU v7x, 32 devices: a whole 2x2x4 slice. The times are simulated.
32 devices in a mesh: sample: 4 (over z), mp: 8 (over y, x, core).
Axes of the slice: x: 2, y: 2, z: 4, core: 2. Of those that a mesh axis runs over, the one named last changes fastest.
Arguments:
- volumes: bfloat16 [64, 4, 2048], P('mp', 'sample'), may hold values from -6 to 6
- w_first: bfloat16 [128, 1728], P('mp'), may hold values from -0.15625 to 0.15625
- w_second: bfloat16 [256, 3456], P('mp'), may hold values from -0.109375 to 0.109375
- cotangent: bfloat16 [256, 4, 2048], P('mp', 'sample'), may hold values from -6 to 6
Outputs:
- features: bfloat16 [256, 4, 2048], P('mp', 'sample')
- input_grad: bfloat16 [64, 4, 2048], P('mp', 'sample')
- grad_first: float32 [128, 1728], P('mp')
- grad_second: float32 [256, 3456], P('mp')
All inputs are finite; a program needn't handle non-finite values.
Results may differ from a plain program's by a relative error of at most 0.024.
Values may be sent and summed in bfloat16 or wider, within the bound.
No kernel may reach another device: no remote copies, remote signals or barrier semaphores. Data moves between devices by JAX's collectives and lax.ppermute only.
A program may use at most 64 MiB of HBM per device.

v0:
```python
import functools
import math

import jax
import jax.numpy as jnp
from jax import lax
from jax.experimental import pallas as pl
from jax.experimental.pallas import tpu as pltpu
from jax.sharding import PartitionSpec as P

SIDE = 16
PLANE = SIDE * SIDE
F32 = jnp.float32
BF16 = jnp.bfloat16
VMEM_LIMIT = 48 * 1024 * 1024


def pitch_of(channels):
    width = 3 * channels
    slack = max((i * width) % 128 for i in range(9))
    return -(-(width + slack) // 128) * 128


def lane_grid(width):
    lane = lax.broadcasted_iota(jnp.int32, (1, width), 1)
    return lane % SIDE, (lane // SIDE) % SIDE


def inside(grid_xy, dy, dx):
    x, y = grid_xy
    ok = None
    for coord, step in ((y, dy), (x, dx)):
        if step < 0:
            now = coord >= -step
        elif step > 0:
            now = coord < SIDE - step
        else:
            continue
        ok = now if ok is None else ok & now
    return ok


def moved(values, grid_xy, dy, dx):
    if dy == 0 and dx == 0:
        return values
    width = values.shape[1]
    rolled = pltpu.roll(values, (-(dy * SIDE + dx)) % width, 1)
    return jnp.where(inside(grid_xy, dy, dx), rolled, 0.0)


def sigmoid(v):
    return 1.0 / (1.0 + jnp.exp(-v))


def dot(a, b):
    return lax.dot_general(a, b, (((1,), (0,)), ((), ())), preferred_element_type=F32)


def dot_nt(a, b):
    return lax.dot_general(a, b, (((1,), (1,)), ((), ())), preferred_element_type=F32)


def chunk_of(cells):
    return 2 * PLANE if cells % (2 * PLANE) == 0 else PLANE


def forward_kernel(n_mp, n_sample, c0, *refs):
    pieces = refs[:n_mp]
    w2r_ref, w2b_ref, cot_ref = refs[n_mp : n_mp + 3]
    outs = refs[n_mp + 3 :]
    feat_ref, pre_ref, vol_ref = outs[:3]
    part_refs = outs[3 : 3 + n_mp]
    grad_refs = outs[3 + n_mp : 3 + n_mp + n_sample]
    vs, w1s, v3, w1r, hid, pre, d9, part, grad = outs[3 + n_mp + n_sample :]

    me = lax.axis_index("mp")
    at = lax.axis_index("sample")
    f1 = w1s.shape[1]
    c1 = n_mp * f1
    f2, cells = cot_ref.shape
    chunk = chunk_of(cells)
    steps = cells // chunk
    pitch = pitch_of(c0)
    grid_xy = lane_grid(chunk)

    for k in range(n_mp):
        piece = pieces[k][...].astype(F32)
        slot = me ^ k
        w1s[slot] = piece[:f1]
        vs[slot] = piece[f1:, :cells]

    lane = lax.broadcasted_iota(jnp.int32, (1, pitch), 1)
    for dz in range(3):
        for dy in range(3):
            start = (dz * 3 + dy) * 3 * c0
            low = start // 128 * 128
            block = w1s[:, :, low : low + pitch].reshape(c1, pitch)
            if start != low:
                block = pltpu.roll(block, pitch - (start - low), 1)
            block = jnp.where(lane < 3 * c0, block, 0.0)
            w1r[dy * c1 : (dy + 1) * c1, dz * pitch : (dz + 1) * pitch] = block.astype(BF16)

    for ref in (v3, hid, d9):
        zero = jnp.zeros((ref.shape[0], PLANE), BF16)
        ref[:, :PLANE] = zero
        ref[:, PLANE + cells :] = zero
    v3[3 * c0 :, PLANE : PLANE + cells] = jnp.zeros((pitch - 3 * c0, cells), BF16)

    def take_volumes(step, carry):
        base = pl.multiple_of(step * chunk, chunk)
        values = vs[:, :, pl.ds(base, chunk)].reshape(c0, chunk)
        vol_ref[:, pl.ds(base, chunk)] = values.astype(BF16)
        for dx in range(3):
            v3[dx * c0 : (dx + 1) * c0, pl.ds(base + PLANE, chunk)] = moved(values, grid_xy, 0, dx - 1).astype(BF16)
        return carry

    lax.fori_loop(0, steps, take_volumes, 0)

    def first_conv(step, carry):
        base = pl.multiple_of(step * chunk, chunk)
        rhs = jnp.concatenate([v3[:, pl.ds(base + dz * PLANE, chunk)] for dz in range(3)], axis=0)
        z = dot(w1r[...], rhs)
        total = z[c1 : 2 * c1]
        total = total + moved(z[:c1], grid_xy, -1, 0)
        total = total + moved(z[2 * c1 :], grid_xy, 1, 0)
        pre[:, pl.ds(base, chunk)] = total
        hid[:, pl.ds(base + PLANE, chunk)] = (total * sigmoid(total)).astype(BF16)
        return carry

    lax.fori_loop(0, steps, first_conv, 0)
    pre_ref[...] = pre[pl.ds(pl.multiple_of(me * f1, f1), f1), :]

    def second_conv(step, carry):
        base = pl.multiple_of(step * chunk, chunk)
        rhs = jnp.concatenate([hid[:, pl.ds(base + dz * PLANE, chunk)] for dz in range(3)], axis=0)
        z = dot(w2r_ref[...], rhs)
        total = None
        for dy in range(3):
            for dx in range(3):
                k = dy * 3 + dx
                term = moved(z[k * f2 : (k + 1) * f2], grid_xy, dy - 1, dx - 1)
                total = term if total is None else total + term
        s = sigmoid(total)
        feat_ref[:, pl.ds(base, chunk)] = (total * s).astype(BF16)
        cot = cot_ref[:, pl.ds(base, chunk)].astype(F32)
        delta = (cot * (s * (1.0 + total * (1.0 - s)))).astype(BF16).astype(F32)
        for dy in range(3):
            for dx in range(3):
                k = dy * 3 + dx
                d9[k * f2 : (k + 1) * f2, pl.ds(base + PLANE, chunk)] = moved(delta, grid_xy, 1 - dy, 1 - dx).astype(BF16)
        return carry

    lax.fori_loop(0, steps, second_conv, 0)

    def data_conv(step, carry):
        base = pl.multiple_of(step * chunk, chunk)
        rhs = jnp.concatenate([d9[:, pl.ds(base + (2 - dz) * PLANE, chunk)] for dz in range(3)], axis=0)
        z = dot(w2b_ref[...], rhs)
        part[:, :, pl.ds(base, chunk)] = z.reshape(n_mp, f1, chunk)
        return carry

    lax.fori_loop(0, steps, data_conv, 0)
    for k in range(n_mp):
        part_refs[k][...] = part[me ^ k].astype(BF16)

    rows = f2 // n_sample
    for dz in range(3):
        g = dot_nt(d9[:, (2 - dz) * PLANE : (2 - dz) * PLANE + cells], hid[:, PLANE : PLANE + cells])
        for k in range(9):
            t = dz * 9 + k
            grad[:, :, t * c1 : (t + 1) * c1] = g[k * f2 : (k + 1) * f2].reshape(n_sample, rows, c1)
    for k in range(n_sample):
        grad_refs[k][...] = grad[at ^ k].astype(BF16)


def backward_kernel(n_mp, *refs):
    parts = refs[:n_mp]
    pre_ref, vol_ref, w1b_ref = refs[n_mp : n_mp + 3]
    out_refs = refs[n_mp + 3 : 2 * n_mp + 3]
    grad_ref, d9, part = refs[2 * n_mp + 3 :]
    me = lax.axis_index("mp")
    f1, cells = pre_ref.shape
    c0 = vol_ref.shape[0]
    chunk = chunk_of(cells)
    steps = cells // chunk
    grid_xy = lane_grid(chunk)

    zero = jnp.zeros((d9.shape[0], PLANE), BF16)
    d9[:, :PLANE] = zero
    d9[:, PLANE + cells :] = zero

    def take(step, carry):
        base = pl.multiple_of(step * chunk, chunk)
        total = parts[0][:, pl.ds(base, chunk)].astype(F32)
        for k in range(1, n_mp):
            total = total + parts[k][:, pl.ds(base, chunk)].astype(F32)
        v = pre_ref[:, pl.ds(base, chunk)]
        s = sigmoid(v)
        delta = (total * (s * (1.0 + v * (1.0 - s)))).astype(BF16).astype(F32)
        shifts = [moved(delta, grid_xy, 1 - dy, 1 - dx) for dy in range(3) for dx in range(3)]
        d9[:, pl.ds(base + PLANE, chunk)] = jnp.concatenate(shifts, axis=0).astype(BF16)
        return carry

    lax.fori_loop(0, steps, take, 0)

    def data_conv(step, carry):
        base = pl.multiple_of(step * chunk, chunk)
        z = None
        for dz in range(3):
            term = dot(w1b_ref[dz], d9[:, pl.ds(base + (2 - dz) * PLANE, chunk)])
            z = term if z is None else z + term
        part[:, :, pl.ds(base, chunk)] = z.reshape(n_mp, c0 // n_mp, chunk)
        return carry

    lax.fori_loop(0, steps, data_conv, 0)
    for k in range(n_mp):
        out_refs[k][...] = part[me ^ k].astype(BF16)

    reps = max(1, 128 // c0)
    span = reps * c0
    vol = vol_ref[...]
    wide = jnp.concatenate([vol] * reps, axis=0) if reps > 1 else vol
    blocks = []
    for dz in range(3):
        g = dot_nt(d9[:, (2 - dz) * PLANE : (2 - dz) * PLANE + cells], wide)
        blocks += [g[k * f1 : (k + 1) * f1] for k in range(9)]
    lane = lax.broadcasted_iota(jnp.int32, (1, span), 1)
    for t in range(0, 27, reps):
        merged = blocks[t]
        for r in range(1, min(reps, 27 - t)):
            merged = jnp.where(lane >= r * c0, blocks[t + r], merged)
        width = min(span, (27 - t) * c0)
        grad_ref[:, t * c0 : t * c0 + width] = merged[:, :width].astype(BF16)


def place_kernel(n_sample, scale, *refs):
    out_ref = refs[n_sample]
    at = lax.axis_index("sample")
    for k in range(n_sample):
        out_ref[at ^ k] = refs[k][...].astype(F32) * scale


def swap(value, axis, k):
    n = lax.axis_size(axis)
    return lax.ppermute(value, axis, [(i, i ^ k) for i in range(n)])


def call(kernel, out_shape, scratch, flops, nbytes):
    return pl.pallas_call(
        kernel,
        out_shape=out_shape,
        scratch_shapes=scratch,
        compiler_params=pltpu.CompilerParams(vmem_limit_bytes=VMEM_LIMIT),
        cost_estimate=pl.CostEstimate(flops=flops, bytes_accessed=nbytes, transcendentals=0),
    )


def local(volumes, w_first, w_second, cotangent):
    n_mp = lax.axis_size("mp")
    n_sample = lax.axis_size("sample")
    rows_in, _, cells = volumes.shape
    f1 = w_first.shape[0]
    f2 = w_second.shape[0]
    c0 = w_first.shape[1] // 27
    c1 = w_second.shape[1] // 27
    pitch = pitch_of(c0)
    scale = 1.0 / math.sqrt(n_sample * volumes.shape[1] * cells)
    volumes = volumes.reshape(rows_in, cells)
    cotangent = cotangent.reshape(f2, cells)
    padded = cells + 2 * PLANE

    need = (8 * 3 * c0) // 128 * 128 + pitch
    wide = max(cells, need)
    piece = jnp.concatenate(
        [
            jnp.pad(w_first, ((0, 0), (0, wide - w_first.shape[1]))),
            jnp.pad(volumes, ((0, 0), (0, wide - cells))),
        ],
        axis=0,
    )
    pieces = [piece] + [swap(piece, "mp", k) for k in range(1, n_mp)]

    w2t = w_second.reshape(f2, 3, 9, c1)
    w2r = jnp.transpose(w2t, (2, 0, 1, 3)).reshape(9 * f2, 3 * c1)
    w2b = jnp.transpose(w2t, (3, 1, 2, 0)).reshape(c1, 27 * f2)
    w1b = jnp.transpose(w_first.reshape(f1, 3, 9, c0), (1, 3, 2, 0)).reshape(3, c0, 9 * f1)

    sds = jax.ShapeDtypeStruct
    outs = call(
        functools.partial(forward_kernel, n_mp, n_sample, c0),
        [sds((f2, cells), BF16), sds((f1, cells), F32), sds((c0, cells), BF16)]
        + [sds((f1, cells), BF16)] * n_mp
        + [sds((f2 // n_sample, 27 * c1), BF16)] * n_sample,
        [
            pltpu.VMEM((n_mp, rows_in, cells), F32),
            pltpu.VMEM((n_mp, f1, wide), F32),
            pltpu.VMEM((pitch, padded), BF16),
            pltpu.VMEM((3 * c1, 3 * pitch), BF16),
            pltpu.VMEM((c1, padded), BF16),
            pltpu.VMEM((c1, cells), F32),
            pltpu.VMEM((9 * f2, padded), BF16),
            pltpu.VMEM((n_mp, f1, cells), F32),
            pltpu.VMEM((n_sample, f2 // n_sample, 27 * c1), F32),
        ],
        2 * cells * 27 * (c0 * c1 + 3 * f2 * c1),
        4 * 1024 * 1024,
    )(*pieces, w2r, w2b, cotangent)
    features, pre_own, vol_all = outs[:3]
    parts = outs[3 : 3 + n_mp]
    grads = outs[3 + n_mp :]

    parts = [parts[0]] + [swap(parts[k], "mp", k) for k in range(1, n_mp)]
    grads = [grads[0]] + [swap(grads[k], "sample", k) for k in range(1, n_sample)]

    outs = call(
        functools.partial(backward_kernel, n_mp),
        [sds((rows_in, cells), BF16)] * n_mp + [sds((f1, 27 * c0), BF16)],
        [
            pltpu.VMEM((9 * f1, padded), BF16),
            pltpu.VMEM((n_mp, rows_in, cells), F32),
        ],
        2 * cells * 27 * 2 * c0 * f1,
        1024 * 1024,
    )(*parts, pre_own, vol_all, w1b)
    ins = outs[:n_mp]
    grad_first = outs[n_mp]
    firsts = [grad_first] + [swap(grad_first, "sample", k) for k in range(1, n_sample)]
    ins = [ins[0]] + [swap(ins[k], "mp", k) for k in range(1, n_mp)]

    def total(values):
        result = values[0].astype(F32)
        for value in values[1:]:
            result = result + value.astype(F32)
        return result

    second = total(grads).astype(BF16)
    seconds = [second] + [swap(second, "sample", k) for k in range(1, n_sample)]
    grad_second = call(
        functools.partial(place_kernel, n_sample, scale),
        sds((n_sample,) + second.shape, F32),
        [],
        0,
        1024 * 1024,
    )(*seconds).reshape(f2, 27 * c1)
    input_grad = total(ins).astype(BF16)
    return (
        features.reshape(f2, 1, cells),
        input_grad.reshape(rows_in, 1, cells),
        total(firsts) * scale,
        grad_second,
    )


def solution(mesh):
    return jax.shard_map(
        local,
        mesh=mesh,
        in_specs=(P("mp", "sample", None), P("mp", None), P("mp", None), P("mp", "sample", None)),
        out_specs=(P("mp", "sample", None), P("mp", "sample", None), P("mp", None), P("mp", None)),
        check_vma=False,
    )
```

profile of v0, /device:TPU:0, one launch (start us, length us, event | category | flops | bytes accessed | tf_op | source)
XLA Modules:
  0.0 62.0 jit_solution(27344543578202040)
XLA Ops:
  0.6 0.8 %fusion.1.refs_0_ = bf16[24,2048]{1,0:T(8,128)(2,1)S(1)} fusion(bf16[16,1728]{1,0:T(8,128)(2,1)} %param.5, bf16[8,2048]{1,0:T(8,128)(2,1)} %bitcast.25), kind=kLoop, calls=%fused_computation.5 | loop fusion | flops 294912 | bytes 186368 | tf_op jit(solution)/shard_map/concatenate | solution.py:274
  1.5 0.5 collective-permute-start
  2.0 2.6 %collective-permute-start.1 = (bf16[24,2048]{1,0:T(8,128)(2,1)S(1)}, bf16[24,2048]{1,0:T(8,128)(2,1)S(1)}, u32[]{:S(2)}, u32[]{:S(2)}) collective-permute-start(bf16[24,2048]{1,0:T(8,128)(2,1)S(1)} %fusion.1.refs_0_), channel_id=1, source_target_pairs={{0,2},{1,3},{2,0},{3,1},{4,6},{5,7},{6,4},{7,5},{8,10},{9,11},{10,... | collective-permute-start | bytes 294920 | tf_op jit(solution)/shard_map/ppermute | solution.py:245
  4.5 0.1 collective-permute-start.2
  4.6 1.8 %collective-permute-start.3 = (bf16[24,2048]{1,0:T(8,128)(2,1)S(1)}, bf16[24,2048]{1,0:T(8,128)(2,1)S(1)}, u32[]{:S(2)}, u32[]{:S(2)}) collective-permute-start(bf16[24,2048]{1,0:T(8,128)(2,1)S(1)} %fusion.1.refs_0_), channel_id=1, source_target_pairs={{0,4},{1,5},{2,6},{3,7},{4,0},{5,1},{6,2},{7,3},{8,12},{9,13},{10,... | collective-permute-start | bytes 294920 | tf_op jit(solution)/shard_map/ppermute | solution.py:245
  6.4 0.0 collective-permute-start.4
  6.4 0.0 collective-permute-done.refs_1_
  6.4 2.6 %collective-permute-start.5 = (bf16[24,2048]{1,0:T(8,128)(2,1)S(1)}, bf16[24,2048]{1,0:T(8,128)(2,1)S(1)}, u32[]{:S(2)}, u32[]{:S(2)}) collective-permute-start(bf16[24,2048]{1,0:T(8,128)(2,1)S(1)} %fusion.1.refs_0_), channel_id=1, source_target_pairs={{0,6},{1,7},{2,4},{3,5},{4,2},{5,3},{6,0},{7,1},{8,14},{9,15},{10,... | collective-permute-start | bytes 294920 | tf_op jit(solution)/shard_map/ppermute | solution.py:245
  9.0 0.0 collective-permute-done.1.refs_2_
  9.0 0.9 %collective-permute-start.6 = (bf16[24,2048]{1,0:T(8,128)(2,1)S(1)}, bf16[24,2048]{1,0:T(8,128)(2,1)S(1)}, u32[]{:S(2)}, u32[]{:S(2)}) collective-permute-start(bf16[24,2048]{1,0:T(8,128)(2,1)S(1)} %fusion.1.refs_0_), channel_id=1, source_target_pairs={{0,7},{1,6},{2,5},{3,4},{4,3},{5,2},{6,1},{7,0},{8,15},{9,14},{10,... | collective-permute-start | bytes 294920 | tf_op jit(solution)/shard_map/ppermute | solution.py:245
  9.9 1.1 %reshape.39 = bf16[32,3,9,128]{3,2,1,0:T(8,128)(2,1)S(1)} reshape(bf16[32,3456]{1,0:T(8,128)(2,1)} %param.6) | data formatting | bytes 442368 | tf_op jit(solution)/shard_map/reshape | solution.py:283
  11.0 0.1 copy.11
  11.1 0.1 copy.12
  11.2 0.0 copy-start
  11.2 0.2 copy.13.refs_9_
  11.4 0.0 collective-permute-done.2.refs_3_
  11.4 0.0 collective-permute-done.3.refs_4_
  11.4 4.3 %collective-permute-done.4.refs_5_ = bf16[24,2048]{1,0:T(8,128)(2,1)S(1)} collective-permute-done((bf16[24,2048]{1,0:T(8,128)(2,1)S(1)}, bf16[24,2048]{1,0:T(8,128)(2,1)S(1)}, u32[]{:S(2)}, u32[]{:S(2)}) %collective-permute-start.4) | collective-permute-done | bytes 98336 | tf_op jit(solution)/shard_map/ppermute | solution.py:245
  15.7 0.0 collective-permute-done.5.refs_6_
  15.7 0.0 collective-permute-done.6.refs_7_
  15.7 0.0 copy-start.1
  15.7 8.0 %shard_map.75 = (bf16[32,2048]{1,0:T(8,128)(2,1)}, f32[16,2048]{1,0:T(8,128)S(1)}, bf16[64,2048]{1,0:T(8,128)(2,1)S(1)}, bf16[16,2048]{1,0:T(8,128)(2,1)S(1)}, b...) custom-call(bf16[24,2048]{1,0:T(8,128)(2,1)S(1)} %fusion.1.refs_0_, ...), custom_call_target="tpu_custom_call" | custom-call | flops 2264924160 | bytes 4194304 | tf_op jit(solution)/shard_map/pallas_call | solution.py:289
  23.8 1.5 %collective-permute-start.10 = (bf16[16,2048]{1,0:T(8,128)(2,1)S(1)}, bf16[16,2048]{1,0:T(8,128)(2,1)S(1)}, u32[]{:S(2)}, u32[]{:S(2)}) collective-permute-start(bf16[16,2048]{1,0:T(8,128)(2,1)S(1)} %get-tuple-element.33), channel_id=1, source_target_pairs={{0,4},{1,5},{2,6},{3,7},{4,0},{5,1},{6,2},{7,3},{8,12},{9,13},{10,... | collective-permute-start | bytes 196616 | tf_op jit(solution)/shard_map/ppermute | solution.py:245
  25.3 0.1 collective-permute-start.11
  25.4 2.6 %collective-permute-start.12 = (bf16[16,2048]{1,0:T(8,128)(2,1)S(1)}, bf16[16,2048]{1,0:T(8,128)(2,1)S(1)}, u32[]{:S(2)}, u32[]{:S(2)}) collective-permute-start(bf16[16,2048]{1,0:T(8,128)(2,1)S(1)} %get-tuple-element.35), channel_id=1, source_target_pairs={{0,6},{1,7},{2,4},{3,5},{4,2},{5,3},{6,0},{7,1},{8,14},{9,15},{10,... | collective-permute-start | bytes 196616 | tf_op jit(solution)/shard_map/ppermute | solution.py:245
  28.0 0.3 collective-permute-start.13
  28.2 0.2 collective-permute-start.7
  28.4 0.0 collective-permute-done.10.refs_4_
  28.4 1.6 %collective-permute-start.8 = (bf16[16,2048]{1,0:T(8,128)(2,1)S(1)}, bf16[16,2048]{1,0:T(8,128)(2,1)S(1)}, u32[]{:S(2)}, u32[]{:S(2)}) collective-permute-start(bf16[16,2048]{1,0:T(8,128)(2,1)S(1)} %get-tuple-element.31), channel_id=1, source_target_pairs={{0,2},{1,3},{2,0},{3,1},{4,6},{5,7},{6,4},{7,5},{8,10},{9,11},{10,... | collective-permute-start | bytes 196616 | tf_op jit(solution)/shard_map/ppermute | solution.py:245
  30.1 0.0 collective-permute-done.11.refs_5_
  30.1 3.4 %collective-permute-start.9 = (bf16[16,2048]{1,0:T(8,128)(2,1)S(1)}, bf16[16,2048]{1,0:T(8,128)(2,1)S(1)}, u32[]{:S(2)}, u32[]{:S(2)}) collective-permute-start(bf16[16,2048]{1,0:T(8,128)(2,1)S(1)} %get-tuple-element.32), channel_id=1, source_target_pairs={{0,3},{1,2},{2,1},{3,0},{4,7},{5,6},{6,5},{7,4},{8,11},{9,10},{10,... | collective-permute-start | bytes 196616 | tf_op jit(solution)/shard_map/ppermute | solution.py:245
  33.4 0.0 collective-permute-done.12.refs_6_
  33.5 1.6 %collective-permute-start.24 = (bf16[8,3456]{1,0:T(8,128)(2,1)S(1)}, bf16[8,3456]{1,0:T(8,128)(2,1)S(1)}, u32[]{:S(2)}, u32[]{:S(2)}) collective-permute-start(bf16[8,3456]{1,0:T(8,128)(2,1)S(1)} %get-tuple-element.49), channel_id=1, source_target_pairs={{0,8},{8,0},{16,24},{24,16},{1,9},{9,1},{17,25},{25,17},{2,10},{10... | collective-permute-start | bytes 165896 | tf_op jit(solution)/shard_map/ppermute | solution.py:245
  35.0 0.0 collective-permute-done.13.refs_7_
  35.0 2.6 %collective-permute-start.25 = (bf16[8,3456]{1,0:T(8,128)(2,1)S(1)}, bf16[8,3456]{1,0:T(8,128)(2,1)S(1)}, u32[]{:S(2)}, u32[]{:S(2)}) collective-permute-start(bf16[8,3456]{1,0:T(8,128)(2,1)S(1)} %get-tuple-element.50), channel_id=1, source_target_pairs={{0,16},{8,24},{16,0},{24,8},{1,17},{9,25},{17,1},{25,9},{2,18},{10... | collective-permute-start | bytes 165896 | tf_op jit(solution)/shard_map/ppermute | solution.py:245
  37.6 0.0 collective-permute-done.7.refs_1_
  37.6 0.2 collective-permute-start.26
  37.9 0.2 reshape.44
  38.1 0.1 copy.15.refs_10_
  38.2 0.0 collective-permute-done.8.refs_2_
  38.2 0.0 collective-permute-done.9.refs_3_
  38.2 2.0 %shard_map.76 = (bf16[8,2048]{1,0:T(8,128)(2,1)S(1)}, bf16[8,2048]{1,0:T(8,128)(2,1)S(1)}, bf16[8,2048]{1,0:T(8,128)(2,1)S(1)}, bf16[8,2048]{1,0:T(8,128)(2,1)S(...) custom-call(bf16[16,2048]{1,0:T(8,128)(2,1)S(1)} %get-tuple-element., ...), custom_call_target="tpu_custom_call" | custom-call | flops 226492416 | bytes 1048576 | tf_op jit(solution)/shard_map/pallas_call | solution.py:315
  40.2 0.1 collective-permute-start.14
  40.3 0.1 collective-permute-start.15
  40.4 0.0 collective-permute-done.24
  40.4 1.8 %collective-permute-start.16 = (bf16[8,2048]{1,0:T(8,128)(2,1)S(1)}, bf16[8,2048]{1,0:T(8,128)(2,1)S(1)}, u32[]{:S(2)}, u32[]{:S(2)}) collective-permute-start(bf16[8,2048]{1,0:T(8,128)(2,1)S(1)} %get-tuple-element.42), channel_id=1, source_target_pairs={{0,3},{1,2},{2,1},{3,0},{4,7},{5,6},{6,5},{7,4},{8,11},{9,10},{10,... | collective-permute-start | bytes 98312 | tf_op jit(solution)/shard_map/ppermute | solution.py:245
  42.2 0.0 collective-permute-done.25
  42.2 1.4 %collective-permute-done.26 = bf16[8,3456]{1,0:T(8,128)(2,1)S(1)} collective-permute-done((bf16[8,3456]{1,0:T(8,128)(2,1)S(1)}, bf16[8,3456]{1,0:T(8,128)(2,1)S(1)}, u32[]{:S(2)}, u32[]{:S(2)}) %collective-permute-start.26) | collective-permute-done | bytes 55328 | tf_op jit(solution)/shard_map/ppermute | solution.py:245
  43.6 0.1 collective-permute-start.27
  43.7 1.2 %collective-permute-start.17 = (bf16[8,2048]{1,0:T(8,128)(2,1)S(1)}, bf16[8,2048]{1,0:T(8,128)(2,1)S(1)}, u32[]{:S(2)}, u32[]{:S(2)}) collective-permute-start(bf16[8,2048]{1,0:T(8,128)(2,1)S(1)} %get-tuple-element.43), channel_id=1, source_target_pairs={{0,4},{1,5},{2,6},{3,7},{4,0},{5,1},{6,2},{7,3},{8,12},{9,13},{10,... | collective-permute-start | bytes 98312 | tf_op jit(solution)/shard_map/ppermute | solution.py:245
  44.9 0.0 collective-permute-done.14
  44.9 0.8 %collective-permute-start.19 = (bf16[8,2048]{1,0:T(8,128)(2,1)S(1)}, bf16[8,2048]{1,0:T(8,128)(2,1)S(1)}, u32[]{:S(2)}, u32[]{:S(2)}) collective-permute-start(bf16[8,2048]{1,0:T(8,128)(2,1)S(1)} %get-tuple-element.45), channel_id=1, source_target_pairs={{0,6},{1,7},{2,4},{3,5},{4,2},{5,3},{6,0},{7,1},{8,14},{9,15},{10,... | collective-permute-start | bytes 98312 | tf_op jit(solution)/shard_map/ppermute | solution.py:245
  45.7 2.5 %collective-permute-start.20 = (bf16[8,2048]{1,0:T(8,128)(2,1)S(1)}, bf16[8,2048]{1,0:T(8,128)(2,1)S(1)}, u32[]{:S(2)}, u32[]{:S(2)}) collective-permute-start(bf16[8,2048]{1,0:T(8,128)(2,1)S(1)} %get-tuple-element.46), channel_id=1, source_target_pairs={{0,7},{1,6},{2,5},{3,4},{4,3},{5,2},{6,1},{7,0},{8,15},{9,14},{10,... | collective-permute-start | bytes 98312 | tf_op jit(solution)/shard_map/ppermute | solution.py:245
  48.2 2.7 %collective-permute-start.28 = (bf16[8,3456]{1,0:T(8,128)(2,1)S(1)}, bf16[8,3456]{1,0:T(8,128)(2,1)S(1)}, u32[]{:S(2)}, u32[]{:S(2)}) collective-permute-start(bf16[8,3456]{1,0:T(8,128)(2,1)S(1)} %add_convert_fusion.refs_0_), channel_id=1, source_target_pairs={{0,16},{8,24},{16,0},{24,8},{1,17},{9,25},{17,1},{25,9},{2,18},{10... | collective-permute-start | bytes 165896 | tf_op jit(solution)/shard_map/ppermute | solution.py:245
  50.9 1.6 %collective-permute-start.29 = (bf16[8,3456]{1,0:T(8,128)(2,1)S(1)}, bf16[8,3456]{1,0:T(8,128)(2,1)S(1)}, u32[]{:S(2)}, u32[]{:S(2)}) collective-permute-start(bf16[8,3456]{1,0:T(8,128)(2,1)S(1)} %add_convert_fusion.refs_0_), channel_id=1, source_target_pairs={{0,24},{8,16},{16,8},{24,0},{1,25},{9,17},{17,9},{25,1},{2,26},{10... | collective-permute-start | bytes 165896 | tf_op jit(solution)/shard_map/ppermute | solution.py:245
  52.5 0.0 collective-permute-done.20
  52.5 2.8 %collective-permute-start.22 = (bf16[16,1728]{1,0:T(8,128)(2,1)S(1)}, bf16[16,1728]{1,0:T(8,128)(2,1)S(1)}, u32[]{:S(2)}, u32[]{:S(2)}) collective-permute-start(bf16[16,1728]{1,0:T(8,128)(2,1)S(1)} %get-tuple-element.47), channel_id=1, source_target_pairs={{0,16},{8,24},{16,0},{24,8},{1,17},{9,25},{17,1},{25,9},{2,18},{10... | collective-permute-start | bytes 165896 | tf_op jit(solution)/shard_map/ppermute | solution.py:245
  55.3 1.6 %collective-permute-start.23 = (bf16[16,1728]{1,0:T(8,128)(2,1)S(1)}, bf16[16,1728]{1,0:T(8,128)(2,1)S(1)}, u32[]{:S(2)}, u32[]{:S(2)}) collective-permute-start(bf16[16,1728]{1,0:T(8,128)(2,1)S(1)} %get-tuple-element.47), channel_id=1, source_target_pairs={{0,24},{8,16},{16,8},{24,0},{1,25},{9,17},{17,9},{25,1},{2,26},{10... | collective-permute-start | bytes 165896 | tf_op jit(solution)/shard_map/ppermute | solution.py:245
  56.9 0.7 %fusion.2 = bf16[8,1,2048]{2,0,1:T(8,128)(2,1)} fusion(bf16[8,2048]{1,0:T(8,128)(2,1)S(1)} %collective-permute-done.20, bf16[8,2048]{1,0:T(8,128)(2,1)S(1)} %collective-permute-done.19, bf16[8,2048]{1,0:T(8,128)(2,1)S(1)} %collective-permute-done.18, bf16[8,2048]{1,0:T(8,128)(2,1)S(1)} %collective-permute-done.17, ...), kind=kLoop, calls=%fused_computation.7 | loop fusion | flops 262144 | bytes 294912 | tf_op jit(solution)/shard_map/reshape | solution.py:348
  57.5 0.0 collective-permute-done.29.refs_3_
  57.5 0.8 %shard_map.77 = f32[4,8,3456]{2,1,0:T(8,128)} custom-call(bf16[8,3456]{1,0:T(8,128)(2,1)S(1)} %add_convert_fusion.refs_0_, bf16[8,3456]{1,0:T(8,128)(2,1)S(1)} %collective-permute-done.27.refs_1_, bf16[8,3456]{1,0:T(8,128)(2,1)S(1)} %collective-permute-done.28.refs_2_, bf16[8,3456]{1,0:T(8,128)(2,1)S(1)} %collective-permute-done.29.refs_3_), custom_call_target="tpu_custom_call" | custom-call | bytes 1048576 | tf_op jit(solution)/shard_map/pallas_call | solution.py:338
  58.3 1.8 %collective-permute-done.22 = bf16[16,1728]{1,0:T(8,128)(2,1)S(1)} collective-permute-done((bf16[16,1728]{1,0:T(8,128)(2,1)S(1)}, bf16[16,1728]{1,0:T(8,128)(2,1)S(1)}, u32[]{:S(2)}, u32[]{:S(2)}) %collective-permute-start.22) | collective-permute-done | bytes 55328 | tf_op jit(solution)/shard_map/ppermute | solution.py:245
  60.1 1.3 %collective-permute-done.23 = bf16[16,1728]{1,0:T(8,128)(2,1)S(1)} collective-permute-done((bf16[16,1728]{1,0:T(8,128)(2,1)S(1)}, bf16[16,1728]{1,0:T(8,128)(2,1)S(1)}, u32[]{:S(2)}, u32[]{:S(2)}) %collective-permute-start.23) | collective-permute-done | bytes 55328 | tf_op jit(solution)/shard_map/ppermute | solution.py:245
  61.4 0.7 %add_multiply_fusion = f32[16,1728]{1,0:T(8,128)} fusion(bf16[16,1728]{1,0:T(8,128)(2,1)S(1)} %collective-permute-done.23, bf16[16,1728]{1,0:T(8,128)(2,1)S(1)} %collective-permute-done.22, bf16[16,1728]{1,0:T(8,128)(2,1)S(1)} %collective-permute-done.21, bf16[16,1728]{1,0:T(8,128)(2,1)S(1)} %get-tuple-element.47), kind=kLoop, calls=%fused_computation.3 | loop fusion | flops 221184 | bytes 331776 | tf_op jit(solution)/shard_map/mul | solution.py:349
  (15 shorter events, 0.1 us)
Async XLA Ops:
  1.5 4.9 %collective-permute-start = (bf16[24,2048]{1,0:T(8,128)(2,1)S(1)}, bf16[24,2048]{1,0:T(8,128)(2,1)S(1)}, u32[]{:S(2)}, u32[]{:S(2)}) collective-permute-start(bf16[24,2048]{1,0:T(8,128)(2,1)S(1)} %fusion.1.refs_0_), channel_id=1, source_target_pairs={{0,1},{1,0},{2,3},{3,2},{4,5},{5,4},{6,7},{7,6},{8,9},{9,8},{10,11... | collective-permute-start | bytes 294920 | tf_op jit(solution)/shard_map/ppermute | solution.py:245
  2.0 7.0 %collective-permute-start.1 = (bf16[24,2048]{1,0:T(8,128)(2,1)S(1)}, bf16[24,2048]{1,0:T(8,128)(2,1)S(1)}, u32[]{:S(2)}, u32[]{:S(2)}) collective-permute-start(bf16[24,2048]{1,0:T(8,128)(2,1)S(1)} %fusion.1.refs_0_), channel_id=1, source_target_pairs={{0,2},{1,3},{2,0},{3,1},{4,6},{5,7},{6,4},{7,5},{8,10},{9,11},{10,... | collective-permute-start | bytes 294920 | tf_op jit(solution)/shard_map/ppermute | solution.py:245
  4.5 6.9 %collective-permute-start.2 = (bf16[24,2048]{1,0:T(8,128)(2,1)S(1)}, bf16[24,2048]{1,0:T(8,128)(2,1)S(1)}, u32[]{:S(2)}, u32[]{:S(2)}) collective-permute-start(bf16[24,2048]{1,0:T(8,128)(2,1)S(1)} %fusion.1.refs_0_), channel_id=1, source_target_pairs={{0,3},{1,2},{2,1},{3,0},{4,7},{5,6},{6,5},{7,4},{8,11},{9,10},{10,... | collective-permute-start | bytes 294920 | tf_op jit(solution)/shard_map/ppermute | solution.py:245
  4.6 6.8 %collective-permute-start.3 = (bf16[24,2048]{1,0:T(8,128)(2,1)S(1)}, bf16[24,2048]{1,0:T(8,128)(2,1)S(1)}, u32[]{:S(2)}, u32[]{:S(2)}) collective-permute-start(bf16[24,2048]{1,0:T(8,128)(2,1)S(1)} %fusion.1.refs_0_), channel_id=1, source_target_pairs={{0,4},{1,5},{2,6},{3,7},{4,0},{5,1},{6,2},{7,3},{8,12},{9,13},{10,... | collective-permute-start | bytes 294920 | tf_op jit(solution)/shard_map/ppermute | solution.py:245
  6.4 9.3 %collective-permute-start.4 = (bf16[24,2048]{1,0:T(8,128)(2,1)S(1)}, bf16[24,2048]{1,0:T(8,128)(2,1)S(1)}, u32[]{:S(2)}, u32[]{:S(2)}) collective-permute-start(bf16[24,2048]{1,0:T(8,128)(2,1)S(1)} %fusion.1.refs_0_), channel_id=1, source_target_pairs={{0,5},{1,4},{2,7},{3,6},{4,1},{5,0},{6,3},{7,2},{8,13},{9,12},{10,... | collective-permute-start | bytes 294920 | tf_op jit(solution)/shard_map/ppermute | solution.py:245
  6.4 9.3 %collective-permute-start.5 = (bf16[24,2048]{1,0:T(8,128)(2,1)S(1)}, bf16[24,2048]{1,0:T(8,128)(2,1)S(1)}, u32[]{:S(2)}, u32[]{:S(2)}) collective-permute-start(bf16[24,2048]{1,0:T(8,128)(2,1)S(1)} %fusion.1.refs_0_), channel_id=1, source_target_pairs={{0,6},{1,7},{2,4},{3,5},{4,2},{5,3},{6,0},{7,1},{8,14},{9,15},{10,... | collective-permute-start | bytes 294920 | tf_op jit(solution)/shard_map/ppermute | solution.py:245
  9.0 6.7 %collective-permute-start.6 = (bf16[24,2048]{1,0:T(8,128)(2,1)S(1)}, bf16[24,2048]{1,0:T(8,128)(2,1)S(1)}, u32[]{:S(2)}, u32[]{:S(2)}) collective-permute-start(bf16[24,2048]{1,0:T(8,128)(2,1)S(1)} %fusion.1.refs_0_), channel_id=1, source_target_pairs={{0,7},{1,6},{2,5},{3,4},{4,3},{5,2},{6,1},{7,0},{8,15},{9,14},{10,... | collective-permute-start | bytes 294920 | tf_op jit(solution)/shard_map/ppermute | solution.py:245
  11.2 4.5 %copy-start = (bf16[32,1,2048]{2,0,1:T(8,128)(2,1)S(1)}, bf16[32,1,2048]{2,0,1:T(8,128)(2,1)}, u32[]{:S(2)}) copy-start(bf16[32,1,2048]{2,0,1:T(8,128)(2,1)} %param.7) | copy-start | bytes 393220
  15.7 22.1 %copy-start.1 = (bf16[16,1728]{1,0:T(8,128)(2,1)S(1)}, bf16[16,1728]{1,0:T(8,128)(2,1)}, u32[]{:S(2)}) copy-start(bf16[16,1728]{1,0:T(8,128)(2,1)} %param.5) | copy-start | bytes 165892
  23.8 4.6 %collective-permute-start.10 = (bf16[16,2048]{1,0:T(8,128)(2,1)S(1)}, bf16[16,2048]{1,0:T(8,128)(2,1)S(1)}, u32[]{:S(2)}, u32[]{:S(2)}) collective-permute-start(bf16[16,2048]{1,0:T(8,128)(2,1)S(1)} %get-tuple-element.33), channel_id=1, source_target_pairs={{0,4},{1,5},{2,6},{3,7},{4,0},{5,1},{6,2},{7,3},{8,12},{9,13},{10,... | collective-permute-start | bytes 196616 | tf_op jit(solution)/shard_map/ppermute | solution.py:245
  25.3 4.8 %collective-permute-start.11 = (bf16[16,2048]{1,0:T(8,128)(2,1)S(1)}, bf16[16,2048]{1,0:T(8,128)(2,1)S(1)}, u32[]{:S(2)}, u32[]{:S(2)}) collective-permute-start(bf16[16,2048]{1,0:T(8,128)(2,1)S(1)} %get-tuple-element.34), channel_id=1, source_target_pairs={{0,5},{1,4},{2,7},{3,6},{4,1},{5,0},{6,3},{7,2},{8,13},{9,12},{10,... | collective-permute-start | bytes 196616 | tf_op jit(solution)/shard_map/ppermute | solution.py:245
  25.4 8.1 %collective-permute-start.12 = (bf16[16,2048]{1,0:T(8,128)(2,1)S(1)}, bf16[16,2048]{1,0:T(8,128)(2,1)S(1)}, u32[]{:S(2)}, u32[]{:S(2)}) collective-permute-start(bf16[16,2048]{1,0:T(8,128)(2,1)S(1)} %get-tuple-element.35), channel_id=1, source_target_pairs={{0,6},{1,7},{2,4},{3,5},{4,2},{5,3},{6,0},{7,1},{8,14},{9,15},{10,... | collective-permute-start | bytes 196616 | tf_op jit(solution)/shard_map/ppermute | solution.py:245
  28.0 7.1 %collective-permute-start.13 = (bf16[16,2048]{1,0:T(8,128)(2,1)S(1)}, bf16[16,2048]{1,0:T(8,128)(2,1)S(1)}, u32[]{:S(2)}, u32[]{:S(2)}) collective-permute-start(bf16[16,2048]{1,0:T(8,128)(2,1)S(1)} %get-tuple-element.36), channel_id=1, source_target_pairs={{0,7},{1,6},{2,5},{3,4},{4,3},{5,2},{6,1},{7,0},{8,15},{9,14},{10,... | collective-permute-start | bytes 196616 | tf_op jit(solution)/shard_map/ppermute | solution.py:245
  28.2 9.4 %collective-permute-start.7 = (bf16[16,2048]{1,0:T(8,128)(2,1)S(1)}, bf16[16,2048]{1,0:T(8,128)(2,1)S(1)}, u32[]{:S(2)}, u32[]{:S(2)}) collective-permute-start(bf16[16,2048]{1,0:T(8,128)(2,1)S(1)} %get-tuple-element.30), channel_id=1, source_target_pairs={{0,1},{1,0},{2,3},{3,2},{4,5},{5,4},{6,7},{7,6},{8,9},{9,8},{10,11... | collective-permute-start | bytes 196616 | tf_op jit(solution)/shard_map/ppermute | solution.py:245
  28.4 9.8 %collective-permute-start.8 = (bf16[16,2048]{1,0:T(8,128)(2,1)S(1)}, bf16[16,2048]{1,0:T(8,128)(2,1)S(1)}, u32[]{:S(2)}, u32[]{:S(2)}) collective-permute-start(bf16[16,2048]{1,0:T(8,128)(2,1)S(1)} %get-tuple-element.31), channel_id=1, source_target_pairs={{0,2},{1,3},{2,0},{3,1},{4,6},{5,7},{6,4},{7,5},{8,10},{9,11},{10,... | collective-permute-start | bytes 196616 | tf_op jit(solution)/shard_map/ppermute | solution.py:245
  30.1 8.1 %collective-permute-start.9 = (bf16[16,2048]{1,0:T(8,128)(2,1)S(1)}, bf16[16,2048]{1,0:T(8,128)(2,1)S(1)}, u32[]{:S(2)}, u32[]{:S(2)}) collective-permute-start(bf16[16,2048]{1,0:T(8,128)(2,1)S(1)} %get-tuple-element.32), channel_id=1, source_target_pairs={{0,3},{1,2},{2,1},{3,0},{4,7},{5,6},{6,5},{7,4},{8,11},{9,10},{10,... | collective-permute-start | bytes 196616 | tf_op jit(solution)/shard_map/ppermute | solution.py:245
  33.5 6.9 %collective-permute-start.24 = (bf16[8,3456]{1,0:T(8,128)(2,1)S(1)}, bf16[8,3456]{1,0:T(8,128)(2,1)S(1)}, u32[]{:S(2)}, u32[]{:S(2)}) collective-permute-start(bf16[8,3456]{1,0:T(8,128)(2,1)S(1)} %get-tuple-element.49), channel_id=1, source_target_pairs={{0,8},{8,0},{16,24},{24,16},{1,9},{9,1},{17,25},{25,17},{2,10},{10... | collective-permute-start | bytes 165896 | tf_op jit(solution)/shard_map/ppermute | solution.py:245
  35.0 7.2 %collective-permute-start.25 = (bf16[8,3456]{1,0:T(8,128)(2,1)S(1)}, bf16[8,3456]{1,0:T(8,128)(2,1)S(1)}, u32[]{:S(2)}, u32[]{:S(2)}) collective-permute-start(bf16[8,3456]{1,0:T(8,128)(2,1)S(1)} %get-tuple-element.50), channel_id=1, source_target_pairs={{0,16},{8,24},{16,0},{24,8},{1,17},{9,25},{17,1},{25,9},{2,18},{10... | collective-permute-start | bytes 165896 | tf_op jit(solution)/shard_map/ppermute | solution.py:245
  37.6 6.0 %collective-permute-start.26 = (bf16[8,3456]{1,0:T(8,128)(2,1)S(1)}, bf16[8,3456]{1,0:T(8,128)(2,1)S(1)}, u32[]{:S(2)}, u32[]{:S(2)}) collective-permute-start(bf16[8,3456]{1,0:T(8,128)(2,1)S(1)} %get-tuple-element.51), channel_id=1, source_target_pairs={{0,24},{8,16},{16,8},{24,0},{1,25},{9,17},{17,9},{25,1},{2,26},{10... | collective-permute-start | bytes 165896 | tf_op jit(solution)/shard_map/ppermute | solution.py:245
  40.2 4.7 %collective-permute-start.14 = (bf16[8,2048]{1,0:T(8,128)(2,1)S(1)}, bf16[8,2048]{1,0:T(8,128)(2,1)S(1)}, u32[]{:S(2)}, u32[]{:S(2)}) collective-permute-start(bf16[8,2048]{1,0:T(8,128)(2,1)S(1)} %get-tuple-element.40), channel_id=1, source_target_pairs={{0,1},{1,0},{2,3},{3,2},{4,5},{5,4},{6,7},{7,6},{8,9},{9,8},{10,11... | collective-permute-start | bytes 98312 | tf_op jit(solution)/shard_map/ppermute | solution.py:245
  40.3 4.6 %collective-permute-start.15 = (bf16[8,2048]{1,0:T(8,128)(2,1)S(1)}, bf16[8,2048]{1,0:T(8,128)(2,1)S(1)}, u32[]{:S(2)}, u32[]{:S(2)}) collective-permute-start(bf16[8,2048]{1,0:T(8,128)(2,1)S(1)} %get-tuple-element.41), channel_id=1, source_target_pairs={{0,2},{1,3},{2,0},{3,1},{4,6},{5,7},{6,4},{7,5},{8,10},{9,11},{10,... | collective-permute-start | bytes 98312 | tf_op jit(solution)/shard_map/ppermute | solution.py:245
  40.4 5.3 %collective-permute-start.16 = (bf16[8,2048]{1,0:T(8,128)(2,1)S(1)}, bf16[8,2048]{1,0:T(8,128)(2,1)S(1)}, u32[]{:S(2)}, u32[]{:S(2)}) collective-permute-start(bf16[8,2048]{1,0:T(8,128)(2,1)S(1)} %get-tuple-element.42), channel_id=1, source_target_pairs={{0,3},{1,2},{2,1},{3,0},{4,7},{5,6},{6,5},{7,4},{8,11},{9,10},{10,... | collective-permute-start | bytes 98312 | tf_op jit(solution)/shard_map/ppermute | solution.py:245
  43.6 11.7 %collective-permute-start.27 = (bf16[8,3456]{1,0:T(8,128)(2,1)S(1)}, bf16[8,3456]{1,0:T(8,128)(2,1)S(1)}, u32[]{:S(2)}, u32[]{:S(2)}) collective-permute-start(bf16[8,3456]{1,0:T(8,128)(2,1)S(1)} %add_convert_fusion.refs_0_), channel_id=1, source_target_pairs={{0,8},{8,0},{16,24},{24,16},{1,9},{9,1},{17,25},{25,17},{2,10},{10... | collective-permute-start | bytes 165896 | tf_op jit(solution)/shard_map/ppermute | solution.py:245
  43.7 4.5 %collective-permute-start.17 = (bf16[8,2048]{1,0:T(8,128)(2,1)S(1)}, bf16[8,2048]{1,0:T(8,128)(2,1)S(1)}, u32[]{:S(2)}, u32[]{:S(2)}) collective-permute-start(bf16[8,2048]{1,0:T(8,128)(2,1)S(1)} %get-tuple-element.43), channel_id=1, source_target_pairs={{0,4},{1,5},{2,6},{3,7},{4,0},{5,1},{6,2},{7,3},{8,12},{9,13},{10,... | collective-permute-start | bytes 98312 | tf_op jit(solution)/shard_map/ppermute | solution.py:245
  44.9 6.0 %collective-permute-start.18 = (bf16[8,2048]{1,0:T(8,128)(2,1)S(1)}, bf16[8,2048]{1,0:T(8,128)(2,1)S(1)}, u32[]{:S(2)}, u32[]{:S(2)}) collective-permute-start(bf16[8,2048]{1,0:T(8,128)(2,1)S(1)} %get-tuple-element.44), channel_id=1, source_target_pairs={{0,5},{1,4},{2,7},{3,6},{4,1},{5,0},{6,3},{7,2},{8,13},{9,12},{10,... | collective-permute-start | bytes 98312 | tf_op jit(solution)/shard_map/ppermute | solution.py:245
  44.9 7.6 %collective-permute-start.19 = (bf16[8,2048]{1,0:T(8,128)(2,1)S(1)}, bf16[8,2048]{1,0:T(8,128)(2,1)S(1)}, u32[]{:S(2)}, u32[]{:S(2)}) collective-permute-start(bf16[8,2048]{1,0:T(8,128)(2,1)S(1)} %get-tuple-element.45), channel_id=1, source_target_pairs={{0,6},{1,7},{2,4},{3,5},{4,2},{5,3},{6,0},{7,1},{8,14},{9,15},{10,... | collective-permute-start | bytes 98312 | tf_op jit(solution)/shard_map/ppermute | solution.py:245
  45.7 6.8 %collective-permute-start.20 = (bf16[8,2048]{1,0:T(8,128)(2,1)S(1)}, bf16[8,2048]{1,0:T(8,128)(2,1)S(1)}, u32[]{:S(2)}, u32[]{:S(2)}) collective-permute-start(bf16[8,2048]{1,0:T(8,128)(2,1)S(1)} %get-tuple-element.46), channel_id=1, source_target_pairs={{0,7},{1,6},{2,5},{3,4},{4,3},{5,2},{6,1},{7,0},{8,15},{9,14},{10,... | collective-permute-start | bytes 98312 | tf_op jit(solution)/shard_map/ppermute | solution.py:245
  48.2 9.4 %collective-permute-start.28 = (bf16[8,3456]{1,0:T(8,128)(2,1)S(1)}, bf16[8,3456]{1,0:T(8,128)(2,1)S(1)}, u32[]{:S(2)}, u32[]{:S(2)}) collective-permute-start(bf16[8,3456]{1,0:T(8,128)(2,1)S(1)} %add_convert_fusion.refs_0_), channel_id=1, source_target_pairs={{0,16},{8,24},{16,0},{24,8},{1,17},{9,25},{17,1},{25,9},{2,18},{10... | collective-permute-start | bytes 165896 | tf_op jit(solution)/shard_map/ppermute | solution.py:245
  50.9 6.7 %collective-permute-start.29 = (bf16[8,3456]{1,0:T(8,128)(2,1)S(1)}, bf16[8,3456]{1,0:T(8,128)(2,1)S(1)}, u32[]{:S(2)}, u32[]{:S(2)}) collective-permute-start(bf16[8,3456]{1,0:T(8,128)(2,1)S(1)} %add_convert_fusion.refs_0_), channel_id=1, source_target_pairs={{0,24},{8,16},{16,8},{24,0},{1,25},{9,17},{17,9},{25,1},{2,26},{10... | collective-permute-start | bytes 165896 | tf_op jit(solution)/shard_map/ppermute | solution.py:245
  52.5 5.9 %collective-permute-start.21 = (bf16[16,1728]{1,0:T(8,128)(2,1)S(1)}, bf16[16,1728]{1,0:T(8,128)(2,1)S(1)}, u32[]{:S(2)}, u32[]{:S(2)}) collective-permute-start(bf16[16,1728]{1,0:T(8,128)(2,1)S(1)} %get-tuple-element.47), channel_id=1, source_target_pairs={{0,8},{8,0},{16,24},{24,16},{1,9},{9,1},{17,25},{25,17},{2,10},{10... | collective-permute-start | bytes 165896 | tf_op jit(solution)/shard_map/ppermute | solution.py:245
  52.5 7.6 %collective-permute-start.22 = (bf16[16,1728]{1,0:T(8,128)(2,1)S(1)}, bf16[16,1728]{1,0:T(8,128)(2,1)S(1)}, u32[]{:S(2)}, u32[]{:S(2)}) collective-permute-start(bf16[16,1728]{1,0:T(8,128)(2,1)S(1)} %get-tuple-element.47), channel_id=1, source_target_pairs={{0,16},{8,24},{16,0},{24,8},{1,17},{9,25},{17,1},{25,9},{2,18},{10... | collective-permute-start | bytes 165896 | tf_op jit(solution)/shard_map/ppermute | solution.py:245
  55.3 6.1 %collective-permute-start.23 = (bf16[16,1728]{1,0:T(8,128)(2,1)S(1)}, bf16[16,1728]{1,0:T(8,128)(2,1)S(1)}, u32[]{:S(2)}, u32[]{:S(2)}) collective-permute-start(bf16[16,1728]{1,0:T(8,128)(2,1)S(1)} %get-tuple-element.47), channel_id=1, source_target_pairs={{0,24},{8,16},{16,8},{24,0},{1,25},{9,17},{17,9},{25,1},{2,26},{10... | collective-permute-start | bytes 165896 | tf_op jit(solution)/shard_map/ppermute | solution.py:245
where the time goes:
time: 62.2 us; the launch traced here: 62 us
  starting transfers between devices  37.6 us (60%)
  Pallas kernels  10.9 us (18%)
  waiting for transfers between devices  8.76 us (14%)
  other arithmetic  2.2 us (4%)
  local copies, waits for them, and re-layouts  1.77 us (3%)
  between operations  0.81 us (1%)
    ppermute x30, starting transfers between devices, swap(): return lax.ppermute(value, axis, [(i, i ^ k) for i in range(n)])  37.6 us
    ppermute x30, waiting for transfers between devices, swap(): return lax.ppermute(value, axis, [(i, i ^ k) for i in range(n)])  8.76 us
    pallas_call x1, Pallas kernels, local(): call(functools.partial(forward_kernel, n_mp, n_sample, c0), [sds((f2, cel...  8.03 us
    pallas_call x1, Pallas kernels, local(): call(functools.partial(backward_kernel, n_mp), [sds((rows_in, cells), BF1...  2.03 us
  transfers between devices with their start and end apart: 30, of which 4 were waited for; matrix products, arithmetic and copies ran while one was open for 4% of the time, Pallas kernels for 5%

commit v1 on v0

--- a/solution.py
+++ b/solution.py
@@ -65,16 +65,10 @@
 
 
 def forward_kernel(n_mp, n_sample, c0, *refs):
-    pieces = refs[:n_mp]
-    w2r_ref, w2b_ref, cot_ref = refs[n_mp : n_mp + 3]
-    outs = refs[n_mp + 3 :]
-    feat_ref, pre_ref, vol_ref = outs[:3]
-    part_refs = outs[3 : 3 + n_mp]
-    grad_refs = outs[3 + n_mp : 3 + n_mp + n_sample]
-    vs, w1s, v3, w1r, hid, pre, d9, part, grad = outs[3 + n_mp + n_sample :]
+    pieces, w2r_ref, w2b_ref, cot_ref, feat_ref, pre_ref, vol_ref, part_ref, grad_ref = refs[:9]
+    vs, w1s, v3, w1r, hid, pre, d9 = refs[9:]
 
     me = lax.axis_index("mp")
-    at = lax.axis_index("sample")
     f1 = w1s.shape[1]
     c1 = n_mp * f1
     f2, cells = cot_ref.shape
@@ -84,10 +78,9 @@
     grid_xy = lane_grid(chunk)
 
     for k in range(n_mp):
-        piece = pieces[k][...].astype(F32)
-        slot = me ^ k
-        w1s[slot] = piece[:f1]
-        vs[slot] = piece[f1:, :cells]
+        piece = pieces[k].astype(F32)
+        w1s[k] = piece[:f1]
+        vs[k] = piece[f1:, :cells]
 
     lane = lax.broadcasted_iota(jnp.int32, (1, pitch), 1)
     for dz in range(3):
@@ -156,29 +149,21 @@
         base = pl.multiple_of(step * chunk, chunk)
         rhs = jnp.concatenate([d9[:, pl.ds(base + (2 - dz) * PLANE, chunk)] for dz in range(3)], axis=0)
         z = dot(w2b_ref[...], rhs)
-        part[:, :, pl.ds(base, chunk)] = z.reshape(n_mp, f1, chunk)
+        part_ref[:, :, pl.ds(base, chunk)] = z.astype(BF16).reshape(n_mp, f1, chunk)
         return carry
 
     lax.fori_loop(0, steps, data_conv, 0)
-    for k in range(n_mp):
-        part_refs[k][...] = part[me ^ k].astype(BF16)
 
     rows = f2 // n_sample
     for dz in range(3):
         g = dot_nt(d9[:, (2 - dz) * PLANE : (2 - dz) * PLANE + cells], hid[:, PLANE : PLANE + cells])
         for k in range(9):
             t = dz * 9 + k
-            grad[:, :, t * c1 : (t + 1) * c1] = g[k * f2 : (k + 1) * f2].reshape(n_sample, rows, c1)
-    for k in range(n_sample):
-        grad_refs[k][...] = grad[at ^ k].astype(BF16)
+            grad_ref[:, :, t * c1 : (t + 1) * c1] = g[k * f2 : (k + 1) * f2].reshape(n_sample, rows, c1).astype(BF16)
 
 
 def backward_kernel(n_mp, *refs):
-    parts = refs[:n_mp]
-    pre_ref, vol_ref, w1b_ref = refs[n_mp : n_mp + 3]
-    out_refs = refs[n_mp + 3 : 2 * n_mp + 3]
-    grad_ref, d9, part = refs[2 * n_mp + 3 :]
-    me = lax.axis_index("mp")
+    parts, pre_ref, vol_ref, w1b_ref, out_ref, grad_ref, d9 = refs
     f1, cells = pre_ref.shape
     c0 = vol_ref.shape[0]
     chunk = chunk_of(cells)
@@ -191,9 +176,9 @@
 
     def take(step, carry):
         base = pl.multiple_of(step * chunk, chunk)
-        total = parts[0][:, pl.ds(base, chunk)].astype(F32)
+        total = parts[0, :, pl.ds(base, chunk)].astype(F32)
         for k in range(1, n_mp):
-            total = total + parts[k][:, pl.ds(base, chunk)].astype(F32)
+            total = total + parts[k, :, pl.ds(base, chunk)].astype(F32)
         v = pre_ref[:, pl.ds(base, chunk)]
         s = sigmoid(v)
         delta = (total * (s * (1.0 + v * (1.0 - s)))).astype(BF16).astype(F32)
@@ -209,12 +194,10 @@
         for dz in range(3):
             term = dot(w1b_ref[dz], d9[:, pl.ds(base + (2 - dz) * PLANE, chunk)])
             z = term if z is None else z + term
-        part[:, :, pl.ds(base, chunk)] = z.reshape(n_mp, c0 // n_mp, chunk)
+        out_ref[:, :, pl.ds(base, chunk)] = z.reshape(n_mp, c0 // n_mp, chunk).astype(BF16)
         return carry
 
     lax.fori_loop(0, steps, data_conv, 0)
-    for k in range(n_mp):
-        out_refs[k][...] = part[me ^ k].astype(BF16)
 
     reps = max(1, 128 // c0)
     span = reps * c0
@@ -233,18 +216,6 @@
         grad_ref[:, t * c0 : t * c0 + width] = merged[:, :width].astype(BF16)
 
 
-def place_kernel(n_sample, scale, *refs):
-    out_ref = refs[n_sample]
-    at = lax.axis_index("sample")
-    for k in range(n_sample):
-        out_ref[at ^ k] = refs[k][...].astype(F32) * scale
-
-
-def swap(value, axis, k):
-    n = lax.axis_size(axis)
-    return lax.ppermute(value, axis, [(i, i ^ k) for i in range(n)])
-
-
 def call(kernel, out_shape, scratch, flops, nbytes):
     return pl.pallas_call(
         kernel,
@@ -278,7 +249,7 @@
         ],
         axis=0,
     )
-    pieces = [piece] + [swap(piece, "mp", k) for k in range(1, n_mp)]
+    pieces = lax.all_gather(piece, "mp", axis=0, tiled=False)
 
     w2t = w_second.reshape(f2, 3, 9, c1)
     w2r = jnp.transpose(w2t, (2, 0, 1, 3)).reshape(9 * f2, 3 * c1)
@@ -286,11 +257,15 @@
     w1b = jnp.transpose(w_first.reshape(f1, 3, 9, c0), (1, 3, 2, 0)).reshape(3, c0, 9 * f1)
 
     sds = jax.ShapeDtypeStruct
-    outs = call(
+    features, pre_own, vol_all, parts, grads = call(
         functools.partial(forward_kernel, n_mp, n_sample, c0),
-        [sds((f2, cells), BF16), sds((f1, cells), F32), sds((c0, cells), BF16)]
-        + [sds((f1, cells), BF16)] * n_mp
-        + [sds((f2 // n_sample, 27 * c1), BF16)] * n_sample,
+        [
+            sds((f2, cells), BF16),
+            sds((f1, cells), F32),
+            sds((c0, cells), BF16),
+            sds((n_mp, f1, cells), BF16),
+            sds((n_sample, f2 // n_sample, 27 * c1), BF16),
+        ],
         [
             pltpu.VMEM((n_mp, rows_in, cells), F32),
             pltpu.VMEM((n_mp, f1, wide), F32),
@@ -299,55 +274,37 @@
             pltpu.VMEM((c1, padded), BF16),
             pltpu.VMEM((c1, cells), F32),
             pltpu.VMEM((9 * f2, padded), BF16),
-            pltpu.VMEM((n_mp, f1, cells), F32),
-            pltpu.VMEM((n_sample, f2 // n_sample, 27 * c1), F32),
         ],
         2 * cells * 27 * (c0 * c1 + 3 * f2 * c1),
         4 * 1024 * 1024,
-    )(*pieces, w2r, w2b, cotangent)
-    features, pre_own, vol_all = outs[:3]
-    parts = outs[3 : 3 + n_mp]
-    grads = outs[3 + n_mp :]
-
-    parts = [parts[0]] + [swap(parts[k], "mp", k) for k in range(1, n_mp)]
-    grads = [grads[0]] + [swap(grads[k], "sample", k) for k in range(1, n_sample)]
-
-    outs = call(
+    )(pieces, w2r, w2b, cotangent)
+
+    parts = lax.all_to_all(parts, "mp", 0, 0, tiled=True)
+    grads = lax.all_to_all(grads, "sample", 0, 0, tiled=True)
+
+    ins, grad_first = call(
         functools.partial(backward_kernel, n_mp),
-        [sds((rows_in, cells), BF16)] * n_mp + [sds((f1, 27 * c0), BF16)],
-        [
-            pltpu.VMEM((9 * f1, padded), BF16),
-            pltpu.VMEM((n_mp, rows_in, cells), F32),
-        ],
+        [sds((n_mp, rows_in, cells), BF16), sds((f1, 27 * c0), BF16)],
+        [pltpu.VMEM((9 * f1, padded), BF16)],
         2 * cells * 27 * 2 * c0 * f1,
         1024 * 1024,
-    )(*parts, pre_own, vol_all, w1b)
-    ins = outs[:n_mp]
-    grad_first = outs[n_mp]
-    firsts = [grad_first] + [swap(grad_first, "sample", k) for k in range(1, n_sample)]
-    ins = [ins[0]] + [swap(ins[k], "mp", k) for k in range(1, n_mp)]
+    )(parts, pre_own, vol_all, w1b)
+    ins = lax.all_to_all(ins, "mp", 0, 0, tiled=True)
 
     def total(values):
         result = values[0].astype(F32)
-        for value in values[1:]:
-            result = result + value.astype(F32)
+        for k in range(1, values.shape[0]):
+            result = result + values[k].astype(F32)
         return result
 
-    second = total(grads).astype(BF16)
-    seconds = [second] + [swap(second, "sample", k) for k in range(1, n_sample)]
-    grad_second = call(
-        functools.partial(place_kernel, n_sample, scale),
-        sds((n_sample,) + second.shape, F32),
-        [],
-        0,
-        1024 * 1024,
-    )(*seconds).reshape(f2, 27 * c1)
-    input_grad = total(ins).astype(BF16)
+    second = total(grads).astype(BF16).reshape(-1, 27 * c0)
+    both = jnp.concatenate([grad_first, second], axis=0)
+    both = lax.all_to_all(jnp.broadcast_to(both, (n_sample,) + both.shape), "sample", 0, 0, tiled=True)
     return (
         features.reshape(f2, 1, cells),
-        input_grad.reshape(rows_in, 1, cells),
-        total(firsts) * scale,
-        grad_second,
+        total(ins).astype(BF16).reshape(rows_in, 1, cells),
+        total(both[:, :f1]) * scale,
+        both[:, f1:].astype(F32).reshape(f2, 27 * c1) * scale,
     )
 
 

time: 62.2 us -> 77.5 us (1.25)
  starting transfers between devices: 37.6 us -> 11.7 us
  blocking collectives: 0 us -> 24.3 us
  waiting for transfers between devices: 8.76 us -> 23.9 us
  local copies, waits for them, and re-layouts: 1.77 us -> 4.21 us
  other arithmetic: 2.2 us -> 1.42 us
    ppermute x30 -> x0, starting transfers between devices: 37.6 us -> none  [swap(): return lax.ppermute(value, axis, [(i, i ^ k) for i in range(n)])]
    all_to_all x0 -> x3, waiting for transfers between devices: none -> 23.9 us  [the longest x1 12 us: local(): lax.all_to_all(jnp.broadcast_to(both, (n_sample,) + both.shape), 'sample'...]
    all_to_all x0 -> x1, blocking collectives: none -> 12.3 us  [local(): parts = lax.all_to_all(parts, 'mp', 0, 0, tiled=True)]
    all_gather x0 -> x1, blocking collectives: none -> 12 us  [local(): pieces = lax.all_gather(piece, 'mp', axis=0, tiled=False)]
    all_to_all x0 -> x3, starting transfers between devices: none -> 11.7 us  [the longest x1 4.87 us: local(): grads = lax.all_to_all(grads, 'sample', 0, 0, tiled=True)]
    ppermute x30 -> x0, waiting for transfers between devices: 8.76 us -> none  [swap(): return lax.ppermute(value, axis, [(i, i ^ k) for i in range(n)])]
    mul x0 -> x1, local copies, waits for them, and re-layouts: none -> 0.89 us  [local(): both[:, f1:].astype(F32).reshape(f2, 27 * c1) * scale]
    concatenate x1, other arithmetic: 0.83 us -> 0.01 us  [local(): jnp.concatenate([jnp.pad(w_first, ((0, 0), (0, wide - w_first.shape[1])))...]
  transfers between devices with their start and end apart: 30 -> 3, of which waited for: 4 -> 3; matrix products, arithmetic and copies ran while one was open for 4% -> 1% of each run, Pallas kernels for 5% -> 3%
where the time goes in v1:
time: 77.5 us; the launch traced here: 77 us
  blocking collectives  24.3 us (31%)
  waiting for transfers between devices  23.9 us (31%)
  starting transfers between devices  11.7 us (15%)
  Pallas kernels  10.6 us (14%)
  local copies, waits for them, and re-layouts  4.21 us (5%)
  other arithmetic  1.42 us (2%)
    all_to_all x1, blocking collectives, local(): parts = lax.all_to_all(parts, 'mp', 0, 0, tiled=True)  12.3 us
    all_to_all x1, waiting for transfers between devices, local(): lax.all_to_all(jnp.broadcast_to(both, (n_sample,) + both.shape), 'sample'...  12 us
    all_gather x1, blocking collectives, local(): pieces = lax.all_gather(piece, 'mp', axis=0, tiled=False)  12 us
    pallas_call x1, Pallas kernels, local(): call(functools.partial(forward_kernel, n_mp, n_sample, c0), [sds((f2, cel...  8.51 us
    all_to_all x1, waiting for transfers between devices, local(): ins = lax.all_to_all(ins, 'mp', 0, 0, tiled=True)  6.7 us
    all_to_all x1, waiting for transfers between devices, local(): grads = lax.all_to_all(grads, 'sample', 0, 0, tiled=True)  5.2 us
    all_to_all x1, starting transfers between devices, local(): grads = lax.all_to_all(grads, 'sample', 0, 0, tiled=True)  4.87 us
    all_to_all x1, starting transfers between devices, local(): lax.all_to_all(jnp.broadcast_to(both, (n_sample,) + both.shape), 'sample'...  3.46 us
  transfers between devices with their start and end apart: 3, of which 3 were waited for; matrix products, arithmetic and copies ran while one was open for 1% of the time, Pallas kernels for 3%

profile of v1, /device:TPU:0, one launch (start us, length us, event | category | flops | bytes accessed | tf_op | source)
XLA Modules:
  0.0 77.0 jit_solution(5764406711332998524)
XLA Ops:
  0.6 1.1 %reshape.176 = bf16[32,3,9,128]{3,2,1,0:T(8,128)(2,1)S(1)} reshape(bf16[32,3456]{1,0:T(8,128)(2,1)} %param.6) | data formatting | bytes 442368 | tf_op jit(solution)/shard_map/reshape | solution.py:254
  1.7 0.1 copy.11
  1.9 0.1 copy.12
  1.9 0.0 copy-start.1
  1.9 0.0 copy-start.2
  2.0 0.2 copy.13.refs_2_
  2.1 0.6 copy-done.1
  2.8 0.0 copy-done.2
  2.8 0.0 copy-start
  2.8 12.0 %all-gather = bf16[192,2048]{1,0:T(8,128)(2,1)S(1)} all-gather(bf16[24,2048]{1,0:T(8,128)(2,1)S(1)} %fusion.1), channel_id=2, replica_groups=mesh['sample'=4,'mp'=8] {'mp'}, dimensions={0}, use_global_device_ids=true | all-gather | bytes 884736 | tf_op jit(solution)/shard_map/all_gather | solution.py:252
  14.8 0.0 copy-done
  14.8 8.5 %shard_map.75 = (bf16[32,2048]{1,0:T(8,128)(2,1)}, f32[16,2048]{1,0:T(8,128)S(1)}, bf16[64,2048]{1,0:T(8,128)(2,1)S(1)}, bf16[8,16,2048]{2,1,0:T(8,128)(2,1)S(1)}, bf16[4,8,3456]{2,1,0:T(8,128)(2,1)}) custom-call(bf16[8,24,2048]{2,1,0:T(8,128)(2,1)S(1)} %bitcast.18, bf16[288,384]{1,0:T(8,128)(2,1)S(1)} %bitcast.19, bf16[128,864]{1,0:T(8,128)(2,1)S(1)} %copy.13.refs_2_, ...), custom_call_target="tpu_custom_call" | custom-call | flops 2264924160 | bytes 4194304 | tf_op jit(solution)/shard_map/pallas_call | solution.py:260
  23.3 12.3 %all_to_all.20.refs_0_ = bf16[8,16,2048]{2,1,0:T(8,128)(2,1)S(1)} all-to-all(bf16[8,16,2048]{2,1,0:T(8,128)(2,1)S(1)} %get-tuple-element.12), channel_id=1, replica_groups=mesh['sample'=4,'mp'=8] {'mp'}, dimensions={0} | all-to-all | bytes 1048576 | tf_op jit(solution)/shard_map/all_to_all | solution.py:282
  35.6 4.9 %all-to-all-start.2 = ((bf16[4,8,3456]{2,1,0:T(8,128)(2,1)}), bf16[4,8,3456]{2,1,0:T(8,128)(2,1)S(1)}, u32[]{:S(2)}, u32[]{:S(2)}) async-start(bf16[4,8,3456]{2,1,0:T(8,128)(2,1)} %get-tuple-element.17), calls=%async_computation.2 | async-start | bytes 442368 | tf_op jit(solution)/shard_map/all_to_all | solution.py:283
  40.5 0.2 reshape.181
  40.7 0.1 copy.15.refs_3_
  40.8 2.1 %shard_map.76 = (bf16[8,8,2048]{2,1,0:T(8,128)(2,1)}, bf16[16,1728]{1,0:T(8,128)(2,1)S(1)}) custom-call(bf16[8,16,2048]{2,1,0:T(8,128)(2,1)S(1)} %all_to_all.20.refs_0_, f32[16,2048]{1,0:T(8,128)S(1)} %get-tuple-element.13.refs_1_, bf16[64,2048]{1,0:T(8,128)(2,1)S(1)} %get-tuple-element.14.refs_2_, bf16[3,64,144]{2,1,0:T(8,128)(2,1)S(1)} %copy.15.refs_3_), custom_call_target="tpu_custom_call" | custom-call | flops 226492416 | bytes 1048576 | tf_op jit(solution)/shard_map/pallas_call | solution.py:285
  42.9 5.2 %all-to-all-done.2 = bf16[4,8,3456]{2,1,0:T(8,128)(2,1)S(1)} async-done(((bf16[4,8,3456]{2,1,0:T(8,128)(2,1)}), bf16[4,8,3456]{2,1,0:T(8,128)(2,1)S(1)}, u32[]{:S(2)}, u32[]{:S(2)}) %all-to-all-start.2) | async-done | bytes 221216 | tf_op jit(solution)/shard_map/all_to_all | solution.py:283
  48.1 3.4 %all-to-all-start.1 = ((bf16[8,8,2048]{2,1,0:T(8,128)(2,1)}), bf16[8,8,2048]{2,1,0:T(8,128)(2,1)S(1)}, u32[]{:S(2)}, u32[]{:S(2)}) async-start(bf16[8,8,2048]{2,1,0:T(8,128)(2,1)} %get-tuple-element.15), calls=%async_computation.1 | async-start | bytes 524288 | tf_op jit(solution)/shard_map/all_to_all | solution.py:292
  51.6 0.1 add.119
  51.7 6.7 %all-to-all-done.1 = bf16[8,8,2048]{2,1,0:T(8,128)(2,1)S(1)} async-done(((bf16[8,8,2048]{2,1,0:T(8,128)(2,1)}), bf16[8,8,2048]{2,1,0:T(8,128)(2,1)S(1)}, u32[]{:S(2)}, u32[]{:S(2)}) %all-to-all-start.1) | async-done | bytes 262176 | tf_op jit(solution)/shard_map/all_to_all | solution.py:292
  58.4 0.8 %broadcast_in_dim.3 = bf16[4,32,1728]{2,1,0:T(8,128)(2,1)} broadcast(bf16[32,1728]{1,0:T(8,128)(2,1)S(1)} %pad_maximum_fusion), dimensions={1,2} | broadcast | bytes 552960 | tf_op jit(solution)/shard_map/broadcast_in_dim | solution.py:302
  59.2 3.5 %all-to-all-start.3 = ((bf16[4,32,1728]{2,1,0:T(8,128)(2,1)}), bf16[4,32,1728]{2,1,0:T(8,128)(2,1)S(1)}, u32[]{:S(2)}, u32[]{:S(2)}) async-start(bf16[4,32,1728]{2,1,0:T(8,128)(2,1)} %broadcast_in_dim.3), calls=%async_computation.3 | async-start | bytes 917504 | tf_op jit(solution)/shard_map/all_to_all | solution.py:302
  62.7 0.7 fusion.2
  63.3 12.0 %all-to-all-done.3 = bf16[4,32,1728]{2,1,0:T(8,128)(2,1)S(1)} async-done(((bf16[4,32,1728]{2,1,0:T(8,128)(2,1)}), bf16[4,32,1728]{2,1,0:T(8,128)(2,1)S(1)}, u32[]{:S(2)}, u32[]{:S(2)}) %all-to-all-start.3) | async-done | bytes 442400 | tf_op jit(solution)/shard_map/all_to_all | solution.py:302
  75.4 0.9 %mul.19 = f32[32,3456]{1,0:T(8,128)} reshape(f32[4,16,1728]{2,1,0:T(8,128)S(1)} %convert_multiply_fusion) | data formatting | bytes 884736 | tf_op jit(solution)/shard_map/mul | solution.py:307
  76.3 0.7 multiply_bitcast_fusion
  (6 shorter events, 0.2 us)
Async XLA Ops:
  1.9 0.8 %copy-start.1 = (bf16[16,1728]{1,0:T(8,128)(2,1)S(1)}, bf16[16,1728]{1,0:T(8,128)(2,1)}, u32[]{:S(2)}) copy-start(bf16[16,1728]{1,0:T(8,128)(2,1)} %param.5) | copy-start | bytes 165892
  1.9 0.8 %copy-start.2 = (bf16[8,1,2048]{2,0,1:T(8,128)(2,1)S(1)}, bf16[8,1,2048]{2,0,1:T(8,128)(2,1)}, u32[]{:S(2)}) copy-start(bf16[8,1,2048]{2,0,1:T(8,128)(2,1)} %param.4) | copy-start | bytes 98308
  2.8 12.0 %copy-start = (bf16[32,1,2048]{2,0,1:T(8,128)(2,1)S(1)}, bf16[32,1,2048]{2,0,1:T(8,128)(2,1)}, u32[]{:S(2)}) copy-start(bf16[32,1,2048]{2,0,1:T(8,128)(2,1)} %param.7) | copy-start | bytes 393220
  35.6 12.5 %all-to-all-start.2 = ((bf16[4,8,3456]{2,1,0:T(8,128)(2,1)}), bf16[4,8,3456]{2,1,0:T(8,128)(2,1)S(1)}, u32[]{:S(2)}, u32[]{:S(2)}) async-start(bf16[4,8,3456]{2,1,0:T(8,128)(2,1)} %get-tuple-element.17), calls=%async_computation.2 | async-start | bytes 442368 | tf_op jit(solution)/shard_map/all_to_all | solution.py:283
  48.1 10.3 %all-to-all-start.1 = ((bf16[8,8,2048]{2,1,0:T(8,128)(2,1)}), bf16[8,8,2048]{2,1,0:T(8,128)(2,1)S(1)}, u32[]{:S(2)}, u32[]{:S(2)}) async-start(bf16[8,8,2048]{2,1,0:T(8,128)(2,1)} %get-tuple-element.15), calls=%async_computation.1 | async-start | bytes 524288 | tf_op jit(solution)/shard_map/all_to_all | solution.py:292
  59.2 16.1 %all-to-all-start.3 = ((bf16[4,32,1728]{2,1,0:T(8,128)(2,1)}), bf16[4,32,1728]{2,1,0:T(8,128)(2,1)S(1)}, u32[]{:S(2)}, u32[]{:S(2)}) async-start(bf16[4,32,1728]{2,1,0:T(8,128)(2,1)} %broadcast_in_dim.3), calls=%async_computation.3 | async-start | bytes 917504 | tf_op jit(solution)/shard_map/all_to_all | solution.py:302

commit v2 on v1

--- a/solution.py
+++ b/solution.py
@@ -65,10 +65,12 @@
 
 
 def forward_kernel(n_mp, n_sample, c0, *refs):
-    pieces, w2r_ref, w2b_ref, cot_ref, feat_ref, pre_ref, vol_ref, part_ref, grad_ref = refs[:9]
-    vs, w1s, v3, w1r, hid, pre, d9 = refs[9:]
+    near_ref, far_ref, w2r_ref, w2b_ref, cot_ref = refs[:5]
+    feat_ref, pre_ref, vol_ref, keep_ref, give_ref, half_keep_ref, half_give_ref = refs[5:12]
+    vs, w1s, v3, w1r, hid, pre, d9, part, grad = refs[12:]
 
     me = lax.axis_index("mp")
+    at = lax.axis_index("sample")
     f1 = w1s.shape[1]
     c1 = n_mp * f1
     f2, cells = cot_ref.shape
@@ -78,9 +80,10 @@
     grid_xy = lane_grid(chunk)
 
     for k in range(n_mp):
-        piece = pieces[k].astype(F32)
-        w1s[k] = piece[:f1]
-        vs[k] = piece[f1:, :cells]
+        piece = (far_ref if k % 2 else near_ref)[k // 2].astype(F32)
+        slot = me ^ k
+        w1s[slot] = piece[:f1]
+        vs[slot] = piece[f1:, :cells]
 
     lane = lax.broadcasted_iota(jnp.int32, (1, pitch), 1)
     for dz in range(3):
@@ -149,21 +152,27 @@
         base = pl.multiple_of(step * chunk, chunk)
         rhs = jnp.concatenate([d9[:, pl.ds(base + (2 - dz) * PLANE, chunk)] for dz in range(3)], axis=0)
         z = dot(w2b_ref[...], rhs)
-        part_ref[:, :, pl.ds(base, chunk)] = z.astype(BF16).reshape(n_mp, f1, chunk)
+        part[:, :, pl.ds(base, chunk)] = z.reshape(n_mp, f1, chunk)
         return carry
 
     lax.fori_loop(0, steps, data_conv, 0)
-
-    rows = f2 // n_sample
+    for k in range(n_mp):
+        (give_ref if k % 2 else keep_ref)[k // 2] = part[me ^ k].astype(BF16)
+
+    rows = f2 // 2
     for dz in range(3):
         g = dot_nt(d9[:, (2 - dz) * PLANE : (2 - dz) * PLANE + cells], hid[:, PLANE : PLANE + cells])
         for k in range(9):
             t = dz * 9 + k
-            grad_ref[:, :, t * c1 : (t + 1) * c1] = g[k * f2 : (k + 1) * f2].reshape(n_sample, rows, c1).astype(BF16)
+            grad[:, :, t * c1 : (t + 1) * c1] = g[k * f2 : (k + 1) * f2].reshape(2, rows, c1)
+    half_keep_ref[...] = grad[at % 2].astype(BF16)
+    half_give_ref[...] = grad[1 - at % 2].astype(BF16)
 
 
 def backward_kernel(n_mp, *refs):
-    parts, pre_ref, vol_ref, w1b_ref, out_ref, grad_ref, d9 = refs
+    parts = refs[: n_mp // 2]
+    pre_ref, vol_ref, w1b_ref, keep_ref, give_ref, grad_ref, d9, part = refs[n_mp // 2 :]
+    me = lax.axis_index("mp")
     f1, cells = pre_ref.shape
     c0 = vol_ref.shape[0]
     chunk = chunk_of(cells)
@@ -176,9 +185,9 @@
 
     def take(step, carry):
         base = pl.multiple_of(step * chunk, chunk)
-        total = parts[0, :, pl.ds(base, chunk)].astype(F32)
-        for k in range(1, n_mp):
-            total = total + parts[k, :, pl.ds(base, chunk)].astype(F32)
+        total = parts[0][:, pl.ds(base, chunk)].astype(F32)
+        for other in parts[1:]:
+            total = total + other[:, pl.ds(base, chunk)].astype(F32)
         v = pre_ref[:, pl.ds(base, chunk)]
         s = sigmoid(v)
         delta = (total * (s * (1.0 + v * (1.0 - s)))).astype(BF16).astype(F32)
@@ -194,10 +203,12 @@
         for dz in range(3):
             term = dot(w1b_ref[dz], d9[:, pl.ds(base + (2 - dz) * PLANE, chunk)])
             z = term if z is None else z + term
-        out_ref[:, :, pl.ds(base, chunk)] = z.reshape(n_mp, c0 // n_mp, chunk).astype(BF16)
+        part[:, :, pl.ds(base, chunk)] = z.reshape(n_mp, c0 // n_mp, chunk)
         return carry
 
     lax.fori_loop(0, steps, data_conv, 0)
+    for k in range(n_mp):
+        (give_ref if k % 2 else keep_ref)[k // 2] = part[me ^ k].astype(BF16)
 
     reps = max(1, 128 // c0)
     span = reps * c0
@@ -216,6 +227,32 @@
         grad_ref[:, t * c0 : t * c0 + width] = merged[:, :width].astype(BF16)
 
 
+def place_kernel(scale, mine_ref, other_ref, out_ref):
+    bit = lax.axis_index("sample") % 2
+    width = out_ref.shape[2]
+    out_ref[bit] = mine_ref[...].astype(F32) * scale
+    out_ref[1 - bit] = other_ref[:, :width].astype(F32) * scale
+
+
+def swap(value, axis, k):
+    n = lax.axis_size(axis)
+    return lax.ppermute(value, axis, [(i, i ^ k) for i in range(n)])
+
+
+def add(a, b):
+    return (a.astype(F32) + b.astype(F32)).astype(BF16)
+
+
+def sum_over_mp(keep, give):
+    got = swap(give, "mp", 1)
+    parts = [add(keep[j], got[j]) for j in range(keep.shape[0])]
+    return [parts[0]] + [swap(parts[j], "mp", 2 * j) for j in range(1, len(parts))]
+
+
+def bits_above(count):
+    return [1 << i for i in range(1, count.bit_length() - 1)]
+
+
 def call(kernel, out_shape, scratch, flops, nbytes):
     return pl.pallas_call(
         kernel,
@@ -249,7 +286,9 @@
         ],
         axis=0,
     )
-    pieces = lax.all_gather(piece, "mp", axis=0, tiled=False)
+    near = [piece] + [swap(piece, "mp", k) for k in range(2, n_mp, 2)]
+    near = jnp.stack(near)
+    far = swap(near, "mp", 1)
 
     w2t = w_second.reshape(f2, 3, 9, c1)
     w2r = jnp.transpose(w2t, (2, 0, 1, 3)).reshape(9 * f2, 3 * c1)
@@ -257,14 +296,17 @@
     w1b = jnp.transpose(w_first.reshape(f1, 3, 9, c0), (1, 3, 2, 0)).reshape(3, c0, 9 * f1)
 
     sds = jax.ShapeDtypeStruct
-    features, pre_own, vol_all, parts, grads = call(
+    half = n_mp // 2
+    features, pre_own, vol_all, keep, give, half_keep, half_give = call(
         functools.partial(forward_kernel, n_mp, n_sample, c0),
         [
             sds((f2, cells), BF16),
             sds((f1, cells), F32),
             sds((c0, cells), BF16),
-            sds((n_mp, f1, cells), BF16),
-            sds((n_sample, f2 // n_sample, 27 * c1), BF16),
+            sds((half, f1, cells), BF16),
+            sds((half, f1, cells), BF16),
+            sds((f2 // 2, 27 * c1), BF16),
+            sds((f2 // 2, 27 * c1), BF16),
         ],
         [
             pltpu.VMEM((n_mp, rows_in, cells), F32),
@@ -274,37 +316,52 @@
             pltpu.VMEM((c1, padded), BF16),
             pltpu.VMEM((c1, cells), F32),
             pltpu.VMEM((9 * f2, padded), BF16),
+            pltpu.VMEM((n_mp, f1, cells), F32),
+            pltpu.VMEM((2, f2 // 2, 27 * c1), F32),
         ],
         2 * cells * 27 * (c0 * c1 + 3 * f2 * c1),
         4 * 1024 * 1024,
-    )(pieces, w2r, w2b, cotangent)
-
-    parts = lax.all_to_all(parts, "mp", 0, 0, tiled=True)
-    grads = lax.all_to_all(grads, "sample", 0, 0, tiled=True)
-
-    ins, grad_first = call(
+    )(near, far, w2r, w2b, cotangent)
+
+    parts = sum_over_mp(keep, give)
+    half_sum = add(half_keep, swap(half_give, "sample", 1))
+    for bit in bits_above(n_sample):
+        half_sum = add(half_sum, swap(half_sum, "sample", bit))
+
+    keep, give, grad_first = call(
         functools.partial(backward_kernel, n_mp),
-        [sds((n_mp, rows_in, cells), BF16), sds((f1, 27 * c0), BF16)],
-        [pltpu.VMEM((9 * f1, padded), BF16)],
+        [
+            sds((half, rows_in, cells), BF16),
+            sds((half, rows_in, cells), BF16),
+            sds((f1, 27 * c0), BF16),
+        ],
+        [pltpu.VMEM((9 * f1, padded), BF16), pltpu.VMEM((n_mp, rows_in, cells), F32)],
         2 * cells * 27 * 2 * c0 * f1,
         1024 * 1024,
-    )(parts, pre_own, vol_all, w1b)
-    ins = lax.all_to_all(ins, "mp", 0, 0, tiled=True)
-
-    def total(values):
-        result = values[0].astype(F32)
-        for k in range(1, values.shape[0]):
-            result = result + values[k].astype(F32)
-        return result
-
-    second = total(grads).astype(BF16).reshape(-1, 27 * c0)
-    both = jnp.concatenate([grad_first, second], axis=0)
-    both = lax.all_to_all(jnp.broadcast_to(both, (n_sample,) + both.shape), "sample", 0, 0, tiled=True)
+    )(*parts, pre_own, vol_all, w1b)
+    ins = sum_over_mp(keep, give)
+
+    both = swap(jnp.concatenate([half_sum, grad_first], axis=1), "sample", 1)
+    grad_first = add(grad_first, both[:, 27 * c1 :])
+    bits = bits_above(n_sample)
+    for bit in bits[:-1]:
+        grad_first = add(grad_first, swap(grad_first, "sample", bit))
+    grad_first = (grad_first.astype(F32) + swap(grad_first, "sample", bits[-1]).astype(F32)) * scale
+    grad_second = call(
+        functools.partial(place_kernel, scale),
+        sds((2, f2 // 2, 27 * c1), F32),
+        [],
+        0,
+        1024 * 1024,
+    )(half_sum, both).reshape(f2, 27 * c1)
+    total = ins[0].astype(F32)
+    for other in ins[1:]:
+        total = total + other.astype(F32)
     return (
         features.reshape(f2, 1, cells),
-        total(ins).astype(BF16).reshape(rows_in, 1, cells),
-        total(both[:, :f1]) * scale,
-        both[:, f1:].astype(F32).reshape(f2, 27 * c1) * scale,
+        total.astype(BF16).reshape(rows_in, 1, cells),
+        grad_first,
+        grad_second,
     )
 
 

time: 77.5 us -> 51.5 us (0.66)
  blocking collectives: 24.3 us -> 0 us
  waiting for transfers between devices: 23.9 us -> 17.1 us
  starting transfers between devices: 11.7 us -> 18.1 us
  local copies, waits for them, and re-layouts: 4.21 us -> 2.01 us
  other arithmetic: 1.42 us -> 2.39 us
    all_to_all x3 -> x0, waiting for transfers between devices: 23.9 us -> none  [the longest x1 12 us: local(): lax.all_to_all(jnp.broadcast_to(both, (n_sample,) + both.shape), 'sample'...]
    ppermute x0 -> x16, starting transfers between devices: none -> 18.1 us  [swap(): return lax.ppermute(value, axis, [(i, i ^ k) for i in range(n)])]
    ppermute x0 -> x16, waiting for transfers between devices: none -> 17.1 us  [swap(): return lax.ppermute(value, axis, [(i, i ^ k) for i in range(n)])]
    all_to_all x1 -> x0, blocking collectives: 12.3 us -> none  [local(): parts = lax.all_to_all(parts, 'mp', 0, 0, tiled=True)]
    all_gather x1 -> x0, blocking collectives: 12 us -> none  [local(): pieces = lax.all_gather(piece, 'mp', axis=0, tiled=False)]
    all_to_all x3 -> x0, starting transfers between devices: 11.7 us -> none  [the longest x1 4.87 us: local(): grads = lax.all_to_all(grads, 'sample', 0, 0, tiled=True)]
    reshape x1, local copies, waits for them, and re-layouts: 1.06 us -> 0.13 us  [local(): w2t = w_second.reshape(f2, 3, 9, c1)]
    mul x1 -> x0, local copies, waits for them, and re-layouts: 0.89 us -> none  [local(): both[:, f1:].astype(F32).reshape(f2, 27 * c1) * scale]
  transfers between devices with their start and end apart: 3 -> 16, of which waited for: 3 -> 13; matrix products, arithmetic and copies ran while one was open for 1% -> 3% of each run, Pallas kernels for 3% -> 2%
where the time goes in v2:
time: 51.5 us; the launch traced here: 51.2 us
  starting transfers between devices  18.1 us (35%)
  waiting for transfers between devices  17.1 us (33%)
  Pallas kernels  10.8 us (21%)
  other arithmetic  2.39 us (5%)
  local copies, waits for them, and re-layouts  2.01 us (4%)
  between operations  0.77 us (1%)
    ppermute x16, starting transfers between devices, swap(): return lax.ppermute(value, axis, [(i, i ^ k) for i in range(n)])  18.1 us
    ppermute x16, waiting for transfers between devices, swap(): return lax.ppermute(value, axis, [(i, i ^ k) for i in range(n)])  17.1 us
    pallas_call x1, Pallas kernels, local(): call(functools.partial(forward_kernel, n_mp, n_sample, c0), [sds((f2, cel...  8.03 us
    pallas_call x1, Pallas kernels, local(): call(functools.partial(backward_kernel, n_mp), [sds((half, rows_in, cells...  1.99 us
    unnamed x7, local copies, waits for them, and re-layouts  1.21 us
  transfers between devices with their start and end apart: 16, of which 13 were waited for; matrix products, arithmetic and copies ran while one was open for 3% of the time, Pallas kernels for 2%

profile of v2, /device:TPU:0, one launch (start us, length us, event | category | flops | bytes accessed | tf_op | source)
XLA Modules:
  0.0 51.2 jit_solution(8139264078407818199)
XLA Ops:
  0.6 0.9 %fusion.14 = (bf16[1,24,2048]{2,1,0:T(8,128)(2,1)S(1)}, bf16[24,2048]{1,0:T(8,128)(2,1)S(1)}) fusion(bf16[8,2048]{1,0:T(8,128)(2,1)} %bitcast.54, bf16[16,1728]{1,0:T(8,128)(2,1)} %param.5), kind=kLoop, calls=%fused_computation.31 | loop fusion | flops 294912 | bytes 284672 | tf_op jit(solution)/shard_map/stack | solution.py:290
  1.5 3.0 %collective-permute-start = (bf16[24,2048]{1,0:T(8,128)(2,1)S(1)}, bf16[24,2048]{1,0:T(8,128)(2,1)S(1)}, u32[]{:S(2)}, u32[]{:S(2)}) collective-permute-start(bf16[24,2048]{1,0:T(8,128)(2,1)S(1)} %get-tuple-element.32), channel_id=1, source_target_pairs={{0,2},{1,3},{2,0},{3,1},{4,6},{5,7},{6,4},{7,5},{8,10},{9,11},{10,... | collective-permute-start | bytes 294920 | tf_op jit(solution)/shard_map/ppermute | solution.py:239
  4.5 1.5 %collective-permute-start.1 = (bf16[24,2048]{1,0:T(8,128)(2,1)S(1)}, bf16[24,2048]{1,0:T(8,128)(2,1)S(1)}, u32[]{:S(2)}, u32[]{:S(2)}) collective-permute-start(bf16[24,2048]{1,0:T(8,128)(2,1)S(1)} %get-tuple-element.32), channel_id=1, source_target_pairs={{0,4},{1,5},{2,6},{3,7},{4,0},{5,1},{6,2},{7,3},{8,12},{9,13},{10,... | collective-permute-start | bytes 294920 | tf_op jit(solution)/shard_map/ppermute | solution.py:239
  6.0 0.0 collective-permute-start.2
  6.0 1.5 %collective-permute-done = bf16[24,2048]{1,0:T(8,128)(2,1)S(1)} collective-permute-done((bf16[24,2048]{1,0:T(8,128)(2,1)S(1)}, bf16[24,2048]{1,0:T(8,128)(2,1)S(1)}, u32[]{:S(2)}, u32[]{:S(2)}) %collective-permute-start) | collective-permute-done | bytes 98336 | tf_op jit(solution)/shard_map/ppermute | solution.py:239
  7.5 2.6 %collective-permute-done.1 = bf16[24,2048]{1,0:T(8,128)(2,1)S(1)} collective-permute-done((bf16[24,2048]{1,0:T(8,128)(2,1)S(1)}, bf16[24,2048]{1,0:T(8,128)(2,1)S(1)}, u32[]{:S(2)}, u32[]{:S(2)}) %collective-permute-start.1) | collective-permute-done | bytes 98336 | tf_op jit(solution)/shard_map/ppermute | solution.py:239
  10.2 1.4 %collective-permute-done.2 = bf16[24,2048]{1,0:T(8,128)(2,1)S(1)} collective-permute-done((bf16[24,2048]{1,0:T(8,128)(2,1)S(1)}, bf16[24,2048]{1,0:T(8,128)(2,1)S(1)}, u32[]{:S(2)}, u32[]{:S(2)}) %collective-permute-start.2) | collective-permute-done | bytes 98336 | tf_op jit(solution)/shard_map/ppermute | solution.py:239
  11.5 0.0 copy-start.2
  11.5 0.1 pad_maximum_fusion.refs_0_
  11.6 0.1 collective-permute-start.3
  11.7 0.8 %copy-done.2 = bf16[32,3456]{1,0:T(8,128)(2,1)S(1)} copy-done((bf16[32,3456]{1,0:T(8,128)(2,1)S(1)}, bf16[32,3456]{1,0:T(8,128)(2,1)}, u32[]{:S(2)}) %copy-start.2) | copy-done | bytes 221208
  12.5 0.1 reshape.73
  12.6 0.1 copy.11
  12.8 0.1 copy.12
  12.8 0.0 copy-start
  12.8 0.2 copy.13.refs_3_
  13.0 0.4 collective-permute-done.3.refs_1_
  13.4 0.4 copy-done
  13.7 0.0 copy-start.1
  13.7 8.0 %shard_map.75 = (bf16[32,2048]{1,0:T(8,128)(2,1)}, f32[16,2048]{1,0:T(8,128)S(1)}, bf16[64,2048]{1,0:T(8,128)(2,1)S(1)}, bf16[4,16,2048]{2,1,0:T(8,128)(2,1)S(1)...) custom-call(bf16[4,24,2048]{2,1,0:T(8,128)(2,1)S(1)} %pad_maximum_fusion.refs_0_, ...), custom_call_target="tpu_custom_call" | custom-call | flops 2264924160 | bytes 4194304 | tf_op jit(solution)/shard_map/pallas_call | solution.py:300
  21.8 1.6 %collective-permute-start.12 = (bf16[16,3456]{1,0:T(8,128)(2,1)S(1)}, bf16[16,3456]{1,0:T(8,128)(2,1)S(1)}, u32[]{:S(2)}, u32[]{:S(2)}) collective-permute-start(bf16[16,3456]{1,0:T(8,128)(2,1)S(1)} %get-tuple-element.23), channel_id=1, source_target_pairs={{0,8},{8,0},{16,24},{24,16},{1,9},{9,1},{17,25},{25,17},{2,10},{10... | collective-permute-start | bytes 331784 | tf_op jit(solution)/shard_map/ppermute | solution.py:239
  23.4 0.0 copy-done.1
  23.4 0.2 reshape.78
  23.6 0.1 copy.15.refs_6_
  23.8 0.1 collective-permute-start.4
  23.8 2.7 %collective-permute-done.12 = bf16[16,3456]{1,0:T(8,128)(2,1)S(1)} collective-permute-done((bf16[16,3456]{1,0:T(8,128)(2,1)S(1)}, bf16[16,3456]{1,0:T(8,128)(2,1)S(1)}, u32[]{:S(2)}, u32[]{:S(2)}) %collective-permute-start.12) | collective-permute-done | bytes 110624 | tf_op jit(solution)/shard_map/ppermute | solution.py:239
  26.6 2.6 %collective-permute-start.13 = (bf16[16,3456]{1,0:T(8,128)(2,1)S(1)}, bf16[16,3456]{1,0:T(8,128)(2,1)S(1)}, u32[]{:S(2)}, u32[]{:S(2)}) collective-permute-start(bf16[16,3456]{1,0:T(8,128)(2,1)S(1)} %add_convert_fusion.1), channel_id=1, source_target_pairs={{0,16},{8,24},{16,0},{24,8},{1,17},{9,25},{17,1},{25,9},{2,18},{10... | collective-permute-start | bytes 331784 | tf_op jit(solution)/shard_map/ppermute | solution.py:239
  29.3 0.0 collective-permute-done.4
  29.3 0.1 fusion.5
  29.3 0.7 %collective-permute-start.5 = (bf16[16,2048]{1,0:T(8,128)(2,1)S(1)}, bf16[16,2048]{1,0:T(8,128)(2,1)S(1)}, u32[]{:S(2)}, u32[]{:S(2)}) collective-permute-start(bf16[16,2048]{1,0:T(8,128)(2,1)S(1)} %get-tuple-element.26), channel_id=1, source_target_pairs={{0,2},{1,3},{2,0},{3,1},{4,6},{5,7},{6,4},{7,5},{8,10},{9,11},{10,... | collective-permute-start | bytes 196616 | tf_op jit(solution)/shard_map/ppermute | solution.py:239
  30.1 1.0 %collective-permute-start.6 = (bf16[16,2048]{1,0:T(8,128)(2,1)S(1)}, bf16[16,2048]{1,0:T(8,128)(2,1)S(1)}, u32[]{:S(2)}, u32[]{:S(2)}) collective-permute-start(bf16[16,2048]{1,0:T(8,128)(2,1)S(1)} %get-tuple-element.25), channel_id=1, source_target_pairs={{0,4},{1,5},{2,6},{3,7},{4,0},{5,1},{6,2},{7,3},{8,12},{9,13},{10,... | collective-permute-start | bytes 196616 | tf_op jit(solution)/shard_map/ppermute | solution.py:239
  31.0 1.9 %collective-permute-start.7 = (bf16[16,2048]{1,0:T(8,128)(2,1)S(1)}, bf16[16,2048]{1,0:T(8,128)(2,1)S(1)}, u32[]{:S(2)}, u32[]{:S(2)}) collective-permute-start(bf16[16,2048]{1,0:T(8,128)(2,1)S(1)} %get-tuple-element.24), channel_id=1, source_target_pairs={{0,6},{1,7},{2,4},{3,5},{4,2},{5,3},{6,0},{7,1},{8,14},{9,15},{10,... | collective-permute-start | bytes 196616 | tf_op jit(solution)/shard_map/ppermute | solution.py:239
  32.9 0.6 %collective-permute-done.13 = bf16[16,3456]{1,0:T(8,128)(2,1)S(1)} collective-permute-done((bf16[16,3456]{1,0:T(8,128)(2,1)S(1)}, bf16[16,3456]{1,0:T(8,128)(2,1)S(1)}, u32[]{:S(2)}, u32[]{:S(2)}) %collective-permute-start.13) | collective-permute-done | bytes 110624 | tf_op jit(solution)/shard_map/ppermute | solution.py:239
  33.6 0.1 collective-permute-done.5.refs_1_
  33.7 0.6 %collective-permute-done.6.refs_2_ = bf16[16,2048]{1,0:T(8,128)(2,1)S(1)} collective-permute-done((bf16[16,2048]{1,0:T(8,128)(2,1)S(1)}, bf16[16,2048]{1,0:T(8,128)(2,1)S(1)}, u32[]{:S(2)}, u32[]{:S(2)}) %collective-permute-start.6) | collective-permute-done | bytes 65568 | tf_op jit(solution)/shard_map/ppermute | solution.py:239
  34.3 1.9 %collective-permute-done.7.refs_3_ = bf16[16,2048]{1,0:T(8,128)(2,1)S(1)} collective-permute-done((bf16[16,2048]{1,0:T(8,128)(2,1)S(1)}, bf16[16,2048]{1,0:T(8,128)(2,1)S(1)}, u32[]{:S(2)}, u32[]{:S(2)}) %collective-permute-start.7) | collective-permute-done | bytes 65568 | tf_op jit(solution)/shard_map/ppermute | solution.py:239
  36.2 2.0 %shard_map.76 = (bf16[4,8,2048]{2,1,0:T(8,128)(2,1)S(1)}, bf16[4,8,2048]{2,1,0:T(8,128)(2,1)S(1)}, bf16[16,1728]{1,0:T(8,128)(2,1)S(1)}) custom-call(bf16[16,2048]{1,0:T(8,128)(2,1)S(1)} %get-tuple-element.27.refs_0_, bf16[16,2048]{1,0:T(8,128)(2,1)S(1)} %collective-permute-done.5.refs_1_, bf16[16,2048]{1,0:T(8,128)(2,1)S(1)} %collective-permute-done.6.refs_2_, ...), custom_call_target="tpu_custom_call" | custom-call | flops 226492416 | bytes 1048576 | tf_op jit(solution)/shard_map/pallas_call | solution.py:331
  38.2 0.1 collective-permute-start.8
  38.3 1.6 %collective-permute-start.14 = (bf16[16,5184]{1,0:T(8,128)(2,1)S(1)}, bf16[16,5184]{1,0:T(8,128)(2,1)S(1)}, u32[]{:S(2)}, u32[]{:S(2)}) collective-permute-start(bf16[16,5184]{1,0:T(8,128)(2,1)S(1)} %pad_maximum_fusion.1), channel_id=1, source_target_pairs={{0,8},{8,0},{16,24},{24,16},{1,9},{9,1},{17,25},{25,17},{2,10},{10... | collective-permute-start | bytes 497672 | tf_op jit(solution)/shard_map/ppermute | solution.py:239
  39.9 0.0 collective-permute-done.8
  40.0 1.1 %collective-permute-start.10 = (bf16[8,2048]{1,0:T(8,128)(2,1)S(1)}, bf16[8,2048]{1,0:T(8,128)(2,1)S(1)}, u32[]{:S(2)}, u32[]{:S(2)}) collective-permute-start(bf16[8,2048]{1,0:T(8,128)(2,1)S(1)} %get-tuple-element.30), channel_id=1, source_target_pairs={{0,4},{1,5},{2,6},{3,7},{4,0},{5,1},{6,2},{7,3},{8,12},{9,13},{10,... | collective-permute-start | bytes 98312 | tf_op jit(solution)/shard_map/ppermute | solution.py:239
  41.1 1.7 %collective-permute-start.11 = (bf16[8,2048]{1,0:T(8,128)(2,1)S(1)}, bf16[8,2048]{1,0:T(8,128)(2,1)S(1)}, u32[]{:S(2)}, u32[]{:S(2)}) collective-permute-start(bf16[8,2048]{1,0:T(8,128)(2,1)S(1)} %get-tuple-element.29), channel_id=1, source_target_pairs={{0,6},{1,7},{2,4},{3,5},{4,2},{5,3},{6,0},{7,1},{8,14},{9,15},{10,... | collective-permute-start | bytes 98312 | tf_op jit(solution)/shard_map/ppermute | solution.py:239
  42.8 0.7 %collective-permute-start.9 = (bf16[8,2048]{1,0:T(8,128)(2,1)S(1)}, bf16[8,2048]{1,0:T(8,128)(2,1)S(1)}, u32[]{:S(2)}, u32[]{:S(2)}) collective-permute-start(bf16[8,2048]{1,0:T(8,128)(2,1)S(1)} %get-tuple-element.28), channel_id=1, source_target_pairs={{0,2},{1,3},{2,0},{3,1},{4,6},{5,7},{6,4},{7,5},{8,10},{9,11},{10,... | collective-permute-start | bytes 98312 | tf_op jit(solution)/shard_map/ppermute | solution.py:239
  43.5 1.5 %collective-permute-done.14.other_ref = bf16[16,5184]{1,0:T(8,128)(2,1)S(1)} collective-permute-done((bf16[16,5184]{1,0:T(8,128)(2,1)S(1)}, bf16[16,5184]{1,0:T(8,128)(2,1)S(1)}, u32[]{:S(2)}, u32[]{:S(2)}) %collective-permute-start.14) | collective-permute-done | bytes 165920 | tf_op jit(solution)/shard_map/ppermute | solution.py:239
  45.1 0.3 collective-permute-start.15
  45.4 0.0 collective-permute-done.10
  45.4 0.8 %collective-permute-done.11 = bf16[8,2048]{1,0:T(8,128)(2,1)S(1)} collective-permute-done((bf16[8,2048]{1,0:T(8,128)(2,1)S(1)}, bf16[8,2048]{1,0:T(8,128)(2,1)S(1)}, u32[]{:S(2)}, u32[]{:S(2)}) %collective-permute-start.11) | collective-permute-done | bytes 32800 | tf_op jit(solution)/shard_map/ppermute | solution.py:239
  46.2 0.5 %collective-permute-done.9 = bf16[8,2048]{1,0:T(8,128)(2,1)S(1)} collective-permute-done((bf16[8,2048]{1,0:T(8,128)(2,1)S(1)}, bf16[8,2048]{1,0:T(8,128)(2,1)S(1)}, u32[]{:S(2)}, u32[]{:S(2)}) %collective-permute-start.9) | collective-permute-done | bytes 32800 | tf_op jit(solution)/shard_map/ppermute | solution.py:239
  46.8 0.6 %fusion.13 = bf16[8,1,2048]{2,0,1:T(8,128)(2,1)} fusion(bf16[8,2048]{1,0:T(8,128)(2,1)S(1)} %collective-permute-done.11, bf16[8,2048]{1,0:T(8,128)(2,1)S(1)} %collective-permute-done.10, bf16[8,2048]{1,0:T(8,128)(2,1)S(1)} %collective-permute-done.9, bf16[4,8,2048]{2,1,0:T(8,128)(2,1)S(1)} %collective-permute-done.8, ...), kind=kLoop, calls=%fused_computation.30 | loop fusion | flops 196608 | bytes 196608 | tf_op jit(solution)/shard_map/reshape | solution.py:362
  47.4 0.8 %shard_map.77 = f32[2,16,3456]{2,1,0:T(8,128)} custom-call(bf16[16,3456]{1,0:T(8,128)(2,1)S(1)} %add_convert_fusion.mine_ref, bf16[16,5184]{1,0:T(8,128)(2,1)S(1)} %collective-permute-done.14.other_ref), custom_call_target="tpu_custom_call" | custom-call | bytes 1048576 | tf_op jit(solution)/shard_map/pallas_call | solution.py:350
  48.2 2.4 %collective-permute-done.15 = bf16[16,1728]{1,0:T(8,128)(2,1)S(1)} collective-permute-done((bf16[16,1728]{1,0:T(8,128)(2,1)S(1)}, bf16[16,1728]{1,0:T(8,128)(2,1)S(1)}, u32[]{:S(2)}, u32[]{:S(2)}) %collective-permute-start.15) | collective-permute-done | bytes 55328 | tf_op jit(solution)/shard_map/ppermute | solution.py:239
  50.6 0.7 %add_multiply_fusion = f32[16,1728]{1,0:T(8,128)} fusion(bf16[16,1728]{1,0:T(8,128)(2,1)S(1)} %collective-permute-done.15, bf16[16,1728]{1,0:T(8,128)(2,1)S(1)} %add_convert_fusion.6), kind=kLoop, calls=%fused_computation.11 | loop fusion | flops 110592 | bytes 221184 | tf_op jit(solution)/shard_map/mul | solution.py:349
  (7 shorter events, 0.2 us)
Async XLA Ops:
  1.5 6.1 %collective-permute-start = (bf16[24,2048]{1,0:T(8,128)(2,1)S(1)}, bf16[24,2048]{1,0:T(8,128)(2,1)S(1)}, u32[]{:S(2)}, u32[]{:S(2)}) collective-permute-start(bf16[24,2048]{1,0:T(8,128)(2,1)S(1)} %get-tuple-element.32), channel_id=1, source_target_pairs={{0,2},{1,3},{2,0},{3,1},{4,6},{5,7},{6,4},{7,5},{8,10},{9,11},{10,... | collective-permute-start | bytes 294920 | tf_op jit(solution)/shard_map/ppermute | solution.py:239
  4.5 5.7 %collective-permute-start.1 = (bf16[24,2048]{1,0:T(8,128)(2,1)S(1)}, bf16[24,2048]{1,0:T(8,128)(2,1)S(1)}, u32[]{:S(2)}, u32[]{:S(2)}) collective-permute-start(bf16[24,2048]{1,0:T(8,128)(2,1)S(1)} %get-tuple-element.32), channel_id=1, source_target_pairs={{0,4},{1,5},{2,6},{3,7},{4,0},{5,1},{6,2},{7,3},{8,12},{9,13},{10,... | collective-permute-start | bytes 294920 | tf_op jit(solution)/shard_map/ppermute | solution.py:239
  6.0 5.5 %collective-permute-start.2 = (bf16[24,2048]{1,0:T(8,128)(2,1)S(1)}, bf16[24,2048]{1,0:T(8,128)(2,1)S(1)}, u32[]{:S(2)}, u32[]{:S(2)}) collective-permute-start(bf16[24,2048]{1,0:T(8,128)(2,1)S(1)} %get-tuple-element.32), channel_id=1, source_target_pairs={{0,6},{1,7},{2,4},{3,5},{4,2},{5,3},{6,0},{7,1},{8,14},{9,15},{10,... | collective-permute-start | bytes 294920 | tf_op jit(solution)/shard_map/ppermute | solution.py:239
  11.5 0.9 %copy-start.2 = (bf16[32,3456]{1,0:T(8,128)(2,1)S(1)}, bf16[32,3456]{1,0:T(8,128)(2,1)}, u32[]{:S(2)}) copy-start(bf16[32,3456]{1,0:T(8,128)(2,1)} %param.6) | copy-start | bytes 663556
  11.6 1.8 %collective-permute-start.3 = (bf16[4,24,2048]{2,1,0:T(8,128)(2,1)S(1)}, bf16[4,24,2048]{2,1,0:T(8,128)(2,1)S(1)}, u32[]{:S(2)}, u32[]{:S(2)}) collective-permute-start(bf16[4,24,2048]{2,1,0:T(8,128)(2,1)S(1)} %pad_maximum_fusion.refs_0_), channel_id=1, source_target_pairs={{0,1},{1,0},{2,3},{3,2},{4,5},{5,4},{6,7},{7,6},{8,9},{9,8},{10,11... | collective-permute-start | bytes 1179656 | tf_op jit(solution)/shard_map/ppermute | solution.py:239
  12.8 0.9 %copy-start = (bf16[32,1,2048]{2,0,1:T(8,128)(2,1)S(1)}, bf16[32,1,2048]{2,0,1:T(8,128)(2,1)}, u32[]{:S(2)}) copy-start(bf16[32,1,2048]{2,0,1:T(8,128)(2,1)} %param.7) | copy-start | bytes 393220
  13.7 9.7 %copy-start.1 = (bf16[16,1728]{1,0:T(8,128)(2,1)S(1)}, bf16[16,1728]{1,0:T(8,128)(2,1)}, u32[]{:S(2)}) copy-start(bf16[16,1728]{1,0:T(8,128)(2,1)} %param.5) | copy-start | bytes 165892
  21.8 4.8 %collective-permute-start.12 = (bf16[16,3456]{1,0:T(8,128)(2,1)S(1)}, bf16[16,3456]{1,0:T(8,128)(2,1)S(1)}, u32[]{:S(2)}, u32[]{:S(2)}) collective-permute-start(bf16[16,3456]{1,0:T(8,128)(2,1)S(1)} %get-tuple-element.23), channel_id=1, source_target_pairs={{0,8},{8,0},{16,24},{24,16},{1,9},{9,1},{17,25},{25,17},{2,10},{10... | collective-permute-start | bytes 331784 | tf_op jit(solution)/shard_map/ppermute | solution.py:239
  23.8 5.5 %collective-permute-start.4 = (bf16[4,16,2048]{2,1,0:T(8,128)(2,1)S(1)}, bf16[4,16,2048]{2,1,0:T(8,128)(2,1)S(1)}, u32[]{:S(2)}, u32[]{:S(2)}) collective-permute-start(bf16[4,16,2048]{2,1,0:T(8,128)(2,1)S(1)} %get-tuple-element.16), channel_id=1, source_target_pairs={{0,1},{1,0},{2,3},{3,2},{4,5},{5,4},{6,7},{7,6},{8,9},{9,8},{10,11... | collective-permute-start | bytes 786440 | tf_op jit(solution)/shard_map/ppermute | solution.py:239
  26.6 6.9 %collective-permute-start.13 = (bf16[16,3456]{1,0:T(8,128)(2,1)S(1)}, bf16[16,3456]{1,0:T(8,128)(2,1)S(1)}, u32[]{:S(2)}, u32[]{:S(2)}) collective-permute-start(bf16[16,3456]{1,0:T(8,128)(2,1)S(1)} %add_convert_fusion.1), channel_id=1, source_target_pairs={{0,16},{8,24},{16,0},{24,8},{1,17},{9,25},{17,1},{25,9},{2,18},{10... | collective-permute-start | bytes 331784 | tf_op jit(solution)/shard_map/ppermute | solution.py:239
  29.3 4.3 %collective-permute-start.5 = (bf16[16,2048]{1,0:T(8,128)(2,1)S(1)}, bf16[16,2048]{1,0:T(8,128)(2,1)S(1)}, u32[]{:S(2)}, u32[]{:S(2)}) collective-permute-start(bf16[16,2048]{1,0:T(8,128)(2,1)S(1)} %get-tuple-element.26), channel_id=1, source_target_pairs={{0,2},{1,3},{2,0},{3,1},{4,6},{5,7},{6,4},{7,5},{8,10},{9,11},{10,... | collective-permute-start | bytes 196616 | tf_op jit(solution)/shard_map/ppermute | solution.py:239
  30.1 4.3 %collective-permute-start.6 = (bf16[16,2048]{1,0:T(8,128)(2,1)S(1)}, bf16[16,2048]{1,0:T(8,128)(2,1)S(1)}, u32[]{:S(2)}, u32[]{:S(2)}) collective-permute-start(bf16[16,2048]{1,0:T(8,128)(2,1)S(1)} %get-tuple-element.25), channel_id=1, source_target_pairs={{0,4},{1,5},{2,6},{3,7},{4,0},{5,1},{6,2},{7,3},{8,12},{9,13},{10,... | collective-permute-start | bytes 196616 | tf_op jit(solution)/shard_map/ppermute | solution.py:239
  31.0 5.2 %collective-permute-start.7 = (bf16[16,2048]{1,0:T(8,128)(2,1)S(1)}, bf16[16,2048]{1,0:T(8,128)(2,1)S(1)}, u32[]{:S(2)}, u32[]{:S(2)}) collective-permute-start(bf16[16,2048]{1,0:T(8,128)(2,1)S(1)} %get-tuple-element.24), channel_id=1, source_target_pairs={{0,6},{1,7},{2,4},{3,5},{4,2},{5,3},{6,0},{7,1},{8,14},{9,15},{10,... | collective-permute-start | bytes 196616 | tf_op jit(solution)/shard_map/ppermute | solution.py:239
  38.2 1.8 %collective-permute-start.8 = (bf16[4,8,2048]{2,1,0:T(8,128)(2,1)S(1)}, bf16[4,8,2048]{2,1,0:T(8,128)(2,1)S(1)}, u32[]{:S(2)}, u32[]{:S(2)}) collective-permute-start(bf16[4,8,2048]{2,1,0:T(8,128)(2,1)S(1)} %get-tuple-element.20), channel_id=1, source_target_pairs={{0,1},{1,0},{2,3},{3,2},{4,5},{5,4},{6,7},{7,6},{8,9},{9,8},{10,11... | collective-permute-start | bytes 393224 | tf_op jit(solution)/shard_map/ppermute | solution.py:239
  38.3 6.7 %collective-permute-start.14 = (bf16[16,5184]{1,0:T(8,128)(2,1)S(1)}, bf16[16,5184]{1,0:T(8,128)(2,1)S(1)}, u32[]{:S(2)}, u32[]{:S(2)}) collective-permute-start(bf16[16,5184]{1,0:T(8,128)(2,1)S(1)} %pad_maximum_fusion.1), channel_id=1, source_target_pairs={{0,8},{8,0},{16,24},{24,16},{1,9},{9,1},{17,25},{25,17},{2,10},{10... | collective-permute-start | bytes 497672 | tf_op jit(solution)/shard_map/ppermute | solution.py:239
  40.0 5.4 %collective-permute-start.10 = (bf16[8,2048]{1,0:T(8,128)(2,1)S(1)}, bf16[8,2048]{1,0:T(8,128)(2,1)S(1)}, u32[]{:S(2)}, u32[]{:S(2)}) collective-permute-start(bf16[8,2048]{1,0:T(8,128)(2,1)S(1)} %get-tuple-element.30), channel_id=1, source_target_pairs={{0,4},{1,5},{2,6},{3,7},{4,0},{5,1},{6,2},{7,3},{8,12},{9,13},{10,... | collective-permute-start | bytes 98312 | tf_op jit(solution)/shard_map/ppermute | solution.py:239
  41.1 5.1 %collective-permute-start.11 = (bf16[8,2048]{1,0:T(8,128)(2,1)S(1)}, bf16[8,2048]{1,0:T(8,128)(2,1)S(1)}, u32[]{:S(2)}, u32[]{:S(2)}) collective-permute-start(bf16[8,2048]{1,0:T(8,128)(2,1)S(1)} %get-tuple-element.29), channel_id=1, source_target_pairs={{0,6},{1,7},{2,4},{3,5},{4,2},{5,3},{6,0},{7,1},{8,14},{9,15},{10,... | collective-permute-start | bytes 98312 | tf_op jit(solution)/shard_map/ppermute | solution.py:239
  42.8 3.9 %collective-permute-start.9 = (bf16[8,2048]{1,0:T(8,128)(2,1)S(1)}, bf16[8,2048]{1,0:T(8,128)(2,1)S(1)}, u32[]{:S(2)}, u32[]{:S(2)}) collective-permute-start(bf16[8,2048]{1,0:T(8,128)(2,1)S(1)} %get-tuple-element.28), channel_id=1, source_target_pairs={{0,2},{1,3},{2,0},{3,1},{4,6},{5,7},{6,4},{7,5},{8,10},{9,11},{10,... | collective-permute-start | bytes 98312 | tf_op jit(solution)/shard_map/ppermute | solution.py:239
  45.1 5.5 %collective-permute-start.15 = (bf16[16,1728]{1,0:T(8,128)(2,1)S(1)}, bf16[16,1728]{1,0:T(8,128)(2,1)S(1)}, u32[]{:S(2)}, u32[]{:S(2)}) collective-permute-start(bf16[16,1728]{1,0:T(8,128)(2,1)S(1)} %add_convert_fusion.6), channel_id=1, source_target_pairs={{0,16},{8,24},{16,0},{24,8},{1,17},{9,25},{17,1},{25,9},{2,18},{10... | collective-permute-start | bytes 165896 | tf_op jit(solution)/shard_map/ppermute | solution.py:239

commit v3 on v2

v3 whole, which is shorter than its diff:
```python
import functools
import math

import jax
import jax.numpy as jnp
from jax import lax
from jax.experimental import pallas as pl
from jax.experimental.pallas import tpu as pltpu
from jax.sharding import PartitionSpec as P

SIDE = 16
PLANE = SIDE * SIDE
F32 = jnp.float32
BF16 = jnp.bfloat16
VMEM_LIMIT = 48 * 1024 * 1024


def pitch_of(channels):
    width = 3 * channels
    slack = max((i * width) % 128 for i in range(9))
    return -(-(width + slack) // 128) * 128


def lane_grid(width):
    lane = lax.broadcasted_iota(jnp.int32, (1, width), 1)
    return lane % SIDE, (lane // SIDE) % SIDE


def inside(grid_xy, dy, dx):
    x, y = grid_xy
    ok = None
    for coord, step in ((y, dy), (x, dx)):
        if step < 0:
            now = coord >= -step
        elif step > 0:
            now = coord < SIDE - step
        else:
            continue
        ok = now if ok is None else ok & now
    return ok


def moved(values, grid_xy, dy, dx):
    if dy == 0 and dx == 0:
        return values
    width = values.shape[1]
    rolled = pltpu.roll(values, (-(dy * SIDE + dx)) % width, 1)
    return jnp.where(inside(grid_xy, dy, dx), rolled, 0.0)


def sigmoid(v):
    return 0.5 + 0.5 * jnp.tanh(0.5 * v)


def dot(a, b):
    return lax.dot_general(a, b, (((1,), (0,)), ((), ())), preferred_element_type=F32)


def dot_nt(a, b):
    return lax.dot_general(a, b, (((1,), (1,)), ((), ())), preferred_element_type=F32)


def chunk_of(cells):
    return 2 * PLANE if cells % (2 * PLANE) == 0 else PLANE


def forward_kernel(n_mp, c0, *refs):
    near_ref, far_ref, w2r_ref, w2b_ref, cot_ref = refs[:5]
    feat_ref, pre_ref, vol_ref, keep_ref, give_ref, grad_ref = refs[5:11]
    vs, w1s, v3, w1r, hid, pre, d9, part, acc = refs[11:]

    me = lax.axis_index("mp")
    f1 = w1s.shape[1]
    c1 = n_mp * f1
    f2, cells = cot_ref.shape
    chunk = chunk_of(cells)
    steps = cells // chunk
    pitch = pitch_of(c0)
    grid_xy = lane_grid(chunk)

    for k in range(n_mp):
        piece = (far_ref if k % 2 else near_ref)[k // 2].astype(F32)
        slot = me ^ k
        w1s[slot] = piece[:f1]
        vs[slot] = piece[f1:, :cells]

    lane = lax.broadcasted_iota(jnp.int32, (1, pitch), 1)
    for dz in range(3):
        for dy in range(3):
            start = (dz * 3 + dy) * 3 * c0
            low = start // 128 * 128
            block = w1s[:, :, low : low + pitch].reshape(c1, pitch)
            if start != low:
                block = pltpu.roll(block, pitch - (start - low), 1)
            block = jnp.where(lane < 3 * c0, block, 0.0)
            w1r[dy * c1 : (dy + 1) * c1, dz * pitch : (dz + 1) * pitch] = block.astype(BF16)

    for ref in (v3, hid, d9):
        zero = jnp.zeros((ref.shape[0], PLANE), BF16)
        ref[:, :PLANE] = zero
        ref[:, PLANE + cells :] = zero
    v3[3 * c0 :, PLANE : PLANE + cells] = jnp.zeros((pitch - 3 * c0, cells), BF16)

    for step in range(steps):
        base = step * chunk
        values = vs[:, :, base : base + chunk].reshape(c0, chunk)
        vol_ref[:, base : base + chunk] = values.astype(BF16)
        for dx in range(3):
            v3[dx * c0 : (dx + 1) * c0, base + PLANE : base + PLANE + chunk] = moved(values, grid_xy, 0, dx - 1).astype(BF16)

    def stacked(ref, base, order):
        return jnp.concatenate([ref[:, base + dz * PLANE : base + dz * PLANE + chunk] for dz in order], axis=0)

    def first_conv(base):
        z = dot(w1r[...], stacked(v3, base, (0, 1, 2)))
        total = z[c1 : 2 * c1]
        total = total + moved(z[:c1], grid_xy, -1, 0)
        total = total + moved(z[2 * c1 :], grid_xy, 1, 0)
        pre[:, base : base + chunk] = total
        hid[:, base + PLANE : base + PLANE + chunk] = (total * sigmoid(total)).astype(BF16)

    def second_conv(base):
        z = dot(w2r_ref[...], stacked(hid, base, (0, 1, 2)))
        total = None
        for dy in range(3):
            for dx in range(3):
                k = dy * 3 + dx
                term = moved(z[k * f2 : (k + 1) * f2], grid_xy, dy - 1, dx - 1)
                total = term if total is None else total + term
        s = sigmoid(total)
        feat_ref[:, base : base + chunk] = (total * s).astype(BF16)
        cot = cot_ref[:, base : base + chunk].astype(F32)
        delta = (cot * (s * (1.0 + total * (1.0 - s)))).astype(BF16).astype(F32)
        for dy in range(3):
            for dx in range(3):
                k = dy * 3 + dx
                d9[k * f2 : (k + 1) * f2, base + PLANE : base + PLANE + chunk] = moved(delta, grid_xy, 1 - dy, 1 - dx).astype(BF16)

    def gradients(base):
        deltas = stacked(d9, base, (2, 1, 0))
        part[:, :, base : base + chunk] = dot(w2b_ref[...], deltas).reshape(n_mp, f1, chunk)
        g = dot_nt(deltas, hid[:, base + PLANE : base + PLANE + chunk])
        acc[...] = g if base == 0 else acc[...] + g

    for step in range(steps + 2):
        if step < steps:
            first_conv(step * chunk)
        if 1 <= step <= steps:
            second_conv((step - 1) * chunk)
        if step >= 2:
            gradients((step - 2) * chunk)

    pre_ref[...] = pre[pl.ds(pl.multiple_of(me * f1, f1), f1), :]
    for k in range(n_mp):
        (give_ref if k % 2 else keep_ref)[k // 2] = part[me ^ k].astype(BF16)
    for t in range(27):
        grad_ref[:, t * c1 : (t + 1) * c1] = acc[t * f2 : (t + 1) * f2].astype(BF16)


def backward_kernel(n_mp, *refs):
    parts = refs[: n_mp // 2]
    pre_ref, vol_ref, w1b_ref, keep_ref, give_ref, grad_ref, d9, part, acc = refs[n_mp // 2 :]
    me = lax.axis_index("mp")
    f1, cells = pre_ref.shape
    c0 = vol_ref.shape[0]
    chunk = chunk_of(cells)
    steps = cells // chunk
    grid_xy = lane_grid(chunk)

    zero = jnp.zeros((d9.shape[0], PLANE), BF16)
    d9[:, :PLANE] = zero
    d9[:, PLANE + cells :] = zero

    reps = max(1, 128 // c0)
    span = reps * c0

    def take(base):
        total = parts[0][:, base : base + chunk].astype(F32)
        for other in parts[1:]:
            total = total + other[:, base : base + chunk].astype(F32)
        v = pre_ref[:, base : base + chunk]
        s = sigmoid(v)
        delta = (total * (s * (1.0 + v * (1.0 - s)))).astype(BF16).astype(F32)
        shifts = [moved(delta, grid_xy, 1 - dy, 1 - dx) for dy in range(3) for dx in range(3)]
        d9[:, base + PLANE : base + PLANE + chunk] = jnp.concatenate(shifts, axis=0).astype(BF16)

    def gradients(base):
        deltas = jnp.concatenate([d9[:, base + dz * PLANE : base + dz * PLANE + chunk] for dz in (2, 1, 0)], axis=0)
        part[:, :, base : base + chunk] = dot(w1b_ref[...], deltas).reshape(n_mp, c0 // n_mp, chunk)
        vol = vol_ref[:, base : base + chunk]
        g = dot_nt(deltas, jnp.concatenate([vol] * reps, axis=0))
        acc[...] = g if base == 0 else acc[...] + g

    for step in range(steps + 1):
        if step < steps:
            take(step * chunk)
        if step >= 1:
            gradients((step - 1) * chunk)
    for k in range(n_mp):
        (give_ref if k % 2 else keep_ref)[k // 2] = part[me ^ k].astype(BF16)

    lane = lax.broadcasted_iota(jnp.int32, (1, span), 1)
    for t in range(0, 27, reps):
        merged = acc[t * f1 : (t + 1) * f1]
        for r in range(1, min(reps, 27 - t)):
            merged = jnp.where(lane >= r * c0, acc[(t + r) * f1 : (t + r + 1) * f1], merged)
        width = min(span, (27 - t) * c0)
        grad_ref[:, t * c0 : t * c0 + width] = merged[:, :width].astype(BF16)


def swap(value, axis, k):
    n = lax.axis_size(axis)
    return lax.ppermute(value, axis, [(i, i ^ k) for i in range(n)])


def add(a, b):
    return (a.astype(F32) + b.astype(F32)).astype(BF16)


def sum_over_chips(keep, got):
    parts = [add(keep[j], got[j]) for j in range(keep.shape[0])]
    return [parts[0]] + [swap(parts[j], "mp", 2 * j) for j in range(1, len(parts))]


def bits_of(count):
    return [1 << i for i in reversed(range(count.bit_length() - 1))]


def call(kernel, out_shape, scratch, flops, nbytes):
    return pl.pallas_call(
        kernel,
        out_shape=out_shape,
        scratch_shapes=scratch,
        compiler_params=pltpu.CompilerParams(vmem_limit_bytes=VMEM_LIMIT),
        cost_estimate=pl.CostEstimate(flops=flops, bytes_accessed=nbytes, transcendentals=0),
    )


def local(volumes, w_first, w_second, cotangent):
    n_mp = lax.axis_size("mp")
    n_sample = lax.axis_size("sample")
    rows_in, _, cells = volumes.shape
    f1 = w_first.shape[0]
    f2 = w_second.shape[0]
    c0 = w_first.shape[1] // 27
    c1 = w_second.shape[1] // 27
    pitch = pitch_of(c0)
    scale = 1.0 / math.sqrt(n_sample * volumes.shape[1] * cells)
    volumes = volumes.reshape(rows_in, cells)
    cotangent = cotangent.reshape(f2, cells)
    padded = cells + 2 * PLANE

    need = (8 * 3 * c0) // 128 * 128 + pitch
    wide = max(cells, need)
    piece = jnp.concatenate(
        [
            jnp.pad(w_first, ((0, 0), (0, wide - w_first.shape[1]))),
            jnp.pad(volumes, ((0, 0), (0, wide - cells))),
        ],
        axis=0,
    )
    near = [piece] + [swap(piece, "mp", k) for k in range(2, n_mp, 2)]
    near = jnp.stack(near)
    far = swap(near, "mp", 1)

    w2t = w_second.reshape(f2, 3, 9, c1)
    w2r = jnp.transpose(w2t, (2, 0, 1, 3)).reshape(9 * f2, 3 * c1)
    w2b = jnp.transpose(w2t, (3, 1, 2, 0)).reshape(c1, 27 * f2)
    w1b = jnp.transpose(w_first.reshape(f1, 27, c0), (2, 1, 0)).reshape(c0, 27 * f1)

    sds = jax.ShapeDtypeStruct
    half = n_mp // 2
    features, pre_own, vol_all, keep, give, grad_second = call(
        functools.partial(forward_kernel, n_mp, c0),
        [
            sds((f2, cells), BF16),
            sds((f1, cells), F32),
            sds((c0, cells), BF16),
            sds((half, f1, cells), BF16),
            sds((half, f1, cells), BF16),
            sds((f2, 27 * c1), BF16),
        ],
        [
            pltpu.VMEM((n_mp, rows_in, cells), F32),
            pltpu.VMEM((n_mp, f1, wide), F32),
            pltpu.VMEM((pitch, padded), BF16),
            pltpu.VMEM((3 * c1, 3 * pitch), BF16),
            pltpu.VMEM((c1, padded), BF16),
            pltpu.VMEM((c1, cells), F32),
            pltpu.VMEM((9 * f2, padded), BF16),
            pltpu.VMEM((n_mp, f1, cells), F32),
            pltpu.VMEM((27 * f2, c1), F32),
        ],
        2 * cells * 27 * (c0 * c1 + 3 * f2 * c1),
        4 * 1024 * 1024,
    )(near, far, w2r, w2b, cotangent)

    bits = bits_of(n_sample)
    parts = sum_over_chips(keep, swap(give, "mp", 1))
    second_got = swap(grad_second, "sample", bits[0])

    keep, give, grad_first = call(
        functools.partial(backward_kernel, n_mp),
        [
            sds((half, rows_in, cells), BF16),
            sds((half, rows_in, cells), BF16),
            sds((f1, 27 * c0), BF16),
        ],
        [
            pltpu.VMEM((9 * f1, padded), BF16),
            pltpu.VMEM((n_mp, rows_in, cells), F32),
            pltpu.VMEM((27 * f1, max(1, 128 // c0) * c0), F32),
        ],
        2 * cells * 27 * 2 * c0 * f1,
        1024 * 1024,
    )(*parts, pre_own, vol_all, w1b)
    ins = sum_over_chips(keep, swap(give, "mp", 1))

    second_got, grad_first = lax.optimization_barrier((second_got, grad_first))
    first_got = swap(grad_first, "sample", bits[0])
    for bit in bits[1:]:
        grad_first = add(grad_first, first_got)
        first_got = swap(grad_first, "sample", bit)
        grad_second = add(grad_second, second_got)
        second_got = swap(grad_second, "sample", bit)
    grad_first = (grad_first.astype(F32) + first_got.astype(F32)) * scale
    grad_second = (grad_second.astype(F32) + second_got.astype(F32)) * scale
    total = ins[0].astype(F32)
    for other in ins[1:]:
        total = total + other.astype(F32)
    return (
        features.reshape(f2, 1, cells),
        total.astype(BF16).reshape(rows_in, 1, cells),
        grad_first,
        grad_second,
    )


def solution(mesh):
    return jax.shard_map(
        local,
        mesh=mesh,
        in_specs=(P("mp", "sample", None), P("mp", None), P("mp", None), P("mp", "sample", None)),
        out_specs=(P("mp", "sample", None), P("mp", "sample", None), P("mp", None), P("mp", None)),
        check_vma=False,
    )
```

time: 51.5 us -> 47.8 us (0.928)
  Pallas kernels: 10.8 us -> 6.94 us
  waiting for transfers between devices: 17.1 us -> 15.7 us
  starting transfers between devices: 18.1 us -> 19 us
  other arithmetic: 2.39 us -> 3.2 us
    pallas_call x2 -> x1, Pallas kernels: 8.84 us -> 5.89 us  [local(): call(functools.partial(forward_kernel, n_mp, c0), [sds((f2, cells), BF16)...]
    ppermute x16, waiting for transfers between devices: 17.1 us -> 15.7 us  [swap(): return lax.ppermute(value, axis, [(i, i ^ k) for i in range(n)])]
    pallas_call x1, Pallas kernels: 1.99 us -> 1.05 us  [local(): call(functools.partial(backward_kernel, n_mp), [sds((half, rows_in, cells...]
    ppermute x16, starting transfers between devices: 18.1 us -> 19 us  [swap(): return lax.ppermute(value, axis, [(i, i ^ k) for i in range(n)])]
    mul x1 -> x2, other arithmetic: 0.66 us -> 1.49 us  [the longest x1 0.82 us: local(): grad_second = (grad_second.astype(F32) + second_got.astype(F32)) * scale]
  transfers between devices with their start and end apart: 16 -> 16, of which waited for: 13 -> 12; matrix products, arithmetic and copies ran while one was open for 3% -> 5% of each run, Pallas kernels for 2% -> 2%
where the time goes in v3:
time: 47.8 us; the launch traced here: 47.6 us
  starting transfers between devices  19 us (40%)
  waiting for transfers between devices  15.7 us (33%)
  Pallas kernels  6.94 us (15%)
  other arithmetic  3.2 us (7%)
  local copies, waits for them, and re-layouts  2.01 us (4%)
  between operations  0.75 us (2%)
    ppermute x16, starting transfers between devices, swap(): return lax.ppermute(value, axis, [(i, i ^ k) for i in range(n)])  19 us
    ppermute x16, waiting for transfers between devices, swap(): return lax.ppermute(value, axis, [(i, i ^ k) for i in range(n)])  15.7 us
    pallas_call x1, Pallas kernels, local(): call(functools.partial(forward_kernel, n_mp, c0), [sds((f2, cells), BF16)...  5.89 us
    unnamed x7, local copies, waits for them, and re-layouts  1.21 us
    pallas_call x1, Pallas kernels, local(): call(functools.partial(backward_kernel, n_mp), [sds((half, rows_in, cells...  1.05 us
  transfers between devices with their start and end apart: 16, of which 12 were waited for; matrix products, arithmetic and copies ran while one was open for 5% of the time, Pallas kernels for 2%

profile of v3, /device:TPU:0, one launch (start us, length us, event | category | flops | bytes accessed | tf_op | source)
XLA Modules:
  0.0 47.6 jit_solution(136796781908070095)
XLA Ops:
  0.6 0.9 %fusion.14 = (bf16[1,24,2048]{2,1,0:T(8,128)(2,1)S(1)}, bf16[24,2048]{1,0:T(8,128)(2,1)S(1)}) fusion(bf16[8,2048]{1,0:T(8,128)(2,1)} %bitcast.52, bf16[16,1728]{1,0:T(8,128)(2,1)} %param.5), kind=kLoop, calls=%fused_computation.30 | loop fusion | flops 294912 | bytes 284672 | tf_op jit(solution)/shard_map/stack | solution.py:263
  1.5 3.0 %collective-permute-start = (bf16[24,2048]{1,0:T(8,128)(2,1)S(1)}, bf16[24,2048]{1,0:T(8,128)(2,1)S(1)}, u32[]{:S(2)}, u32[]{:S(2)}) collective-permute-start(bf16[24,2048]{1,0:T(8,128)(2,1)S(1)} %get-tuple-element.34), channel_id=1, source_target_pairs={{0,2},{1,3},{2,0},{3,1},{4,6},{5,7},{6,4},{7,5},{8,10},{9,11},{10,... | collective-permute-start | bytes 294920 | tf_op jit(solution)/shard_map/ppermute | solution.py:213
  4.5 1.5 %collective-permute-start.1 = (bf16[24,2048]{1,0:T(8,128)(2,1)S(1)}, bf16[24,2048]{1,0:T(8,128)(2,1)S(1)}, u32[]{:S(2)}, u32[]{:S(2)}) collective-permute-start(bf16[24,2048]{1,0:T(8,128)(2,1)S(1)} %get-tuple-element.34), channel_id=1, source_target_pairs={{0,4},{1,5},{2,6},{3,7},{4,0},{5,1},{6,2},{7,3},{8,12},{9,13},{10,... | collective-permute-start | bytes 294920 | tf_op jit(solution)/shard_map/ppermute | solution.py:213
  6.0 0.0 collective-permute-start.2
  6.0 1.5 %collective-permute-done = bf16[24,2048]{1,0:T(8,128)(2,1)S(1)} collective-permute-done((bf16[24,2048]{1,0:T(8,128)(2,1)S(1)}, bf16[24,2048]{1,0:T(8,128)(2,1)S(1)}, u32[]{:S(2)}, u32[]{:S(2)}) %collective-permute-start) | collective-permute-done | bytes 98336 | tf_op jit(solution)/shard_map/ppermute | solution.py:213
  7.5 2.6 %collective-permute-done.1 = bf16[24,2048]{1,0:T(8,128)(2,1)S(1)} collective-permute-done((bf16[24,2048]{1,0:T(8,128)(2,1)S(1)}, bf16[24,2048]{1,0:T(8,128)(2,1)S(1)}, u32[]{:S(2)}, u32[]{:S(2)}) %collective-permute-start.1) | collective-permute-done | bytes 98336 | tf_op jit(solution)/shard_map/ppermute | solution.py:213
  10.2 1.4 %collective-permute-done.2 = bf16[24,2048]{1,0:T(8,128)(2,1)S(1)} collective-permute-done((bf16[24,2048]{1,0:T(8,128)(2,1)S(1)}, bf16[24,2048]{1,0:T(8,128)(2,1)S(1)}, u32[]{:S(2)}, u32[]{:S(2)}) %collective-permute-start.2) | collective-permute-done | bytes 98336 | tf_op jit(solution)/shard_map/ppermute | solution.py:213
  11.5 0.0 copy-start.2
  11.5 0.1 pad_maximum_fusion.refs_0_
  11.6 0.1 collective-permute-start.3
  11.7 0.8 %copy-done.2 = bf16[32,3456]{1,0:T(8,128)(2,1)S(1)} copy-done((bf16[32,3456]{1,0:T(8,128)(2,1)S(1)}, bf16[32,3456]{1,0:T(8,128)(2,1)}, u32[]{:S(2)}) %copy-start.2) | copy-done | bytes 221208
  12.5 0.1 reshape.70
  12.6 0.1 copy.11
  12.8 0.1 copy.12
  12.8 0.0 copy-start
  12.8 0.2 copy.13.refs_3_
  13.0 0.4 collective-permute-done.3.refs_1_
  13.4 0.4 copy-done
  13.7 5.9 %shard_map.75 = (bf16[32,2048]{1,0:T(8,128)(2,1)}, f32[16,2048]{1,0:T(8,128)S(1)}, bf16[64,2048]{1,0:T(8,128)(2,1)S(1)}, bf16[4,16,2048]{2,1,0:T(8,128)(2,1)S(1)...) custom-call(bf16[4,24,2048]{2,1,0:T(8,128)(2,1)S(1)} %pad_maximum_fusion.refs_0_, ...), custom_call_target="tpu_custom_call" | custom-call | flops 2264924160 | bytes 4194304 | tf_op jit(solution)/shard_map/pallas_call | solution.py:273
  19.6 0.0 collective-permute-start.4
  19.6 2.6 %collective-permute-start.12 = (bf16[32,3456]{1,0:T(8,128)(2,1)S(1)}, bf16[32,3456]{1,0:T(8,128)(2,1)S(1)}, u32[]{:S(2)}, u32[]{:S(2)}) collective-permute-start(bf16[32,3456]{1,0:T(8,128)(2,1)S(1)} %get-tuple-element.22), channel_id=1, source_target_pairs={{0,16},{8,24},{16,0},{24,8},{1,17},{9,25},{17,1},{25,9},{2,18},{10... | collective-permute-start | bytes 663560 | tf_op jit(solution)/shard_map/ppermute | solution.py:213
  22.3 0.0 collective-permute-done.4
  22.3 0.0 copy-start.1
  22.3 0.1 fusion.5
  22.4 0.7 %collective-permute-start.5 = (bf16[16,2048]{1,0:T(8,128)(2,1)S(1)}, bf16[16,2048]{1,0:T(8,128)(2,1)S(1)}, u32[]{:S(2)}, u32[]{:S(2)}) collective-permute-start(bf16[16,2048]{1,0:T(8,128)(2,1)S(1)} %get-tuple-element.28), channel_id=1, source_target_pairs={{0,2},{1,3},{2,0},{3,1},{4,6},{5,7},{6,4},{7,5},{8,10},{9,11},{10,... | collective-permute-start | bytes 196616 | tf_op jit(solution)/shard_map/ppermute | solution.py:213
  23.1 1.0 %collective-permute-start.6 = (bf16[16,2048]{1,0:T(8,128)(2,1)S(1)}, bf16[16,2048]{1,0:T(8,128)(2,1)S(1)}, u32[]{:S(2)}, u32[]{:S(2)}) collective-permute-start(bf16[16,2048]{1,0:T(8,128)(2,1)S(1)} %get-tuple-element.27), channel_id=1, source_target_pairs={{0,4},{1,5},{2,6},{3,7},{4,0},{5,1},{6,2},{7,3},{8,12},{9,13},{10,... | collective-permute-start | bytes 196616 | tf_op jit(solution)/shard_map/ppermute | solution.py:213
  24.0 1.9 %collective-permute-start.7 = (bf16[16,2048]{1,0:T(8,128)(2,1)S(1)}, bf16[16,2048]{1,0:T(8,128)(2,1)S(1)}, u32[]{:S(2)}, u32[]{:S(2)}) collective-permute-start(bf16[16,2048]{1,0:T(8,128)(2,1)S(1)} %get-tuple-element.26), channel_id=1, source_target_pairs={{0,6},{1,7},{2,4},{3,5},{4,2},{5,3},{6,0},{7,1},{8,14},{9,15},{10,... | collective-permute-start | bytes 196616 | tf_op jit(solution)/shard_map/ppermute | solution.py:213
  25.9 0.0 copy-done.1
  25.9 0.2 reshape.75
  26.1 0.1 copy.15.refs_6_
  26.3 0.4 collective-permute-done.5.refs_1_
  26.7 1.3 %collective-permute-done.6.refs_2_ = bf16[16,2048]{1,0:T(8,128)(2,1)S(1)} collective-permute-done((bf16[16,2048]{1,0:T(8,128)(2,1)S(1)}, bf16[16,2048]{1,0:T(8,128)(2,1)S(1)}, u32[]{:S(2)}, u32[]{:S(2)}) %collective-permute-start.6) | collective-permute-done | bytes 65568 | tf_op jit(solution)/shard_map/ppermute | solution.py:213
  28.0 1.2 %collective-permute-done.7.refs_3_ = bf16[16,2048]{1,0:T(8,128)(2,1)S(1)} collective-permute-done((bf16[16,2048]{1,0:T(8,128)(2,1)S(1)}, bf16[16,2048]{1,0:T(8,128)(2,1)S(1)}, u32[]{:S(2)}, u32[]{:S(2)}) %collective-permute-start.7) | collective-permute-done | bytes 65568 | tf_op jit(solution)/shard_map/ppermute | solution.py:213
  29.2 1.1 %shard_map.76 = (bf16[4,8,2048]{2,1,0:T(8,128)(2,1)S(1)}, bf16[4,8,2048]{2,1,0:T(8,128)(2,1)S(1)}, bf16[16,1728]{1,0:T(8,128)(2,1)S(1)}) custom-call(bf16[16,2048]{1,0:T(8,128)(2,1)S(1)} %get-tuple-element.29.refs_0_, bf16[16,2048]{1,0:T(8,128)(2,1)S(1)} %collective-permute-done.5.refs_1_, bf16[16,2048]{1,0:T(8,128)(2,1)S(1)} %collective-permute-done.6.refs_2_, ...), custom_call_target="tpu_custom_call" | custom-call | flops 226492416 | bytes 1048576 | tf_op jit(solution)/shard_map/pallas_call | solution.py:302
  30.2 2.9 %collective-permute-done.12 = bf16[32,3456]{1,0:T(8,128)(2,1)S(1)} collective-permute-done((bf16[32,3456]{1,0:T(8,128)(2,1)S(1)}, bf16[32,3456]{1,0:T(8,128)(2,1)S(1)}, u32[]{:S(2)}, u32[]{:S(2)}) %collective-permute-start.12) | collective-permute-done | bytes 221216 | tf_op jit(solution)/shard_map/ppermute | solution.py:213
  33.1 0.0 collective-permute-start.13
  33.1 0.1 add_convert_fusion
  33.2 4.1 %collective-permute-start.15 = (bf16[32,3456]{1,0:T(8,128)(2,1)S(1)}, bf16[32,3456]{1,0:T(8,128)(2,1)S(1)}, u32[]{:S(2)}, u32[]{:S(2)}) collective-permute-start(bf16[32,3456]{1,0:T(8,128)(2,1)S(1)} %add_convert_fusion), channel_id=1, source_target_pairs={{0,8},{8,0},{16,24},{24,16},{1,9},{9,1},{17,25},{25,17},{2,10},{10... | collective-permute-start | bytes 663560 | tf_op jit(solution)/shard_map/ppermute | solution.py:213
  37.3 0.0 collective-permute-start.8
  37.3 2.2 %collective-permute-done.13 = bf16[16,1728]{1,0:T(8,128)(2,1)S(1)} collective-permute-done((bf16[16,1728]{1,0:T(8,128)(2,1)S(1)}, bf16[16,1728]{1,0:T(8,128)(2,1)S(1)}, u32[]{:S(2)}, u32[]{:S(2)}) %collective-permute-start.13) | collective-permute-done | bytes 55328 | tf_op jit(solution)/shard_map/ppermute | solution.py:213
  39.5 0.5 %collective-permute-start.14 = (bf16[16,1728]{1,0:T(8,128)(2,1)S(1)}, bf16[16,1728]{1,0:T(8,128)(2,1)S(1)}, u32[]{:S(2)}, u32[]{:S(2)}) collective-permute-start(bf16[16,1728]{1,0:T(8,128)(2,1)S(1)} %add_convert_fusion.5), channel_id=1, source_target_pairs={{0,8},{8,0},{16,24},{24,16},{1,9},{9,1},{17,25},{25,17},{2,10},{10... | collective-permute-start | bytes 165896 | tf_op jit(solution)/shard_map/ppermute | solution.py:213
  40.0 0.0 collective-permute-done.8
  40.0 1.0 %collective-permute-start.10 = (bf16[8,2048]{1,0:T(8,128)(2,1)S(1)}, bf16[8,2048]{1,0:T(8,128)(2,1)S(1)}, u32[]{:S(2)}, u32[]{:S(2)}) collective-permute-start(bf16[8,2048]{1,0:T(8,128)(2,1)S(1)} %get-tuple-element.32), channel_id=1, source_target_pairs={{0,4},{1,5},{2,6},{3,7},{4,0},{5,1},{6,2},{7,3},{8,12},{9,13},{10,... | collective-permute-start | bytes 98312 | tf_op jit(solution)/shard_map/ppermute | solution.py:213
  41.0 1.2 %collective-permute-start.11 = (bf16[8,2048]{1,0:T(8,128)(2,1)S(1)}, bf16[8,2048]{1,0:T(8,128)(2,1)S(1)}, u32[]{:S(2)}, u32[]{:S(2)}) collective-permute-start(bf16[8,2048]{1,0:T(8,128)(2,1)S(1)} %get-tuple-element.31), channel_id=1, source_target_pairs={{0,6},{1,7},{2,4},{3,5},{4,2},{5,3},{6,0},{7,1},{8,14},{9,15},{10,... | collective-permute-start | bytes 98312 | tf_op jit(solution)/shard_map/ppermute | solution.py:213
  42.2 1.4 %collective-permute-start.9 = (bf16[8,2048]{1,0:T(8,128)(2,1)S(1)}, bf16[8,2048]{1,0:T(8,128)(2,1)S(1)}, u32[]{:S(2)}, u32[]{:S(2)}) collective-permute-start(bf16[8,2048]{1,0:T(8,128)(2,1)S(1)} %get-tuple-element.30), channel_id=1, source_target_pairs={{0,2},{1,3},{2,0},{3,1},{4,6},{5,7},{6,4},{7,5},{8,10},{9,11},{10,... | collective-permute-start | bytes 98312 | tf_op jit(solution)/shard_map/ppermute | solution.py:213
  43.6 0.9 %collective-permute-done.14 = bf16[16,1728]{1,0:T(8,128)(2,1)S(1)} collective-permute-done((bf16[16,1728]{1,0:T(8,128)(2,1)S(1)}, bf16[16,1728]{1,0:T(8,128)(2,1)S(1)}, u32[]{:S(2)}, u32[]{:S(2)}) %collective-permute-start.14) | collective-permute-done | bytes 55328 | tf_op jit(solution)/shard_map/ppermute | solution.py:213
  44.5 0.7 %add_multiply_fusion.1 = f32[16,1728]{1,0:T(8,128)} fusion(bf16[16,1728]{1,0:T(8,128)(2,1)S(1)} %collective-permute-done.14, bf16[16,1728]{1,0:T(8,128)(2,1)S(1)} %add_convert_fusion.5), kind=kLoop, calls=%fused_computation.10 | loop fusion | flops 110592 | bytes 221184 | tf_op jit(solution)/shard_map/mul | solution.py:326
  45.2 0.0 collective-permute-done.10
  45.2 0.6 %collective-permute-done.11 = bf16[8,2048]{1,0:T(8,128)(2,1)S(1)} collective-permute-done((bf16[8,2048]{1,0:T(8,128)(2,1)S(1)}, bf16[8,2048]{1,0:T(8,128)(2,1)S(1)}, u32[]{:S(2)}, u32[]{:S(2)}) %collective-permute-start.11) | collective-permute-done | bytes 32800 | tf_op jit(solution)/shard_map/ppermute | solution.py:213
  45.8 0.3 collective-permute-done.9
  46.1 0.6 %fusion.13 = bf16[8,1,2048]{2,0,1:T(8,128)(2,1)} fusion(bf16[8,2048]{1,0:T(8,128)(2,1)S(1)} %collective-permute-done.11, bf16[8,2048]{1,0:T(8,128)(2,1)S(1)} %collective-permute-done.10, bf16[8,2048]{1,0:T(8,128)(2,1)S(1)} %collective-permute-done.9, bf16[4,8,2048]{2,1,0:T(8,128)(2,1)S(1)} %collective-permute-done.8, ...), kind=kLoop, calls=%fused_computation.29 | loop fusion | flops 196608 | bytes 196608 | tf_op jit(solution)/shard_map/reshape | solution.py:333
  46.7 0.0 collective-permute-done.15
  46.7 0.8 %add_multiply_fusion = f32[32,3456]{1,0:T(8,128)} fusion(bf16[32,3456]{1,0:T(8,128)(2,1)S(1)} %collective-permute-done.15, bf16[32,3456]{1,0:T(8,128)(2,1)S(1)} %add_convert_fusion), kind=kLoop, calls=%fused_computation | loop fusion | flops 442368 | bytes 884736 | tf_op jit(solution)/shard_map/mul | solution.py:327
  (4 shorter events, 0.1 us)
Async XLA Ops:
  1.5 6.1 %collective-permute-start = (bf16[24,2048]{1,0:T(8,128)(2,1)S(1)}, bf16[24,2048]{1,0:T(8,128)(2,1)S(1)}, u32[]{:S(2)}, u32[]{:S(2)}) collective-permute-start(bf16[24,2048]{1,0:T(8,128)(2,1)S(1)} %get-tuple-element.34), channel_id=1, source_target_pairs={{0,2},{1,3},{2,0},{3,1},{4,6},{5,7},{6,4},{7,5},{8,10},{9,11},{10,... | collective-permute-start | bytes 294920 | tf_op jit(solution)/shard_map/ppermute | solution.py:213
  4.5 5.7 %collective-permute-start.1 = (bf16[24,2048]{1,0:T(8,128)(2,1)S(1)}, bf16[24,2048]{1,0:T(8,128)(2,1)S(1)}, u32[]{:S(2)}, u32[]{:S(2)}) collective-permute-start(bf16[24,2048]{1,0:T(8,128)(2,1)S(1)} %get-tuple-element.34), channel_id=1, source_target_pairs={{0,4},{1,5},{2,6},{3,7},{4,0},{5,1},{6,2},{7,3},{8,12},{9,13},{10,... | collective-permute-start | bytes 294920 | tf_op jit(solution)/shard_map/ppermute | solution.py:213
  6.0 5.5 %collective-permute-start.2 = (bf16[24,2048]{1,0:T(8,128)(2,1)S(1)}, bf16[24,2048]{1,0:T(8,128)(2,1)S(1)}, u32[]{:S(2)}, u32[]{:S(2)}) collective-permute-start(bf16[24,2048]{1,0:T(8,128)(2,1)S(1)} %get-tuple-element.34), channel_id=1, source_target_pairs={{0,6},{1,7},{2,4},{3,5},{4,2},{5,3},{6,0},{7,1},{8,14},{9,15},{10,... | collective-permute-start | bytes 294920 | tf_op jit(solution)/shard_map/ppermute | solution.py:213
  11.5 0.9 %copy-start.2 = (bf16[32,3456]{1,0:T(8,128)(2,1)S(1)}, bf16[32,3456]{1,0:T(8,128)(2,1)}, u32[]{:S(2)}) copy-start(bf16[32,3456]{1,0:T(8,128)(2,1)} %param.6) | copy-start | bytes 663556
  11.6 1.8 %collective-permute-start.3 = (bf16[4,24,2048]{2,1,0:T(8,128)(2,1)S(1)}, bf16[4,24,2048]{2,1,0:T(8,128)(2,1)S(1)}, u32[]{:S(2)}, u32[]{:S(2)}) collective-permute-start(bf16[4,24,2048]{2,1,0:T(8,128)(2,1)S(1)} %pad_maximum_fusion.refs_0_), channel_id=1, source_target_pairs={{0,1},{1,0},{2,3},{3,2},{4,5},{5,4},{6,7},{7,6},{8,9},{9,8},{10,11... | collective-permute-start | bytes 1179656 | tf_op jit(solution)/shard_map/ppermute | solution.py:213
  12.8 0.9 %copy-start = (bf16[32,1,2048]{2,0,1:T(8,128)(2,1)S(1)}, bf16[32,1,2048]{2,0,1:T(8,128)(2,1)}, u32[]{:S(2)}) copy-start(bf16[32,1,2048]{2,0,1:T(8,128)(2,1)} %param.7) | copy-start | bytes 393220
  19.6 2.7 %collective-permute-start.4 = (bf16[4,16,2048]{2,1,0:T(8,128)(2,1)S(1)}, bf16[4,16,2048]{2,1,0:T(8,128)(2,1)S(1)}, u32[]{:S(2)}, u32[]{:S(2)}) collective-permute-start(bf16[4,16,2048]{2,1,0:T(8,128)(2,1)S(1)} %get-tuple-element.17), channel_id=1, source_target_pairs={{0,1},{1,0},{2,3},{3,2},{4,5},{5,4},{6,7},{7,6},{8,9},{9,8},{10,11... | collective-permute-start | bytes 786440 | tf_op jit(solution)/shard_map/ppermute | solution.py:213
  19.6 13.5 %collective-permute-start.12 = (bf16[32,3456]{1,0:T(8,128)(2,1)S(1)}, bf16[32,3456]{1,0:T(8,128)(2,1)S(1)}, u32[]{:S(2)}, u32[]{:S(2)}) collective-permute-start(bf16[32,3456]{1,0:T(8,128)(2,1)S(1)} %get-tuple-element.22), channel_id=1, source_target_pairs={{0,16},{8,24},{16,0},{24,8},{1,17},{9,25},{17,1},{25,9},{2,18},{10... | collective-permute-start | bytes 663560 | tf_op jit(solution)/shard_map/ppermute | solution.py:213
  22.3 3.6 %copy-start.1 = (bf16[16,1728]{1,0:T(8,128)(2,1)S(1)}, bf16[16,1728]{1,0:T(8,128)(2,1)}, u32[]{:S(2)}) copy-start(bf16[16,1728]{1,0:T(8,128)(2,1)} %param.5) | copy-start | bytes 165892
  22.4 4.3 %collective-permute-start.5 = (bf16[16,2048]{1,0:T(8,128)(2,1)S(1)}, bf16[16,2048]{1,0:T(8,128)(2,1)S(1)}, u32[]{:S(2)}, u32[]{:S(2)}) collective-permute-start(bf16[16,2048]{1,0:T(8,128)(2,1)S(1)} %get-tuple-element.28), channel_id=1, source_target_pairs={{0,2},{1,3},{2,0},{3,1},{4,6},{5,7},{6,4},{7,5},{8,10},{9,11},{10,... | collective-permute-start | bytes 196616 | tf_op jit(solution)/shard_map/ppermute | solution.py:213
  23.1 5.0 %collective-permute-start.6 = (bf16[16,2048]{1,0:T(8,128)(2,1)S(1)}, bf16[16,2048]{1,0:T(8,128)(2,1)S(1)}, u32[]{:S(2)}, u32[]{:S(2)}) collective-permute-start(bf16[16,2048]{1,0:T(8,128)(2,1)S(1)} %get-tuple-element.27), channel_id=1, source_target_pairs={{0,4},{1,5},{2,6},{3,7},{4,0},{5,1},{6,2},{7,3},{8,12},{9,13},{10,... | collective-permute-start | bytes 196616 | tf_op jit(solution)/shard_map/ppermute | solution.py:213
  24.0 5.2 %collective-permute-start.7 = (bf16[16,2048]{1,0:T(8,128)(2,1)S(1)}, bf16[16,2048]{1,0:T(8,128)(2,1)S(1)}, u32[]{:S(2)}, u32[]{:S(2)}) collective-permute-start(bf16[16,2048]{1,0:T(8,128)(2,1)S(1)} %get-tuple-element.26), channel_id=1, source_target_pairs={{0,6},{1,7},{2,4},{3,5},{4,2},{5,3},{6,0},{7,1},{8,14},{9,15},{10,... | collective-permute-start | bytes 196616 | tf_op jit(solution)/shard_map/ppermute | solution.py:213
  33.1 6.4 %collective-permute-start.13 = (bf16[16,1728]{1,0:T(8,128)(2,1)S(1)}, bf16[16,1728]{1,0:T(8,128)(2,1)S(1)}, u32[]{:S(2)}, u32[]{:S(2)}) collective-permute-start(bf16[16,1728]{1,0:T(8,128)(2,1)S(1)} %get-tuple-element.24), channel_id=1, source_target_pairs={{0,16},{8,24},{16,0},{24,8},{1,17},{9,25},{17,1},{25,9},{2,18},{10... | collective-permute-start | bytes 165896 | tf_op jit(solution)/shard_map/ppermute | solution.py:213
  33.2 13.5 %collective-permute-start.15 = (bf16[32,3456]{1,0:T(8,128)(2,1)S(1)}, bf16[32,3456]{1,0:T(8,128)(2,1)S(1)}, u32[]{:S(2)}, u32[]{:S(2)}) collective-permute-start(bf16[32,3456]{1,0:T(8,128)(2,1)S(1)} %add_convert_fusion), channel_id=1, source_target_pairs={{0,8},{8,0},{16,24},{24,16},{1,9},{9,1},{17,25},{25,17},{2,10},{10... | collective-permute-start | bytes 663560 | tf_op jit(solution)/shard_map/ppermute | solution.py:213
  37.3 2.7 %collective-permute-start.8 = (bf16[4,8,2048]{2,1,0:T(8,128)(2,1)S(1)}, bf16[4,8,2048]{2,1,0:T(8,128)(2,1)S(1)}, u32[]{:S(2)}, u32[]{:S(2)}) collective-permute-start(bf16[4,8,2048]{2,1,0:T(8,128)(2,1)S(1)} %get-tuple-element.21), channel_id=1, source_target_pairs={{0,1},{1,0},{2,3},{3,2},{4,5},{5,4},{6,7},{7,6},{8,9},{9,8},{10,11... | collective-permute-start | bytes 393224 | tf_op jit(solution)/shard_map/ppermute | solution.py:213
  39.5 5.0 %collective-permute-start.14 = (bf16[16,1728]{1,0:T(8,128)(2,1)S(1)}, bf16[16,1728]{1,0:T(8,128)(2,1)S(1)}, u32[]{:S(2)}, u32[]{:S(2)}) collective-permute-start(bf16[16,1728]{1,0:T(8,128)(2,1)S(1)} %add_convert_fusion.5), channel_id=1, source_target_pairs={{0,8},{8,0},{16,24},{24,16},{1,9},{9,1},{17,25},{25,17},{2,10},{10... | collective-permute-start | bytes 165896 | tf_op jit(solution)/shard_map/ppermute | solution.py:213
  40.0 5.2 %collective-permute-start.10 = (bf16[8,2048]{1,0:T(8,128)(2,1)S(1)}, bf16[8,2048]{1,0:T(8,128)(2,1)S(1)}, u32[]{:S(2)}, u32[]{:S(2)}) collective-permute-start(bf16[8,2048]{1,0:T(8,128)(2,1)S(1)} %get-tuple-element.32), channel_id=1, source_target_pairs={{0,4},{1,5},{2,6},{3,7},{4,0},{5,1},{6,2},{7,3},{8,12},{9,13},{10,... | collective-permute-start | bytes 98312 | tf_op jit(solution)/shard_map/ppermute | solution.py:213
  41.0 4.8 %collective-permute-start.11 = (bf16[8,2048]{1,0:T(8,128)(2,1)S(1)}, bf16[8,2048]{1,0:T(8,128)(2,1)S(1)}, u32[]{:S(2)}, u32[]{:S(2)}) collective-permute-start(bf16[8,2048]{1,0:T(8,128)(2,1)S(1)} %get-tuple-element.31), channel_id=1, source_target_pairs={{0,6},{1,7},{2,4},{3,5},{4,2},{5,3},{6,0},{7,1},{8,14},{9,15},{10,... | collective-permute-start | bytes 98312 | tf_op jit(solution)/shard_map/ppermute | solution.py:213
  42.2 3.9 %collective-permute-start.9 = (bf16[8,2048]{1,0:T(8,128)(2,1)S(1)}, bf16[8,2048]{1,0:T(8,128)(2,1)S(1)}, u32[]{:S(2)}, u32[]{:S(2)}) collective-permute-start(bf16[8,2048]{1,0:T(8,128)(2,1)S(1)} %get-tuple-element.30), channel_id=1, source_target_pairs={{0,2},{1,3},{2,0},{3,1},{4,6},{5,7},{6,4},{7,5},{8,10},{9,11},{10,... | collective-permute-start | bytes 98312 | tf_op jit(solution)/shard_map/ppermute | solution.py:213

commit v4 on v3

--- a/solution.py
+++ b/solution.py
@@ -64,13 +64,29 @@
     return 2 * PLANE if cells % (2 * PLANE) == 0 else PLANE
 
 
+def pack_kernel(w_ref, v_ref, out_ref):
+    f1, width = w_ref.shape
+    rows_in, cells = v_ref.shape
+    run = cells * rows_in // f1
+    lanes = out_ref.shape[1] - run
+    out_ref[:, :width] = w_ref[...]
+    if lanes > width:
+        out_ref[:, width:lanes] = jnp.zeros((f1, lanes - width), BF16)
+    folded = [v_ref[:, i * run : (i + 1) * run].astype(F32) for i in range(f1 // rows_in)]
+    out_ref[:, lanes:] = jnp.concatenate(folded, axis=0).astype(BF16)
+
+
 def forward_kernel(n_mp, c0, *refs):
-    near_ref, far_ref, w2r_ref, w2b_ref, cot_ref = refs[:5]
-    feat_ref, pre_ref, vol_ref, keep_ref, give_ref, grad_ref = refs[5:11]
-    vs, w1s, v3, w1r, hid, pre, d9, part, acc = refs[11:]
+    near_ref, far_ref, w2r_ref, cot_ref = refs[:4]
+    feat_ref, pre_ref, vol_ref, d9, half_keep_ref, half_give_ref = refs[4:10]
+    vs, w1s, v3, w1r, hid, pre, acc = refs[10:]
 
     me = lax.axis_index("mp")
-    f1 = w1s.shape[1]
+    low_half = lax.axis_index("sample") % 2 == 0
+    _, f1, lanes = w1s.shape
+    rows_in = vs.shape[1]
+    folds = f1 // rows_in
+    run = near_ref.shape[2] - lanes
     c1 = n_mp * f1
     f2, cells = cot_ref.shape
     chunk = chunk_of(cells)
@@ -81,8 +97,9 @@
     for k in range(n_mp):
         piece = (far_ref if k % 2 else near_ref)[k // 2].astype(F32)
         slot = me ^ k
-        w1s[slot] = piece[:f1]
-        vs[slot] = piece[f1:, :cells]
+        w1s[slot] = piece[:, :lanes]
+        for i in range(folds):
+            vs[slot, :, i * run : (i + 1) * run] = piece[i * rows_in : (i + 1) * rows_in, lanes:]
 
     lane = lax.broadcasted_iota(jnp.int32, (1, pitch), 1)
     for dz in range(3):
@@ -138,7 +155,6 @@
 
     def gradients(base):
         deltas = stacked(d9, base, (2, 1, 0))
-        part[:, :, base : base + chunk] = dot(w2b_ref[...], deltas).reshape(n_mp, f1, chunk)
         g = dot_nt(deltas, hid[:, base + PLANE : base + PLANE + chunk])
         acc[...] = g if base == 0 else acc[...] + g
 
@@ -151,10 +167,23 @@
             gradients((step - 2) * chunk)
 
     pre_ref[...] = pre[pl.ds(pl.multiple_of(me * f1, f1), f1), :]
+    half = f2 // 2
+    for t in range(27):
+        low = acc[t * f2 : t * f2 + half]
+        high = acc[t * f2 + half : (t + 1) * f2]
+        half_keep_ref[:, t * c1 : (t + 1) * c1] = jnp.where(low_half, low, high).astype(BF16)
+        half_give_ref[:, t * c1 : (t + 1) * c1] = jnp.where(low_half, high, low).astype(BF16)
+
+
+def data_kernel(n_mp, d9, w2b_ref, keep_ref, give_ref, part):
+    me = lax.axis_index("mp")
+    _, f1, cells = part.shape
+    chunk = chunk_of(cells)
+    for base in range(0, cells, chunk):
+        deltas = jnp.concatenate([d9[:, base + dz * PLANE : base + dz * PLANE + chunk] for dz in (2, 1, 0)], axis=0)
+        part[:, :, base : base + chunk] = dot(w2b_ref[...], deltas).reshape(n_mp, f1, chunk)
     for k in range(n_mp):
         (give_ref if k % 2 else keep_ref)[k // 2] = part[me ^ k].astype(BF16)
-    for t in range(27):
-        grad_ref[:, t * c1 : (t + 1) * c1] = acc[t * f2 : (t + 1) * f2].astype(BF16)
 
 
 def backward_kernel(n_mp, *refs):
@@ -208,6 +237,13 @@
         grad_ref[:, t * c0 : t * c0 + width] = merged[:, :width].astype(BF16)
 
 
+def place_kernel(scale, mine_ref, other_ref, out_ref):
+    bit = lax.axis_index("sample") % 2
+    width = out_ref.shape[2]
+    out_ref[bit] = mine_ref[...].astype(F32) * scale
+    out_ref[1 - bit] = other_ref[:, :width].astype(F32) * scale
+
+
 def swap(value, axis, k):
     n = lax.axis_size(axis)
     return lax.ppermute(value, axis, [(i, i ^ k) for i in range(n)])
@@ -222,8 +258,8 @@
     return [parts[0]] + [swap(parts[j], "mp", 2 * j) for j in range(1, len(parts))]
 
 
-def bits_of(count):
-    return [1 << i for i in reversed(range(count.bit_length() - 1))]
+def bits_above(count):
+    return [1 << i for i in range(1, count.bit_length() - 1)]
 
 
 def call(kernel, out_shape, scratch, flops, nbytes):
@@ -250,15 +286,15 @@
     cotangent = cotangent.reshape(f2, cells)
     padded = cells + 2 * PLANE
 
-    need = (8 * 3 * c0) // 128 * 128 + pitch
-    wide = max(cells, need)
-    piece = jnp.concatenate(
-        [
-            jnp.pad(w_first, ((0, 0), (0, wide - w_first.shape[1]))),
-            jnp.pad(volumes, ((0, 0), (0, wide - cells))),
-        ],
-        axis=0,
-    )
+    lanes = (8 * 3 * c0) // 128 * 128 + pitch
+    run = cells * rows_in // f1
+    piece = call(
+        pack_kernel,
+        jax.ShapeDtypeStruct((f1, lanes + run), BF16),
+        [],
+        0,
+        256 * 1024,
+    )(w_first, volumes)
     near = [piece] + [swap(piece, "mp", k) for k in range(2, n_mp, 2)]
     near = jnp.stack(near)
     far = swap(near, "mp", 1)
@@ -270,34 +306,43 @@
 
     sds = jax.ShapeDtypeStruct
     half = n_mp // 2
-    features, pre_own, vol_all, keep, give, grad_second = call(
+    features, pre_own, vol_all, d9, half_keep, half_give = call(
         functools.partial(forward_kernel, n_mp, c0),
         [
             sds((f2, cells), BF16),
             sds((f1, cells), F32),
             sds((c0, cells), BF16),
-            sds((half, f1, cells), BF16),
-            sds((half, f1, cells), BF16),
-            sds((f2, 27 * c1), BF16),
+            sds((9 * f2, padded), BF16),
+            sds((f2 // 2, 27 * c1), BF16),
+            sds((f2 // 2, 27 * c1), BF16),
         ],
         [
             pltpu.VMEM((n_mp, rows_in, cells), F32),
-            pltpu.VMEM((n_mp, f1, wide), F32),
+            pltpu.VMEM((n_mp, f1, lanes), F32),
             pltpu.VMEM((pitch, padded), BF16),
             pltpu.VMEM((3 * c1, 3 * pitch), BF16),
             pltpu.VMEM((c1, padded), BF16),
             pltpu.VMEM((c1, cells), F32),
-            pltpu.VMEM((9 * f2, padded), BF16),
-            pltpu.VMEM((n_mp, f1, cells), F32),
             pltpu.VMEM((27 * f2, c1), F32),
         ],
-        2 * cells * 27 * (c0 * c1 + 3 * f2 * c1),
+        2 * cells * 27 * (c0 * c1 + 2 * f2 * c1),
         4 * 1024 * 1024,
-    )(near, far, w2r, w2b, cotangent)
-
-    bits = bits_of(n_sample)
+    )(near, far, w2r, cotangent)
+
+    half_got = swap(half_give, "sample", 1)
+    keep, give = call(
+        functools.partial(data_kernel, n_mp),
+        [sds((half, f1, cells), BF16), sds((half, f1, cells), BF16)],
+        [pltpu.VMEM((n_mp, f1, cells), F32)],
+        2 * cells * 27 * f2 * c1,
+        2 * 1024 * 1024,
+    )(d9, w2b)
     parts = sum_over_chips(keep, swap(give, "mp", 1))
-    second_got = swap(grad_second, "sample", bits[0])
+    half_sum = add(half_keep, half_got)
+    bits = bits_above(n_sample)
+    for bit in bits[:-1]:
+        half_sum = add(half_sum, swap(half_sum, "sample", bit))
+    half_got = swap(half_sum, "sample", bits[-1])
 
     keep, give, grad_first = call(
         functools.partial(backward_kernel, n_mp),
@@ -316,15 +361,20 @@
     )(*parts, pre_own, vol_all, w1b)
     ins = sum_over_chips(keep, swap(give, "mp", 1))
 
-    second_got, grad_first = lax.optimization_barrier((second_got, grad_first))
-    first_got = swap(grad_first, "sample", bits[0])
-    for bit in bits[1:]:
-        grad_first = add(grad_first, first_got)
-        first_got = swap(grad_first, "sample", bit)
-        grad_second = add(grad_second, second_got)
-        second_got = swap(grad_second, "sample", bit)
-    grad_first = (grad_first.astype(F32) + first_got.astype(F32)) * scale
-    grad_second = (grad_second.astype(F32) + second_got.astype(F32)) * scale
+    half_got, grad_first = lax.optimization_barrier((half_got, grad_first))
+    half_sum = add(half_sum, half_got)
+    both = swap(jnp.concatenate([half_sum, grad_first], axis=1), "sample", 1)
+    grad_first = add(grad_first, both[:, 27 * c1 :])
+    for bit in bits[:-1]:
+        grad_first = add(grad_first, swap(grad_first, "sample", bit))
+    grad_first = (grad_first.astype(F32) + swap(grad_first, "sample", bits[-1]).astype(F32)) * scale
+    grad_second = call(
+        functools.partial(place_kernel, scale),
+        sds((2, f2 // 2, 27 * c1), F32),
+        [],
+        0,
+        1024 * 1024,
+    )(half_sum, both).reshape(f2, 27 * c1)
     total = ins[0].astype(F32)
     for other in ins[1:]:
         total = total + other.astype(F32)

time: 47.8 us -> 47.4 us (level)
  other arithmetic: 3.2 us -> 1.54 us
  local copies, waits for them, and re-layouts: 2.01 us -> 3.35 us
  starting transfers between devices: 19 us -> 18.3 us
  Pallas kernels: 6.94 us -> 7.58 us
    pallas_call x0 -> x3, Pallas kernels: none -> 1.59 us  [the longest x1 0.81 us: local(): call(functools.partial(place_kernel, scale), sds((2, f2 // 2, 27 * c1), F...]
    pallas_call x1, Pallas kernels: 5.89 us -> 4.93 us  [local(): call(functools.partial(forward_kernel, n_mp, c0), [sds((f2, cells), BF16)...]
    reshape x1, local copies, waits for them, and re-layouts: 0.13 us -> 1.06 us  [local(): w2t = w_second.reshape(f2, 3, 9, c1)]
    another operation x2 -> x1, other arithmetic: 0.91 us -> 0.05 us  [local(): near = jnp.stack(near)]
    mul x2 -> x1, other arithmetic: 1.49 us -> 0.66 us  [local(): (grad_first.astype(F32) + swap(grad_first, 'sample', bits[-1]).astype(F32...]
    ppermute x16, starting transfers between devices: 19 us -> 18.3 us  [swap(): return lax.ppermute(value, axis, [(i, i ^ k) for i in range(n)])]
    unnamed x7 -> x9, local copies, waits for them, and re-layouts: 1.21 us -> 1.62 us
  transfers between devices with their start and end apart: 16 -> 16, of which waited for: 12 -> 12; matrix products, arithmetic and copies ran while one was open for 5% -> 5% of each run, Pallas kernels for 2% -> 6%
where the time goes in v4:
time: 47.4 us; the launch traced here: 47.1 us
  starting transfers between devices  18.3 us (39%)
  waiting for transfers between devices  15.6 us (33%)
  Pallas kernels  7.58 us (16%)
  local copies, waits for them, and re-layouts  3.35 us (7%)
  other arithmetic  1.54 us (3%)
  between operations  0.8 us (2%)
    ppermute x16, starting transfers between devices, swap(): return lax.ppermute(value, axis, [(i, i ^ k) for i in range(n)])  18.3 us
    ppermute x16, waiting for transfers between devices, swap(): return lax.ppermute(value, axis, [(i, i ^ k) for i in range(n)])  15.6 us
    pallas_call x1, Pallas kernels, local(): call(functools.partial(forward_kernel, n_mp, c0), [sds((f2, cells), BF16)...  4.93 us
    unnamed x9, local copies, waits for them, and re-layouts  1.62 us
    reshape x1, local copies, waits for them, and re-layouts, local(): w2t = w_second.reshape(f2, 3, 9, c1)  1.06 us
    pallas_call x1, Pallas kernels, local(): call(functools.partial(backward_kernel, n_mp), [sds((half, rows_in, cells...  1.06 us
  transfers between devices with their start and end apart: 16, of which 12 were waited for; matrix products, arithmetic and copies ran while one was open for 5% of the time, Pallas kernels for 6%

profile of v4, /device:TPU:0, one launch (start us, length us, event | category | flops | bytes accessed | tf_op | source)
XLA Modules:
  0.0 47.1 jit_solution(9626058261378966762)
XLA Ops:
  0.6 0.0 copy-start
  0.6 0.8 %copy-done = bf16[16,1728]{1,0:T(8,128)(2,1)S(1)} copy-done((bf16[16,1728]{1,0:T(8,128)(2,1)S(1)}, bf16[16,1728]{1,0:T(8,128)(2,1)}, u32[]{:S(2)}) %copy-start) | copy-done | bytes 55320
  1.5 0.0 copy-start.2
  1.5 0.8 %copy-done.2 = bf16[8,1,2048]{2,0,1:T(8,128)(2,1)S(1)} copy-done((bf16[8,1,2048]{2,0,1:T(8,128)(2,1)S(1)}, bf16[8,1,2048]{2,0,1:T(8,128)(2,1)}, u32[]{:S(2)}) %copy-start.2) | copy-done | bytes 32792
  2.2 0.0 copy-start.3
  2.2 4.0 %collective-permute-start.2 = (bf16[16,2816]{1,0:T(8,128)(2,1)S(1)}, bf16[16,2816]{1,0:T(8,128)(2,1)S(1)}, u32[]{:S(2)}, u32[]{:S(2)}) collective-permute-start(bf16[16,2816]{1,0:T(8,128)(2,1)S(1)} %shard_map.75), channel_id=1, source_target_pairs={{0,6},{1,7},{2,4},{3,5},{4,2},{5,3},{6,0},{7,1},{8,14},{9,15},{10,... | collective-permute-start | bytes 270344 | tf_op jit(solution)/shard_map/ppermute | solution.py:249
  6.2 0.5 %collective-permute-start.1 = (bf16[16,2816]{1,0:T(8,128)(2,1)S(1)}, bf16[16,2816]{1,0:T(8,128)(2,1)S(1)}, u32[]{:S(2)}, u32[]{:S(2)}) collective-permute-start(bf16[16,2816]{1,0:T(8,128)(2,1)S(1)} %shard_map.75), channel_id=1, source_target_pairs={{0,4},{1,5},{2,6},{3,7},{4,0},{5,1},{6,2},{7,3},{8,12},{9,13},{10,... | collective-permute-start | bytes 270344 | tf_op jit(solution)/shard_map/ppermute | solution.py:249
  6.7 0.1 collective-permute-start
  6.8 2.2 %collective-permute-done.2 = bf16[16,2816]{1,0:T(8,128)(2,1)S(1)} collective-permute-done((bf16[16,2816]{1,0:T(8,128)(2,1)S(1)}, bf16[16,2816]{1,0:T(8,128)(2,1)S(1)}, u32[]{:S(2)}, u32[]{:S(2)}) %collective-permute-start.2) | collective-permute-done | bytes 90144 | tf_op jit(solution)/shard_map/ppermute | solution.py:249
  9.0 1.7 %collective-permute-done.1 = bf16[16,2816]{1,0:T(8,128)(2,1)S(1)} collective-permute-done((bf16[16,2816]{1,0:T(8,128)(2,1)S(1)}, bf16[16,2816]{1,0:T(8,128)(2,1)S(1)}, u32[]{:S(2)}, u32[]{:S(2)}) %collective-permute-start.1) | collective-permute-done | bytes 90144 | tf_op jit(solution)/shard_map/ppermute | solution.py:249
  10.7 0.5 %collective-permute-done = bf16[16,2816]{1,0:T(8,128)(2,1)S(1)} collective-permute-done((bf16[16,2816]{1,0:T(8,128)(2,1)S(1)}, bf16[16,2816]{1,0:T(8,128)(2,1)S(1)}, u32[]{:S(2)}, u32[]{:S(2)}) %collective-permute-start) | collective-permute-done | bytes 90144 | tf_op jit(solution)/shard_map/ppermute | solution.py:249
  11.3 0.1 collective-permute-start.3
  11.4 1.1 %reshape.73 = bf16[32,3,9,128]{3,2,1,0:T(8,128)(2,1)S(1)} reshape(bf16[32,3456]{1,0:T(8,128)(2,1)} %param.6) | data formatting | bytes 442368 | tf_op jit(solution)/shard_map/reshape | solution.py:302
  12.4 0.1 copy.11
  12.6 0.4 collective-permute-done.3.refs_1_
  13.0 0.0 copy-done.3
  13.0 4.9 %shard_map.76 = (bf16[32,2048]{1,0:T(8,128)(2,1)}, f32[16,2048]{1,0:T(8,128)S(1)}, bf16[64,2048]{1,0:T(8,128)(2,1)S(1)}, bf16[288,2560]{1,0:T(8,128)(2,1)S(1)}, ...) custom-call(bf16[4,16,2816]{2,1,0:T(8,128)(2,1)S(1)} %pad_maximum_fusion.refs_0_, ...), custom_call_target="tpu_custom_call" | custom-call | flops 1811939328 | bytes 4194304 | tf_op jit(solution)/shard_map/pallas_call | solution.py:309
  18.0 1.6 %collective-permute-start.12 = (bf16[16,3456]{1,0:T(8,128)(2,1)S(1)}, bf16[16,3456]{1,0:T(8,128)(2,1)S(1)}, u32[]{:S(2)}, u32[]{:S(2)}) collective-permute-start(bf16[16,3456]{1,0:T(8,128)(2,1)S(1)} %get-tuple-element.26), channel_id=1, source_target_pairs={{0,8},{8,0},{16,24},{24,16},{1,9},{9,1},{17,25},{25,17},{2,10},{10... | collective-permute-start | bytes 331784 | tf_op jit(solution)/shard_map/ppermute | solution.py:249
  19.6 0.1 copy.12
  19.7 0.2 copy.13.w2b_ref
  19.8 0.0 copy-start.1
  19.8 0.8 %shard_map.77 = (bf16[4,16,2048]{2,1,0:T(8,128)(2,1)S(1)}, bf16[4,16,2048]{2,1,0:T(8,128)(2,1)S(1)}) custom-call(bf16[288,2560]{1,0:T(8,128)(2,1)S(1)} %get-tuple-element.18.d9, bf16[128,864]{1,0:T(8,128)(2,1)S(1)} %copy.13.w2b_ref), custom_call_target="tpu_custom_call" | custom-call | flops 452984832 | bytes 2097152 | tf_op jit(solution)/shard_map/pallas_call | solution.py:333
  20.6 0.1 collective-permute-start.4
  20.7 2.4 %collective-permute-done.12 = bf16[16,3456]{1,0:T(8,128)(2,1)S(1)} collective-permute-done((bf16[16,3456]{1,0:T(8,128)(2,1)S(1)}, bf16[16,3456]{1,0:T(8,128)(2,1)S(1)}, u32[]{:S(2)}, u32[]{:S(2)}) %collective-permute-start.12) | collective-permute-done | bytes 110624 | tf_op jit(solution)/shard_map/ppermute | solution.py:249
  23.2 2.6 %collective-permute-start.13 = (bf16[16,3456]{1,0:T(8,128)(2,1)S(1)}, bf16[16,3456]{1,0:T(8,128)(2,1)S(1)}, u32[]{:S(2)}, u32[]{:S(2)}) collective-permute-start(bf16[16,3456]{1,0:T(8,128)(2,1)S(1)} %add_convert_fusion.1), channel_id=1, source_target_pairs={{0,16},{8,24},{16,0},{24,8},{1,17},{9,25},{17,1},{25,9},{2,18},{10... | collective-permute-start | bytes 331784 | tf_op jit(solution)/shard_map/ppermute | solution.py:249
  25.8 0.0 collective-permute-done.4
  25.8 0.1 fusion.3
  25.9 1.6 %collective-permute-start.7 = (bf16[16,2048]{1,0:T(8,128)(2,1)S(1)}, bf16[16,2048]{1,0:T(8,128)(2,1)S(1)}, u32[]{:S(2)}, u32[]{:S(2)}) collective-permute-start(bf16[16,2048]{1,0:T(8,128)(2,1)S(1)} %get-tuple-element.30), channel_id=1, source_target_pairs={{0,6},{1,7},{2,4},{3,5},{4,2},{5,3},{6,0},{7,1},{8,14},{9,15},{10,... | collective-permute-start | bytes 196616 | tf_op jit(solution)/shard_map/ppermute | solution.py:249
  27.4 1.2 %collective-permute-start.6 = (bf16[16,2048]{1,0:T(8,128)(2,1)S(1)}, bf16[16,2048]{1,0:T(8,128)(2,1)S(1)}, u32[]{:S(2)}, u32[]{:S(2)}) collective-permute-start(bf16[16,2048]{1,0:T(8,128)(2,1)S(1)} %get-tuple-element.31), channel_id=1, source_target_pairs={{0,4},{1,5},{2,6},{3,7},{4,0},{5,1},{6,2},{7,3},{8,12},{9,13},{10,... | collective-permute-start | bytes 196616 | tf_op jit(solution)/shard_map/ppermute | solution.py:249
  28.7 0.8 %collective-permute-start.5 = (bf16[16,2048]{1,0:T(8,128)(2,1)S(1)}, bf16[16,2048]{1,0:T(8,128)(2,1)S(1)}, u32[]{:S(2)}, u32[]{:S(2)}) collective-permute-start(bf16[16,2048]{1,0:T(8,128)(2,1)S(1)} %get-tuple-element.32), channel_id=1, source_target_pairs={{0,2},{1,3},{2,0},{3,1},{4,6},{5,7},{6,4},{7,5},{8,10},{9,11},{10,... | collective-permute-start | bytes 196616 | tf_op jit(solution)/shard_map/ppermute | solution.py:249
  29.4 0.0 copy-done.1
  29.4 0.2 reshape.78
  29.7 0.1 copy.15.refs_6_
  29.8 1.6 %collective-permute-done.7.refs_3_ = bf16[16,2048]{1,0:T(8,128)(2,1)S(1)} collective-permute-done((bf16[16,2048]{1,0:T(8,128)(2,1)S(1)}, bf16[16,2048]{1,0:T(8,128)(2,1)S(1)}, u32[]{:S(2)}, u32[]{:S(2)}) %collective-permute-start.7) | collective-permute-done | bytes 65568 | tf_op jit(solution)/shard_map/ppermute | solution.py:249
  31.4 0.7 %collective-permute-done.6.refs_2_ = bf16[16,2048]{1,0:T(8,128)(2,1)S(1)} collective-permute-done((bf16[16,2048]{1,0:T(8,128)(2,1)S(1)}, bf16[16,2048]{1,0:T(8,128)(2,1)S(1)}, u32[]{:S(2)}, u32[]{:S(2)}) %collective-permute-start.6) | collective-permute-done | bytes 65568 | tf_op jit(solution)/shard_map/ppermute | solution.py:249
  32.1 0.9 %collective-permute-done.5.refs_1_ = bf16[16,2048]{1,0:T(8,128)(2,1)S(1)} collective-permute-done((bf16[16,2048]{1,0:T(8,128)(2,1)S(1)}, bf16[16,2048]{1,0:T(8,128)(2,1)S(1)}, u32[]{:S(2)}, u32[]{:S(2)}) %collective-permute-start.5) | collective-permute-done | bytes 65568 | tf_op jit(solution)/shard_map/ppermute | solution.py:249
  32.9 1.1 %shard_map.78 = (bf16[4,8,2048]{2,1,0:T(8,128)(2,1)S(1)}, bf16[4,8,2048]{2,1,0:T(8,128)(2,1)S(1)}, bf16[16,1728]{1,0:T(8,128)(2,1)S(1)}) custom-call(bf16[16,2048]{1,0:T(8,128)(2,1)S(1)} %get-tuple-element.33.refs_0_, bf16[16,2048]{1,0:T(8,128)(2,1)S(1)} %collective-permute-done.5.refs_1_, bf16[16,2048]{1,0:T(8,128)(2,1)S(1)} %collective-permute-done.6.refs_2_, ...), custom_call_target="tpu_custom_call" | custom-call | flops 226492416 | bytes 1048576 | tf_op jit(solution)/shard_map/pallas_call | solution.py:347
  34.0 0.0 collective-permute-done.13
  34.0 0.1 collective-permute-start.8
  34.1 1.6 %collective-permute-start.14 = (bf16[16,5184]{1,0:T(8,128)(2,1)S(1)}, bf16[16,5184]{1,0:T(8,128)(2,1)S(1)}, u32[]{:S(2)}, u32[]{:S(2)}) collective-permute-start(bf16[16,5184]{1,0:T(8,128)(2,1)S(1)} %pad_maximum_fusion.1), channel_id=1, source_target_pairs={{0,8},{8,0},{16,24},{24,16},{1,9},{9,1},{17,25},{25,17},{2,10},{10... | collective-permute-start | bytes 497672 | tf_op jit(solution)/shard_map/ppermute | solution.py:249
  35.8 0.0 collective-permute-done.8
  35.8 0.8 %collective-permute-start.9 = (bf16[8,2048]{1,0:T(8,128)(2,1)S(1)}, bf16[8,2048]{1,0:T(8,128)(2,1)S(1)}, u32[]{:S(2)}, u32[]{:S(2)}) collective-permute-start(bf16[8,2048]{1,0:T(8,128)(2,1)S(1)} %get-tuple-element.34), channel_id=1, source_target_pairs={{0,2},{1,3},{2,0},{3,1},{4,6},{5,7},{6,4},{7,5},{8,10},{9,11},{10,... | collective-permute-start | bytes 98312 | tf_op jit(solution)/shard_map/ppermute | solution.py:249
  36.7 1.5 %collective-permute-start.11 = (bf16[8,2048]{1,0:T(8,128)(2,1)S(1)}, bf16[8,2048]{1,0:T(8,128)(2,1)S(1)}, u32[]{:S(2)}, u32[]{:S(2)}) collective-permute-start(bf16[8,2048]{1,0:T(8,128)(2,1)S(1)} %get-tuple-element.35), channel_id=1, source_target_pairs={{0,6},{1,7},{2,4},{3,5},{4,2},{5,3},{6,0},{7,1},{8,14},{9,15},{10,... | collective-permute-start | bytes 98312 | tf_op jit(solution)/shard_map/ppermute | solution.py:249
  38.1 1.2 %collective-permute-start.10 = (bf16[8,2048]{1,0:T(8,128)(2,1)S(1)}, bf16[8,2048]{1,0:T(8,128)(2,1)S(1)}, u32[]{:S(2)}, u32[]{:S(2)}) collective-permute-start(bf16[8,2048]{1,0:T(8,128)(2,1)S(1)} %get-tuple-element.36), channel_id=1, source_target_pairs={{0,4},{1,5},{2,6},{3,7},{4,0},{5,1},{6,2},{7,3},{8,12},{9,13},{10,... | collective-permute-start | bytes 98312 | tf_op jit(solution)/shard_map/ppermute | solution.py:249
  39.4 1.5 %collective-permute-done.14.other_ref = bf16[16,5184]{1,0:T(8,128)(2,1)S(1)} collective-permute-done((bf16[16,5184]{1,0:T(8,128)(2,1)S(1)}, bf16[16,5184]{1,0:T(8,128)(2,1)S(1)}, u32[]{:S(2)}, u32[]{:S(2)}) %collective-permute-start.14) | collective-permute-done | bytes 165920 | tf_op jit(solution)/shard_map/ppermute | solution.py:249
  40.9 0.4 collective-permute-start.15
  41.3 0.0 collective-permute-done.9
  41.3 0.1 collective-permute-done.11
  41.5 0.6 %collective-permute-done.10 = bf16[8,2048]{1,0:T(8,128)(2,1)S(1)} collective-permute-done((bf16[8,2048]{1,0:T(8,128)(2,1)S(1)}, bf16[8,2048]{1,0:T(8,128)(2,1)S(1)}, u32[]{:S(2)}, u32[]{:S(2)}) %collective-permute-start.10) | collective-permute-done | bytes 32800 | tf_op jit(solution)/shard_map/ppermute | solution.py:249
  42.1 0.6 %fusion.11 = bf16[8,1,2048]{2,0,1:T(8,128)(2,1)} fusion(bf16[8,2048]{1,0:T(8,128)(2,1)S(1)} %collective-permute-done.11, bf16[8,2048]{1,0:T(8,128)(2,1)S(1)} %collective-permute-done.10, bf16[8,2048]{1,0:T(8,128)(2,1)S(1)} %collective-permute-done.9, bf16[4,8,2048]{2,1,0:T(8,128)(2,1)S(1)} %collective-permute-done.8, ...), kind=kLoop, calls=%fused_computation.27 | loop fusion | flops 196608 | bytes 196608 | tf_op jit(solution)/shard_map/reshape | solution.py:383
  42.7 0.8 %shard_map.79 = f32[2,16,3456]{2,1,0:T(8,128)} custom-call(bf16[16,3456]{1,0:T(8,128)(2,1)S(1)} %add_convert_fusion.mine_ref, bf16[16,5184]{1,0:T(8,128)(2,1)S(1)} %collective-permute-done.14.other_ref), custom_call_target="tpu_custom_call" | custom-call | bytes 1048576 | tf_op jit(solution)/shard_map/pallas_call | solution.py:371
  43.5 2.9 %collective-permute-done.15 = bf16[16,1728]{1,0:T(8,128)(2,1)S(1)} collective-permute-done((bf16[16,1728]{1,0:T(8,128)(2,1)S(1)}, bf16[16,1728]{1,0:T(8,128)(2,1)S(1)}, u32[]{:S(2)}, u32[]{:S(2)}) %collective-permute-start.15) | collective-permute-done | bytes 55328 | tf_op jit(solution)/shard_map/ppermute | solution.py:249
  46.4 0.7 %add_multiply_fusion = f32[16,1728]{1,0:T(8,128)} fusion(bf16[16,1728]{1,0:T(8,128)(2,1)S(1)} %collective-permute-done.15, bf16[16,1728]{1,0:T(8,128)(2,1)S(1)} %add_convert_fusion.6), kind=kLoop, calls=%fused_computation.9 | loop fusion | flops 110592 | bytes 221184 | tf_op jit(solution)/shard_map/mul | solution.py:370
  (9 shorter events, 0.3 us)
Async XLA Ops:
  0.6 0.8 %copy-start = (bf16[16,1728]{1,0:T(8,128)(2,1)S(1)}, bf16[16,1728]{1,0:T(8,128)(2,1)}, u32[]{:S(2)}) copy-start(bf16[16,1728]{1,0:T(8,128)(2,1)} %w_ref.1) | copy-start | bytes 165892
  1.5 0.8 %copy-start.2 = (bf16[8,1,2048]{2,0,1:T(8,128)(2,1)S(1)}, bf16[8,1,2048]{2,0,1:T(8,128)(2,1)}, u32[]{:S(2)}) copy-start(bf16[8,1,2048]{2,0,1:T(8,128)(2,1)} %param.4) | copy-start | bytes 98308
  2.2 10.8 %copy-start.3 = (bf16[32,1,2048]{2,0,1:T(8,128)(2,1)S(1)}, bf16[32,1,2048]{2,0,1:T(8,128)(2,1)}, u32[]{:S(2)}) copy-start(bf16[32,1,2048]{2,0,1:T(8,128)(2,1)} %param.7) | copy-start | bytes 393220
  2.2 6.8 %collective-permute-start.2 = (bf16[16,2816]{1,0:T(8,128)(2,1)S(1)}, bf16[16,2816]{1,0:T(8,128)(2,1)S(1)}, u32[]{:S(2)}, u32[]{:S(2)}) collective-permute-start(bf16[16,2816]{1,0:T(8,128)(2,1)S(1)} %shard_map.75), channel_id=1, source_target_pairs={{0,6},{1,7},{2,4},{3,5},{4,2},{5,3},{6,0},{7,1},{8,14},{9,15},{10,... | collective-permute-start | bytes 270344 | tf_op jit(solution)/shard_map/ppermute | solution.py:249
  6.2 4.5 %collective-permute-start.1 = (bf16[16,2816]{1,0:T(8,128)(2,1)S(1)}, bf16[16,2816]{1,0:T(8,128)(2,1)S(1)}, u32[]{:S(2)}, u32[]{:S(2)}) collective-permute-start(bf16[16,2816]{1,0:T(8,128)(2,1)S(1)} %shard_map.75), channel_id=1, source_target_pairs={{0,4},{1,5},{2,6},{3,7},{4,0},{5,1},{6,2},{7,3},{8,12},{9,13},{10,... | collective-permute-start | bytes 270344 | tf_op jit(solution)/shard_map/ppermute | solution.py:249
  6.7 4.5 %collective-permute-start = (bf16[16,2816]{1,0:T(8,128)(2,1)S(1)}, bf16[16,2816]{1,0:T(8,128)(2,1)S(1)}, u32[]{:S(2)}, u32[]{:S(2)}) collective-permute-start(bf16[16,2816]{1,0:T(8,128)(2,1)S(1)} %shard_map.75), channel_id=1, source_target_pairs={{0,2},{1,3},{2,0},{3,1},{4,6},{5,7},{6,4},{7,5},{8,10},{9,11},{10,... | collective-permute-start | bytes 270344 | tf_op jit(solution)/shard_map/ppermute | solution.py:249
  11.3 1.7 %collective-permute-start.3 = (bf16[4,16,2816]{2,1,0:T(8,128)(2,1)S(1)}, bf16[4,16,2816]{2,1,0:T(8,128)(2,1)S(1)}, u32[]{:S(2)}, u32[]{:S(2)}) collective-permute-start(bf16[4,16,2816]{2,1,0:T(8,128)(2,1)S(1)} %pad_maximum_fusion.refs_0_), channel_id=1, source_target_pairs={{0,1},{1,0},{2,3},{3,2},{4,5},{5,4},{6,7},{7,6},{8,9},{9,8},{10,11... | collective-permute-start | bytes 1081352 | tf_op jit(solution)/shard_map/ppermute | solution.py:249
  18.0 5.2 %collective-permute-start.12 = (bf16[16,3456]{1,0:T(8,128)(2,1)S(1)}, bf16[16,3456]{1,0:T(8,128)(2,1)S(1)}, u32[]{:S(2)}, u32[]{:S(2)}) collective-permute-start(bf16[16,3456]{1,0:T(8,128)(2,1)S(1)} %get-tuple-element.26), channel_id=1, source_target_pairs={{0,8},{8,0},{16,24},{24,16},{1,9},{9,1},{17,25},{25,17},{2,10},{10... | collective-permute-start | bytes 331784 | tf_op jit(solution)/shard_map/ppermute | solution.py:249
  19.8 9.6 %copy-start.1 = (bf16[16,1728]{1,0:T(8,128)(2,1)S(1)}, bf16[16,1728]{1,0:T(8,128)(2,1)}, u32[]{:S(2)}) copy-start(bf16[16,1728]{1,0:T(8,128)(2,1)} %w_ref.1) | copy-start | bytes 165892
  20.6 5.2 %collective-permute-start.4 = (bf16[4,16,2048]{2,1,0:T(8,128)(2,1)S(1)}, bf16[4,16,2048]{2,1,0:T(8,128)(2,1)S(1)}, u32[]{:S(2)}, u32[]{:S(2)}) collective-permute-start(bf16[4,16,2048]{2,1,0:T(8,128)(2,1)S(1)} %get-tuple-element.20), channel_id=1, source_target_pairs={{0,1},{1,0},{2,3},{3,2},{4,5},{5,4},{6,7},{7,6},{8,9},{9,8},{10,11... | collective-permute-start | bytes 786440 | tf_op jit(solution)/shard_map/ppermute | solution.py:249
  23.2 10.8 %collective-permute-start.13 = (bf16[16,3456]{1,0:T(8,128)(2,1)S(1)}, bf16[16,3456]{1,0:T(8,128)(2,1)S(1)}, u32[]{:S(2)}, u32[]{:S(2)}) collective-permute-start(bf16[16,3456]{1,0:T(8,128)(2,1)S(1)} %add_convert_fusion.1), channel_id=1, source_target_pairs={{0,16},{8,24},{16,0},{24,8},{1,17},{9,25},{17,1},{25,9},{2,18},{10... | collective-permute-start | bytes 331784 | tf_op jit(solution)/shard_map/ppermute | solution.py:249
  25.9 5.5 %collective-permute-start.7 = (bf16[16,2048]{1,0:T(8,128)(2,1)S(1)}, bf16[16,2048]{1,0:T(8,128)(2,1)S(1)}, u32[]{:S(2)}, u32[]{:S(2)}) collective-permute-start(bf16[16,2048]{1,0:T(8,128)(2,1)S(1)} %get-tuple-element.30), channel_id=1, source_target_pairs={{0,6},{1,7},{2,4},{3,5},{4,2},{5,3},{6,0},{7,1},{8,14},{9,15},{10,... | collective-permute-start | bytes 196616 | tf_op jit(solution)/shard_map/ppermute | solution.py:249
  27.4 4.6 %collective-permute-start.6 = (bf16[16,2048]{1,0:T(8,128)(2,1)S(1)}, bf16[16,2048]{1,0:T(8,128)(2,1)S(1)}, u32[]{:S(2)}, u32[]{:S(2)}) collective-permute-start(bf16[16,2048]{1,0:T(8,128)(2,1)S(1)} %get-tuple-element.31), channel_id=1, source_target_pairs={{0,4},{1,5},{2,6},{3,7},{4,0},{5,1},{6,2},{7,3},{8,12},{9,13},{10,... | collective-permute-start | bytes 196616 | tf_op jit(solution)/shard_map/ppermute | solution.py:249
  28.7 4.3 %collective-permute-start.5 = (bf16[16,2048]{1,0:T(8,128)(2,1)S(1)}, bf16[16,2048]{1,0:T(8,128)(2,1)S(1)}, u32[]{:S(2)}, u32[]{:S(2)}) collective-permute-start(bf16[16,2048]{1,0:T(8,128)(2,1)S(1)} %get-tuple-element.32), channel_id=1, source_target_pairs={{0,2},{1,3},{2,0},{3,1},{4,6},{5,7},{6,4},{7,5},{8,10},{9,11},{10,... | collective-permute-start | bytes 196616 | tf_op jit(solution)/shard_map/ppermute | solution.py:249
  34.0 1.7 %collective-permute-start.8 = (bf16[4,8,2048]{2,1,0:T(8,128)(2,1)S(1)}, bf16[4,8,2048]{2,1,0:T(8,128)(2,1)S(1)}, u32[]{:S(2)}, u32[]{:S(2)}) collective-permute-start(bf16[4,8,2048]{2,1,0:T(8,128)(2,1)S(1)} %get-tuple-element.24), channel_id=1, source_target_pairs={{0,1},{1,0},{2,3},{3,2},{4,5},{5,4},{6,7},{7,6},{8,9},{9,8},{10,11... | collective-permute-start | bytes 393224 | tf_op jit(solution)/shard_map/ppermute | solution.py:249
  34.1 6.7 %collective-permute-start.14 = (bf16[16,5184]{1,0:T(8,128)(2,1)S(1)}, bf16[16,5184]{1,0:T(8,128)(2,1)S(1)}, u32[]{:S(2)}, u32[]{:S(2)}) collective-permute-start(bf16[16,5184]{1,0:T(8,128)(2,1)S(1)} %pad_maximum_fusion.1), channel_id=1, source_target_pairs={{0,8},{8,0},{16,24},{24,16},{1,9},{9,1},{17,25},{25,17},{2,10},{10... | collective-permute-start | bytes 497672 | tf_op jit(solution)/shard_map/ppermute | solution.py:249
  35.8 5.5 %collective-permute-start.9 = (bf16[8,2048]{1,0:T(8,128)(2,1)S(1)}, bf16[8,2048]{1,0:T(8,128)(2,1)S(1)}, u32[]{:S(2)}, u32[]{:S(2)}) collective-permute-start(bf16[8,2048]{1,0:T(8,128)(2,1)S(1)} %get-tuple-element.34), channel_id=1, source_target_pairs={{0,2},{1,3},{2,0},{3,1},{4,6},{5,7},{6,4},{7,5},{8,10},{9,11},{10,... | collective-permute-start | bytes 98312 | tf_op jit(solution)/shard_map/ppermute | solution.py:249
  36.7 4.8 %collective-permute-start.11 = (bf16[8,2048]{1,0:T(8,128)(2,1)S(1)}, bf16[8,2048]{1,0:T(8,128)(2,1)S(1)}, u32[]{:S(2)}, u32[]{:S(2)}) collective-permute-start(bf16[8,2048]{1,0:T(8,128)(2,1)S(1)} %get-tuple-element.35), channel_id=1, source_target_pairs={{0,6},{1,7},{2,4},{3,5},{4,2},{5,3},{6,0},{7,1},{8,14},{9,15},{10,... | collective-permute-start | bytes 98312 | tf_op jit(solution)/shard_map/ppermute | solution.py:249
  38.1 3.9 %collective-permute-start.10 = (bf16[8,2048]{1,0:T(8,128)(2,1)S(1)}, bf16[8,2048]{1,0:T(8,128)(2,1)S(1)}, u32[]{:S(2)}, u32[]{:S(2)}) collective-permute-start(bf16[8,2048]{1,0:T(8,128)(2,1)S(1)} %get-tuple-element.36), channel_id=1, source_target_pairs={{0,4},{1,5},{2,6},{3,7},{4,0},{5,1},{6,2},{7,3},{8,12},{9,13},{10,... | collective-permute-start | bytes 98312 | tf_op jit(solution)/shard_map/ppermute | solution.py:249
  40.9 5.5 %collective-permute-start.15 = (bf16[16,1728]{1,0:T(8,128)(2,1)S(1)}, bf16[16,1728]{1,0:T(8,128)(2,1)S(1)}, u32[]{:S(2)}, u32[]{:S(2)}) collective-permute-start(bf16[16,1728]{1,0:T(8,128)(2,1)S(1)} %add_convert_fusion.6), channel_id=1, source_target_pairs={{0,16},{8,24},{16,0},{24,8},{1,17},{9,25},{17,1},{25,9},{2,18},{10... | collective-permute-start | bytes 165896 | tf_op jit(solution)/shard_map/ppermute | solution.py:249

commit v5 on v4

--- a/solution.py
+++ b/solution.py
@@ -64,18 +64,6 @@
     return 2 * PLANE if cells % (2 * PLANE) == 0 else PLANE
 
 
-def pack_kernel(w_ref, v_ref, out_ref):
-    f1, width = w_ref.shape
-    rows_in, cells = v_ref.shape
-    run = cells * rows_in // f1
-    lanes = out_ref.shape[1] - run
-    out_ref[:, :width] = w_ref[...]
-    if lanes > width:
-        out_ref[:, width:lanes] = jnp.zeros((f1, lanes - width), BF16)
-    folded = [v_ref[:, i * run : (i + 1) * run].astype(F32) for i in range(f1 // rows_in)]
-    out_ref[:, lanes:] = jnp.concatenate(folded, axis=0).astype(BF16)
-
-
 def forward_kernel(n_mp, c0, *refs):
     near_ref, far_ref, w2r_ref, cot_ref = refs[:4]
     feat_ref, pre_ref, vol_ref, d9, half_keep_ref, half_give_ref = refs[4:10]
@@ -84,9 +72,6 @@
     me = lax.axis_index("mp")
     low_half = lax.axis_index("sample") % 2 == 0
     _, f1, lanes = w1s.shape
-    rows_in = vs.shape[1]
-    folds = f1 // rows_in
-    run = near_ref.shape[2] - lanes
     c1 = n_mp * f1
     f2, cells = cot_ref.shape
     chunk = chunk_of(cells)
@@ -97,9 +82,8 @@
     for k in range(n_mp):
         piece = (far_ref if k % 2 else near_ref)[k // 2].astype(F32)
         slot = me ^ k
-        w1s[slot] = piece[:, :lanes]
-        for i in range(folds):
-            vs[slot, :, i * run : (i + 1) * run] = piece[i * rows_in : (i + 1) * rows_in, lanes:]
+        w1s[slot] = piece[:f1, :lanes]
+        vs[slot] = piece[f1:, :cells]
 
     lane = lax.broadcasted_iota(jnp.int32, (1, pitch), 1)
     for dz in range(3):
@@ -253,6 +237,13 @@
     return (a.astype(F32) + b.astype(F32)).astype(BF16)
 
 
+def total(values):
+    result = values[0].astype(F32)
+    for value in values[1:]:
+        result = result + value.astype(F32)
+    return result
+
+
 def sum_over_chips(keep, got):
     parts = [add(keep[j], got[j]) for j in range(keep.shape[0])]
     return [parts[0]] + [swap(parts[j], "mp", 2 * j) for j in range(1, len(parts))]
@@ -287,14 +278,14 @@
     padded = cells + 2 * PLANE
 
     lanes = (8 * 3 * c0) // 128 * 128 + pitch
-    run = cells * rows_in // f1
-    piece = call(
-        pack_kernel,
-        jax.ShapeDtypeStruct((f1, lanes + run), BF16),
-        [],
-        0,
-        256 * 1024,
-    )(w_first, volumes)
+    wide = max(cells, lanes)
+    piece = jnp.concatenate(
+        [
+            jnp.pad(w_first, ((0, 0), (0, wide - w_first.shape[1]))),
+            jnp.pad(volumes, ((0, 0), (0, wide - cells))),
+        ],
+        axis=0,
+    )
     near = [piece] + [swap(piece, "mp", k) for k in range(2, n_mp, 2)]
     near = jnp.stack(near)
     far = swap(near, "mp", 1)
@@ -338,6 +329,7 @@
         2 * 1024 * 1024,
     )(d9, w2b)
     parts = sum_over_chips(keep, swap(give, "mp", 1))
+    *parts, half_got = lax.optimization_barrier((*parts, half_got))
     half_sum = add(half_keep, half_got)
     bits = bits_above(n_sample)
     for bit in bits[:-1]:
@@ -359,15 +351,15 @@
         2 * cells * 27 * 2 * c0 * f1,
         1024 * 1024,
     )(*parts, pre_own, vol_all, w1b)
-    ins = sum_over_chips(keep, swap(give, "mp", 1))
-
-    half_got, grad_first = lax.optimization_barrier((half_got, grad_first))
+    got = swap(give, "mp", 1)
+
+    half_got, _ = lax.optimization_barrier((half_got, grad_first))
     half_sum = add(half_sum, half_got)
+    got, half_sum = lax.optimization_barrier((got, half_sum))
+    ins = sum_over_chips(keep, got)
     both = swap(jnp.concatenate([half_sum, grad_first], axis=1), "sample", 1)
-    grad_first = add(grad_first, both[:, 27 * c1 :])
-    for bit in bits[:-1]:
-        grad_first = add(grad_first, swap(grad_first, "sample", bit))
-    grad_first = (grad_first.astype(F32) + swap(grad_first, "sample", bits[-1]).astype(F32)) * scale
+    firsts = [grad_first] + [swap(grad_first, "sample", k) for k in range(2, n_sample)] + [both[:, 27 * c1 :]]
+    grad_first = total(firsts) * scale
     grad_second = call(
         functools.partial(place_kernel, scale),
         sds((2, f2 // 2, 27 * c1), F32),
@@ -375,12 +367,9 @@
         0,
         1024 * 1024,
     )(half_sum, both).reshape(f2, 27 * c1)
-    total = ins[0].astype(F32)
-    for other in ins[1:]:
-        total = total + other.astype(F32)
     return (
         features.reshape(f2, 1, cells),
-        total.astype(BF16).reshape(rows_in, 1, cells),
+        total(ins).astype(BF16).reshape(rows_in, 1, cells),
         grad_first,
         grad_second,
     )

time: 47.4 us -> 48.5 us (1.023)
  starting transfers between devices: 18.3 us -> 21.1 us
  local copies, waits for them, and re-layouts: 3.35 us -> 1.78 us
  waiting for transfers between devices: 15.6 us -> 14.6 us
  other arithmetic: 1.54 us -> 2.4 us
    ppermute x16 -> x17, starting transfers between devices: 18.3 us -> 21.1 us  [swap(): return lax.ppermute(value, axis, [(i, i ^ k) for i in range(n)])]
    unnamed x9 -> x5, local copies, waits for them, and re-layouts: 1.62 us -> 0.05 us
    ppermute x16 -> x17, waiting for transfers between devices: 15.6 us -> 14.6 us  [swap(): return lax.ppermute(value, axis, [(i, i ^ k) for i in range(n)])]
    another operation x1 -> x2, other arithmetic: 0.05 us -> 0.91 us  [local(): near = jnp.stack(near)]
  transfers between devices with their start and end apart: 16 -> 17, of which waited for: 12 -> 12; matrix products, arithmetic and copies ran while one was open for 5% -> 5% of each run, Pallas kernels for 6% -> 4%
where the time goes in v5:
time: 48.5 us; the launch traced here: 48.3 us
  starting transfers between devices  21.1 us (44%)
  waiting for transfers between devices  14.6 us (30%)
  Pallas kernels  7.56 us (16%)
  other arithmetic  2.4 us (5%)
  local copies, waits for them, and re-layouts  1.78 us (4%)
  between operations  0.78 us (2%)
    ppermute x17, starting transfers between devices, swap(): return lax.ppermute(value, axis, [(i, i ^ k) for i in range(n)])  21.1 us
    ppermute x17, waiting for transfers between devices, swap(): return lax.ppermute(value, axis, [(i, i ^ k) for i in range(n)])  14.6 us
    pallas_call x1, Pallas kernels, local(): call(functools.partial(forward_kernel, n_mp, c0), [sds((f2, cells), BF16)...  4.94 us
    reshape x1, local copies, waits for them, and re-layouts, local(): w2t = w_second.reshape(f2, 3, 9, c1)  1.06 us
    pallas_call x1, Pallas kernels, local(): call(functools.partial(backward_kernel, n_mp), [sds((half, rows_in, cells...  1.05 us
  transfers between devices with their start and end apart: 17, of which 12 were waited for; matrix products, arithmetic and copies ran while one was open for 5% of the time, Pallas kernels for 4%

profile of v5, /device:TPU:0, one launch (start us, length us, event | category | flops | bytes accessed | tf_op | source)
XLA Modules:
  0.0 48.3 jit_solution(3560909063878998912)
XLA Ops:
  0.6 0.9 %fusion.14 = (bf16[1,24,2048]{2,1,0:T(8,128)(2,1)S(1)}, bf16[24,2048]{1,0:T(8,128)(2,1)S(1)}) fusion(bf16[8,2048]{1,0:T(8,128)(2,1)} %bitcast.54, bf16[16,1728]{1,0:T(8,128)(2,1)} %param.5), kind=kLoop, calls=%fused_computation.30 | loop fusion | flops 294912 | bytes 284672 | tf_op jit(solution)/shard_map/stack | solution.py:290
  1.5 3.0 %collective-permute-start.1 = (bf16[24,2048]{1,0:T(8,128)(2,1)S(1)}, bf16[24,2048]{1,0:T(8,128)(2,1)S(1)}, u32[]{:S(2)}, u32[]{:S(2)}) collective-permute-start(bf16[24,2048]{1,0:T(8,128)(2,1)S(1)} %get-tuple-element.50), channel_id=1, source_target_pairs={{0,4},{1,5},{2,6},{3,7},{4,0},{5,1},{6,2},{7,3},{8,12},{9,13},{10,... | collective-permute-start | bytes 294920 | tf_op jit(solution)/shard_map/ppermute | solution.py:233
  4.5 1.5 %collective-permute-start = (bf16[24,2048]{1,0:T(8,128)(2,1)S(1)}, bf16[24,2048]{1,0:T(8,128)(2,1)S(1)}, u32[]{:S(2)}, u32[]{:S(2)}) collective-permute-start(bf16[24,2048]{1,0:T(8,128)(2,1)S(1)} %get-tuple-element.50), channel_id=1, source_target_pairs={{0,2},{1,3},{2,0},{3,1},{4,6},{5,7},{6,4},{7,5},{8,10},{9,11},{10,... | collective-permute-start | bytes 294920 | tf_op jit(solution)/shard_map/ppermute | solution.py:233
  6.0 0.0 collective-permute-start.2
  6.1 1.3 %collective-permute-done.1 = bf16[24,2048]{1,0:T(8,128)(2,1)S(1)} collective-permute-done((bf16[24,2048]{1,0:T(8,128)(2,1)S(1)}, bf16[24,2048]{1,0:T(8,128)(2,1)S(1)}, u32[]{:S(2)}, u32[]{:S(2)}) %collective-permute-start.1) | collective-permute-done | bytes 98336 | tf_op jit(solution)/shard_map/ppermute | solution.py:233
  7.3 2.6 %collective-permute-done = bf16[24,2048]{1,0:T(8,128)(2,1)S(1)} collective-permute-done((bf16[24,2048]{1,0:T(8,128)(2,1)S(1)}, bf16[24,2048]{1,0:T(8,128)(2,1)S(1)}, u32[]{:S(2)}, u32[]{:S(2)}) %collective-permute-start) | collective-permute-done | bytes 98336 | tf_op jit(solution)/shard_map/ppermute | solution.py:233
  9.9 1.6 %collective-permute-done.2 = bf16[24,2048]{1,0:T(8,128)(2,1)S(1)} collective-permute-done((bf16[24,2048]{1,0:T(8,128)(2,1)S(1)}, bf16[24,2048]{1,0:T(8,128)(2,1)S(1)}, u32[]{:S(2)}, u32[]{:S(2)}) %collective-permute-start.2) | collective-permute-done | bytes 98336 | tf_op jit(solution)/shard_map/ppermute | solution.py:233
  11.5 0.1 pad_maximum_fusion.refs_0_
  11.6 0.0 copy-start
  11.6 0.1 collective-permute-start.3
  11.7 1.1 %reshape.73 = bf16[32,3,9,128]{3,2,1,0:T(8,128)(2,1)S(1)} reshape(bf16[32,3456]{1,0:T(8,128)(2,1)} %param.6) | data formatting | bytes 442368 | tf_op jit(solution)/shard_map/reshape | solution.py:293
  12.7 0.1 copy.12
  12.8 0.2 copy.13.w2b_ref
  13.0 0.1 copy.11
  13.1 0.2 collective-permute-done.3.refs_1_
  13.4 0.0 copy-done
  13.4 4.9 %shard_map.75 = (bf16[32,2048]{1,0:T(8,128)(2,1)}, f32[16,2048]{1,0:T(8,128)S(1)}, bf16[64,2048]{1,0:T(8,128)(2,1)S(1)}, bf16[288,2560]{1,0:T(8,128)(2,1)S(1)}, ...) custom-call(bf16[4,24,2048]{2,1,0:T(8,128)(2,1)S(1)} %pad_maximum_fusion.refs_0_, ...), custom_call_target="tpu_custom_call" | custom-call | flops 1811939328 | bytes 4194304 | tf_op jit(solution)/shard_map/pallas_call | solution.py:300
  18.3 0.0 copy-start.1
  18.3 0.8 %shard_map.76 = (bf16[4,16,2048]{2,1,0:T(8,128)(2,1)S(1)}, bf16[4,16,2048]{2,1,0:T(8,128)(2,1)S(1)}) custom-call(bf16[288,2560]{1,0:T(8,128)(2,1)S(1)} %get-tuple-element.24.d9, bf16[128,864]{1,0:T(8,128)(2,1)S(1)} %copy.13.w2b_ref), custom_call_target="tpu_custom_call" | custom-call | flops 452984832 | bytes 2097152 | tf_op jit(solution)/shard_map/pallas_call | solution.py:324
  19.1 0.3 collective-permute-start.4
  19.5 1.6 %collective-permute-start.8 = (bf16[16,3456]{1,0:T(8,128)(2,1)S(1)}, bf16[16,3456]{1,0:T(8,128)(2,1)S(1)}, u32[]{:S(2)}, u32[]{:S(2)}) collective-permute-start(bf16[16,3456]{1,0:T(8,128)(2,1)S(1)} %get-tuple-element.27), channel_id=1, source_target_pairs={{0,8},{8,0},{16,24},{24,16},{1,9},{9,1},{17,25},{25,17},{2,10},{10... | collective-permute-start | bytes 331784 | tf_op jit(solution)/shard_map/ppermute | solution.py:233
  21.0 0.0 collective-permute-done.4
  21.0 0.1 fusion.5
  21.1 1.8 %collective-permute-start.7 = (bf16[16,2048]{1,0:T(8,128)(2,1)S(1)}, bf16[16,2048]{1,0:T(8,128)(2,1)S(1)}, u32[]{:S(2)}, u32[]{:S(2)}) collective-permute-start(bf16[16,2048]{1,0:T(8,128)(2,1)S(1)} %get-tuple-element.42), channel_id=1, source_target_pairs={{0,6},{1,7},{2,4},{3,5},{4,2},{5,3},{6,0},{7,1},{8,14},{9,15},{10,... | collective-permute-start | bytes 196616 | tf_op jit(solution)/shard_map/ppermute | solution.py:233
  22.9 0.7 %collective-permute-start.6 = (bf16[16,2048]{1,0:T(8,128)(2,1)S(1)}, bf16[16,2048]{1,0:T(8,128)(2,1)S(1)}, u32[]{:S(2)}, u32[]{:S(2)}) collective-permute-start(bf16[16,2048]{1,0:T(8,128)(2,1)S(1)} %get-tuple-element.43), channel_id=1, source_target_pairs={{0,4},{1,5},{2,6},{3,7},{4,0},{5,1},{6,2},{7,3},{8,12},{9,13},{10,... | collective-permute-start | bytes 196616 | tf_op jit(solution)/shard_map/ppermute | solution.py:233
  23.6 1.1 %collective-permute-start.5 = (bf16[16,2048]{1,0:T(8,128)(2,1)S(1)}, bf16[16,2048]{1,0:T(8,128)(2,1)S(1)}, u32[]{:S(2)}, u32[]{:S(2)}) collective-permute-start(bf16[16,2048]{1,0:T(8,128)(2,1)S(1)} %get-tuple-element.44), channel_id=1, source_target_pairs={{0,2},{1,3},{2,0},{3,1},{4,6},{5,7},{6,4},{7,5},{8,10},{9,11},{10,... | collective-permute-start | bytes 196616 | tf_op jit(solution)/shard_map/ppermute | solution.py:233
  24.7 0.0 collective-permute-done.8
  24.7 1.7 %collective-permute-done.7.refs_3_ = bf16[16,2048]{1,0:T(8,128)(2,1)S(1)} collective-permute-done((bf16[16,2048]{1,0:T(8,128)(2,1)S(1)}, bf16[16,2048]{1,0:T(8,128)(2,1)S(1)}, u32[]{:S(2)}, u32[]{:S(2)}) %collective-permute-start.7) | collective-permute-done | bytes 65568 | tf_op jit(solution)/shard_map/ppermute | solution.py:233
  26.4 1.0 %collective-permute-done.6.refs_2_ = bf16[16,2048]{1,0:T(8,128)(2,1)S(1)} collective-permute-done((bf16[16,2048]{1,0:T(8,128)(2,1)S(1)}, bf16[16,2048]{1,0:T(8,128)(2,1)S(1)}, u32[]{:S(2)}, u32[]{:S(2)}) %collective-permute-start.6) | collective-permute-done | bytes 65568 | tf_op jit(solution)/shard_map/ppermute | solution.py:233
  27.4 0.4 collective-permute-done.5.refs_1_
  27.9 2.7 %collective-permute-start.10 = (bf16[16,3456]{1,0:T(8,128)(2,1)S(1)}, bf16[16,3456]{1,0:T(8,128)(2,1)S(1)}, u32[]{:S(2)}, u32[]{:S(2)}) collective-permute-start(bf16[16,3456]{1,0:T(8,128)(2,1)S(1)} %add_convert_fusion.1), channel_id=1, source_target_pairs={{0,16},{8,24},{16,0},{24,8},{1,17},{9,25},{17,1},{25,9},{2,18},{10... | collective-permute-start | bytes 331784 | tf_op jit(solution)/shard_map/ppermute | solution.py:233
  30.5 0.0 copy-done.1
  30.5 0.2 reshape.78
  30.8 0.1 copy.15.refs_6_
  30.9 1.1 %shard_map.77 = (bf16[4,8,2048]{2,1,0:T(8,128)(2,1)S(1)}, bf16[4,8,2048]{2,1,0:T(8,128)(2,1)S(1)}, bf16[16,1728]{1,0:T(8,128)(2,1)S(1)}) custom-call(bf16[16,2048]{1,0:T(8,128)(2,1)S(1)} %get-tuple-element.28.refs_0_, bf16[16,2048]{1,0:T(8,128)(2,1)S(1)} %collective-permute-done.5.refs_1_, bf16[16,2048]{1,0:T(8,128)(2,1)S(1)} %collective-permute-done.6.refs_2_, ...), custom_call_target="tpu_custom_call" | custom-call | flops 226492416 | bytes 1048576 | tf_op jit(solution)/shard_map/pallas_call | solution.py:339
  31.9 1.1 %collective-permute-start.15 = (bf16[16,1728]{1,0:T(8,128)(2,1)S(1)}, bf16[16,1728]{1,0:T(8,128)(2,1)S(1)}, u32[]{:S(2)}, u32[]{:S(2)}) collective-permute-start(bf16[16,1728]{1,0:T(8,128)(2,1)S(1)} %get-tuple-element.38), channel_id=1, source_target_pairs={{0,24},{8,16},{16,8},{24,0},{1,25},{9,17},{17,9},{25,1},{2,26},{10... | collective-permute-start | bytes 165896 | tf_op jit(solution)/shard_map/ppermute | solution.py:233
  33.0 1.7 %collective-permute-start.14 = (bf16[16,1728]{1,0:T(8,128)(2,1)S(1)}, bf16[16,1728]{1,0:T(8,128)(2,1)S(1)}, u32[]{:S(2)}, u32[]{:S(2)}) collective-permute-start(bf16[16,1728]{1,0:T(8,128)(2,1)S(1)} %get-tuple-element.38), channel_id=1, source_target_pairs={{0,16},{8,24},{16,0},{24,8},{1,17},{9,25},{17,1},{25,9},{2,18},{10... | collective-permute-start | bytes 165896 | tf_op jit(solution)/shard_map/ppermute | solution.py:233
  34.7 0.0 collective-permute-start.9
  34.7 2.6 %collective-permute-done.10 = bf16[16,3456]{1,0:T(8,128)(2,1)S(1)} collective-permute-done((bf16[16,3456]{1,0:T(8,128)(2,1)S(1)}, bf16[16,3456]{1,0:T(8,128)(2,1)S(1)}, u32[]{:S(2)}, u32[]{:S(2)}) %collective-permute-start.10) | collective-permute-done | bytes 110624 | tf_op jit(solution)/shard_map/ppermute | solution.py:233
  37.4 0.0 collective-permute-done.9
  37.4 1.1 %collective-permute-start.11 = (bf16[8,2048]{1,0:T(8,128)(2,1)S(1)}, bf16[8,2048]{1,0:T(8,128)(2,1)S(1)}, u32[]{:S(2)}, u32[]{:S(2)}) collective-permute-start(bf16[8,2048]{1,0:T(8,128)(2,1)S(1)} %get-tuple-element.46), channel_id=1, source_target_pairs={{0,2},{1,3},{2,0},{3,1},{4,6},{5,7},{6,4},{7,5},{8,10},{9,11},{10,... | collective-permute-start | bytes 98312 | tf_op jit(solution)/shard_map/ppermute | solution.py:233
  38.5 2.1 %collective-permute-start.13 = (bf16[8,2048]{1,0:T(8,128)(2,1)S(1)}, bf16[8,2048]{1,0:T(8,128)(2,1)S(1)}, u32[]{:S(2)}, u32[]{:S(2)}) collective-permute-start(bf16[8,2048]{1,0:T(8,128)(2,1)S(1)} %get-tuple-element.47), channel_id=1, source_target_pairs={{0,6},{1,7},{2,4},{3,5},{4,2},{5,3},{6,0},{7,1},{8,14},{9,15},{10,... | collective-permute-start | bytes 98312 | tf_op jit(solution)/shard_map/ppermute | solution.py:233
  40.6 0.5 %collective-permute-start.12 = (bf16[8,2048]{1,0:T(8,128)(2,1)S(1)}, bf16[8,2048]{1,0:T(8,128)(2,1)S(1)}, u32[]{:S(2)}, u32[]{:S(2)}) collective-permute-start(bf16[8,2048]{1,0:T(8,128)(2,1)S(1)} %get-tuple-element.48), channel_id=1, source_target_pairs={{0,4},{1,5},{2,6},{3,7},{4,0},{5,1},{6,2},{7,3},{8,12},{9,13},{10,... | collective-permute-start | bytes 98312 | tf_op jit(solution)/shard_map/ppermute | solution.py:233
  41.1 0.3 collective-permute-done.11
  41.4 1.9 %collective-permute-start.16 = (bf16[16,5184]{1,0:T(8,128)(2,1)S(1)}, bf16[16,5184]{1,0:T(8,128)(2,1)S(1)}, u32[]{:S(2)}, u32[]{:S(2)}) collective-permute-start(bf16[16,5184]{1,0:T(8,128)(2,1)S(1)} %pad_maximum_fusion.1), channel_id=1, source_target_pairs={{0,8},{8,0},{16,24},{24,16},{1,9},{9,1},{17,25},{25,17},{2,10},{10... | collective-permute-start | bytes 497672 | tf_op jit(solution)/shard_map/ppermute | solution.py:233
  43.3 0.1 collective-permute-done.13
  43.4 1.2 %collective-permute-done.12 = bf16[8,2048]{1,0:T(8,128)(2,1)S(1)} collective-permute-done((bf16[8,2048]{1,0:T(8,128)(2,1)S(1)}, bf16[8,2048]{1,0:T(8,128)(2,1)S(1)}, u32[]{:S(2)}, u32[]{:S(2)}) %collective-permute-start.12) | collective-permute-done | bytes 32800 | tf_op jit(solution)/shard_map/ppermute | solution.py:233
  44.5 0.6 %fusion.13 = bf16[8,1,2048]{2,0,1:T(8,128)(2,1)} fusion(bf16[8,2048]{1,0:T(8,128)(2,1)S(1)} %collective-permute-done.13, bf16[8,2048]{1,0:T(8,128)(2,1)S(1)} %collective-permute-done.12, bf16[8,2048]{1,0:T(8,128)(2,1)S(1)} %collective-permute-done.11, bf16[4,8,2048]{2,1,0:T(8,128)(2,1)S(1)} %collective-permute-done.9, ...), kind=kLoop, calls=%fused_computation.29 | loop fusion | flops 196608 | bytes 196608 | tf_op jit(solution)/shard_map/reshape | solution.py:372
  45.2 1.6 %collective-permute-done.16.other_ref = bf16[16,5184]{1,0:T(8,128)(2,1)S(1)} collective-permute-done((bf16[16,5184]{1,0:T(8,128)(2,1)S(1)}, bf16[16,5184]{1,0:T(8,128)(2,1)S(1)}, u32[]{:S(2)}, u32[]{:S(2)}) %collective-permute-start.16) | collective-permute-done | bytes 165920 | tf_op jit(solution)/shard_map/ppermute | solution.py:233
  46.8 0.8 %shard_map.78 = f32[2,16,3456]{2,1,0:T(8,128)} custom-call(bf16[16,3456]{1,0:T(8,128)(2,1)S(1)} %add_convert_fusion.mine_ref, bf16[16,5184]{1,0:T(8,128)(2,1)S(1)} %collective-permute-done.16.other_ref), custom_call_target="tpu_custom_call" | custom-call | bytes 1048576 | tf_op jit(solution)/shard_map/pallas_call | solution.py:363
  47.6 0.0 collective-permute-done.15
  47.6 0.0 collective-permute-done.14
  47.6 0.7 %add_multiply_fusion = f32[16,1728]{1,0:T(8,128)} fusion(bf16[16,1728]{1,0:T(8,128)(2,1)S(1)} %collective-permute-done.15, bf16[16,1728]{1,0:T(8,128)(2,1)S(1)} %collective-permute-done.14, bf16[16,1728]{1,0:T(8,128)(2,1)S(1)} %get-tuple-element.38, bf16[16,5184]{1,0:T(8,128)(2,1)S(1)} %collective-permute-done.16.other_ref), kind=kLoop, calls=%fused_computation.11 | loop fusion | flops 221184 | bytes 331776 | tf_op jit(solution)/shard_map/mul | solution.py:362
  (6 shorter events, 0.2 us)
Async XLA Ops:
  1.5 5.8 %collective-permute-start.1 = (bf16[24,2048]{1,0:T(8,128)(2,1)S(1)}, bf16[24,2048]{1,0:T(8,128)(2,1)S(1)}, u32[]{:S(2)}, u32[]{:S(2)}) collective-permute-start(bf16[24,2048]{1,0:T(8,128)(2,1)S(1)} %get-tuple-element.50), channel_id=1, source_target_pairs={{0,4},{1,5},{2,6},{3,7},{4,0},{5,1},{6,2},{7,3},{8,12},{9,13},{10,... | collective-permute-start | bytes 294920 | tf_op jit(solution)/shard_map/ppermute | solution.py:233
  4.5 5.4 %collective-permute-start = (bf16[24,2048]{1,0:T(8,128)(2,1)S(1)}, bf16[24,2048]{1,0:T(8,128)(2,1)S(1)}, u32[]{:S(2)}, u32[]{:S(2)}) collective-permute-start(bf16[24,2048]{1,0:T(8,128)(2,1)S(1)} %get-tuple-element.50), channel_id=1, source_target_pairs={{0,2},{1,3},{2,0},{3,1},{4,6},{5,7},{6,4},{7,5},{8,10},{9,11},{10,... | collective-permute-start | bytes 294920 | tf_op jit(solution)/shard_map/ppermute | solution.py:233
  6.0 5.5 %collective-permute-start.2 = (bf16[24,2048]{1,0:T(8,128)(2,1)S(1)}, bf16[24,2048]{1,0:T(8,128)(2,1)S(1)}, u32[]{:S(2)}, u32[]{:S(2)}) collective-permute-start(bf16[24,2048]{1,0:T(8,128)(2,1)S(1)} %get-tuple-element.50), channel_id=1, source_target_pairs={{0,6},{1,7},{2,4},{3,5},{4,2},{5,3},{6,0},{7,1},{8,14},{9,15},{10,... | collective-permute-start | bytes 294920 | tf_op jit(solution)/shard_map/ppermute | solution.py:233
  11.6 1.8 %copy-start = (bf16[32,1,2048]{2,0,1:T(8,128)(2,1)S(1)}, bf16[32,1,2048]{2,0,1:T(8,128)(2,1)}, u32[]{:S(2)}) copy-start(bf16[32,1,2048]{2,0,1:T(8,128)(2,1)} %param.7) | copy-start | bytes 393220
  11.6 1.8 %collective-permute-start.3 = (bf16[4,24,2048]{2,1,0:T(8,128)(2,1)S(1)}, bf16[4,24,2048]{2,1,0:T(8,128)(2,1)S(1)}, u32[]{:S(2)}, u32[]{:S(2)}) collective-permute-start(bf16[4,24,2048]{2,1,0:T(8,128)(2,1)S(1)} %pad_maximum_fusion.refs_0_), channel_id=1, source_target_pairs={{0,1},{1,0},{2,3},{3,2},{4,5},{5,4},{6,7},{7,6},{8,9},{9,8},{10,11... | collective-permute-start | bytes 1179656 | tf_op jit(solution)/shard_map/ppermute | solution.py:233
  18.3 12.2 %copy-start.1 = (bf16[16,1728]{1,0:T(8,128)(2,1)S(1)}, bf16[16,1728]{1,0:T(8,128)(2,1)}, u32[]{:S(2)}) copy-start(bf16[16,1728]{1,0:T(8,128)(2,1)} %param.5) | copy-start | bytes 165892
  19.1 1.9 %collective-permute-start.4 = (bf16[4,16,2048]{2,1,0:T(8,128)(2,1)S(1)}, bf16[4,16,2048]{2,1,0:T(8,128)(2,1)S(1)}, u32[]{:S(2)}, u32[]{:S(2)}) collective-permute-start(bf16[4,16,2048]{2,1,0:T(8,128)(2,1)S(1)} %get-tuple-element.26), channel_id=1, source_target_pairs={{0,1},{1,0},{2,3},{3,2},{4,5},{5,4},{6,7},{7,6},{8,9},{9,8},{10,11... | collective-permute-start | bytes 786440 | tf_op jit(solution)/shard_map/ppermute | solution.py:233
  19.5 5.2 %collective-permute-start.8 = (bf16[16,3456]{1,0:T(8,128)(2,1)S(1)}, bf16[16,3456]{1,0:T(8,128)(2,1)S(1)}, u32[]{:S(2)}, u32[]{:S(2)}) collective-permute-start(bf16[16,3456]{1,0:T(8,128)(2,1)S(1)} %get-tuple-element.27), channel_id=1, source_target_pairs={{0,8},{8,0},{16,24},{24,16},{1,9},{9,1},{17,25},{25,17},{2,10},{10... | collective-permute-start | bytes 331784 | tf_op jit(solution)/shard_map/ppermute | solution.py:233
  21.1 5.3 %collective-permute-start.7 = (bf16[16,2048]{1,0:T(8,128)(2,1)S(1)}, bf16[16,2048]{1,0:T(8,128)(2,1)S(1)}, u32[]{:S(2)}, u32[]{:S(2)}) collective-permute-start(bf16[16,2048]{1,0:T(8,128)(2,1)S(1)} %get-tuple-element.42), channel_id=1, source_target_pairs={{0,6},{1,7},{2,4},{3,5},{4,2},{5,3},{6,0},{7,1},{8,14},{9,15},{10,... | collective-permute-start | bytes 196616 | tf_op jit(solution)/shard_map/ppermute | solution.py:233
  22.9 4.5 %collective-permute-start.6 = (bf16[16,2048]{1,0:T(8,128)(2,1)S(1)}, bf16[16,2048]{1,0:T(8,128)(2,1)S(1)}, u32[]{:S(2)}, u32[]{:S(2)}) collective-permute-start(bf16[16,2048]{1,0:T(8,128)(2,1)S(1)} %get-tuple-element.43), channel_id=1, source_target_pairs={{0,4},{1,5},{2,6},{3,7},{4,0},{5,1},{6,2},{7,3},{8,12},{9,13},{10,... | collective-permute-start | bytes 196616 | tf_op jit(solution)/shard_map/ppermute | solution.py:233
  23.6 4.3 %collective-permute-start.5 = (bf16[16,2048]{1,0:T(8,128)(2,1)S(1)}, bf16[16,2048]{1,0:T(8,128)(2,1)S(1)}, u32[]{:S(2)}, u32[]{:S(2)}) collective-permute-start(bf16[16,2048]{1,0:T(8,128)(2,1)S(1)} %get-tuple-element.44), channel_id=1, source_target_pairs={{0,2},{1,3},{2,0},{3,1},{4,6},{5,7},{6,4},{7,5},{8,10},{9,11},{10,... | collective-permute-start | bytes 196616 | tf_op jit(solution)/shard_map/ppermute | solution.py:233
  27.9 9.5 %collective-permute-start.10 = (bf16[16,3456]{1,0:T(8,128)(2,1)S(1)}, bf16[16,3456]{1,0:T(8,128)(2,1)S(1)}, u32[]{:S(2)}, u32[]{:S(2)}) collective-permute-start(bf16[16,3456]{1,0:T(8,128)(2,1)S(1)} %add_convert_fusion.1), channel_id=1, source_target_pairs={{0,16},{8,24},{16,0},{24,8},{1,17},{9,25},{17,1},{25,9},{2,18},{10... | collective-permute-start | bytes 331784 | tf_op jit(solution)/shard_map/ppermute | solution.py:233
  31.9 15.6 %collective-permute-start.15 = (bf16[16,1728]{1,0:T(8,128)(2,1)S(1)}, bf16[16,1728]{1,0:T(8,128)(2,1)S(1)}, u32[]{:S(2)}, u32[]{:S(2)}) collective-permute-start(bf16[16,1728]{1,0:T(8,128)(2,1)S(1)} %get-tuple-element.38), channel_id=1, source_target_pairs={{0,24},{8,16},{16,8},{24,0},{1,25},{9,17},{17,9},{25,1},{2,26},{10... | collective-permute-start | bytes 165896 | tf_op jit(solution)/shard_map/ppermute | solution.py:233
  33.0 14.5 %collective-permute-start.14 = (bf16[16,1728]{1,0:T(8,128)(2,1)S(1)}, bf16[16,1728]{1,0:T(8,128)(2,1)S(1)}, u32[]{:S(2)}, u32[]{:S(2)}) collective-permute-start(bf16[16,1728]{1,0:T(8,128)(2,1)S(1)} %get-tuple-element.38), channel_id=1, source_target_pairs={{0,16},{8,24},{16,0},{24,8},{1,17},{9,25},{17,1},{25,9},{2,18},{10... | collective-permute-start | bytes 165896 | tf_op jit(solution)/shard_map/ppermute | solution.py:233
  34.7 2.6 %collective-permute-start.9 = (bf16[4,8,2048]{2,1,0:T(8,128)(2,1)S(1)}, bf16[4,8,2048]{2,1,0:T(8,128)(2,1)S(1)}, u32[]{:S(2)}, u32[]{:S(2)}) collective-permute-start(bf16[4,8,2048]{2,1,0:T(8,128)(2,1)S(1)} %get-tuple-element.35), channel_id=1, source_target_pairs={{0,1},{1,0},{2,3},{3,2},{4,5},{5,4},{6,7},{7,6},{8,9},{9,8},{10,11... | collective-permute-start | bytes 393224 | tf_op jit(solution)/shard_map/ppermute | solution.py:233
  37.4 4.0 %collective-permute-start.11 = (bf16[8,2048]{1,0:T(8,128)(2,1)S(1)}, bf16[8,2048]{1,0:T(8,128)(2,1)S(1)}, u32[]{:S(2)}, u32[]{:S(2)}) collective-permute-start(bf16[8,2048]{1,0:T(8,128)(2,1)S(1)} %get-tuple-element.46), channel_id=1, source_target_pairs={{0,2},{1,3},{2,0},{3,1},{4,6},{5,7},{6,4},{7,5},{8,10},{9,11},{10,... | collective-permute-start | bytes 98312 | tf_op jit(solution)/shard_map/ppermute | solution.py:233
  38.5 4.8 %collective-permute-start.13 = (bf16[8,2048]{1,0:T(8,128)(2,1)S(1)}, bf16[8,2048]{1,0:T(8,128)(2,1)S(1)}, u32[]{:S(2)}, u32[]{:S(2)}) collective-permute-start(bf16[8,2048]{1,0:T(8,128)(2,1)S(1)} %get-tuple-element.47), channel_id=1, source_target_pairs={{0,6},{1,7},{2,4},{3,5},{4,2},{5,3},{6,0},{7,1},{8,14},{9,15},{10,... | collective-permute-start | bytes 98312 | tf_op jit(solution)/shard_map/ppermute | solution.py:233
  40.6 3.9 %collective-permute-start.12 = (bf16[8,2048]{1,0:T(8,128)(2,1)S(1)}, bf16[8,2048]{1,0:T(8,128)(2,1)S(1)}, u32[]{:S(2)}, u32[]{:S(2)}) collective-permute-start(bf16[8,2048]{1,0:T(8,128)(2,1)S(1)} %get-tuple-element.48), channel_id=1, source_target_pairs={{0,4},{1,5},{2,6},{3,7},{4,0},{5,1},{6,2},{7,3},{8,12},{9,13},{10,... | collective-permute-start | bytes 98312 | tf_op jit(solution)/shard_map/ppermute | solution.py:233
  41.4 5.4 %collective-permute-start.16 = (bf16[16,5184]{1,0:T(8,128)(2,1)S(1)}, bf16[16,5184]{1,0:T(8,128)(2,1)S(1)}, u32[]{:S(2)}, u32[]{:S(2)}) collective-permute-start(bf16[16,5184]{1,0:T(8,128)(2,1)S(1)} %pad_maximum_fusion.1), channel_id=1, source_target_pairs={{0,8},{8,0},{16,24},{24,16},{1,9},{9,1},{17,25},{25,17},{2,10},{10... | collective-permute-start | bytes 497672 | tf_op jit(solution)/shard_map/ppermute | solution.py:233

commit v6 on v5

--- a/solution.py
+++ b/solution.py
@@ -13,6 +13,7 @@
 F32 = jnp.float32
 BF16 = jnp.bfloat16
 VMEM_LIMIT = 48 * 1024 * 1024
+COVER = 10**12
 
 
 def pitch_of(channels):
@@ -329,7 +330,6 @@
         2 * 1024 * 1024,
     )(d9, w2b)
     parts = sum_over_chips(keep, swap(give, "mp", 1))
-    *parts, half_got = lax.optimization_barrier((*parts, half_got))
     half_sum = add(half_keep, half_got)
     bits = bits_above(n_sample)
     for bit in bits[:-1]:
@@ -348,18 +348,18 @@
             pltpu.VMEM((n_mp, rows_in, cells), F32),
             pltpu.VMEM((27 * f1, max(1, 128 // c0) * c0), F32),
         ],
-        2 * cells * 27 * 2 * c0 * f1,
+        COVER,
         1024 * 1024,
     )(*parts, pre_own, vol_all, w1b)
     got = swap(give, "mp", 1)
-
-    half_got, _ = lax.optimization_barrier((half_got, grad_first))
+    ins = sum_over_chips(keep, got)
+    input_grad = total(ins).astype(BF16)
+    firsts = [grad_first] + [swap(grad_first, "sample", k) for k in range(1, n_sample)]
+    grad_first = total(firsts) * scale
+
     half_sum = add(half_sum, half_got)
-    got, half_sum = lax.optimization_barrier((got, half_sum))
-    ins = sum_over_chips(keep, got)
-    both = swap(jnp.concatenate([half_sum, grad_first], axis=1), "sample", 1)
-    firsts = [grad_first] + [swap(grad_first, "sample", k) for k in range(2, n_sample)] + [both[:, 27 * c1 :]]
-    grad_first = total(firsts) * scale
+    both = swap(half_sum, "sample", 1)
+    both, *_ = lax.optimization_barrier((both, grad_first, input_grad))
     grad_second = call(
         functools.partial(place_kernel, scale),
         sds((2, f2 // 2, 27 * c1), F32),
@@ -369,7 +369,7 @@
     )(half_sum, both).reshape(f2, 27 * c1)
     return (
         features.reshape(f2, 1, cells),
-        total(ins).astype(BF16).reshape(rows_in, 1, cells),
+        input_grad.reshape(rows_in, 1, cells),
         grad_first,
         grad_second,
     )

time: 48.5 us -> 50.6 us (1.043)
  other arithmetic: 2.4 us -> 3.97 us
    convert_element_type x4, other arithmetic: 0.15 us -> 1.74 us  [add(): return (a.astype(F32) + b.astype(F32)).astype(BF16)]
    convert_element_type x0 -> x1, other arithmetic: none -> 0.64 us  [local(): input_grad = total(ins).astype(BF16)]
    reshape x1 -> x0, other arithmetic: 0.64 us -> none  [local(): total(ins).astype(BF16).reshape(rows_in, 1, cells)]
    ppermute x17 -> x18, waiting for transfers between devices: 14.6 us -> 15 us  [swap(): return lax.ppermute(value, axis, [(i, i ^ k) for i in range(n)])]
    ppermute x17 -> x18, starting transfers between devices: 21.1 us -> 21.4 us  [swap(): return lax.ppermute(value, axis, [(i, i ^ k) for i in range(n)])]
  transfers between devices with their start and end apart: 17 -> 18, of which waited for: 12 -> 8; matrix products, arithmetic and copies ran while one was open for 5% -> 10% of each run, Pallas kernels for 4% -> 2%
where the time goes in v6:
time: 50.6 us; the launch traced here: 50.4 us
  starting transfers between devices  21.4 us (42%)
  waiting for transfers between devices  15 us (30%)
  Pallas kernels  7.57 us (15%)
  other arithmetic  3.97 us (8%)
  local copies, waits for them, and re-layouts  1.78 us (4%)
  between operations  0.77 us (2%)
    ppermute x18, starting transfers between devices, swap(): return lax.ppermute(value, axis, [(i, i ^ k) for i in range(n)])  21.4 us
    ppermute x18, waiting for transfers between devices, swap(): return lax.ppermute(value, axis, [(i, i ^ k) for i in range(n)])  15 us
    pallas_call x1, Pallas kernels, local(): call(functools.partial(forward_kernel, n_mp, c0), [sds((f2, cells), BF16)...  4.93 us
    convert_element_type x4, other arithmetic, add(): return (a.astype(F32) + b.astype(F32)).astype(BF16)  1.74 us
    reshape x1, local copies, waits for them, and re-layouts, local(): w2t = w_second.reshape(f2, 3, 9, c1)  1.06 us
    pallas_call x1, Pallas kernels, local(): call(functools.partial(backward_kernel, n_mp), [sds((half, rows_in, cells...  1.06 us
  transfers between devices with their start and end apart: 18, of which 8 were waited for; matrix products, arithmetic and copies ran while one was open for 10% of the time, Pallas kernels for 2%

profile of v6, /device:TPU:0, one launch (start us, length us, event | category | flops | bytes accessed | tf_op | source)
XLA Modules:
  0.0 50.4 jit_solution(8664857593299236378)
XLA Ops:
  0.6 0.9 %fusion.13 = (bf16[1,24,2048]{2,1,0:T(8,128)(2,1)S(1)}, bf16[24,2048]{1,0:T(8,128)(2,1)S(1)}) fusion(bf16[8,2048]{1,0:T(8,128)(2,1)} %bitcast.51, bf16[16,1728]{1,0:T(8,128)(2,1)} %param.5), kind=kLoop, calls=%fused_computation.28 | loop fusion | flops 294912 | bytes 284672 | tf_op jit(solution)/shard_map/stack | solution.py:291
  1.5 3.0 %collective-permute-start.1 = (bf16[24,2048]{1,0:T(8,128)(2,1)S(1)}, bf16[24,2048]{1,0:T(8,128)(2,1)S(1)}, u32[]{:S(2)}, u32[]{:S(2)}) collective-permute-start(bf16[24,2048]{1,0:T(8,128)(2,1)S(1)} %get-tuple-element.36), channel_id=1, source_target_pairs={{0,4},{1,5},{2,6},{3,7},{4,0},{5,1},{6,2},{7,3},{8,12},{9,13},{10,... | collective-permute-start | bytes 294920 | tf_op jit(solution)/shard_map/ppermute | solution.py:234
  4.5 1.5 %collective-permute-start = (bf16[24,2048]{1,0:T(8,128)(2,1)S(1)}, bf16[24,2048]{1,0:T(8,128)(2,1)S(1)}, u32[]{:S(2)}, u32[]{:S(2)}) collective-permute-start(bf16[24,2048]{1,0:T(8,128)(2,1)S(1)} %get-tuple-element.36), channel_id=1, source_target_pairs={{0,2},{1,3},{2,0},{3,1},{4,6},{5,7},{6,4},{7,5},{8,10},{9,11},{10,... | collective-permute-start | bytes 294920 | tf_op jit(solution)/shard_map/ppermute | solution.py:234
  6.0 0.0 collective-permute-start.2
  6.1 1.3 %collective-permute-done.1 = bf16[24,2048]{1,0:T(8,128)(2,1)S(1)} collective-permute-done((bf16[24,2048]{1,0:T(8,128)(2,1)S(1)}, bf16[24,2048]{1,0:T(8,128)(2,1)S(1)}, u32[]{:S(2)}, u32[]{:S(2)}) %collective-permute-start.1) | collective-permute-done | bytes 98336 | tf_op jit(solution)/shard_map/ppermute | solution.py:234
  7.3 2.6 %collective-permute-done = bf16[24,2048]{1,0:T(8,128)(2,1)S(1)} collective-permute-done((bf16[24,2048]{1,0:T(8,128)(2,1)S(1)}, bf16[24,2048]{1,0:T(8,128)(2,1)S(1)}, u32[]{:S(2)}, u32[]{:S(2)}) %collective-permute-start) | collective-permute-done | bytes 98336 | tf_op jit(solution)/shard_map/ppermute | solution.py:234
  9.9 1.6 %collective-permute-done.2 = bf16[24,2048]{1,0:T(8,128)(2,1)S(1)} collective-permute-done((bf16[24,2048]{1,0:T(8,128)(2,1)S(1)}, bf16[24,2048]{1,0:T(8,128)(2,1)S(1)}, u32[]{:S(2)}, u32[]{:S(2)}) %collective-permute-start.2) | collective-permute-done | bytes 98336 | tf_op jit(solution)/shard_map/ppermute | solution.py:234
  11.5 0.1 pad_maximum_fusion.refs_0_
  11.6 0.0 copy-start
  11.6 0.1 collective-permute-start.3
  11.7 1.1 %reshape.73 = bf16[32,3,9,128]{3,2,1,0:T(8,128)(2,1)S(1)} reshape(bf16[32,3456]{1,0:T(8,128)(2,1)} %param.6) | data formatting | bytes 442368 | tf_op jit(solution)/shard_map/reshape | solution.py:294
  12.7 0.1 copy.12
  12.8 0.2 copy.13.w2b_ref
  13.0 0.1 copy.11
  13.1 0.2 collective-permute-done.3.refs_1_
  13.4 0.0 copy-done
  13.4 4.9 %shard_map.75 = (bf16[32,2048]{1,0:T(8,128)(2,1)}, f32[16,2048]{1,0:T(8,128)S(1)}, bf16[64,2048]{1,0:T(8,128)(2,1)S(1)}, bf16[288,2560]{1,0:T(8,128)(2,1)S(1)}, ...) custom-call(bf16[4,24,2048]{2,1,0:T(8,128)(2,1)S(1)} %pad_maximum_fusion.refs_0_, ...), custom_call_target="tpu_custom_call" | custom-call | flops 1811939328 | bytes 4194304 | tf_op jit(solution)/shard_map/pallas_call | solution.py:301
  18.3 0.0 copy-start.1
  18.3 0.8 %shard_map.76 = (bf16[4,16,2048]{2,1,0:T(8,128)(2,1)S(1)}, bf16[4,16,2048]{2,1,0:T(8,128)(2,1)S(1)}) custom-call(bf16[288,2560]{1,0:T(8,128)(2,1)S(1)} %get-tuple-element.17.d9, bf16[128,864]{1,0:T(8,128)(2,1)S(1)} %copy.13.w2b_ref), custom_call_target="tpu_custom_call" | custom-call | flops 452984832 | bytes 2097152 | tf_op jit(solution)/shard_map/pallas_call | solution.py:325
  19.1 0.3 collective-permute-start.4
  19.5 0.0 copy-done.1
  19.5 0.2 reshape.78
  19.7 0.1 copy.15.refs_6_
  19.8 1.6 %collective-permute-start.15 = (bf16[16,3456]{1,0:T(8,128)(2,1)S(1)}, bf16[16,3456]{1,0:T(8,128)(2,1)S(1)}, u32[]{:S(2)}, u32[]{:S(2)}) collective-permute-start(bf16[16,3456]{1,0:T(8,128)(2,1)S(1)} %get-tuple-element.26), channel_id=1, source_target_pairs={{0,8},{8,0},{16,24},{24,16},{1,9},{9,1},{17,25},{25,17},{2,10},{10... | collective-permute-start | bytes 331784 | tf_op jit(solution)/shard_map/ppermute | solution.py:234
  21.4 0.0 collective-permute-done.4
  21.4 0.1 fusion.5
  21.5 1.8 %collective-permute-start.7 = (bf16[16,2048]{1,0:T(8,128)(2,1)S(1)}, bf16[16,2048]{1,0:T(8,128)(2,1)S(1)}, u32[]{:S(2)}, u32[]{:S(2)}) collective-permute-start(bf16[16,2048]{1,0:T(8,128)(2,1)S(1)} %get-tuple-element.28), channel_id=1, source_target_pairs={{0,6},{1,7},{2,4},{3,5},{4,2},{5,3},{6,0},{7,1},{8,14},{9,15},{10,... | collective-permute-start | bytes 196616 | tf_op jit(solution)/shard_map/ppermute | solution.py:234
  23.3 0.7 %collective-permute-start.6 = (bf16[16,2048]{1,0:T(8,128)(2,1)S(1)}, bf16[16,2048]{1,0:T(8,128)(2,1)S(1)}, u32[]{:S(2)}, u32[]{:S(2)}) collective-permute-start(bf16[16,2048]{1,0:T(8,128)(2,1)S(1)} %get-tuple-element.29), channel_id=1, source_target_pairs={{0,4},{1,5},{2,6},{3,7},{4,0},{5,1},{6,2},{7,3},{8,12},{9,13},{10,... | collective-permute-start | bytes 196616 | tf_op jit(solution)/shard_map/ppermute | solution.py:234
  24.0 1.1 %collective-permute-start.5 = (bf16[16,2048]{1,0:T(8,128)(2,1)S(1)}, bf16[16,2048]{1,0:T(8,128)(2,1)S(1)}, u32[]{:S(2)}, u32[]{:S(2)}) collective-permute-start(bf16[16,2048]{1,0:T(8,128)(2,1)S(1)} %get-tuple-element.30), channel_id=1, source_target_pairs={{0,2},{1,3},{2,0},{3,1},{4,6},{5,7},{6,4},{7,5},{8,10},{9,11},{10,... | collective-permute-start | bytes 196616 | tf_op jit(solution)/shard_map/ppermute | solution.py:234
  25.1 0.0 collective-permute-done.15
  25.1 0.7 %add_convert_fusion.1 = bf16[16,3456]{1,0:T(8,128)(2,1)} fusion(bf16[16,3456]{1,0:T(8,128)(2,1)S(1)} %collective-permute-done.15, bf16[16,3456]{1,0:T(8,128)(2,1)S(1)} %get-tuple-element.25), kind=kLoop, calls=%fused_computation.3 | loop fusion | flops 221184 | bytes 331776 | tf_op jit(solution)/shard_map/convert_element_type | solution.py:238
  25.7 2.6 %collective-permute-start.16 = (bf16[16,3456]{1,0:T(8,128)(2,1)}, bf16[16,3456]{1,0:T(8,128)(2,1)}, u32[]{:S(2)}, u32[]{:S(2)}) collective-permute-start(bf16[16,3456]{1,0:T(8,128)(2,1)} %add_convert_fusion.1), channel_id=1, source_target_pairs={{0,16},{8,24},{16,0},{24,8},{1,17},{9,25},{17,1},{25,9},{2,18},{10... | collective-permute-start | bytes 331784 | tf_op jit(solution)/shard_map/ppermute | solution.py:234
  28.3 0.0 collective-permute-done.7.refs_3_
  28.3 0.0 collective-permute-done.6.refs_2_
  28.3 0.0 collective-permute-done.5.refs_1_
  28.4 1.1 %shard_map.77 = (bf16[4,8,2048]{2,1,0:T(8,128)(2,1)S(1)}, bf16[4,8,2048]{2,1,0:T(8,128)(2,1)S(1)}, bf16[16,1728]{1,0:T(8,128)(2,1)S(1)}) custom-call(bf16[16,2048]{1,0:T(8,128)(2,1)S(1)} %get-tuple-element.31.refs_0_, bf16[16,2048]{1,0:T(8,128)(2,1)S(1)} %collective-permute-done.5.refs_1_, bf16[16,2048]{1,0:T(8,128)(2,1)S(1)} %collective-permute-done.6.refs_2_, ...), custom_call_target="tpu_custom_call" | custom-call | flops 999999995904 | bytes 1048576 | tf_op jit(solution)/shard_map/pallas_call | solution.py:339
  29.4 0.1 collective-permute-start.8
  29.5 4.2 %collective-permute-done.16 = bf16[16,3456]{1,0:T(8,128)(2,1)} collective-permute-done((bf16[16,3456]{1,0:T(8,128)(2,1)}, bf16[16,3456]{1,0:T(8,128)(2,1)}, u32[]{:S(2)}, u32[]{:S(2)}) %collective-permute-start.16) | collective-permute-done | bytes 110624 | tf_op jit(solution)/shard_map/ppermute | solution.py:234
  33.7 1.0 %add_convert_fusion.mine_ref = bf16[16,3456]{1,0:T(8,128)(2,1)S(1)} fusion(bf16[16,3456]{1,0:T(8,128)(2,1)} %collective-permute-done.16, bf16[16,3456]{1,0:T(8,128)(2,1)} %add_convert_fusion.1), kind=kLoop, calls=%fused_computation.2 | loop fusion | flops 221184 | bytes 331776 | tf_op jit(solution)/shard_map/convert_element_type | solution.py:238
  34.7 0.7 %collective-permute-start.17 = (bf16[16,3456]{1,0:T(8,128)(2,1)S(1)}, bf16[16,3456]{1,0:T(8,128)(2,1)S(1)}, u32[]{:S(2)}, u32[]{:S(2)}) collective-permute-start(bf16[16,3456]{1,0:T(8,128)(2,1)S(1)} %add_convert_fusion.mine_ref), channel_id=1, source_target_pairs={{0,8},{8,0},{16,24},{24,16},{1,9},{9,1},{17,25},{25,17},{2,10},{10... | collective-permute-start | bytes 331784 | tf_op jit(solution)/shard_map/ppermute | solution.py:234
  35.4 2.9 %collective-permute-start.14 = (bf16[16,1728]{1,0:T(8,128)(2,1)S(1)}, bf16[16,1728]{1,0:T(8,128)(2,1)S(1)}, u32[]{:S(2)}, u32[]{:S(2)}) collective-permute-start(bf16[16,1728]{1,0:T(8,128)(2,1)S(1)} %get-tuple-element.24), channel_id=1, source_target_pairs={{0,24},{8,16},{16,8},{24,0},{1,25},{9,17},{17,9},{25,1},{2,26},{10... | collective-permute-start | bytes 165896 | tf_op jit(solution)/shard_map/ppermute | solution.py:234
  38.3 0.5 collective-permute-start.13
  38.8 1.0 %collective-permute-start.12 = (bf16[16,1728]{1,0:T(8,128)(2,1)S(1)}, bf16[16,1728]{1,0:T(8,128)(2,1)S(1)}, u32[]{:S(2)}, u32[]{:S(2)}) collective-permute-start(bf16[16,1728]{1,0:T(8,128)(2,1)S(1)} %get-tuple-element.24), channel_id=1, source_target_pairs={{0,8},{8,0},{16,24},{24,16},{1,9},{9,1},{17,25},{25,17},{2,10},{10... | collective-permute-start | bytes 165896 | tf_op jit(solution)/shard_map/ppermute | solution.py:234
  39.8 0.0 collective-permute-done.8
  39.8 1.0 %collective-permute-start.9 = (bf16[8,2048]{1,0:T(8,128)(2,1)S(1)}, bf16[8,2048]{1,0:T(8,128)(2,1)S(1)}, u32[]{:S(2)}, u32[]{:S(2)}) collective-permute-start(bf16[8,2048]{1,0:T(8,128)(2,1)S(1)} %get-tuple-element.32), channel_id=1, source_target_pairs={{0,2},{1,3},{2,0},{3,1},{4,6},{5,7},{6,4},{7,5},{8,10},{9,11},{10,... | collective-permute-start | bytes 98312 | tf_op jit(solution)/shard_map/ppermute | solution.py:234
  40.8 2.5 %collective-permute-done.14 = bf16[16,1728]{1,0:T(8,128)(2,1)S(1)} collective-permute-done((bf16[16,1728]{1,0:T(8,128)(2,1)S(1)}, bf16[16,1728]{1,0:T(8,128)(2,1)S(1)}, u32[]{:S(2)}, u32[]{:S(2)}) %collective-permute-start.14) | collective-permute-done | bytes 55328 | tf_op jit(solution)/shard_map/ppermute | solution.py:234
  43.3 1.7 %collective-permute-start.11 = (bf16[8,2048]{1,0:T(8,128)(2,1)S(1)}, bf16[8,2048]{1,0:T(8,128)(2,1)S(1)}, u32[]{:S(2)}, u32[]{:S(2)}) collective-permute-start(bf16[8,2048]{1,0:T(8,128)(2,1)S(1)} %get-tuple-element.33), channel_id=1, source_target_pairs={{0,6},{1,7},{2,4},{3,5},{4,2},{5,3},{6,0},{7,1},{8,14},{9,15},{10,... | collective-permute-start | bytes 98312 | tf_op jit(solution)/shard_map/ppermute | solution.py:234
  45.0 0.0 collective-permute-done.13
  45.0 0.6 %collective-permute-start.10 = (bf16[8,2048]{1,0:T(8,128)(2,1)S(1)}, bf16[8,2048]{1,0:T(8,128)(2,1)S(1)}, u32[]{:S(2)}, u32[]{:S(2)}) collective-permute-start(bf16[8,2048]{1,0:T(8,128)(2,1)S(1)} %get-tuple-element.34), channel_id=1, source_target_pairs={{0,4},{1,5},{2,6},{3,7},{4,0},{5,1},{6,2},{7,3},{8,12},{9,13},{10,... | collective-permute-start | bytes 98312 | tf_op jit(solution)/shard_map/ppermute | solution.py:234
  45.7 0.0 collective-permute-done.12
  45.7 0.7 %add_multiply_fusion = f32[16,1728]{1,0:T(8,128)} fusion(bf16[16,1728]{1,0:T(8,128)(2,1)S(1)} %collective-permute-done.14, bf16[16,1728]{1,0:T(8,128)(2,1)S(1)} %collective-permute-done.13, bf16[16,1728]{1,0:T(8,128)(2,1)S(1)} %collective-permute-done.12, bf16[16,1728]{1,0:T(8,128)(2,1)S(1)} %get-tuple-element.24), kind=kLoop, calls=%fused_computation.10 | loop fusion | flops 221184 | bytes 331776 | tf_op jit(solution)/shard_map/mul | solution.py:358
  46.4 0.0 collective-permute-done.9
  46.4 1.7 %collective-permute-done.11 = bf16[8,2048]{1,0:T(8,128)(2,1)S(1)} collective-permute-done((bf16[8,2048]{1,0:T(8,128)(2,1)S(1)}, bf16[8,2048]{1,0:T(8,128)(2,1)S(1)}, u32[]{:S(2)}, u32[]{:S(2)}) %collective-permute-start.11) | collective-permute-done | bytes 32800 | tf_op jit(solution)/shard_map/ppermute | solution.py:234
  48.1 0.8 %collective-permute-done.10 = bf16[8,2048]{1,0:T(8,128)(2,1)S(1)} collective-permute-done((bf16[8,2048]{1,0:T(8,128)(2,1)S(1)}, bf16[8,2048]{1,0:T(8,128)(2,1)S(1)}, u32[]{:S(2)}, u32[]{:S(2)}) %collective-permute-start.10) | collective-permute-done | bytes 32800 | tf_op jit(solution)/shard_map/ppermute | solution.py:234
  49.0 0.6 %fusion.8 = bf16[8,2048]{1,0:T(8,128)(2,1)} fusion(bf16[8,2048]{1,0:T(8,128)(2,1)S(1)} %collective-permute-done.11, bf16[8,2048]{1,0:T(8,128)(2,1)S(1)} %collective-permute-done.10, bf16[8,2048]{1,0:T(8,128)(2,1)S(1)} %collective-permute-done.9, bf16[4,8,2048]{2,1,0:T(8,128)(2,1)S(1)} %collective-permute-done.8, bf16[4,8,2048]{2,1,0:T(8,128)(2,1)S(1)} %get-tuple-element.22), kind=kLoop, calls=%fused_computation.19 | loop fusion | flops 196608 | bytes 196608 | tf_op jit(solution)/shard_map/convert_element_type | solution.py:356
  49.6 0.0 collective-permute-done.17.other_ref
  49.6 0.8 %shard_map.78 = f32[2,16,3456]{2,1,0:T(8,128)} custom-call(bf16[16,3456]{1,0:T(8,128)(2,1)S(1)} %add_convert_fusion.mine_ref, bf16[16,3456]{1,0:T(8,128)(2,1)S(1)} %collective-permute-done.17.other_ref), custom_call_target="tpu_custom_call" | custom-call | bytes 1048576 | tf_op jit(solution)/shard_map/pallas_call | solution.py:363
  (3 shorter events, 0.1 us)
Async XLA Ops:
  1.5 5.8 %collective-permute-start.1 = (bf16[24,2048]{1,0:T(8,128)(2,1)S(1)}, bf16[24,2048]{1,0:T(8,128)(2,1)S(1)}, u32[]{:S(2)}, u32[]{:S(2)}) collective-permute-start(bf16[24,2048]{1,0:T(8,128)(2,1)S(1)} %get-tuple-element.36), channel_id=1, source_target_pairs={{0,4},{1,5},{2,6},{3,7},{4,0},{5,1},{6,2},{7,3},{8,12},{9,13},{10,... | collective-permute-start | bytes 294920 | tf_op jit(solution)/shard_map/ppermute | solution.py:234
  4.5 5.4 %collective-permute-start = (bf16[24,2048]{1,0:T(8,128)(2,1)S(1)}, bf16[24,2048]{1,0:T(8,128)(2,1)S(1)}, u32[]{:S(2)}, u32[]{:S(2)}) collective-permute-start(bf16[24,2048]{1,0:T(8,128)(2,1)S(1)} %get-tuple-element.36), channel_id=1, source_target_pairs={{0,2},{1,3},{2,0},{3,1},{4,6},{5,7},{6,4},{7,5},{8,10},{9,11},{10,... | collective-permute-start | bytes 294920 | tf_op jit(solution)/shard_map/ppermute | solution.py:234
  6.0 5.5 %collective-permute-start.2 = (bf16[24,2048]{1,0:T(8,128)(2,1)S(1)}, bf16[24,2048]{1,0:T(8,128)(2,1)S(1)}, u32[]{:S(2)}, u32[]{:S(2)}) collective-permute-start(bf16[24,2048]{1,0:T(8,128)(2,1)S(1)} %get-tuple-element.36), channel_id=1, source_target_pairs={{0,6},{1,7},{2,4},{3,5},{4,2},{5,3},{6,0},{7,1},{8,14},{9,15},{10,... | collective-permute-start | bytes 294920 | tf_op jit(solution)/shard_map/ppermute | solution.py:234
  11.6 1.8 %copy-start = (bf16[32,1,2048]{2,0,1:T(8,128)(2,1)S(1)}, bf16[32,1,2048]{2,0,1:T(8,128)(2,1)}, u32[]{:S(2)}) copy-start(bf16[32,1,2048]{2,0,1:T(8,128)(2,1)} %param.7) | copy-start | bytes 393220
  11.6 1.8 %collective-permute-start.3 = (bf16[4,24,2048]{2,1,0:T(8,128)(2,1)S(1)}, bf16[4,24,2048]{2,1,0:T(8,128)(2,1)S(1)}, u32[]{:S(2)}, u32[]{:S(2)}) collective-permute-start(bf16[4,24,2048]{2,1,0:T(8,128)(2,1)S(1)} %pad_maximum_fusion.refs_0_), channel_id=1, source_target_pairs={{0,1},{1,0},{2,3},{3,2},{4,5},{5,4},{6,7},{7,6},{8,9},{9,8},{10,11... | collective-permute-start | bytes 1179656 | tf_op jit(solution)/shard_map/ppermute | solution.py:234
  18.3 1.1 %copy-start.1 = (bf16[16,1728]{1,0:T(8,128)(2,1)S(1)}, bf16[16,1728]{1,0:T(8,128)(2,1)}, u32[]{:S(2)}) copy-start(bf16[16,1728]{1,0:T(8,128)(2,1)} %param.5) | copy-start | bytes 165892
  19.1 2.3 %collective-permute-start.4 = (bf16[4,16,2048]{2,1,0:T(8,128)(2,1)S(1)}, bf16[4,16,2048]{2,1,0:T(8,128)(2,1)S(1)}, u32[]{:S(2)}, u32[]{:S(2)}) collective-permute-start(bf16[4,16,2048]{2,1,0:T(8,128)(2,1)S(1)} %get-tuple-element.19), channel_id=1, source_target_pairs={{0,1},{1,0},{2,3},{3,2},{4,5},{5,4},{6,7},{7,6},{8,9},{9,8},{10,11... | collective-permute-start | bytes 786440 | tf_op jit(solution)/shard_map/ppermute | solution.py:234
  19.8 5.3 %collective-permute-start.15 = (bf16[16,3456]{1,0:T(8,128)(2,1)S(1)}, bf16[16,3456]{1,0:T(8,128)(2,1)S(1)}, u32[]{:S(2)}, u32[]{:S(2)}) collective-permute-start(bf16[16,3456]{1,0:T(8,128)(2,1)S(1)} %get-tuple-element.26), channel_id=1, source_target_pairs={{0,8},{8,0},{16,24},{24,16},{1,9},{9,1},{17,25},{25,17},{2,10},{10... | collective-permute-start | bytes 331784 | tf_op jit(solution)/shard_map/ppermute | solution.py:234
  21.5 6.8 %collective-permute-start.7 = (bf16[16,2048]{1,0:T(8,128)(2,1)S(1)}, bf16[16,2048]{1,0:T(8,128)(2,1)S(1)}, u32[]{:S(2)}, u32[]{:S(2)}) collective-permute-start(bf16[16,2048]{1,0:T(8,128)(2,1)S(1)} %get-tuple-element.28), channel_id=1, source_target_pairs={{0,6},{1,7},{2,4},{3,5},{4,2},{5,3},{6,0},{7,1},{8,14},{9,15},{10,... | collective-permute-start | bytes 196616 | tf_op jit(solution)/shard_map/ppermute | solution.py:234
  23.3 5.0 %collective-permute-start.6 = (bf16[16,2048]{1,0:T(8,128)(2,1)S(1)}, bf16[16,2048]{1,0:T(8,128)(2,1)S(1)}, u32[]{:S(2)}, u32[]{:S(2)}) collective-permute-start(bf16[16,2048]{1,0:T(8,128)(2,1)S(1)} %get-tuple-element.29), channel_id=1, source_target_pairs={{0,4},{1,5},{2,6},{3,7},{4,0},{5,1},{6,2},{7,3},{8,12},{9,13},{10,... | collective-permute-start | bytes 196616 | tf_op jit(solution)/shard_map/ppermute | solution.py:234
  24.0 4.4 %collective-permute-start.5 = (bf16[16,2048]{1,0:T(8,128)(2,1)S(1)}, bf16[16,2048]{1,0:T(8,128)(2,1)S(1)}, u32[]{:S(2)}, u32[]{:S(2)}) collective-permute-start(bf16[16,2048]{1,0:T(8,128)(2,1)S(1)} %get-tuple-element.30), channel_id=1, source_target_pairs={{0,2},{1,3},{2,0},{3,1},{4,6},{5,7},{6,4},{7,5},{8,10},{9,11},{10,... | collective-permute-start | bytes 196616 | tf_op jit(solution)/shard_map/ppermute | solution.py:234
  25.7 8.0 %collective-permute-start.16 = (bf16[16,3456]{1,0:T(8,128)(2,1)}, bf16[16,3456]{1,0:T(8,128)(2,1)}, u32[]{:S(2)}, u32[]{:S(2)}) collective-permute-start(bf16[16,3456]{1,0:T(8,128)(2,1)} %add_convert_fusion.1), channel_id=1, source_target_pairs={{0,16},{8,24},{16,0},{24,8},{1,17},{9,25},{17,1},{25,9},{2,18},{10... | collective-permute-start | bytes 331784 | tf_op jit(solution)/shard_map/ppermute | solution.py:234
  29.4 10.4 %collective-permute-start.8 = (bf16[4,8,2048]{2,1,0:T(8,128)(2,1)S(1)}, bf16[4,8,2048]{2,1,0:T(8,128)(2,1)S(1)}, u32[]{:S(2)}, u32[]{:S(2)}) collective-permute-start(bf16[4,8,2048]{2,1,0:T(8,128)(2,1)S(1)} %get-tuple-element.23), channel_id=1, source_target_pairs={{0,1},{1,0},{2,3},{3,2},{4,5},{5,4},{6,7},{7,6},{8,9},{9,8},{10,11... | collective-permute-start | bytes 393224 | tf_op jit(solution)/shard_map/ppermute | solution.py:234
  34.7 14.9 %collective-permute-start.17 = (bf16[16,3456]{1,0:T(8,128)(2,1)S(1)}, bf16[16,3456]{1,0:T(8,128)(2,1)S(1)}, u32[]{:S(2)}, u32[]{:S(2)}) collective-permute-start(bf16[16,3456]{1,0:T(8,128)(2,1)S(1)} %add_convert_fusion.mine_ref), channel_id=1, source_target_pairs={{0,8},{8,0},{16,24},{24,16},{1,9},{9,1},{17,25},{25,17},{2,10},{10... | collective-permute-start | bytes 331784 | tf_op jit(solution)/shard_map/ppermute | solution.py:234
  35.4 7.9 %collective-permute-start.14 = (bf16[16,1728]{1,0:T(8,128)(2,1)S(1)}, bf16[16,1728]{1,0:T(8,128)(2,1)S(1)}, u32[]{:S(2)}, u32[]{:S(2)}) collective-permute-start(bf16[16,1728]{1,0:T(8,128)(2,1)S(1)} %get-tuple-element.24), channel_id=1, source_target_pairs={{0,24},{8,16},{16,8},{24,0},{1,25},{9,17},{17,9},{25,1},{2,26},{10... | collective-permute-start | bytes 165896 | tf_op jit(solution)/shard_map/ppermute | solution.py:234
  38.3 6.7 %collective-permute-start.13 = (bf16[16,1728]{1,0:T(8,128)(2,1)S(1)}, bf16[16,1728]{1,0:T(8,128)(2,1)S(1)}, u32[]{:S(2)}, u32[]{:S(2)}) collective-permute-start(bf16[16,1728]{1,0:T(8,128)(2,1)S(1)} %get-tuple-element.24), channel_id=1, source_target_pairs={{0,16},{8,24},{16,0},{24,8},{1,17},{9,25},{17,1},{25,9},{2,18},{10... | collective-permute-start | bytes 165896 | tf_op jit(solution)/shard_map/ppermute | solution.py:234
  38.8 6.9 %collective-permute-start.12 = (bf16[16,1728]{1,0:T(8,128)(2,1)S(1)}, bf16[16,1728]{1,0:T(8,128)(2,1)S(1)}, u32[]{:S(2)}, u32[]{:S(2)}) collective-permute-start(bf16[16,1728]{1,0:T(8,128)(2,1)S(1)} %get-tuple-element.24), channel_id=1, source_target_pairs={{0,8},{8,0},{16,24},{24,16},{1,9},{9,1},{17,25},{25,17},{2,10},{10... | collective-permute-start | bytes 165896 | tf_op jit(solution)/shard_map/ppermute | solution.py:234
  39.8 6.5 %collective-permute-start.9 = (bf16[8,2048]{1,0:T(8,128)(2,1)S(1)}, bf16[8,2048]{1,0:T(8,128)(2,1)S(1)}, u32[]{:S(2)}, u32[]{:S(2)}) collective-permute-start(bf16[8,2048]{1,0:T(8,128)(2,1)S(1)} %get-tuple-element.32), channel_id=1, source_target_pairs={{0,2},{1,3},{2,0},{3,1},{4,6},{5,7},{6,4},{7,5},{8,10},{9,11},{10,... | collective-permute-start | bytes 98312 | tf_op jit(solution)/shard_map/ppermute | solution.py:234
  43.3 4.8 %collective-permute-start.11 = (bf16[8,2048]{1,0:T(8,128)(2,1)S(1)}, bf16[8,2048]{1,0:T(8,128)(2,1)S(1)}, u32[]{:S(2)}, u32[]{:S(2)}) collective-permute-start(bf16[8,2048]{1,0:T(8,128)(2,1)S(1)} %get-tuple-element.33), channel_id=1, source_target_pairs={{0,6},{1,7},{2,4},{3,5},{4,2},{5,3},{6,0},{7,1},{8,14},{9,15},{10,... | collective-permute-start | bytes 98312 | tf_op jit(solution)/shard_map/ppermute | solution.py:234
  45.0 3.9 %collective-permute-start.10 = (bf16[8,2048]{1,0:T(8,128)(2,1)S(1)}, bf16[8,2048]{1,0:T(8,128)(2,1)S(1)}, u32[]{:S(2)}, u32[]{:S(2)}) collective-permute-start(bf16[8,2048]{1,0:T(8,128)(2,1)S(1)} %get-tuple-element.34), channel_id=1, source_target_pairs={{0,4},{1,5},{2,6},{3,7},{4,0},{5,1},{6,2},{7,3},{8,12},{9,13},{10,... | collective-permute-start | bytes 98312 | tf_op jit(solution)/shard_map/ppermute | solution.py:234

commit v7 on v3

--- a/solution.py
+++ b/solution.py
@@ -314,13 +314,14 @@
         2 * cells * 27 * 2 * c0 * f1,
         1024 * 1024,
     )(*parts, pre_own, vol_all, w1b)
-    ins = sum_over_chips(keep, swap(give, "mp", 1))
-
-    second_got, grad_first = lax.optimization_barrier((second_got, grad_first))
-    first_got = swap(grad_first, "sample", bits[0])
+    got = swap(give, "mp", 1)
+    ins = sum_over_chips(keep, got)
+
+    second_got, *_ = lax.optimization_barrier((second_got, grad_first))
+    for bit in bits[::-1][:-1]:
+        grad_first = add(grad_first, swap(grad_first, "sample", bit))
+    first_got = swap(grad_first, "sample", bits[::-1][-1])
     for bit in bits[1:]:
-        grad_first = add(grad_first, first_got)
-        first_got = swap(grad_first, "sample", bit)
         grad_second = add(grad_second, second_got)
         second_got = swap(grad_second, "sample", bit)
     grad_first = (grad_first.astype(F32) + first_got.astype(F32)) * scale

time: 47.8 us -> 45.3 us (0.948)
  waiting for transfers between devices: 15.7 us -> 12.5 us
  starting transfers between devices: 19 us -> 19.7 us
    ppermute x16, waiting for transfers between devices: 15.7 us -> 12.5 us  [swap(): return lax.ppermute(value, axis, [(i, i ^ k) for i in range(n)])]
    ppermute x16, starting transfers between devices: 19 us -> 19.7 us  [swap(): return lax.ppermute(value, axis, [(i, i ^ k) for i in range(n)])]
  transfers between devices with their start and end apart: 16 -> 16, of which waited for: 12 -> 11; matrix products, arithmetic and copies ran while one was open for 5% -> 5% of each run, Pallas kernels for 2% -> 2%
where the time goes in v7:
time: 45.3 us; the launch traced here: 45.1 us
  starting transfers between devices  19.7 us (43%)
  waiting for transfers between devices  12.5 us (28%)
  Pallas kernels  6.94 us (15%)
  other arithmetic  3.2 us (7%)
  local copies, waits for them, and re-layouts  2.01 us (4%)
  between operations  0.75 us (2%)
    ppermute x16, starting transfers between devices, swap(): return lax.ppermute(value, axis, [(i, i ^ k) for i in range(n)])  19.7 us
    ppermute x16, waiting for transfers between devices, swap(): return lax.ppermute(value, axis, [(i, i ^ k) for i in range(n)])  12.5 us
    pallas_call x1, Pallas kernels, local(): call(functools.partial(forward_kernel, n_mp, c0), [sds((f2, cells), BF16)...  5.89 us
    unnamed x7, local copies, waits for them, and re-layouts  1.21 us
    pallas_call x1, Pallas kernels, local(): call(functools.partial(backward_kernel, n_mp), [sds((half, rows_in, cells...  1.05 us
  transfers between devices with their start and end apart: 16, of which 11 were waited for; matrix products, arithmetic and copies ran while one was open for 5% of the time, Pallas kernels for 2%

profile of v7, /device:TPU:0, one launch (start us, length us, event | category | flops | bytes accessed | tf_op | source)
XLA Modules:
  0.0 45.1 jit_solution(1109501634303156263)
XLA Ops:
  0.6 0.9 %fusion.14 = (bf16[1,24,2048]{2,1,0:T(8,128)(2,1)S(1)}, bf16[24,2048]{1,0:T(8,128)(2,1)S(1)}) fusion(bf16[8,2048]{1,0:T(8,128)(2,1)} %bitcast.52, bf16[16,1728]{1,0:T(8,128)(2,1)} %param.5), kind=kLoop, calls=%fused_computation.30 | loop fusion | flops 294912 | bytes 284672 | tf_op jit(solution)/shard_map/stack | solution.py:263
  1.5 3.0 %collective-permute-start = (bf16[24,2048]{1,0:T(8,128)(2,1)S(1)}, bf16[24,2048]{1,0:T(8,128)(2,1)S(1)}, u32[]{:S(2)}, u32[]{:S(2)}) collective-permute-start(bf16[24,2048]{1,0:T(8,128)(2,1)S(1)} %get-tuple-element.32), channel_id=1, source_target_pairs={{0,2},{1,3},{2,0},{3,1},{4,6},{5,7},{6,4},{7,5},{8,10},{9,11},{10,... | collective-permute-start | bytes 294920 | tf_op jit(solution)/shard_map/ppermute | solution.py:213
  4.5 1.5 %collective-permute-start.1 = (bf16[24,2048]{1,0:T(8,128)(2,1)S(1)}, bf16[24,2048]{1,0:T(8,128)(2,1)S(1)}, u32[]{:S(2)}, u32[]{:S(2)}) collective-permute-start(bf16[24,2048]{1,0:T(8,128)(2,1)S(1)} %get-tuple-element.32), channel_id=1, source_target_pairs={{0,4},{1,5},{2,6},{3,7},{4,0},{5,1},{6,2},{7,3},{8,12},{9,13},{10,... | collective-permute-start | bytes 294920 | tf_op jit(solution)/shard_map/ppermute | solution.py:213
  6.0 0.0 collective-permute-start.2
  6.0 1.5 %collective-permute-done = bf16[24,2048]{1,0:T(8,128)(2,1)S(1)} collective-permute-done((bf16[24,2048]{1,0:T(8,128)(2,1)S(1)}, bf16[24,2048]{1,0:T(8,128)(2,1)S(1)}, u32[]{:S(2)}, u32[]{:S(2)}) %collective-permute-start) | collective-permute-done | bytes 98336 | tf_op jit(solution)/shard_map/ppermute | solution.py:213
  7.5 2.6 %collective-permute-done.1 = bf16[24,2048]{1,0:T(8,128)(2,1)S(1)} collective-permute-done((bf16[24,2048]{1,0:T(8,128)(2,1)S(1)}, bf16[24,2048]{1,0:T(8,128)(2,1)S(1)}, u32[]{:S(2)}, u32[]{:S(2)}) %collective-permute-start.1) | collective-permute-done | bytes 98336 | tf_op jit(solution)/shard_map/ppermute | solution.py:213
  10.2 1.4 %collective-permute-done.2 = bf16[24,2048]{1,0:T(8,128)(2,1)S(1)} collective-permute-done((bf16[24,2048]{1,0:T(8,128)(2,1)S(1)}, bf16[24,2048]{1,0:T(8,128)(2,1)S(1)}, u32[]{:S(2)}, u32[]{:S(2)}) %collective-permute-start.2) | collective-permute-done | bytes 98336 | tf_op jit(solution)/shard_map/ppermute | solution.py:213
  11.5 0.0 copy-start.2
  11.5 0.1 pad_maximum_fusion.refs_0_
  11.6 0.1 collective-permute-start.3
  11.7 0.8 %copy-done.2 = bf16[32,3456]{1,0:T(8,128)(2,1)S(1)} copy-done((bf16[32,3456]{1,0:T(8,128)(2,1)S(1)}, bf16[32,3456]{1,0:T(8,128)(2,1)}, u32[]{:S(2)}) %copy-start.2) | copy-done | bytes 221208
  12.5 0.1 reshape.70
  12.6 0.1 copy.11
  12.8 0.1 copy.12
  12.8 0.0 copy-start
  12.8 0.2 copy.13.refs_3_
  13.0 0.4 collective-permute-done.3.refs_1_
  13.4 0.4 copy-done
  13.7 5.9 %shard_map.75 = (bf16[32,2048]{1,0:T(8,128)(2,1)}, f32[16,2048]{1,0:T(8,128)S(1)}, bf16[64,2048]{1,0:T(8,128)(2,1)S(1)}, bf16[4,16,2048]{2,1,0:T(8,128)(2,1)S(1)...) custom-call(bf16[4,24,2048]{2,1,0:T(8,128)(2,1)S(1)} %pad_maximum_fusion.refs_0_, ...), custom_call_target="tpu_custom_call" | custom-call | flops 2264924160 | bytes 4194304 | tf_op jit(solution)/shard_map/pallas_call | solution.py:273
  19.6 0.0 collective-permute-start.4
  19.6 2.6 %collective-permute-start.14 = (bf16[32,3456]{1,0:T(8,128)(2,1)S(1)}, bf16[32,3456]{1,0:T(8,128)(2,1)S(1)}, u32[]{:S(2)}, u32[]{:S(2)}) collective-permute-start(bf16[32,3456]{1,0:T(8,128)(2,1)S(1)} %get-tuple-element.22), channel_id=1, source_target_pairs={{0,16},{8,24},{16,0},{24,8},{1,17},{9,25},{17,1},{25,9},{2,18},{10... | collective-permute-start | bytes 663560 | tf_op jit(solution)/shard_map/ppermute | solution.py:213
  22.3 0.0 collective-permute-done.4
  22.3 0.0 copy-start.1
  22.3 0.1 fusion.5
  22.4 0.7 %collective-permute-start.5 = (bf16[16,2048]{1,0:T(8,128)(2,1)S(1)}, bf16[16,2048]{1,0:T(8,128)(2,1)S(1)}, u32[]{:S(2)}, u32[]{:S(2)}) collective-permute-start(bf16[16,2048]{1,0:T(8,128)(2,1)S(1)} %get-tuple-element.26), channel_id=1, source_target_pairs={{0,2},{1,3},{2,0},{3,1},{4,6},{5,7},{6,4},{7,5},{8,10},{9,11},{10,... | collective-permute-start | bytes 196616 | tf_op jit(solution)/shard_map/ppermute | solution.py:213
  23.1 1.0 %collective-permute-start.6 = (bf16[16,2048]{1,0:T(8,128)(2,1)S(1)}, bf16[16,2048]{1,0:T(8,128)(2,1)S(1)}, u32[]{:S(2)}, u32[]{:S(2)}) collective-permute-start(bf16[16,2048]{1,0:T(8,128)(2,1)S(1)} %get-tuple-element.25), channel_id=1, source_target_pairs={{0,4},{1,5},{2,6},{3,7},{4,0},{5,1},{6,2},{7,3},{8,12},{9,13},{10,... | collective-permute-start | bytes 196616 | tf_op jit(solution)/shard_map/ppermute | solution.py:213
  24.0 1.9 %collective-permute-start.7 = (bf16[16,2048]{1,0:T(8,128)(2,1)S(1)}, bf16[16,2048]{1,0:T(8,128)(2,1)S(1)}, u32[]{:S(2)}, u32[]{:S(2)}) collective-permute-start(bf16[16,2048]{1,0:T(8,128)(2,1)S(1)} %get-tuple-element.24), channel_id=1, source_target_pairs={{0,6},{1,7},{2,4},{3,5},{4,2},{5,3},{6,0},{7,1},{8,14},{9,15},{10,... | collective-permute-start | bytes 196616 | tf_op jit(solution)/shard_map/ppermute | solution.py:213
  25.9 0.0 copy-done.1
  25.9 0.2 reshape.75
  26.1 0.1 copy.15.refs_6_
  26.3 0.4 collective-permute-done.5.refs_1_
  26.7 1.3 %collective-permute-done.6.refs_2_ = bf16[16,2048]{1,0:T(8,128)(2,1)S(1)} collective-permute-done((bf16[16,2048]{1,0:T(8,128)(2,1)S(1)}, bf16[16,2048]{1,0:T(8,128)(2,1)S(1)}, u32[]{:S(2)}, u32[]{:S(2)}) %collective-permute-start.6) | collective-permute-done | bytes 65568 | tf_op jit(solution)/shard_map/ppermute | solution.py:213
  28.0 1.2 %collective-permute-done.7.refs_3_ = bf16[16,2048]{1,0:T(8,128)(2,1)S(1)} collective-permute-done((bf16[16,2048]{1,0:T(8,128)(2,1)S(1)}, bf16[16,2048]{1,0:T(8,128)(2,1)S(1)}, u32[]{:S(2)}, u32[]{:S(2)}) %collective-permute-start.7) | collective-permute-done | bytes 65568 | tf_op jit(solution)/shard_map/ppermute | solution.py:213
  29.2 1.1 %shard_map.76 = (bf16[4,8,2048]{2,1,0:T(8,128)(2,1)S(1)}, bf16[4,8,2048]{2,1,0:T(8,128)(2,1)S(1)}, bf16[16,1728]{1,0:T(8,128)(2,1)S(1)}) custom-call(bf16[16,2048]{1,0:T(8,128)(2,1)S(1)} %get-tuple-element.27.refs_0_, bf16[16,2048]{1,0:T(8,128)(2,1)S(1)} %collective-permute-done.5.refs_1_, bf16[16,2048]{1,0:T(8,128)(2,1)S(1)} %collective-permute-done.6.refs_2_, ...), custom_call_target="tpu_custom_call" | custom-call | flops 226492416 | bytes 1048576 | tf_op jit(solution)/shard_map/pallas_call | solution.py:302
  30.2 1.6 %collective-permute-start.12 = (bf16[16,1728]{1,0:T(8,128)(2,1)S(1)}, bf16[16,1728]{1,0:T(8,128)(2,1)S(1)}, u32[]{:S(2)}, u32[]{:S(2)}) collective-permute-start(bf16[16,1728]{1,0:T(8,128)(2,1)S(1)} %get-tuple-element.21), channel_id=1, source_target_pairs={{0,8},{8,0},{16,24},{24,16},{1,9},{9,1},{17,25},{25,17},{2,10},{10... | collective-permute-start | bytes 165896 | tf_op jit(solution)/shard_map/ppermute | solution.py:213
  31.9 1.3 %collective-permute-done.14 = bf16[32,3456]{1,0:T(8,128)(2,1)S(1)} collective-permute-done((bf16[32,3456]{1,0:T(8,128)(2,1)S(1)}, bf16[32,3456]{1,0:T(8,128)(2,1)S(1)}, u32[]{:S(2)}, u32[]{:S(2)}) %collective-permute-start.14) | collective-permute-done | bytes 221216 | tf_op jit(solution)/shard_map/ppermute | solution.py:213
  33.2 0.1 add_convert_fusion
  33.3 0.7 %collective-permute-start.15 = (bf16[32,3456]{1,0:T(8,128)(2,1)S(1)}, bf16[32,3456]{1,0:T(8,128)(2,1)S(1)}, u32[]{:S(2)}, u32[]{:S(2)}) collective-permute-start(bf16[32,3456]{1,0:T(8,128)(2,1)S(1)} %add_convert_fusion), channel_id=1, source_target_pairs={{0,8},{8,0},{16,24},{24,16},{1,9},{9,1},{17,25},{25,17},{2,10},{10... | collective-permute-start | bytes 663560 | tf_op jit(solution)/shard_map/ppermute | solution.py:213
  34.0 0.0 collective-permute-start.8
  34.0 0.5 %collective-permute-done.12 = bf16[16,1728]{1,0:T(8,128)(2,1)S(1)} collective-permute-done((bf16[16,1728]{1,0:T(8,128)(2,1)S(1)}, bf16[16,1728]{1,0:T(8,128)(2,1)S(1)}, u32[]{:S(2)}, u32[]{:S(2)}) %collective-permute-start.12) | collective-permute-done | bytes 55328 | tf_op jit(solution)/shard_map/ppermute | solution.py:213
  34.5 3.0 %collective-permute-start.13 = (bf16[16,1728]{1,0:T(8,128)(2,1)S(1)}, bf16[16,1728]{1,0:T(8,128)(2,1)S(1)}, u32[]{:S(2)}, u32[]{:S(2)}) collective-permute-start(bf16[16,1728]{1,0:T(8,128)(2,1)S(1)} %add_convert_fusion.5), channel_id=1, source_target_pairs={{0,16},{8,24},{16,0},{24,8},{1,17},{9,25},{17,1},{25,9},{2,18},{10... | collective-permute-start | bytes 165896 | tf_op jit(solution)/shard_map/ppermute | solution.py:213
  37.5 0.0 collective-permute-done.8
  37.5 1.0 %collective-permute-start.10 = (bf16[8,2048]{1,0:T(8,128)(2,1)S(1)}, bf16[8,2048]{1,0:T(8,128)(2,1)S(1)}, u32[]{:S(2)}, u32[]{:S(2)}) collective-permute-start(bf16[8,2048]{1,0:T(8,128)(2,1)S(1)} %get-tuple-element.30), channel_id=1, source_target_pairs={{0,4},{1,5},{2,6},{3,7},{4,0},{5,1},{6,2},{7,3},{8,12},{9,13},{10,... | collective-permute-start | bytes 98312 | tf_op jit(solution)/shard_map/ppermute | solution.py:213
  38.5 1.2 %collective-permute-start.11 = (bf16[8,2048]{1,0:T(8,128)(2,1)S(1)}, bf16[8,2048]{1,0:T(8,128)(2,1)S(1)}, u32[]{:S(2)}, u32[]{:S(2)}) collective-permute-start(bf16[8,2048]{1,0:T(8,128)(2,1)S(1)} %get-tuple-element.29), channel_id=1, source_target_pairs={{0,6},{1,7},{2,4},{3,5},{4,2},{5,3},{6,0},{7,1},{8,14},{9,15},{10,... | collective-permute-start | bytes 98312 | tf_op jit(solution)/shard_map/ppermute | solution.py:213
  39.7 1.4 %collective-permute-start.9 = (bf16[8,2048]{1,0:T(8,128)(2,1)S(1)}, bf16[8,2048]{1,0:T(8,128)(2,1)S(1)}, u32[]{:S(2)}, u32[]{:S(2)}) collective-permute-start(bf16[8,2048]{1,0:T(8,128)(2,1)S(1)} %get-tuple-element.28), channel_id=1, source_target_pairs={{0,2},{1,3},{2,0},{3,1},{4,6},{5,7},{6,4},{7,5},{8,10},{9,11},{10,... | collective-permute-start | bytes 98312 | tf_op jit(solution)/shard_map/ppermute | solution.py:213
  41.1 0.0 collective-permute-done.13
  41.1 0.7 %add_multiply_fusion.1 = f32[16,1728]{1,0:T(8,128)} fusion(bf16[16,1728]{1,0:T(8,128)(2,1)S(1)} %collective-permute-done.13, bf16[16,1728]{1,0:T(8,128)(2,1)S(1)} %add_convert_fusion.5), kind=kLoop, calls=%fused_computation.10 | loop fusion | flops 110592 | bytes 221184 | tf_op jit(solution)/shard_map/mul | solution.py:327
  41.8 0.0 collective-permute-done.10
  41.8 1.6 %collective-permute-done.11 = bf16[8,2048]{1,0:T(8,128)(2,1)S(1)} collective-permute-done((bf16[8,2048]{1,0:T(8,128)(2,1)S(1)}, bf16[8,2048]{1,0:T(8,128)(2,1)S(1)}, u32[]{:S(2)}, u32[]{:S(2)}) %collective-permute-start.11) | collective-permute-done | bytes 32800 | tf_op jit(solution)/shard_map/ppermute | solution.py:213
  43.3 0.3 collective-permute-done.9
  43.6 0.6 %fusion.13 = bf16[8,1,2048]{2,0,1:T(8,128)(2,1)} fusion(bf16[8,2048]{1,0:T(8,128)(2,1)S(1)} %collective-permute-done.11, bf16[8,2048]{1,0:T(8,128)(2,1)S(1)} %collective-permute-done.10, bf16[8,2048]{1,0:T(8,128)(2,1)S(1)} %collective-permute-done.9, bf16[4,8,2048]{2,1,0:T(8,128)(2,1)S(1)} %collective-permute-done.8, ...), kind=kLoop, calls=%fused_computation.29 | loop fusion | flops 196608 | bytes 196608 | tf_op jit(solution)/shard_map/reshape | solution.py:334
  44.3 0.0 collective-permute-done.15
  44.3 0.8 %add_multiply_fusion = f32[32,3456]{1,0:T(8,128)} fusion(bf16[32,3456]{1,0:T(8,128)(2,1)S(1)} %collective-permute-done.15, bf16[32,3456]{1,0:T(8,128)(2,1)S(1)} %add_convert_fusion), kind=kLoop, calls=%fused_computation | loop fusion | flops 442368 | bytes 884736 | tf_op jit(solution)/shard_map/mul | solution.py:328
  (4 shorter events, 0.1 us)
Async XLA Ops:
  1.5 6.1 %collective-permute-start = (bf16[24,2048]{1,0:T(8,128)(2,1)S(1)}, bf16[24,2048]{1,0:T(8,128)(2,1)S(1)}, u32[]{:S(2)}, u32[]{:S(2)}) collective-permute-start(bf16[24,2048]{1,0:T(8,128)(2,1)S(1)} %get-tuple-element.32), channel_id=1, source_target_pairs={{0,2},{1,3},{2,0},{3,1},{4,6},{5,7},{6,4},{7,5},{8,10},{9,11},{10,... | collective-permute-start | bytes 294920 | tf_op jit(solution)/shard_map/ppermute | solution.py:213
  4.5 5.7 %collective-permute-start.1 = (bf16[24,2048]{1,0:T(8,128)(2,1)S(1)}, bf16[24,2048]{1,0:T(8,128)(2,1)S(1)}, u32[]{:S(2)}, u32[]{:S(2)}) collective-permute-start(bf16[24,2048]{1,0:T(8,128)(2,1)S(1)} %get-tuple-element.32), channel_id=1, source_target_pairs={{0,4},{1,5},{2,6},{3,7},{4,0},{5,1},{6,2},{7,3},{8,12},{9,13},{10,... | collective-permute-start | bytes 294920 | tf_op jit(solution)/shard_map/ppermute | solution.py:213
  6.0 5.5 %collective-permute-start.2 = (bf16[24,2048]{1,0:T(8,128)(2,1)S(1)}, bf16[24,2048]{1,0:T(8,128)(2,1)S(1)}, u32[]{:S(2)}, u32[]{:S(2)}) collective-permute-start(bf16[24,2048]{1,0:T(8,128)(2,1)S(1)} %get-tuple-element.32), channel_id=1, source_target_pairs={{0,6},{1,7},{2,4},{3,5},{4,2},{5,3},{6,0},{7,1},{8,14},{9,15},{10,... | collective-permute-start | bytes 294920 | tf_op jit(solution)/shard_map/ppermute | solution.py:213
  11.5 0.9 %copy-start.2 = (bf16[32,3456]{1,0:T(8,128)(2,1)S(1)}, bf16[32,3456]{1,0:T(8,128)(2,1)}, u32[]{:S(2)}) copy-start(bf16[32,3456]{1,0:T(8,128)(2,1)} %param.6) | copy-start | bytes 663556
  11.6 1.8 %collective-permute-start.3 = (bf16[4,24,2048]{2,1,0:T(8,128)(2,1)S(1)}, bf16[4,24,2048]{2,1,0:T(8,128)(2,1)S(1)}, u32[]{:S(2)}, u32[]{:S(2)}) collective-permute-start(bf16[4,24,2048]{2,1,0:T(8,128)(2,1)S(1)} %pad_maximum_fusion.refs_0_), channel_id=1, source_target_pairs={{0,1},{1,0},{2,3},{3,2},{4,5},{5,4},{6,7},{7,6},{8,9},{9,8},{10,11... | collective-permute-start | bytes 1179656 | tf_op jit(solution)/shard_map/ppermute | solution.py:213
  12.8 0.9 %copy-start = (bf16[32,1,2048]{2,0,1:T(8,128)(2,1)S(1)}, bf16[32,1,2048]{2,0,1:T(8,128)(2,1)}, u32[]{:S(2)}) copy-start(bf16[32,1,2048]{2,0,1:T(8,128)(2,1)} %param.7) | copy-start | bytes 393220
  19.6 2.7 %collective-permute-start.4 = (bf16[4,16,2048]{2,1,0:T(8,128)(2,1)S(1)}, bf16[4,16,2048]{2,1,0:T(8,128)(2,1)S(1)}, u32[]{:S(2)}, u32[]{:S(2)}) collective-permute-start(bf16[4,16,2048]{2,1,0:T(8,128)(2,1)S(1)} %get-tuple-element.16), channel_id=1, source_target_pairs={{0,1},{1,0},{2,3},{3,2},{4,5},{5,4},{6,7},{7,6},{8,9},{9,8},{10,11... | collective-permute-start | bytes 786440 | tf_op jit(solution)/shard_map/ppermute | solution.py:213
  19.6 13.6 %collective-permute-start.14 = (bf16[32,3456]{1,0:T(8,128)(2,1)S(1)}, bf16[32,3456]{1,0:T(8,128)(2,1)S(1)}, u32[]{:S(2)}, u32[]{:S(2)}) collective-permute-start(bf16[32,3456]{1,0:T(8,128)(2,1)S(1)} %get-tuple-element.22), channel_id=1, source_target_pairs={{0,16},{8,24},{16,0},{24,8},{1,17},{9,25},{17,1},{25,9},{2,18},{10... | collective-permute-start | bytes 663560 | tf_op jit(solution)/shard_map/ppermute | solution.py:213
  22.3 3.6 %copy-start.1 = (bf16[16,1728]{1,0:T(8,128)(2,1)S(1)}, bf16[16,1728]{1,0:T(8,128)(2,1)}, u32[]{:S(2)}) copy-start(bf16[16,1728]{1,0:T(8,128)(2,1)} %param.5) | copy-start | bytes 165892
  22.4 4.3 %collective-permute-start.5 = (bf16[16,2048]{1,0:T(8,128)(2,1)S(1)}, bf16[16,2048]{1,0:T(8,128)(2,1)S(1)}, u32[]{:S(2)}, u32[]{:S(2)}) collective-permute-start(bf16[16,2048]{1,0:T(8,128)(2,1)S(1)} %get-tuple-element.26), channel_id=1, source_target_pairs={{0,2},{1,3},{2,0},{3,1},{4,6},{5,7},{6,4},{7,5},{8,10},{9,11},{10,... | collective-permute-start | bytes 196616 | tf_op jit(solution)/shard_map/ppermute | solution.py:213
  23.1 5.0 %collective-permute-start.6 = (bf16[16,2048]{1,0:T(8,128)(2,1)S(1)}, bf16[16,2048]{1,0:T(8,128)(2,1)S(1)}, u32[]{:S(2)}, u32[]{:S(2)}) collective-permute-start(bf16[16,2048]{1,0:T(8,128)(2,1)S(1)} %get-tuple-element.25), channel_id=1, source_target_pairs={{0,4},{1,5},{2,6},{3,7},{4,0},{5,1},{6,2},{7,3},{8,12},{9,13},{10,... | collective-permute-start | bytes 196616 | tf_op jit(solution)/shard_map/ppermute | solution.py:213
  24.0 5.2 %collective-permute-start.7 = (bf16[16,2048]{1,0:T(8,128)(2,1)S(1)}, bf16[16,2048]{1,0:T(8,128)(2,1)S(1)}, u32[]{:S(2)}, u32[]{:S(2)}) collective-permute-start(bf16[16,2048]{1,0:T(8,128)(2,1)S(1)} %get-tuple-element.24), channel_id=1, source_target_pairs={{0,6},{1,7},{2,4},{3,5},{4,2},{5,3},{6,0},{7,1},{8,14},{9,15},{10,... | collective-permute-start | bytes 196616 | tf_op jit(solution)/shard_map/ppermute | solution.py:213
  30.2 4.2 %collective-permute-start.12 = (bf16[16,1728]{1,0:T(8,128)(2,1)S(1)}, bf16[16,1728]{1,0:T(8,128)(2,1)S(1)}, u32[]{:S(2)}, u32[]{:S(2)}) collective-permute-start(bf16[16,1728]{1,0:T(8,128)(2,1)S(1)} %get-tuple-element.21), channel_id=1, source_target_pairs={{0,8},{8,0},{16,24},{24,16},{1,9},{9,1},{17,25},{25,17},{2,10},{10... | collective-permute-start | bytes 165896 | tf_op jit(solution)/shard_map/ppermute | solution.py:213
  33.3 11.0 %collective-permute-start.15 = (bf16[32,3456]{1,0:T(8,128)(2,1)S(1)}, bf16[32,3456]{1,0:T(8,128)(2,1)S(1)}, u32[]{:S(2)}, u32[]{:S(2)}) collective-permute-start(bf16[32,3456]{1,0:T(8,128)(2,1)S(1)} %add_convert_fusion), channel_id=1, source_target_pairs={{0,8},{8,0},{16,24},{24,16},{1,9},{9,1},{17,25},{25,17},{2,10},{10... | collective-permute-start | bytes 663560 | tf_op jit(solution)/shard_map/ppermute | solution.py:213
  34.0 3.5 %collective-permute-start.8 = (bf16[4,8,2048]{2,1,0:T(8,128)(2,1)S(1)}, bf16[4,8,2048]{2,1,0:T(8,128)(2,1)S(1)}, u32[]{:S(2)}, u32[]{:S(2)}) collective-permute-start(bf16[4,8,2048]{2,1,0:T(8,128)(2,1)S(1)} %get-tuple-element.20), channel_id=1, source_target_pairs={{0,1},{1,0},{2,3},{3,2},{4,5},{5,4},{6,7},{7,6},{8,9},{9,8},{10,11... | collective-permute-start | bytes 393224 | tf_op jit(solution)/shard_map/ppermute | solution.py:213
  34.5 6.6 %collective-permute-start.13 = (bf16[16,1728]{1,0:T(8,128)(2,1)S(1)}, bf16[16,1728]{1,0:T(8,128)(2,1)S(1)}, u32[]{:S(2)}, u32[]{:S(2)}) collective-permute-start(bf16[16,1728]{1,0:T(8,128)(2,1)S(1)} %add_convert_fusion.5), channel_id=1, source_target_pairs={{0,16},{8,24},{16,0},{24,8},{1,17},{9,25},{17,1},{25,9},{2,18},{10... | collective-permute-start | bytes 165896 | tf_op jit(solution)/shard_map/ppermute | solution.py:213
  37.5 4.2 %collective-permute-start.10 = (bf16[8,2048]{1,0:T(8,128)(2,1)S(1)}, bf16[8,2048]{1,0:T(8,128)(2,1)S(1)}, u32[]{:S(2)}, u32[]{:S(2)}) collective-permute-start(bf16[8,2048]{1,0:T(8,128)(2,1)S(1)} %get-tuple-element.30), channel_id=1, source_target_pairs={{0,4},{1,5},{2,6},{3,7},{4,0},{5,1},{6,2},{7,3},{8,12},{9,13},{10,... | collective-permute-start | bytes 98312 | tf_op jit(solution)/shard_map/ppermute | solution.py:213
  38.5 4.8 %collective-permute-start.11 = (bf16[8,2048]{1,0:T(8,128)(2,1)S(1)}, bf16[8,2048]{1,0:T(8,128)(2,1)S(1)}, u32[]{:S(2)}, u32[]{:S(2)}) collective-permute-start(bf16[8,2048]{1,0:T(8,128)(2,1)S(1)} %get-tuple-element.29), channel_id=1, source_target_pairs={{0,6},{1,7},{2,4},{3,5},{4,2},{5,3},{6,0},{7,1},{8,14},{9,15},{10,... | collective-permute-start | bytes 98312 | tf_op jit(solution)/shard_map/ppermute | solution.py:213
  39.7 3.9 %collective-permute-start.9 = (bf16[8,2048]{1,0:T(8,128)(2,1)S(1)}, bf16[8,2048]{1,0:T(8,128)(2,1)S(1)}, u32[]{:S(2)}, u32[]{:S(2)}) collective-permute-start(bf16[8,2048]{1,0:T(8,128)(2,1)S(1)} %get-tuple-element.28), channel_id=1, source_target_pairs={{0,2},{1,3},{2,0},{3,1},{4,6},{5,7},{6,4},{7,5},{8,10},{9,11},{10,... | collective-permute-start | bytes 98312 | tf_op jit(solution)/shard_map/ppermute | solution.py:213

commit v8 on v7

--- a/solution.py
+++ b/solution.py
@@ -61,7 +61,7 @@
 
 
 def chunk_of(cells):
-    return 2 * PLANE if cells % (2 * PLANE) == 0 else PLANE
+    return PLANE
 
 
 def forward_kernel(n_mp, c0, *refs):
@@ -208,6 +208,19 @@
         grad_ref[:, t * c0 : t * c0 + width] = merged[:, :width].astype(BF16)
 
 
+def finish_kernel(scale, count, *refs):
+    ins = refs[:count]
+    first_ref, first_got_ref, second_ref, second_got_ref, feat_in_ref = refs[count : count + 5]
+    feat_ref, input_ref, first_out_ref, second_out_ref = refs[count + 5 :]
+    second_out_ref[...] = (second_ref[...].astype(F32) + second_got_ref[...].astype(F32)) * scale
+    feat_ref[...] = feat_in_ref[...]
+    first_out_ref[...] = (first_ref[...].astype(F32) + first_got_ref[...].astype(F32)) * scale
+    total = ins[0][...].astype(F32)
+    for other in ins[1:]:
+        total = total + other[...].astype(F32)
+    input_ref[...] = total.astype(BF16)
+
+
 def swap(value, axis, k):
     n = lax.axis_size(axis)
     return lax.ppermute(value, axis, [(i, i ^ k) for i in range(n)])
@@ -324,14 +337,21 @@
     for bit in bits[1:]:
         grad_second = add(grad_second, second_got)
         second_got = swap(grad_second, "sample", bit)
-    grad_first = (grad_first.astype(F32) + first_got.astype(F32)) * scale
-    grad_second = (grad_second.astype(F32) + second_got.astype(F32)) * scale
-    total = ins[0].astype(F32)
-    for other in ins[1:]:
-        total = total + other.astype(F32)
+    features, input_grad, grad_first, grad_second = call(
+        functools.partial(finish_kernel, scale, half),
+        [
+            sds((f2, cells), BF16),
+            sds((rows_in, cells), BF16),
+            sds((f1, 27 * c0), F32),
+            sds((f2, 27 * c1), F32),
+        ],
+        [],
+        0,
+        2 * 1024 * 1024,
+    )(*ins, grad_first, first_got, grad_second, second_got, features)
     return (
         features.reshape(f2, 1, cells),
-        total.astype(BF16).reshape(rows_in, 1, cells),
+        input_grad.reshape(rows_in, 1, cells),
         grad_first,
         grad_second,
     )

time: 45.3 us -> 45.9 us (1.013)
  other arithmetic: 3.2 us -> 1.08 us
  Pallas kernels: 6.94 us -> 8.8 us
  waiting for transfers between devices: 12.5 us -> 13.1 us
    mul x2 -> x0, other arithmetic: 1.49 us -> none  [the longest x1 0.82 us: local(): grad_second = (grad_second.astype(F32) + second_got.astype(F32)) * scale]
    pallas_call x1, Pallas kernels: 5.89 us -> 6.94 us  [local(): call(functools.partial(forward_kernel, n_mp, c0), [sds((f2, cells), BF16)...]
    pallas_call x0 -> x1, Pallas kernels: none -> 0.88 us  [local(): call(functools.partial(finish_kernel, scale, half), [sds((f2, cells), BF1...]
    ppermute x16, waiting for transfers between devices: 12.5 us -> 13.1 us  [swap(): return lax.ppermute(value, axis, [(i, i ^ k) for i in range(n)])]
    reshape x1 -> x0, other arithmetic: 0.64 us -> none  [local(): total.astype(BF16).reshape(rows_in, 1, cells)]
  transfers between devices with their start and end apart: 16 -> 16, of which waited for: 11 -> 12; matrix products, arithmetic and copies ran while one was open for 5% -> 2% of each run, Pallas kernels for 2% -> 2%
where the time goes in v8:
time: 45.9 us; the launch traced here: 45.6 us
  starting transfers between devices  19.9 us (43%)
  waiting for transfers between devices  13.1 us (29%)
  Pallas kernels  8.8 us (19%)
  local copies, waits for them, and re-layouts  2.01 us (4%)
  other arithmetic  1.08 us (2%)
  between operations  0.76 us (2%)
    ppermute x16, starting transfers between devices, swap(): return lax.ppermute(value, axis, [(i, i ^ k) for i in range(n)])  19.9 us
    ppermute x16, waiting for transfers between devices, swap(): return lax.ppermute(value, axis, [(i, i ^ k) for i in range(n)])  13.1 us
    pallas_call x1, Pallas kernels, local(): call(functools.partial(forward_kernel, n_mp, c0), [sds((f2, cells), BF16)...  6.94 us
    unnamed x7, local copies, waits for them, and re-layouts  1.21 us
    pallas_call x1, Pallas kernels, local(): call(functools.partial(backward_kernel, n_mp), [sds((half, rows_in, cells...  0.98 us
  transfers between devices with their start and end apart: 16, of which 12 were waited for; matrix products, arithmetic and copies ran while one was open for 2% of the time, Pallas kernels for 2%

profile of v8, /device:TPU:0, one launch (start us, length us, event | category | flops | bytes accessed | tf_op | source)
XLA Modules:
  0.0 45.6 jit_solution(5754214863075054237)
XLA Ops:
  0.6 0.9 %fusion.10 = (bf16[1,24,2048]{2,1,0:T(8,128)(2,1)S(1)}, bf16[24,2048]{1,0:T(8,128)(2,1)S(1)}) fusion(bf16[8,2048]{1,0:T(8,128)(2,1)} %bitcast.46, bf16[16,1728]{1,0:T(8,128)(2,1)} %param.5), kind=kLoop, calls=%fused_computation.23 | loop fusion | flops 294912 | bytes 284672 | tf_op jit(solution)/shard_map/stack | solution.py:276
  1.5 3.0 %collective-permute-start = (bf16[24,2048]{1,0:T(8,128)(2,1)S(1)}, bf16[24,2048]{1,0:T(8,128)(2,1)S(1)}, u32[]{:S(2)}, u32[]{:S(2)}) collective-permute-start(bf16[24,2048]{1,0:T(8,128)(2,1)S(1)} %get-tuple-element.41), channel_id=1, source_target_pairs={{0,2},{1,3},{2,0},{3,1},{4,6},{5,7},{6,4},{7,5},{8,10},{9,11},{10,... | collective-permute-start | bytes 294920 | tf_op jit(solution)/shard_map/ppermute | solution.py:226
  4.5 1.5 %collective-permute-start.1 = (bf16[24,2048]{1,0:T(8,128)(2,1)S(1)}, bf16[24,2048]{1,0:T(8,128)(2,1)S(1)}, u32[]{:S(2)}, u32[]{:S(2)}) collective-permute-start(bf16[24,2048]{1,0:T(8,128)(2,1)S(1)} %get-tuple-element.41), channel_id=1, source_target_pairs={{0,4},{1,5},{2,6},{3,7},{4,0},{5,1},{6,2},{7,3},{8,12},{9,13},{10,... | collective-permute-start | bytes 294920 | tf_op jit(solution)/shard_map/ppermute | solution.py:226
  6.0 0.0 collective-permute-start.2
  6.0 1.5 %collective-permute-done = bf16[24,2048]{1,0:T(8,128)(2,1)S(1)} collective-permute-done((bf16[24,2048]{1,0:T(8,128)(2,1)S(1)}, bf16[24,2048]{1,0:T(8,128)(2,1)S(1)}, u32[]{:S(2)}, u32[]{:S(2)}) %collective-permute-start) | collective-permute-done | bytes 98336 | tf_op jit(solution)/shard_map/ppermute | solution.py:226
  7.5 2.6 %collective-permute-done.1 = bf16[24,2048]{1,0:T(8,128)(2,1)S(1)} collective-permute-done((bf16[24,2048]{1,0:T(8,128)(2,1)S(1)}, bf16[24,2048]{1,0:T(8,128)(2,1)S(1)}, u32[]{:S(2)}, u32[]{:S(2)}) %collective-permute-start.1) | collective-permute-done | bytes 98336 | tf_op jit(solution)/shard_map/ppermute | solution.py:226
  10.2 1.4 %collective-permute-done.2 = bf16[24,2048]{1,0:T(8,128)(2,1)S(1)} collective-permute-done((bf16[24,2048]{1,0:T(8,128)(2,1)S(1)}, bf16[24,2048]{1,0:T(8,128)(2,1)S(1)}, u32[]{:S(2)}, u32[]{:S(2)}) %collective-permute-start.2) | collective-permute-done | bytes 98336 | tf_op jit(solution)/shard_map/ppermute | solution.py:226
  11.5 0.0 copy-start.2
  11.5 0.1 pad_maximum_fusion.refs_0_
  11.6 0.1 collective-permute-start.3
  11.7 0.8 %copy-done.2 = bf16[32,3456]{1,0:T(8,128)(2,1)S(1)} copy-done((bf16[32,3456]{1,0:T(8,128)(2,1)S(1)}, bf16[32,3456]{1,0:T(8,128)(2,1)}, u32[]{:S(2)}) %copy-start.2) | copy-done | bytes 221208
  12.5 0.1 reshape.68
  12.6 0.1 copy.11
  12.8 0.1 copy.12
  12.8 0.0 copy-start
  12.8 0.2 copy.13.refs_3_
  13.0 0.4 collective-permute-done.3.refs_1_
  13.4 0.4 copy-done
  13.7 6.9 %shard_map.75 = (bf16[32,2048]{1,0:T(8,128)(2,1)S(1)}, f32[16,2048]{1,0:T(8,128)S(1)}, bf16[64,2048]{1,0:T(8,128)(2,1)S(1)}, bf16[4,16,2048]{2,1,0:T(8,128)(2,1)...) custom-call(bf16[4,24,2048]{2,1,0:T(8,128)(2,1)S(1)} %pad_maximum_fusion.refs_0_, ...), custom_call_target="tpu_custom_call" | custom-call | flops 2264924160 | bytes 4194304 | tf_op jit(solution)/shard_map/pallas_call | solution.py:286
  20.7 0.1 collective-permute-start.4
  20.8 2.7 %collective-permute-start.14 = (bf16[32,3456]{1,0:T(8,128)(2,1)S(1)}, bf16[32,3456]{1,0:T(8,128)(2,1)S(1)}, u32[]{:S(2)}, u32[]{:S(2)}) collective-permute-start(bf16[32,3456]{1,0:T(8,128)(2,1)S(1)} %get-tuple-element.25), channel_id=1, source_target_pairs={{0,16},{8,24},{16,0},{24,8},{1,17},{9,25},{17,1},{25,9},{2,18},{10... | collective-permute-start | bytes 663560 | tf_op jit(solution)/shard_map/ppermute | solution.py:226
  23.4 0.0 collective-permute-done.4
  23.4 0.0 copy-start.1
  23.4 0.1 fusion.5
  23.5 0.7 %collective-permute-start.5 = (bf16[16,2048]{1,0:T(8,128)(2,1)S(1)}, bf16[16,2048]{1,0:T(8,128)(2,1)S(1)}, u32[]{:S(2)}, u32[]{:S(2)}) collective-permute-start(bf16[16,2048]{1,0:T(8,128)(2,1)S(1)} %get-tuple-element.34), channel_id=1, source_target_pairs={{0,2},{1,3},{2,0},{3,1},{4,6},{5,7},{6,4},{7,5},{8,10},{9,11},{10,... | collective-permute-start | bytes 196616 | tf_op jit(solution)/shard_map/ppermute | solution.py:226
  24.2 1.0 %collective-permute-start.6 = (bf16[16,2048]{1,0:T(8,128)(2,1)S(1)}, bf16[16,2048]{1,0:T(8,128)(2,1)S(1)}, u32[]{:S(2)}, u32[]{:S(2)}) collective-permute-start(bf16[16,2048]{1,0:T(8,128)(2,1)S(1)} %get-tuple-element.33), channel_id=1, source_target_pairs={{0,4},{1,5},{2,6},{3,7},{4,0},{5,1},{6,2},{7,3},{8,12},{9,13},{10,... | collective-permute-start | bytes 196616 | tf_op jit(solution)/shard_map/ppermute | solution.py:226
  25.2 1.9 %collective-permute-start.7 = (bf16[16,2048]{1,0:T(8,128)(2,1)S(1)}, bf16[16,2048]{1,0:T(8,128)(2,1)S(1)}, u32[]{:S(2)}, u32[]{:S(2)}) collective-permute-start(bf16[16,2048]{1,0:T(8,128)(2,1)S(1)} %get-tuple-element.32), channel_id=1, source_target_pairs={{0,6},{1,7},{2,4},{3,5},{4,2},{5,3},{6,0},{7,1},{8,14},{9,15},{10,... | collective-permute-start | bytes 196616 | tf_op jit(solution)/shard_map/ppermute | solution.py:226
  27.1 0.0 copy-done.1
  27.1 0.2 reshape.72
  27.3 0.1 copy.15.refs_6_
  27.4 0.4 collective-permute-done.5.refs_1_
  27.8 1.3 %collective-permute-done.6.refs_2_ = bf16[16,2048]{1,0:T(8,128)(2,1)S(1)} collective-permute-done((bf16[16,2048]{1,0:T(8,128)(2,1)S(1)}, bf16[16,2048]{1,0:T(8,128)(2,1)S(1)}, u32[]{:S(2)}, u32[]{:S(2)}) %collective-permute-start.6) | collective-permute-done | bytes 65568 | tf_op jit(solution)/shard_map/ppermute | solution.py:226
  29.2 1.2 %collective-permute-done.7.refs_3_ = bf16[16,2048]{1,0:T(8,128)(2,1)S(1)} collective-permute-done((bf16[16,2048]{1,0:T(8,128)(2,1)S(1)}, bf16[16,2048]{1,0:T(8,128)(2,1)S(1)}, u32[]{:S(2)}, u32[]{:S(2)}) %collective-permute-start.7) | collective-permute-done | bytes 65568 | tf_op jit(solution)/shard_map/ppermute | solution.py:226
  30.3 1.0 %shard_map.76 = (bf16[4,8,2048]{2,1,0:T(8,128)(2,1)S(1)}, bf16[4,8,2048]{2,1,0:T(8,128)(2,1)S(1)}, bf16[16,1728]{1,0:T(8,128)(2,1)S(1)}) custom-call(bf16[16,2048]{1,0:T(8,128)(2,1)S(1)} %get-tuple-element.35.refs_0_, bf16[16,2048]{1,0:T(8,128)(2,1)S(1)} %collective-permute-done.5.refs_1_, bf16[16,2048]{1,0:T(8,128)(2,1)S(1)} %collective-permute-done.6.refs_2_, ...), custom_call_target="tpu_custom_call" | custom-call | flops 226492416 | bytes 1048576 | tf_op jit(solution)/shard_map/pallas_call | solution.py:315
  31.3 1.6 %collective-permute-start.12 = (bf16[16,1728]{1,0:T(8,128)(2,1)S(1)}, bf16[16,1728]{1,0:T(8,128)(2,1)S(1)}, u32[]{:S(2)}, u32[]{:S(2)}) collective-permute-start(bf16[16,1728]{1,0:T(8,128)(2,1)S(1)} %get-tuple-element.24), channel_id=1, source_target_pairs={{0,8},{8,0},{16,24},{24,16},{1,9},{9,1},{17,25},{25,17},{2,10},{10... | collective-permute-start | bytes 165896 | tf_op jit(solution)/shard_map/ppermute | solution.py:226
  33.0 1.4 %collective-permute-done.14 = bf16[32,3456]{1,0:T(8,128)(2,1)S(1)} collective-permute-done((bf16[32,3456]{1,0:T(8,128)(2,1)S(1)}, bf16[32,3456]{1,0:T(8,128)(2,1)S(1)}, u32[]{:S(2)}, u32[]{:S(2)}) %collective-permute-start.14) | collective-permute-done | bytes 221216 | tf_op jit(solution)/shard_map/ppermute | solution.py:226
  34.4 0.1 add_convert_fusion.refs_6_
  34.4 0.7 %collective-permute-start.15 = (bf16[32,3456]{1,0:T(8,128)(2,1)S(1)}, bf16[32,3456]{1,0:T(8,128)(2,1)S(1)}, u32[]{:S(2)}, u32[]{:S(2)}) collective-permute-start(bf16[32,3456]{1,0:T(8,128)(2,1)S(1)} %add_convert_fusion.refs_6_), channel_id=1, source_target_pairs={{0,8},{8,0},{16,24},{24,16},{1,9},{9,1},{17,25},{25,17},{2,10},{10... | collective-permute-start | bytes 663560 | tf_op jit(solution)/shard_map/ppermute | solution.py:226
  35.1 0.0 collective-permute-start.8
  35.1 0.4 collective-permute-done.12
  35.6 3.1 %collective-permute-start.13 = (bf16[16,1728]{1,0:T(8,128)(2,1)S(1)}, bf16[16,1728]{1,0:T(8,128)(2,1)S(1)}, u32[]{:S(2)}, u32[]{:S(2)}) collective-permute-start(bf16[16,1728]{1,0:T(8,128)(2,1)S(1)} %add_convert_fusion.5.refs_4_), channel_id=1, source_target_pairs={{0,16},{8,24},{16,0},{24,8},{1,17},{9,25},{17,1},{25,9},{2,18},{10... | collective-permute-start | bytes 165896 | tf_op jit(solution)/shard_map/ppermute | solution.py:226
  38.6 0.0 collective-permute-done.8
  38.7 1.0 %collective-permute-start.10 = (bf16[8,2048]{1,0:T(8,128)(2,1)S(1)}, bf16[8,2048]{1,0:T(8,128)(2,1)S(1)}, u32[]{:S(2)}, u32[]{:S(2)}) collective-permute-start(bf16[8,2048]{1,0:T(8,128)(2,1)S(1)} %get-tuple-element.37), channel_id=1, source_target_pairs={{0,4},{1,5},{2,6},{3,7},{4,0},{5,1},{6,2},{7,3},{8,12},{9,13},{10,... | collective-permute-start | bytes 98312 | tf_op jit(solution)/shard_map/ppermute | solution.py:226
  39.7 1.2 %collective-permute-start.11 = (bf16[8,2048]{1,0:T(8,128)(2,1)S(1)}, bf16[8,2048]{1,0:T(8,128)(2,1)S(1)}, u32[]{:S(2)}, u32[]{:S(2)}) collective-permute-start(bf16[8,2048]{1,0:T(8,128)(2,1)S(1)} %get-tuple-element.36), channel_id=1, source_target_pairs={{0,6},{1,7},{2,4},{3,5},{4,2},{5,3},{6,0},{7,1},{8,14},{9,15},{10,... | collective-permute-start | bytes 98312 | tf_op jit(solution)/shard_map/ppermute | solution.py:226
  40.8 1.4 %collective-permute-start.9 = (bf16[8,2048]{1,0:T(8,128)(2,1)S(1)}, bf16[8,2048]{1,0:T(8,128)(2,1)S(1)}, u32[]{:S(2)}, u32[]{:S(2)}) collective-permute-start(bf16[8,2048]{1,0:T(8,128)(2,1)S(1)} %get-tuple-element.38), channel_id=1, source_target_pairs={{0,2},{1,3},{2,0},{3,1},{4,6},{5,7},{6,4},{7,5},{8,10},{9,11},{10,... | collective-permute-start | bytes 98312 | tf_op jit(solution)/shard_map/ppermute | solution.py:226
  42.2 0.0 collective-permute-done.13.refs_5_
  42.2 0.4 collective-permute-done.10.refs_2_
  42.7 1.8 %collective-permute-done.11.refs_3_ = bf16[8,2048]{1,0:T(8,128)(2,1)S(1)} collective-permute-done((bf16[8,2048]{1,0:T(8,128)(2,1)S(1)}, bf16[8,2048]{1,0:T(8,128)(2,1)S(1)}, u32[]{:S(2)}, u32[]{:S(2)}) %collective-permute-start.11) | collective-permute-done | bytes 32800 | tf_op jit(solution)/shard_map/ppermute | solution.py:226
  44.5 0.3 collective-permute-done.9.refs_1_
  44.8 0.0 collective-permute-done.15.refs_7_
  44.8 0.9 %shard_map.77 = (bf16[32,2048]{1,0:T(8,128)(2,1)}, bf16[8,2048]{1,0:T(8,128)(2,1)}, f32[16,1728]{1,0:T(8,128)}, f32[32,3456]{1,0:T(8,128)}) custom-call(bf16[8,2048]{1,0:T(8,128)(2,1)S(1)} %get-tuple-element.39.refs_0_, bf16[8,2048]{1,0:T(8,128)(2,1)S(1)} %collective-permute-done.9.refs_1_, bf16[8,2048]{1,0:T(8,128)(2,1)S(1)} %collective-permute-done.10.refs_2_, ...), custom_call_target="tpu_custom_call" | custom-call | bytes 2097152 | tf_op jit(solution)/shard_map/pallas_call | solution.py:340
  (4 shorter events, 0.1 us)
Async XLA Ops:
  1.5 6.1 %collective-permute-start = (bf16[24,2048]{1,0:T(8,128)(2,1)S(1)}, bf16[24,2048]{1,0:T(8,128)(2,1)S(1)}, u32[]{:S(2)}, u32[]{:S(2)}) collective-permute-start(bf16[24,2048]{1,0:T(8,128)(2,1)S(1)} %get-tuple-element.41), channel_id=1, source_target_pairs={{0,2},{1,3},{2,0},{3,1},{4,6},{5,7},{6,4},{7,5},{8,10},{9,11},{10,... | collective-permute-start | bytes 294920 | tf_op jit(solution)/shard_map/ppermute | solution.py:226
  4.5 5.7 %collective-permute-start.1 = (bf16[24,2048]{1,0:T(8,128)(2,1)S(1)}, bf16[24,2048]{1,0:T(8,128)(2,1)S(1)}, u32[]{:S(2)}, u32[]{:S(2)}) collective-permute-start(bf16[24,2048]{1,0:T(8,128)(2,1)S(1)} %get-tuple-element.41), channel_id=1, source_target_pairs={{0,4},{1,5},{2,6},{3,7},{4,0},{5,1},{6,2},{7,3},{8,12},{9,13},{10,... | collective-permute-start | bytes 294920 | tf_op jit(solution)/shard_map/ppermute | solution.py:226
  6.0 5.5 %collective-permute-start.2 = (bf16[24,2048]{1,0:T(8,128)(2,1)S(1)}, bf16[24,2048]{1,0:T(8,128)(2,1)S(1)}, u32[]{:S(2)}, u32[]{:S(2)}) collective-permute-start(bf16[24,2048]{1,0:T(8,128)(2,1)S(1)} %get-tuple-element.41), channel_id=1, source_target_pairs={{0,6},{1,7},{2,4},{3,5},{4,2},{5,3},{6,0},{7,1},{8,14},{9,15},{10,... | collective-permute-start | bytes 294920 | tf_op jit(solution)/shard_map/ppermute | solution.py:226
  11.5 0.9 %copy-start.2 = (bf16[32,3456]{1,0:T(8,128)(2,1)S(1)}, bf16[32,3456]{1,0:T(8,128)(2,1)}, u32[]{:S(2)}) copy-start(bf16[32,3456]{1,0:T(8,128)(2,1)} %param.6) | copy-start | bytes 663556
  11.6 1.8 %collective-permute-start.3 = (bf16[4,24,2048]{2,1,0:T(8,128)(2,1)S(1)}, bf16[4,24,2048]{2,1,0:T(8,128)(2,1)S(1)}, u32[]{:S(2)}, u32[]{:S(2)}) collective-permute-start(bf16[4,24,2048]{2,1,0:T(8,128)(2,1)S(1)} %pad_maximum_fusion.refs_0_), channel_id=1, source_target_pairs={{0,1},{1,0},{2,3},{3,2},{4,5},{5,4},{6,7},{7,6},{8,9},{9,8},{10,11... | collective-permute-start | bytes 1179656 | tf_op jit(solution)/shard_map/ppermute | solution.py:226
  12.8 0.9 %copy-start = (bf16[32,1,2048]{2,0,1:T(8,128)(2,1)S(1)}, bf16[32,1,2048]{2,0,1:T(8,128)(2,1)}, u32[]{:S(2)}) copy-start(bf16[32,1,2048]{2,0,1:T(8,128)(2,1)} %param.7) | copy-start | bytes 393220
  20.7 2.7 %collective-permute-start.4 = (bf16[4,16,2048]{2,1,0:T(8,128)(2,1)S(1)}, bf16[4,16,2048]{2,1,0:T(8,128)(2,1)S(1)}, u32[]{:S(2)}, u32[]{:S(2)}) collective-permute-start(bf16[4,16,2048]{2,1,0:T(8,128)(2,1)S(1)} %get-tuple-element.19), channel_id=1, source_target_pairs={{0,1},{1,0},{2,3},{3,2},{4,5},{5,4},{6,7},{7,6},{8,9},{9,8},{10,11... | collective-permute-start | bytes 786440 | tf_op jit(solution)/shard_map/ppermute | solution.py:226
  20.8 13.6 %collective-permute-start.14 = (bf16[32,3456]{1,0:T(8,128)(2,1)S(1)}, bf16[32,3456]{1,0:T(8,128)(2,1)S(1)}, u32[]{:S(2)}, u32[]{:S(2)}) collective-permute-start(bf16[32,3456]{1,0:T(8,128)(2,1)S(1)} %get-tuple-element.25), channel_id=1, source_target_pairs={{0,16},{8,24},{16,0},{24,8},{1,17},{9,25},{17,1},{25,9},{2,18},{10... | collective-permute-start | bytes 663560 | tf_op jit(solution)/shard_map/ppermute | solution.py:226
  23.4 3.6 %copy-start.1 = (bf16[16,1728]{1,0:T(8,128)(2,1)S(1)}, bf16[16,1728]{1,0:T(8,128)(2,1)}, u32[]{:S(2)}) copy-start(bf16[16,1728]{1,0:T(8,128)(2,1)} %param.5) | copy-start | bytes 165892
  23.5 4.3 %collective-permute-start.5 = (bf16[16,2048]{1,0:T(8,128)(2,1)S(1)}, bf16[16,2048]{1,0:T(8,128)(2,1)S(1)}, u32[]{:S(2)}, u32[]{:S(2)}) collective-permute-start(bf16[16,2048]{1,0:T(8,128)(2,1)S(1)} %get-tuple-element.34), channel_id=1, source_target_pairs={{0,2},{1,3},{2,0},{3,1},{4,6},{5,7},{6,4},{7,5},{8,10},{9,11},{10,... | collective-permute-start | bytes 196616 | tf_op jit(solution)/shard_map/ppermute | solution.py:226
  24.2 5.0 %collective-permute-start.6 = (bf16[16,2048]{1,0:T(8,128)(2,1)S(1)}, bf16[16,2048]{1,0:T(8,128)(2,1)S(1)}, u32[]{:S(2)}, u32[]{:S(2)}) collective-permute-start(bf16[16,2048]{1,0:T(8,128)(2,1)S(1)} %get-tuple-element.33), channel_id=1, source_target_pairs={{0,4},{1,5},{2,6},{3,7},{4,0},{5,1},{6,2},{7,3},{8,12},{9,13},{10,... | collective-permute-start | bytes 196616 | tf_op jit(solution)/shard_map/ppermute | solution.py:226
  25.2 5.2 %collective-permute-start.7 = (bf16[16,2048]{1,0:T(8,128)(2,1)S(1)}, bf16[16,2048]{1,0:T(8,128)(2,1)S(1)}, u32[]{:S(2)}, u32[]{:S(2)}) collective-permute-start(bf16[16,2048]{1,0:T(8,128)(2,1)S(1)} %get-tuple-element.32), channel_id=1, source_target_pairs={{0,6},{1,7},{2,4},{3,5},{4,2},{5,3},{6,0},{7,1},{8,14},{9,15},{10,... | collective-permute-start | bytes 196616 | tf_op jit(solution)/shard_map/ppermute | solution.py:226
  31.3 4.2 %collective-permute-start.12 = (bf16[16,1728]{1,0:T(8,128)(2,1)S(1)}, bf16[16,1728]{1,0:T(8,128)(2,1)S(1)}, u32[]{:S(2)}, u32[]{:S(2)}) collective-permute-start(bf16[16,1728]{1,0:T(8,128)(2,1)S(1)} %get-tuple-element.24), channel_id=1, source_target_pairs={{0,8},{8,0},{16,24},{24,16},{1,9},{9,1},{17,25},{25,17},{2,10},{10... | collective-permute-start | bytes 165896 | tf_op jit(solution)/shard_map/ppermute | solution.py:226
  34.4 10.3 %collective-permute-start.15 = (bf16[32,3456]{1,0:T(8,128)(2,1)S(1)}, bf16[32,3456]{1,0:T(8,128)(2,1)S(1)}, u32[]{:S(2)}, u32[]{:S(2)}) collective-permute-start(bf16[32,3456]{1,0:T(8,128)(2,1)S(1)} %add_convert_fusion.refs_6_), channel_id=1, source_target_pairs={{0,8},{8,0},{16,24},{24,16},{1,9},{9,1},{17,25},{25,17},{2,10},{10... | collective-permute-start | bytes 663560 | tf_op jit(solution)/shard_map/ppermute | solution.py:226
  35.1 3.5 %collective-permute-start.8 = (bf16[4,8,2048]{2,1,0:T(8,128)(2,1)S(1)}, bf16[4,8,2048]{2,1,0:T(8,128)(2,1)S(1)}, u32[]{:S(2)}, u32[]{:S(2)}) collective-permute-start(bf16[4,8,2048]{2,1,0:T(8,128)(2,1)S(1)} %get-tuple-element.23), channel_id=1, source_target_pairs={{0,1},{1,0},{2,3},{3,2},{4,5},{5,4},{6,7},{7,6},{8,9},{9,8},{10,11... | collective-permute-start | bytes 393224 | tf_op jit(solution)/shard_map/ppermute | solution.py:226
  35.6 6.7 %collective-permute-start.13 = (bf16[16,1728]{1,0:T(8,128)(2,1)S(1)}, bf16[16,1728]{1,0:T(8,128)(2,1)S(1)}, u32[]{:S(2)}, u32[]{:S(2)}) collective-permute-start(bf16[16,1728]{1,0:T(8,128)(2,1)S(1)} %add_convert_fusion.5.refs_4_), channel_id=1, source_target_pairs={{0,16},{8,24},{16,0},{24,8},{1,17},{9,25},{17,1},{25,9},{2,18},{10... | collective-permute-start | bytes 165896 | tf_op jit(solution)/shard_map/ppermute | solution.py:226
  38.7 4.0 %collective-permute-start.10 = (bf16[8,2048]{1,0:T(8,128)(2,1)S(1)}, bf16[8,2048]{1,0:T(8,128)(2,1)S(1)}, u32[]{:S(2)}, u32[]{:S(2)}) collective-permute-start(bf16[8,2048]{1,0:T(8,128)(2,1)S(1)} %get-tuple-element.37), channel_id=1, source_target_pairs={{0,4},{1,5},{2,6},{3,7},{4,0},{5,1},{6,2},{7,3},{8,12},{9,13},{10,... | collective-permute-start | bytes 98312 | tf_op jit(solution)/shard_map/ppermute | solution.py:226
  39.7 4.8 %collective-permute-start.11 = (bf16[8,2048]{1,0:T(8,128)(2,1)S(1)}, bf16[8,2048]{1,0:T(8,128)(2,1)S(1)}, u32[]{:S(2)}, u32[]{:S(2)}) collective-permute-start(bf16[8,2048]{1,0:T(8,128)(2,1)S(1)} %get-tuple-element.36), channel_id=1, source_target_pairs={{0,6},{1,7},{2,4},{3,5},{4,2},{5,3},{6,0},{7,1},{8,14},{9,15},{10,... | collective-permute-start | bytes 98312 | tf_op jit(solution)/shard_map/ppermute | solution.py:226
  40.8 3.9 %collective-permute-start.9 = (bf16[8,2048]{1,0:T(8,128)(2,1)S(1)}, bf16[8,2048]{1,0:T(8,128)(2,1)S(1)}, u32[]{:S(2)}, u32[]{:S(2)}) collective-permute-start(bf16[8,2048]{1,0:T(8,128)(2,1)S(1)} %get-tuple-element.38), channel_id=1, source_target_pairs={{0,2},{1,3},{2,0},{3,1},{4,6},{5,7},{6,4},{7,5},{8,10},{9,11},{10,... | collective-permute-start | bytes 98312 | tf_op jit(solution)/shard_map/ppermute | solution.py:226

commit v9 on v8

--- a/solution.py
+++ b/solution.py
@@ -60,8 +60,10 @@
     return lax.dot_general(a, b, (((1,), (1,)), ((), ())), preferred_element_type=F32)
 
 
-def chunk_of(cells):
-    return PLANE
+def chunk_of(cells, planes):
+    while cells % (planes * PLANE):
+        planes //= 2
+    return planes * PLANE
 
 
 def forward_kernel(n_mp, c0, *refs):
@@ -73,7 +75,7 @@
     f1 = w1s.shape[1]
     c1 = n_mp * f1
     f2, cells = cot_ref.shape
-    chunk = chunk_of(cells)
+    chunk = chunk_of(cells, 4)
     steps = cells // chunk
     pitch = pitch_of(c0)
     grid_xy = lane_grid(chunk)
@@ -163,7 +165,7 @@
     me = lax.axis_index("mp")
     f1, cells = pre_ref.shape
     c0 = vol_ref.shape[0]
-    chunk = chunk_of(cells)
+    chunk = chunk_of(cells, 1)
     steps = cells // chunk
     grid_xy = lane_grid(chunk)
 

time: 45.9 us -> 43 us (0.937)
  Pallas kernels: 8.8 us -> 5.89 us
    pallas_call x1, Pallas kernels: 6.94 us -> 4.03 us  [local(): call(functools.partial(forward_kernel, n_mp, c0), [sds((f2, cells), BF16)...]
where the time goes in v9:
time: 43 us; the launch traced here: 42.7 us
  starting transfers between devices  19.8 us (46%)
  waiting for transfers between devices  13.2 us (31%)
  Pallas kernels  5.89 us (14%)
  local copies, waits for them, and re-layouts  2.01 us (5%)
  other arithmetic  1.08 us (3%)
  between operations  0.76 us (2%)
    ppermute x16, starting transfers between devices, swap(): return lax.ppermute(value, axis, [(i, i ^ k) for i in range(n)])  19.8 us
    ppermute x16, waiting for transfers between devices, swap(): return lax.ppermute(value, axis, [(i, i ^ k) for i in range(n)])  13.2 us
    pallas_call x1, Pallas kernels, local(): call(functools.partial(forward_kernel, n_mp, c0), [sds((f2, cells), BF16)...  4.03 us
    unnamed x7, local copies, waits for them, and re-layouts  1.21 us
    pallas_call x1, Pallas kernels, local(): call(functools.partial(backward_kernel, n_mp), [sds((half, rows_in, cells...  0.98 us
    another operation x2, other arithmetic, local(): near = jnp.stack(near)  0.91 us
    pallas_call x1, Pallas kernels, local(): call(functools.partial(finish_kernel, scale, half), [sds((f2, cells), BF1...  0.88 us
  transfers between devices with their start and end apart: 16, of which 12 were waited for; matrix products, arithmetic and copies ran while one was open for 2% of the time, Pallas kernels for 2%

profile of v9, /device:TPU:0, one launch (start us, length us, event | category | flops | bytes accessed | tf_op | source)
XLA Modules:
  0.0 42.7 jit_solution(16655900709771069527)
XLA Ops:
  0.6 0.9 %fusion.10 = (bf16[1,24,2048]{2,1,0:T(8,128)(2,1)S(1)}, bf16[24,2048]{1,0:T(8,128)(2,1)S(1)}) fusion(bf16[8,2048]{1,0:T(8,128)(2,1)} %bitcast.46, bf16[16,1728]{1,0:T(8,128)(2,1)} %param.5), kind=kLoop, calls=%fused_computation.23 | loop fusion | flops 294912 | bytes 284672 | tf_op jit(solution)/shard_map/stack | solution.py:278
  1.5 3.0 %collective-permute-start = (bf16[24,2048]{1,0:T(8,128)(2,1)S(1)}, bf16[24,2048]{1,0:T(8,128)(2,1)S(1)}, u32[]{:S(2)}, u32[]{:S(2)}) collective-permute-start(bf16[24,2048]{1,0:T(8,128)(2,1)S(1)} %get-tuple-element.41), channel_id=1, source_target_pairs={{0,2},{1,3},{2,0},{3,1},{4,6},{5,7},{6,4},{7,5},{8,10},{9,11},{10,... | collective-permute-start | bytes 294920 | tf_op jit(solution)/shard_map/ppermute | solution.py:228
  4.5 1.5 %collective-permute-start.1 = (bf16[24,2048]{1,0:T(8,128)(2,1)S(1)}, bf16[24,2048]{1,0:T(8,128)(2,1)S(1)}, u32[]{:S(2)}, u32[]{:S(2)}) collective-permute-start(bf16[24,2048]{1,0:T(8,128)(2,1)S(1)} %get-tuple-element.41), channel_id=1, source_target_pairs={{0,4},{1,5},{2,6},{3,7},{4,0},{5,1},{6,2},{7,3},{8,12},{9,13},{10,... | collective-permute-start | bytes 294920 | tf_op jit(solution)/shard_map/ppermute | solution.py:228
  6.0 0.0 collective-permute-start.2
  6.0 1.5 %collective-permute-done = bf16[24,2048]{1,0:T(8,128)(2,1)S(1)} collective-permute-done((bf16[24,2048]{1,0:T(8,128)(2,1)S(1)}, bf16[24,2048]{1,0:T(8,128)(2,1)S(1)}, u32[]{:S(2)}, u32[]{:S(2)}) %collective-permute-start) | collective-permute-done | bytes 98336 | tf_op jit(solution)/shard_map/ppermute | solution.py:228
  7.5 2.6 %collective-permute-done.1 = bf16[24,2048]{1,0:T(8,128)(2,1)S(1)} collective-permute-done((bf16[24,2048]{1,0:T(8,128)(2,1)S(1)}, bf16[24,2048]{1,0:T(8,128)(2,1)S(1)}, u32[]{:S(2)}, u32[]{:S(2)}) %collective-permute-start.1) | collective-permute-done | bytes 98336 | tf_op jit(solution)/shard_map/ppermute | solution.py:228
  10.2 1.4 %collective-permute-done.2 = bf16[24,2048]{1,0:T(8,128)(2,1)S(1)} collective-permute-done((bf16[24,2048]{1,0:T(8,128)(2,1)S(1)}, bf16[24,2048]{1,0:T(8,128)(2,1)S(1)}, u32[]{:S(2)}, u32[]{:S(2)}) %collective-permute-start.2) | collective-permute-done | bytes 98336 | tf_op jit(solution)/shard_map/ppermute | solution.py:228
  11.5 0.0 copy-start.2
  11.5 0.1 pad_maximum_fusion.refs_0_
  11.6 0.1 collective-permute-start.3
  11.7 0.8 %copy-done.2 = bf16[32,3456]{1,0:T(8,128)(2,1)S(1)} copy-done((bf16[32,3456]{1,0:T(8,128)(2,1)S(1)}, bf16[32,3456]{1,0:T(8,128)(2,1)}, u32[]{:S(2)}) %copy-start.2) | copy-done | bytes 221208
  12.5 0.1 reshape.68
  12.6 0.1 copy.11
  12.8 0.1 copy.12
  12.8 0.0 copy-start
  12.8 0.2 copy.13.refs_3_
  13.0 0.4 collective-permute-done.3.refs_1_
  13.4 0.4 copy-done
  13.7 4.0 %shard_map.75 = (bf16[32,2048]{1,0:T(8,128)(2,1)S(1)}, f32[16,2048]{1,0:T(8,128)S(1)}, bf16[64,2048]{1,0:T(8,128)(2,1)S(1)}, bf16[4,16,2048]{2,1,0:T(8,128)(2,1)...) custom-call(bf16[4,24,2048]{2,1,0:T(8,128)(2,1)S(1)} %pad_maximum_fusion.refs_0_, ...), custom_call_target="tpu_custom_call" | custom-call | flops 2264924160 | bytes 4194304 | tf_op jit(solution)/shard_map/pallas_call | solution.py:288
  17.8 0.1 collective-permute-start.4
  17.9 2.7 %collective-permute-start.14 = (bf16[32,3456]{1,0:T(8,128)(2,1)S(1)}, bf16[32,3456]{1,0:T(8,128)(2,1)S(1)}, u32[]{:S(2)}, u32[]{:S(2)}) collective-permute-start(bf16[32,3456]{1,0:T(8,128)(2,1)S(1)} %get-tuple-element.25), channel_id=1, source_target_pairs={{0,16},{8,24},{16,0},{24,8},{1,17},{9,25},{17,1},{25,9},{2,18},{10... | collective-permute-start | bytes 663560 | tf_op jit(solution)/shard_map/ppermute | solution.py:228
  20.5 0.0 collective-permute-done.4
  20.5 0.0 copy-start.1
  20.5 0.1 fusion.5
  20.6 0.7 %collective-permute-start.5 = (bf16[16,2048]{1,0:T(8,128)(2,1)S(1)}, bf16[16,2048]{1,0:T(8,128)(2,1)S(1)}, u32[]{:S(2)}, u32[]{:S(2)}) collective-permute-start(bf16[16,2048]{1,0:T(8,128)(2,1)S(1)} %get-tuple-element.34), channel_id=1, source_target_pairs={{0,2},{1,3},{2,0},{3,1},{4,6},{5,7},{6,4},{7,5},{8,10},{9,11},{10,... | collective-permute-start | bytes 196616 | tf_op jit(solution)/shard_map/ppermute | solution.py:228
  21.3 1.0 %collective-permute-start.6 = (bf16[16,2048]{1,0:T(8,128)(2,1)S(1)}, bf16[16,2048]{1,0:T(8,128)(2,1)S(1)}, u32[]{:S(2)}, u32[]{:S(2)}) collective-permute-start(bf16[16,2048]{1,0:T(8,128)(2,1)S(1)} %get-tuple-element.33), channel_id=1, source_target_pairs={{0,4},{1,5},{2,6},{3,7},{4,0},{5,1},{6,2},{7,3},{8,12},{9,13},{10,... | collective-permute-start | bytes 196616 | tf_op jit(solution)/shard_map/ppermute | solution.py:228
  22.3 1.9 %collective-permute-start.7 = (bf16[16,2048]{1,0:T(8,128)(2,1)S(1)}, bf16[16,2048]{1,0:T(8,128)(2,1)S(1)}, u32[]{:S(2)}, u32[]{:S(2)}) collective-permute-start(bf16[16,2048]{1,0:T(8,128)(2,1)S(1)} %get-tuple-element.32), channel_id=1, source_target_pairs={{0,6},{1,7},{2,4},{3,5},{4,2},{5,3},{6,0},{7,1},{8,14},{9,15},{10,... | collective-permute-start | bytes 196616 | tf_op jit(solution)/shard_map/ppermute | solution.py:228
  24.1 0.0 copy-done.1
  24.1 0.2 reshape.72
  24.4 0.1 copy.15.refs_6_
  24.5 0.4 %collective-permute-done.5.refs_1_ = bf16[16,2048]{1,0:T(8,128)(2,1)S(1)} collective-permute-done((bf16[16,2048]{1,0:T(8,128)(2,1)S(1)}, bf16[16,2048]{1,0:T(8,128)(2,1)S(1)}, u32[]{:S(2)}, u32[]{:S(2)}) %collective-permute-start.5) | collective-permute-done | bytes 65568 | tf_op jit(solution)/shard_map/ppermute | solution.py:228
  24.9 1.4 %collective-permute-done.6.refs_2_ = bf16[16,2048]{1,0:T(8,128)(2,1)S(1)} collective-permute-done((bf16[16,2048]{1,0:T(8,128)(2,1)S(1)}, bf16[16,2048]{1,0:T(8,128)(2,1)S(1)}, u32[]{:S(2)}, u32[]{:S(2)}) %collective-permute-start.6) | collective-permute-done | bytes 65568 | tf_op jit(solution)/shard_map/ppermute | solution.py:228
  26.3 1.2 %collective-permute-done.7.refs_3_ = bf16[16,2048]{1,0:T(8,128)(2,1)S(1)} collective-permute-done((bf16[16,2048]{1,0:T(8,128)(2,1)S(1)}, bf16[16,2048]{1,0:T(8,128)(2,1)S(1)}, u32[]{:S(2)}, u32[]{:S(2)}) %collective-permute-start.7) | collective-permute-done | bytes 65568 | tf_op jit(solution)/shard_map/ppermute | solution.py:228
  27.4 1.0 %shard_map.76 = (bf16[4,8,2048]{2,1,0:T(8,128)(2,1)S(1)}, bf16[4,8,2048]{2,1,0:T(8,128)(2,1)S(1)}, bf16[16,1728]{1,0:T(8,128)(2,1)S(1)}) custom-call(bf16[16,2048]{1,0:T(8,128)(2,1)S(1)} %get-tuple-element.35.refs_0_, bf16[16,2048]{1,0:T(8,128)(2,1)S(1)} %collective-permute-done.5.refs_1_, bf16[16,2048]{1,0:T(8,128)(2,1)S(1)} %collective-permute-done.6.refs_2_, ...), custom_call_target="tpu_custom_call" | custom-call | flops 226492416 | bytes 1048576 | tf_op jit(solution)/shard_map/pallas_call | solution.py:317
  28.4 1.6 %collective-permute-start.12 = (bf16[16,1728]{1,0:T(8,128)(2,1)S(1)}, bf16[16,1728]{1,0:T(8,128)(2,1)S(1)}, u32[]{:S(2)}, u32[]{:S(2)}) collective-permute-start(bf16[16,1728]{1,0:T(8,128)(2,1)S(1)} %get-tuple-element.24), channel_id=1, source_target_pairs={{0,8},{8,0},{16,24},{24,16},{1,9},{9,1},{17,25},{25,17},{2,10},{10... | collective-permute-start | bytes 165896 | tf_op jit(solution)/shard_map/ppermute | solution.py:228
  30.0 1.4 %collective-permute-done.14 = bf16[32,3456]{1,0:T(8,128)(2,1)S(1)} collective-permute-done((bf16[32,3456]{1,0:T(8,128)(2,1)S(1)}, bf16[32,3456]{1,0:T(8,128)(2,1)S(1)}, u32[]{:S(2)}, u32[]{:S(2)}) %collective-permute-start.14) | collective-permute-done | bytes 221216 | tf_op jit(solution)/shard_map/ppermute | solution.py:228
  31.5 0.1 add_convert_fusion.refs_6_
  31.5 0.7 %collective-permute-start.15 = (bf16[32,3456]{1,0:T(8,128)(2,1)S(1)}, bf16[32,3456]{1,0:T(8,128)(2,1)S(1)}, u32[]{:S(2)}, u32[]{:S(2)}) collective-permute-start(bf16[32,3456]{1,0:T(8,128)(2,1)S(1)} %add_convert_fusion.refs_6_), channel_id=1, source_target_pairs={{0,8},{8,0},{16,24},{24,16},{1,9},{9,1},{17,25},{25,17},{2,10},{10... | collective-permute-start | bytes 663560 | tf_op jit(solution)/shard_map/ppermute | solution.py:228
  32.2 0.0 collective-permute-start.8
  32.2 0.4 %collective-permute-done.12 = bf16[16,1728]{1,0:T(8,128)(2,1)S(1)} collective-permute-done((bf16[16,1728]{1,0:T(8,128)(2,1)S(1)}, bf16[16,1728]{1,0:T(8,128)(2,1)S(1)}, u32[]{:S(2)}, u32[]{:S(2)}) %collective-permute-start.12) | collective-permute-done | bytes 55328 | tf_op jit(solution)/shard_map/ppermute | solution.py:228
  32.7 3.0 %collective-permute-start.13 = (bf16[16,1728]{1,0:T(8,128)(2,1)S(1)}, bf16[16,1728]{1,0:T(8,128)(2,1)S(1)}, u32[]{:S(2)}, u32[]{:S(2)}) collective-permute-start(bf16[16,1728]{1,0:T(8,128)(2,1)S(1)} %add_convert_fusion.5.refs_4_), channel_id=1, source_target_pairs={{0,16},{8,24},{16,0},{24,8},{1,17},{9,25},{17,1},{25,9},{2,18},{10... | collective-permute-start | bytes 165896 | tf_op jit(solution)/shard_map/ppermute | solution.py:228
  35.7 0.0 collective-permute-done.8
  35.8 1.0 %collective-permute-start.10 = (bf16[8,2048]{1,0:T(8,128)(2,1)S(1)}, bf16[8,2048]{1,0:T(8,128)(2,1)S(1)}, u32[]{:S(2)}, u32[]{:S(2)}) collective-permute-start(bf16[8,2048]{1,0:T(8,128)(2,1)S(1)} %get-tuple-element.37), channel_id=1, source_target_pairs={{0,4},{1,5},{2,6},{3,7},{4,0},{5,1},{6,2},{7,3},{8,12},{9,13},{10,... | collective-permute-start | bytes 98312 | tf_op jit(solution)/shard_map/ppermute | solution.py:228
  36.8 1.2 %collective-permute-start.11 = (bf16[8,2048]{1,0:T(8,128)(2,1)S(1)}, bf16[8,2048]{1,0:T(8,128)(2,1)S(1)}, u32[]{:S(2)}, u32[]{:S(2)}) collective-permute-start(bf16[8,2048]{1,0:T(8,128)(2,1)S(1)} %get-tuple-element.36), channel_id=1, source_target_pairs={{0,6},{1,7},{2,4},{3,5},{4,2},{5,3},{6,0},{7,1},{8,14},{9,15},{10,... | collective-permute-start | bytes 98312 | tf_op jit(solution)/shard_map/ppermute | solution.py:228
  37.9 1.4 %collective-permute-start.9 = (bf16[8,2048]{1,0:T(8,128)(2,1)S(1)}, bf16[8,2048]{1,0:T(8,128)(2,1)S(1)}, u32[]{:S(2)}, u32[]{:S(2)}) collective-permute-start(bf16[8,2048]{1,0:T(8,128)(2,1)S(1)} %get-tuple-element.38), channel_id=1, source_target_pairs={{0,2},{1,3},{2,0},{3,1},{4,6},{5,7},{6,4},{7,5},{8,10},{9,11},{10,... | collective-permute-start | bytes 98312 | tf_op jit(solution)/shard_map/ppermute | solution.py:228
  39.3 0.0 collective-permute-done.13.refs_5_
  39.3 0.4 collective-permute-done.10.refs_2_
  39.7 1.8 %collective-permute-done.11.refs_3_ = bf16[8,2048]{1,0:T(8,128)(2,1)S(1)} collective-permute-done((bf16[8,2048]{1,0:T(8,128)(2,1)S(1)}, bf16[8,2048]{1,0:T(8,128)(2,1)S(1)}, u32[]{:S(2)}, u32[]{:S(2)}) %collective-permute-start.11) | collective-permute-done | bytes 32800 | tf_op jit(solution)/shard_map/ppermute | solution.py:228
  41.6 0.3 collective-permute-done.9.refs_1_
  41.9 0.0 collective-permute-done.15.refs_7_
  41.9 0.9 %shard_map.77 = (bf16[32,2048]{1,0:T(8,128)(2,1)}, bf16[8,2048]{1,0:T(8,128)(2,1)}, f32[16,1728]{1,0:T(8,128)}, f32[32,3456]{1,0:T(8,128)}) custom-call(bf16[8,2048]{1,0:T(8,128)(2,1)S(1)} %get-tuple-element.39.refs_0_, bf16[8,2048]{1,0:T(8,128)(2,1)S(1)} %collective-permute-done.9.refs_1_, bf16[8,2048]{1,0:T(8,128)(2,1)S(1)} %collective-permute-done.10.refs_2_, ...), custom_call_target="tpu_custom_call" | custom-call | bytes 2097152 | tf_op jit(solution)/shard_map/pallas_call | solution.py:342
  (4 shorter events, 0.1 us)
Async XLA Ops:
  1.5 6.1 %collective-permute-start = (bf16[24,2048]{1,0:T(8,128)(2,1)S(1)}, bf16[24,2048]{1,0:T(8,128)(2,1)S(1)}, u32[]{:S(2)}, u32[]{:S(2)}) collective-permute-start(bf16[24,2048]{1,0:T(8,128)(2,1)S(1)} %get-tuple-element.41), channel_id=1, source_target_pairs={{0,2},{1,3},{2,0},{3,1},{4,6},{5,7},{6,4},{7,5},{8,10},{9,11},{10,... | collective-permute-start | bytes 294920 | tf_op jit(solution)/shard_map/ppermute | solution.py:228
  4.5 5.7 %collective-permute-start.1 = (bf16[24,2048]{1,0:T(8,128)(2,1)S(1)}, bf16[24,2048]{1,0:T(8,128)(2,1)S(1)}, u32[]{:S(2)}, u32[]{:S(2)}) collective-permute-start(bf16[24,2048]{1,0:T(8,128)(2,1)S(1)} %get-tuple-element.41), channel_id=1, source_target_pairs={{0,4},{1,5},{2,6},{3,7},{4,0},{5,1},{6,2},{7,3},{8,12},{9,13},{10,... | collective-permute-start | bytes 294920 | tf_op jit(solution)/shard_map/ppermute | solution.py:228
  6.0 5.5 %collective-permute-start.2 = (bf16[24,2048]{1,0:T(8,128)(2,1)S(1)}, bf16[24,2048]{1,0:T(8,128)(2,1)S(1)}, u32[]{:S(2)}, u32[]{:S(2)}) collective-permute-start(bf16[24,2048]{1,0:T(8,128)(2,1)S(1)} %get-tuple-element.41), channel_id=1, source_target_pairs={{0,6},{1,7},{2,4},{3,5},{4,2},{5,3},{6,0},{7,1},{8,14},{9,15},{10,... | collective-permute-start | bytes 294920 | tf_op jit(solution)/shard_map/ppermute | solution.py:228
  11.5 0.9 %copy-start.2 = (bf16[32,3456]{1,0:T(8,128)(2,1)S(1)}, bf16[32,3456]{1,0:T(8,128)(2,1)}, u32[]{:S(2)}) copy-start(bf16[32,3456]{1,0:T(8,128)(2,1)} %param.6) | copy-start | bytes 663556
  11.6 1.8 %collective-permute-start.3 = (bf16[4,24,2048]{2,1,0:T(8,128)(2,1)S(1)}, bf16[4,24,2048]{2,1,0:T(8,128)(2,1)S(1)}, u32[]{:S(2)}, u32[]{:S(2)}) collective-permute-start(bf16[4,24,2048]{2,1,0:T(8,128)(2,1)S(1)} %pad_maximum_fusion.refs_0_), channel_id=1, source_target_pairs={{0,1},{1,0},{2,3},{3,2},{4,5},{5,4},{6,7},{7,6},{8,9},{9,8},{10,11... | collective-permute-start | bytes 1179656 | tf_op jit(solution)/shard_map/ppermute | solution.py:228
  12.8 0.9 %copy-start = (bf16[32,1,2048]{2,0,1:T(8,128)(2,1)S(1)}, bf16[32,1,2048]{2,0,1:T(8,128)(2,1)}, u32[]{:S(2)}) copy-start(bf16[32,1,2048]{2,0,1:T(8,128)(2,1)} %param.7) | copy-start | bytes 393220
  17.8 2.7 %collective-permute-start.4 = (bf16[4,16,2048]{2,1,0:T(8,128)(2,1)S(1)}, bf16[4,16,2048]{2,1,0:T(8,128)(2,1)S(1)}, u32[]{:S(2)}, u32[]{:S(2)}) collective-permute-start(bf16[4,16,2048]{2,1,0:T(8,128)(2,1)S(1)} %get-tuple-element.19), channel_id=1, source_target_pairs={{0,1},{1,0},{2,3},{3,2},{4,5},{5,4},{6,7},{7,6},{8,9},{9,8},{10,11... | collective-permute-start | bytes 786440 | tf_op jit(solution)/shard_map/ppermute | solution.py:228
  17.9 13.6 %collective-permute-start.14 = (bf16[32,3456]{1,0:T(8,128)(2,1)S(1)}, bf16[32,3456]{1,0:T(8,128)(2,1)S(1)}, u32[]{:S(2)}, u32[]{:S(2)}) collective-permute-start(bf16[32,3456]{1,0:T(8,128)(2,1)S(1)} %get-tuple-element.25), channel_id=1, source_target_pairs={{0,16},{8,24},{16,0},{24,8},{1,17},{9,25},{17,1},{25,9},{2,18},{10... | collective-permute-start | bytes 663560 | tf_op jit(solution)/shard_map/ppermute | solution.py:228
  20.5 3.6 %copy-start.1 = (bf16[16,1728]{1,0:T(8,128)(2,1)S(1)}, bf16[16,1728]{1,0:T(8,128)(2,1)}, u32[]{:S(2)}) copy-start(bf16[16,1728]{1,0:T(8,128)(2,1)} %param.5) | copy-start | bytes 165892
  20.6 4.3 %collective-permute-start.5 = (bf16[16,2048]{1,0:T(8,128)(2,1)S(1)}, bf16[16,2048]{1,0:T(8,128)(2,1)S(1)}, u32[]{:S(2)}, u32[]{:S(2)}) collective-permute-start(bf16[16,2048]{1,0:T(8,128)(2,1)S(1)} %get-tuple-element.34), channel_id=1, source_target_pairs={{0,2},{1,3},{2,0},{3,1},{4,6},{5,7},{6,4},{7,5},{8,10},{9,11},{10,... | collective-permute-start | bytes 196616 | tf_op jit(solution)/shard_map/ppermute | solution.py:228
  21.3 5.0 %collective-permute-start.6 = (bf16[16,2048]{1,0:T(8,128)(2,1)S(1)}, bf16[16,2048]{1,0:T(8,128)(2,1)S(1)}, u32[]{:S(2)}, u32[]{:S(2)}) collective-permute-start(bf16[16,2048]{1,0:T(8,128)(2,1)S(1)} %get-tuple-element.33), channel_id=1, source_target_pairs={{0,4},{1,5},{2,6},{3,7},{4,0},{5,1},{6,2},{7,3},{8,12},{9,13},{10,... | collective-permute-start | bytes 196616 | tf_op jit(solution)/shard_map/ppermute | solution.py:228
  22.3 5.2 %collective-permute-start.7 = (bf16[16,2048]{1,0:T(8,128)(2,1)S(1)}, bf16[16,2048]{1,0:T(8,128)(2,1)S(1)}, u32[]{:S(2)}, u32[]{:S(2)}) collective-permute-start(bf16[16,2048]{1,0:T(8,128)(2,1)S(1)} %get-tuple-element.32), channel_id=1, source_target_pairs={{0,6},{1,7},{2,4},{3,5},{4,2},{5,3},{6,0},{7,1},{8,14},{9,15},{10,... | collective-permute-start | bytes 196616 | tf_op jit(solution)/shard_map/ppermute | solution.py:228
  28.4 4.2 %collective-permute-start.12 = (bf16[16,1728]{1,0:T(8,128)(2,1)S(1)}, bf16[16,1728]{1,0:T(8,128)(2,1)S(1)}, u32[]{:S(2)}, u32[]{:S(2)}) collective-permute-start(bf16[16,1728]{1,0:T(8,128)(2,1)S(1)} %get-tuple-element.24), channel_id=1, source_target_pairs={{0,8},{8,0},{16,24},{24,16},{1,9},{9,1},{17,25},{25,17},{2,10},{10... | collective-permute-start | bytes 165896 | tf_op jit(solution)/shard_map/ppermute | solution.py:228
  31.5 10.3 %collective-permute-start.15 = (bf16[32,3456]{1,0:T(8,128)(2,1)S(1)}, bf16[32,3456]{1,0:T(8,128)(2,1)S(1)}, u32[]{:S(2)}, u32[]{:S(2)}) collective-permute-start(bf16[32,3456]{1,0:T(8,128)(2,1)S(1)} %add_convert_fusion.refs_6_), channel_id=1, source_target_pairs={{0,8},{8,0},{16,24},{24,16},{1,9},{9,1},{17,25},{25,17},{2,10},{10... | collective-permute-start | bytes 663560 | tf_op jit(solution)/shard_map/ppermute | solution.py:228
  32.2 3.5 %collective-permute-start.8 = (bf16[4,8,2048]{2,1,0:T(8,128)(2,1)S(1)}, bf16[4,8,2048]{2,1,0:T(8,128)(2,1)S(1)}, u32[]{:S(2)}, u32[]{:S(2)}) collective-permute-start(bf16[4,8,2048]{2,1,0:T(8,128)(2,1)S(1)} %get-tuple-element.23), channel_id=1, source_target_pairs={{0,1},{1,0},{2,3},{3,2},{4,5},{5,4},{6,7},{7,6},{8,9},{9,8},{10,11... | collective-permute-start | bytes 393224 | tf_op jit(solution)/shard_map/ppermute | solution.py:228
  32.7 6.6 %collective-permute-start.13 = (bf16[16,1728]{1,0:T(8,128)(2,1)S(1)}, bf16[16,1728]{1,0:T(8,128)(2,1)S(1)}, u32[]{:S(2)}, u32[]{:S(2)}) collective-permute-start(bf16[16,1728]{1,0:T(8,128)(2,1)S(1)} %add_convert_fusion.5.refs_4_), channel_id=1, source_target_pairs={{0,16},{8,24},{16,0},{24,8},{1,17},{9,25},{17,1},{25,9},{2,18},{10... | collective-permute-start | bytes 165896 | tf_op jit(solution)/shard_map/ppermute | solution.py:228
  35.8 4.0 %collective-permute-start.10 = (bf16[8,2048]{1,0:T(8,128)(2,1)S(1)}, bf16[8,2048]{1,0:T(8,128)(2,1)S(1)}, u32[]{:S(2)}, u32[]{:S(2)}) collective-permute-start(bf16[8,2048]{1,0:T(8,128)(2,1)S(1)} %get-tuple-element.37), channel_id=1, source_target_pairs={{0,4},{1,5},{2,6},{3,7},{4,0},{5,1},{6,2},{7,3},{8,12},{9,13},{10,... | collective-permute-start | bytes 98312 | tf_op jit(solution)/shard_map/ppermute | solution.py:228
  36.8 4.8 %collective-permute-start.11 = (bf16[8,2048]{1,0:T(8,128)(2,1)S(1)}, bf16[8,2048]{1,0:T(8,128)(2,1)S(1)}, u32[]{:S(2)}, u32[]{:S(2)}) collective-permute-start(bf16[8,2048]{1,0:T(8,128)(2,1)S(1)} %get-tuple-element.36), channel_id=1, source_target_pairs={{0,6},{1,7},{2,4},{3,5},{4,2},{5,3},{6,0},{7,1},{8,14},{9,15},{10,... | collective-permute-start | bytes 98312 | tf_op jit(solution)/shard_map/ppermute | solution.py:228
  37.9 3.9 %collective-permute-start.9 = (bf16[8,2048]{1,0:T(8,128)(2,1)S(1)}, bf16[8,2048]{1,0:T(8,128)(2,1)S(1)}, u32[]{:S(2)}, u32[]{:S(2)}) collective-permute-start(bf16[8,2048]{1,0:T(8,128)(2,1)S(1)} %get-tuple-element.38), channel_id=1, source_target_pairs={{0,2},{1,3},{2,0},{3,1},{4,6},{5,7},{6,4},{7,5},{8,10},{9,11},{10,... | collective-permute-start | bytes 98312 | tf_op jit(solution)/shard_map/ppermute | solution.py:228

commit v10 on v9

--- a/solution.py
+++ b/solution.py
@@ -75,7 +75,7 @@
     f1 = w1s.shape[1]
     c1 = n_mp * f1
     f2, cells = cot_ref.shape
-    chunk = chunk_of(cells, 4)
+    chunk = chunk_of(cells, 8)
     steps = cells // chunk
     pitch = pitch_of(c0)
     grid_xy = lane_grid(chunk)
@@ -165,7 +165,7 @@
     me = lax.axis_index("mp")
     f1, cells = pre_ref.shape
     c0 = vol_ref.shape[0]
-    chunk = chunk_of(cells, 1)
+    chunk = chunk_of(cells, 8)
     steps = cells // chunk
     grid_xy = lane_grid(chunk)
 

time: 43 us -> 43.4 us (level)
  Pallas kernels: 5.89 us -> 6.4 us
where the time goes in v10:
time: 43.4 us; the launch traced here: 43.2 us
  starting transfers between devices  19.7 us (45%)
  waiting for transfers between devices  13.2 us (30%)
  Pallas kernels  6.4 us (15%)
  local copies, waits for them, and re-layouts  2.01 us (5%)
  other arithmetic  1.08 us (2%)
  between operations  0.76 us (2%)
    ppermute x16, starting transfers between devices, swap(): return lax.ppermute(value, axis, [(i, i ^ k) for i in range(n)])  19.7 us
    ppermute x16, waiting for transfers between devices, swap(): return lax.ppermute(value, axis, [(i, i ^ k) for i in range(n)])  13.2 us
    pallas_call x1, Pallas kernels, local(): call(functools.partial(forward_kernel, n_mp, c0), [sds((f2, cells), BF16)...  4.45 us
    unnamed x7, local copies, waits for them, and re-layouts  1.21 us
    pallas_call x1, Pallas kernels, local(): call(functools.partial(backward_kernel, n_mp), [sds((half, rows_in, cells...  1.07 us
    another operation x2, other arithmetic, local(): near = jnp.stack(near)  0.91 us
    pallas_call x1, Pallas kernels, local(): call(functools.partial(finish_kernel, scale, half), [sds((f2, cells), BF1...  0.88 us
  transfers between devices with their start and end apart: 16, of which 12 were waited for; matrix products, arithmetic and copies ran while one was open for 2% of the time, Pallas kernels for 2%

profile of v10, /device:TPU:0, one launch (start us, length us, event | category | flops | bytes accessed | tf_op | source)
XLA Modules:
  0.0 43.2 jit_solution(16283056388656970566)
XLA Ops:
  0.6 0.9 %fusion.10 = (bf16[1,24,2048]{2,1,0:T(8,128)(2,1)S(1)}, bf16[24,2048]{1,0:T(8,128)(2,1)S(1)}) fusion(bf16[8,2048]{1,0:T(8,128)(2,1)} %bitcast.46, bf16[16,1728]{1,0:T(8,128)(2,1)} %param.5), kind=kLoop, calls=%fused_computation.23 | loop fusion | flops 294912 | bytes 284672 | tf_op jit(solution)/shard_map/stack | solution.py:278
  1.5 3.0 %collective-permute-start = (bf16[24,2048]{1,0:T(8,128)(2,1)S(1)}, bf16[24,2048]{1,0:T(8,128)(2,1)S(1)}, u32[]{:S(2)}, u32[]{:S(2)}) collective-permute-start(bf16[24,2048]{1,0:T(8,128)(2,1)S(1)} %get-tuple-element.41), channel_id=1, source_target_pairs={{0,2},{1,3},{2,0},{3,1},{4,6},{5,7},{6,4},{7,5},{8,10},{9,11},{10,... | collective-permute-start | bytes 294920 | tf_op jit(solution)/shard_map/ppermute | solution.py:228
  4.5 1.5 %collective-permute-start.1 = (bf16[24,2048]{1,0:T(8,128)(2,1)S(1)}, bf16[24,2048]{1,0:T(8,128)(2,1)S(1)}, u32[]{:S(2)}, u32[]{:S(2)}) collective-permute-start(bf16[24,2048]{1,0:T(8,128)(2,1)S(1)} %get-tuple-element.41), channel_id=1, source_target_pairs={{0,4},{1,5},{2,6},{3,7},{4,0},{5,1},{6,2},{7,3},{8,12},{9,13},{10,... | collective-permute-start | bytes 294920 | tf_op jit(solution)/shard_map/ppermute | solution.py:228
  6.0 0.0 collective-permute-start.2
  6.0 1.5 %collective-permute-done = bf16[24,2048]{1,0:T(8,128)(2,1)S(1)} collective-permute-done((bf16[24,2048]{1,0:T(8,128)(2,1)S(1)}, bf16[24,2048]{1,0:T(8,128)(2,1)S(1)}, u32[]{:S(2)}, u32[]{:S(2)}) %collective-permute-start) | collective-permute-done | bytes 98336 | tf_op jit(solution)/shard_map/ppermute | solution.py:228
  7.5 2.6 %collective-permute-done.1 = bf16[24,2048]{1,0:T(8,128)(2,1)S(1)} collective-permute-done((bf16[24,2048]{1,0:T(8,128)(2,1)S(1)}, bf16[24,2048]{1,0:T(8,128)(2,1)S(1)}, u32[]{:S(2)}, u32[]{:S(2)}) %collective-permute-start.1) | collective-permute-done | bytes 98336 | tf_op jit(solution)/shard_map/ppermute | solution.py:228
  10.2 1.4 %collective-permute-done.2 = bf16[24,2048]{1,0:T(8,128)(2,1)S(1)} collective-permute-done((bf16[24,2048]{1,0:T(8,128)(2,1)S(1)}, bf16[24,2048]{1,0:T(8,128)(2,1)S(1)}, u32[]{:S(2)}, u32[]{:S(2)}) %collective-permute-start.2) | collective-permute-done | bytes 98336 | tf_op jit(solution)/shard_map/ppermute | solution.py:228
  11.5 0.0 copy-start.2
  11.5 0.1 pad_maximum_fusion.refs_0_
  11.6 0.1 collective-permute-start.3
  11.7 0.8 %copy-done.2 = bf16[32,3456]{1,0:T(8,128)(2,1)S(1)} copy-done((bf16[32,3456]{1,0:T(8,128)(2,1)S(1)}, bf16[32,3456]{1,0:T(8,128)(2,1)}, u32[]{:S(2)}) %copy-start.2) | copy-done | bytes 221208
  12.5 0.1 reshape.68
  12.6 0.1 copy.11
  12.8 0.1 copy.12
  12.8 0.0 copy-start
  12.8 0.2 copy.13.refs_3_
  13.0 0.4 collective-permute-done.3.refs_1_
  13.4 0.4 copy-done
  13.7 4.5 %shard_map.75 = (bf16[32,2048]{1,0:T(8,128)(2,1)S(1)}, f32[16,2048]{1,0:T(8,128)S(1)}, bf16[64,2048]{1,0:T(8,128)(2,1)S(1)}, bf16[4,16,2048]{2,1,0:T(8,128)(2,1)...) custom-call(bf16[4,24,2048]{2,1,0:T(8,128)(2,1)S(1)} %pad_maximum_fusion.refs_0_, ...), custom_call_target="tpu_custom_call" | custom-call | flops 2264924160 | bytes 4194304 | tf_op jit(solution)/shard_map/pallas_call | solution.py:288
  18.2 0.1 collective-permute-start.4
  18.3 2.7 %collective-permute-start.14 = (bf16[32,3456]{1,0:T(8,128)(2,1)S(1)}, bf16[32,3456]{1,0:T(8,128)(2,1)S(1)}, u32[]{:S(2)}, u32[]{:S(2)}) collective-permute-start(bf16[32,3456]{1,0:T(8,128)(2,1)S(1)} %get-tuple-element.25), channel_id=1, source_target_pairs={{0,16},{8,24},{16,0},{24,8},{1,17},{9,25},{17,1},{25,9},{2,18},{10... | collective-permute-start | bytes 663560 | tf_op jit(solution)/shard_map/ppermute | solution.py:228
  20.9 0.0 collective-permute-done.4
  20.9 0.0 copy-start.1
  20.9 0.1 fusion.5
  21.0 0.7 %collective-permute-start.5 = (bf16[16,2048]{1,0:T(8,128)(2,1)S(1)}, bf16[16,2048]{1,0:T(8,128)(2,1)S(1)}, u32[]{:S(2)}, u32[]{:S(2)}) collective-permute-start(bf16[16,2048]{1,0:T(8,128)(2,1)S(1)} %get-tuple-element.34), channel_id=1, source_target_pairs={{0,2},{1,3},{2,0},{3,1},{4,6},{5,7},{6,4},{7,5},{8,10},{9,11},{10,... | collective-permute-start | bytes 196616 | tf_op jit(solution)/shard_map/ppermute | solution.py:228
  21.7 1.0 %collective-permute-start.6 = (bf16[16,2048]{1,0:T(8,128)(2,1)S(1)}, bf16[16,2048]{1,0:T(8,128)(2,1)S(1)}, u32[]{:S(2)}, u32[]{:S(2)}) collective-permute-start(bf16[16,2048]{1,0:T(8,128)(2,1)S(1)} %get-tuple-element.33), channel_id=1, source_target_pairs={{0,4},{1,5},{2,6},{3,7},{4,0},{5,1},{6,2},{7,3},{8,12},{9,13},{10,... | collective-permute-start | bytes 196616 | tf_op jit(solution)/shard_map/ppermute | solution.py:228
  22.7 1.9 %collective-permute-start.7 = (bf16[16,2048]{1,0:T(8,128)(2,1)S(1)}, bf16[16,2048]{1,0:T(8,128)(2,1)S(1)}, u32[]{:S(2)}, u32[]{:S(2)}) collective-permute-start(bf16[16,2048]{1,0:T(8,128)(2,1)S(1)} %get-tuple-element.32), channel_id=1, source_target_pairs={{0,6},{1,7},{2,4},{3,5},{4,2},{5,3},{6,0},{7,1},{8,14},{9,15},{10,... | collective-permute-start | bytes 196616 | tf_op jit(solution)/shard_map/ppermute | solution.py:228
  24.6 0.0 copy-done.1
  24.6 0.2 reshape.72
  24.8 0.1 copy.15.refs_6_
  24.9 0.4 %collective-permute-done.5.refs_1_ = bf16[16,2048]{1,0:T(8,128)(2,1)S(1)} collective-permute-done((bf16[16,2048]{1,0:T(8,128)(2,1)S(1)}, bf16[16,2048]{1,0:T(8,128)(2,1)S(1)}, u32[]{:S(2)}, u32[]{:S(2)}) %collective-permute-start.5) | collective-permute-done | bytes 65568 | tf_op jit(solution)/shard_map/ppermute | solution.py:228
  25.3 1.3 %collective-permute-done.6.refs_2_ = bf16[16,2048]{1,0:T(8,128)(2,1)S(1)} collective-permute-done((bf16[16,2048]{1,0:T(8,128)(2,1)S(1)}, bf16[16,2048]{1,0:T(8,128)(2,1)S(1)}, u32[]{:S(2)}, u32[]{:S(2)}) %collective-permute-start.6) | collective-permute-done | bytes 65568 | tf_op jit(solution)/shard_map/ppermute | solution.py:228
  26.7 1.2 %collective-permute-done.7.refs_3_ = bf16[16,2048]{1,0:T(8,128)(2,1)S(1)} collective-permute-done((bf16[16,2048]{1,0:T(8,128)(2,1)S(1)}, bf16[16,2048]{1,0:T(8,128)(2,1)S(1)}, u32[]{:S(2)}, u32[]{:S(2)}) %collective-permute-start.7) | collective-permute-done | bytes 65568 | tf_op jit(solution)/shard_map/ppermute | solution.py:228
  27.9 1.1 %shard_map.76 = (bf16[4,8,2048]{2,1,0:T(8,128)(2,1)S(1)}, bf16[4,8,2048]{2,1,0:T(8,128)(2,1)S(1)}, bf16[16,1728]{1,0:T(8,128)(2,1)S(1)}) custom-call(bf16[16,2048]{1,0:T(8,128)(2,1)S(1)} %get-tuple-element.35.refs_0_, bf16[16,2048]{1,0:T(8,128)(2,1)S(1)} %collective-permute-done.5.refs_1_, bf16[16,2048]{1,0:T(8,128)(2,1)S(1)} %collective-permute-done.6.refs_2_, ...), custom_call_target="tpu_custom_call" | custom-call | flops 226492416 | bytes 1048576 | tf_op jit(solution)/shard_map/pallas_call | solution.py:317
  28.9 1.6 %collective-permute-start.12 = (bf16[16,1728]{1,0:T(8,128)(2,1)S(1)}, bf16[16,1728]{1,0:T(8,128)(2,1)S(1)}, u32[]{:S(2)}, u32[]{:S(2)}) collective-permute-start(bf16[16,1728]{1,0:T(8,128)(2,1)S(1)} %get-tuple-element.24), channel_id=1, source_target_pairs={{0,8},{8,0},{16,24},{24,16},{1,9},{9,1},{17,25},{25,17},{2,10},{10... | collective-permute-start | bytes 165896 | tf_op jit(solution)/shard_map/ppermute | solution.py:228
  30.6 1.3 %collective-permute-done.14 = bf16[32,3456]{1,0:T(8,128)(2,1)S(1)} collective-permute-done((bf16[32,3456]{1,0:T(8,128)(2,1)S(1)}, bf16[32,3456]{1,0:T(8,128)(2,1)S(1)}, u32[]{:S(2)}, u32[]{:S(2)}) %collective-permute-start.14) | collective-permute-done | bytes 221216 | tf_op jit(solution)/shard_map/ppermute | solution.py:228
  31.9 0.1 add_convert_fusion.refs_6_
  31.9 0.7 %collective-permute-start.15 = (bf16[32,3456]{1,0:T(8,128)(2,1)S(1)}, bf16[32,3456]{1,0:T(8,128)(2,1)S(1)}, u32[]{:S(2)}, u32[]{:S(2)}) collective-permute-start(bf16[32,3456]{1,0:T(8,128)(2,1)S(1)} %add_convert_fusion.refs_6_), channel_id=1, source_target_pairs={{0,8},{8,0},{16,24},{24,16},{1,9},{9,1},{17,25},{25,17},{2,10},{10... | collective-permute-start | bytes 663560 | tf_op jit(solution)/shard_map/ppermute | solution.py:228
  32.6 0.0 collective-permute-start.8
  32.6 0.5 %collective-permute-done.12 = bf16[16,1728]{1,0:T(8,128)(2,1)S(1)} collective-permute-done((bf16[16,1728]{1,0:T(8,128)(2,1)S(1)}, bf16[16,1728]{1,0:T(8,128)(2,1)S(1)}, u32[]{:S(2)}, u32[]{:S(2)}) %collective-permute-start.12) | collective-permute-done | bytes 55328 | tf_op jit(solution)/shard_map/ppermute | solution.py:228
  33.2 3.0 %collective-permute-start.13 = (bf16[16,1728]{1,0:T(8,128)(2,1)S(1)}, bf16[16,1728]{1,0:T(8,128)(2,1)S(1)}, u32[]{:S(2)}, u32[]{:S(2)}) collective-permute-start(bf16[16,1728]{1,0:T(8,128)(2,1)S(1)} %add_convert_fusion.5.refs_4_), channel_id=1, source_target_pairs={{0,16},{8,24},{16,0},{24,8},{1,17},{9,25},{17,1},{25,9},{2,18},{10... | collective-permute-start | bytes 165896 | tf_op jit(solution)/shard_map/ppermute | solution.py:228
  36.1 0.0 collective-permute-done.8
  36.2 1.0 %collective-permute-start.10 = (bf16[8,2048]{1,0:T(8,128)(2,1)S(1)}, bf16[8,2048]{1,0:T(8,128)(2,1)S(1)}, u32[]{:S(2)}, u32[]{:S(2)}) collective-permute-start(bf16[8,2048]{1,0:T(8,128)(2,1)S(1)} %get-tuple-element.37), channel_id=1, source_target_pairs={{0,4},{1,5},{2,6},{3,7},{4,0},{5,1},{6,2},{7,3},{8,12},{9,13},{10,... | collective-permute-start | bytes 98312 | tf_op jit(solution)/shard_map/ppermute | solution.py:228
  37.2 1.2 %collective-permute-start.11 = (bf16[8,2048]{1,0:T(8,128)(2,1)S(1)}, bf16[8,2048]{1,0:T(8,128)(2,1)S(1)}, u32[]{:S(2)}, u32[]{:S(2)}) collective-permute-start(bf16[8,2048]{1,0:T(8,128)(2,1)S(1)} %get-tuple-element.36), channel_id=1, source_target_pairs={{0,6},{1,7},{2,4},{3,5},{4,2},{5,3},{6,0},{7,1},{8,14},{9,15},{10,... | collective-permute-start | bytes 98312 | tf_op jit(solution)/shard_map/ppermute | solution.py:228
  38.4 1.4 %collective-permute-start.9 = (bf16[8,2048]{1,0:T(8,128)(2,1)S(1)}, bf16[8,2048]{1,0:T(8,128)(2,1)S(1)}, u32[]{:S(2)}, u32[]{:S(2)}) collective-permute-start(bf16[8,2048]{1,0:T(8,128)(2,1)S(1)} %get-tuple-element.38), channel_id=1, source_target_pairs={{0,2},{1,3},{2,0},{3,1},{4,6},{5,7},{6,4},{7,5},{8,10},{9,11},{10,... | collective-permute-start | bytes 98312 | tf_op jit(solution)/shard_map/ppermute | solution.py:228
  39.7 0.0 collective-permute-done.13.refs_5_
  39.7 0.4 collective-permute-done.10.refs_2_
  40.2 1.8 %collective-permute-done.11.refs_3_ = bf16[8,2048]{1,0:T(8,128)(2,1)S(1)} collective-permute-done((bf16[8,2048]{1,0:T(8,128)(2,1)S(1)}, bf16[8,2048]{1,0:T(8,128)(2,1)S(1)}, u32[]{:S(2)}, u32[]{:S(2)}) %collective-permute-start.11) | collective-permute-done | bytes 32800 | tf_op jit(solution)/shard_map/ppermute | solution.py:228
  42.0 0.3 collective-permute-done.9.refs_1_
  42.3 0.0 collective-permute-done.15.refs_7_
  42.3 0.9 %shard_map.77 = (bf16[32,2048]{1,0:T(8,128)(2,1)}, bf16[8,2048]{1,0:T(8,128)(2,1)}, f32[16,1728]{1,0:T(8,128)}, f32[32,3456]{1,0:T(8,128)}) custom-call(bf16[8,2048]{1,0:T(8,128)(2,1)S(1)} %get-tuple-element.39.refs_0_, bf16[8,2048]{1,0:T(8,128)(2,1)S(1)} %collective-permute-done.9.refs_1_, bf16[8,2048]{1,0:T(8,128)(2,1)S(1)} %collective-permute-done.10.refs_2_, ...), custom_call_target="tpu_custom_call" | custom-call | bytes 2097152 | tf_op jit(solution)/shard_map/pallas_call | solution.py:342
  (4 shorter events, 0.1 us)
Async XLA Ops:
  1.5 6.1 %collective-permute-start = (bf16[24,2048]{1,0:T(8,128)(2,1)S(1)}, bf16[24,2048]{1,0:T(8,128)(2,1)S(1)}, u32[]{:S(2)}, u32[]{:S(2)}) collective-permute-start(bf16[24,2048]{1,0:T(8,128)(2,1)S(1)} %get-tuple-element.41), channel_id=1, source_target_pairs={{0,2},{1,3},{2,0},{3,1},{4,6},{5,7},{6,4},{7,5},{8,10},{9,11},{10,... | collective-permute-start | bytes 294920 | tf_op jit(solution)/shard_map/ppermute | solution.py:228
  4.5 5.7 %collective-permute-start.1 = (bf16[24,2048]{1,0:T(8,128)(2,1)S(1)}, bf16[24,2048]{1,0:T(8,128)(2,1)S(1)}, u32[]{:S(2)}, u32[]{:S(2)}) collective-permute-start(bf16[24,2048]{1,0:T(8,128)(2,1)S(1)} %get-tuple-element.41), channel_id=1, source_target_pairs={{0,4},{1,5},{2,6},{3,7},{4,0},{5,1},{6,2},{7,3},{8,12},{9,13},{10,... | collective-permute-start | bytes 294920 | tf_op jit(solution)/shard_map/ppermute | solution.py:228
  6.0 5.5 %collective-permute-start.2 = (bf16[24,2048]{1,0:T(8,128)(2,1)S(1)}, bf16[24,2048]{1,0:T(8,128)(2,1)S(1)}, u32[]{:S(2)}, u32[]{:S(2)}) collective-permute-start(bf16[24,2048]{1,0:T(8,128)(2,1)S(1)} %get-tuple-element.41), channel_id=1, source_target_pairs={{0,6},{1,7},{2,4},{3,5},{4,2},{5,3},{6,0},{7,1},{8,14},{9,15},{10,... | collective-permute-start | bytes 294920 | tf_op jit(solution)/shard_map/ppermute | solution.py:228
  11.5 0.9 %copy-start.2 = (bf16[32,3456]{1,0:T(8,128)(2,1)S(1)}, bf16[32,3456]{1,0:T(8,128)(2,1)}, u32[]{:S(2)}) copy-start(bf16[32,3456]{1,0:T(8,128)(2,1)} %param.6) | copy-start | bytes 663556
  11.6 1.8 %collective-permute-start.3 = (bf16[4,24,2048]{2,1,0:T(8,128)(2,1)S(1)}, bf16[4,24,2048]{2,1,0:T(8,128)(2,1)S(1)}, u32[]{:S(2)}, u32[]{:S(2)}) collective-permute-start(bf16[4,24,2048]{2,1,0:T(8,128)(2,1)S(1)} %pad_maximum_fusion.refs_0_), channel_id=1, source_target_pairs={{0,1},{1,0},{2,3},{3,2},{4,5},{5,4},{6,7},{7,6},{8,9},{9,8},{10,11... | collective-permute-start | bytes 1179656 | tf_op jit(solution)/shard_map/ppermute | solution.py:228
  12.8 0.9 %copy-start = (bf16[32,1,2048]{2,0,1:T(8,128)(2,1)S(1)}, bf16[32,1,2048]{2,0,1:T(8,128)(2,1)}, u32[]{:S(2)}) copy-start(bf16[32,1,2048]{2,0,1:T(8,128)(2,1)} %param.7) | copy-start | bytes 393220
  18.2 2.7 %collective-permute-start.4 = (bf16[4,16,2048]{2,1,0:T(8,128)(2,1)S(1)}, bf16[4,16,2048]{2,1,0:T(8,128)(2,1)S(1)}, u32[]{:S(2)}, u32[]{:S(2)}) collective-permute-start(bf16[4,16,2048]{2,1,0:T(8,128)(2,1)S(1)} %get-tuple-element.19), channel_id=1, source_target_pairs={{0,1},{1,0},{2,3},{3,2},{4,5},{5,4},{6,7},{7,6},{8,9},{9,8},{10,11... | collective-permute-start | bytes 786440 | tf_op jit(solution)/shard_map/ppermute | solution.py:228
  18.3 13.6 %collective-permute-start.14 = (bf16[32,3456]{1,0:T(8,128)(2,1)S(1)}, bf16[32,3456]{1,0:T(8,128)(2,1)S(1)}, u32[]{:S(2)}, u32[]{:S(2)}) collective-permute-start(bf16[32,3456]{1,0:T(8,128)(2,1)S(1)} %get-tuple-element.25), channel_id=1, source_target_pairs={{0,16},{8,24},{16,0},{24,8},{1,17},{9,25},{17,1},{25,9},{2,18},{10... | collective-permute-start | bytes 663560 | tf_op jit(solution)/shard_map/ppermute | solution.py:228
  20.9 3.6 %copy-start.1 = (bf16[16,1728]{1,0:T(8,128)(2,1)S(1)}, bf16[16,1728]{1,0:T(8,128)(2,1)}, u32[]{:S(2)}) copy-start(bf16[16,1728]{1,0:T(8,128)(2,1)} %param.5) | copy-start | bytes 165892
  21.0 4.3 %collective-permute-start.5 = (bf16[16,2048]{1,0:T(8,128)(2,1)S(1)}, bf16[16,2048]{1,0:T(8,128)(2,1)S(1)}, u32[]{:S(2)}, u32[]{:S(2)}) collective-permute-start(bf16[16,2048]{1,0:T(8,128)(2,1)S(1)} %get-tuple-element.34), channel_id=1, source_target_pairs={{0,2},{1,3},{2,0},{3,1},{4,6},{5,7},{6,4},{7,5},{8,10},{9,11},{10,... | collective-permute-start | bytes 196616 | tf_op jit(solution)/shard_map/ppermute | solution.py:228
  21.7 5.0 %collective-permute-start.6 = (bf16[16,2048]{1,0:T(8,128)(2,1)S(1)}, bf16[16,2048]{1,0:T(8,128)(2,1)S(1)}, u32[]{:S(2)}, u32[]{:S(2)}) collective-permute-start(bf16[16,2048]{1,0:T(8,128)(2,1)S(1)} %get-tuple-element.33), channel_id=1, source_target_pairs={{0,4},{1,5},{2,6},{3,7},{4,0},{5,1},{6,2},{7,3},{8,12},{9,13},{10,... | collective-permute-start | bytes 196616 | tf_op jit(solution)/shard_map/ppermute | solution.py:228
  22.7 5.2 %collective-permute-start.7 = (bf16[16,2048]{1,0:T(8,128)(2,1)S(1)}, bf16[16,2048]{1,0:T(8,128)(2,1)S(1)}, u32[]{:S(2)}, u32[]{:S(2)}) collective-permute-start(bf16[16,2048]{1,0:T(8,128)(2,1)S(1)} %get-tuple-element.32), channel_id=1, source_target_pairs={{0,6},{1,7},{2,4},{3,5},{4,2},{5,3},{6,0},{7,1},{8,14},{9,15},{10,... | collective-permute-start | bytes 196616 | tf_op jit(solution)/shard_map/ppermute | solution.py:228
  28.9 4.2 %collective-permute-start.12 = (bf16[16,1728]{1,0:T(8,128)(2,1)S(1)}, bf16[16,1728]{1,0:T(8,128)(2,1)S(1)}, u32[]{:S(2)}, u32[]{:S(2)}) collective-permute-start(bf16[16,1728]{1,0:T(8,128)(2,1)S(1)} %get-tuple-element.24), channel_id=1, source_target_pairs={{0,8},{8,0},{16,24},{24,16},{1,9},{9,1},{17,25},{25,17},{2,10},{10... | collective-permute-start | bytes 165896 | tf_op jit(solution)/shard_map/ppermute | solution.py:228
  31.9 10.3 %collective-permute-start.15 = (bf16[32,3456]{1,0:T(8,128)(2,1)S(1)}, bf16[32,3456]{1,0:T(8,128)(2,1)S(1)}, u32[]{:S(2)}, u32[]{:S(2)}) collective-permute-start(bf16[32,3456]{1,0:T(8,128)(2,1)S(1)} %add_convert_fusion.refs_6_), channel_id=1, source_target_pairs={{0,8},{8,0},{16,24},{24,16},{1,9},{9,1},{17,25},{25,17},{2,10},{10... | collective-permute-start | bytes 663560 | tf_op jit(solution)/shard_map/ppermute | solution.py:228
  32.6 3.5 %collective-permute-start.8 = (bf16[4,8,2048]{2,1,0:T(8,128)(2,1)S(1)}, bf16[4,8,2048]{2,1,0:T(8,128)(2,1)S(1)}, u32[]{:S(2)}, u32[]{:S(2)}) collective-permute-start(bf16[4,8,2048]{2,1,0:T(8,128)(2,1)S(1)} %get-tuple-element.23), channel_id=1, source_target_pairs={{0,1},{1,0},{2,3},{3,2},{4,5},{5,4},{6,7},{7,6},{8,9},{9,8},{10,11... | collective-permute-start | bytes 393224 | tf_op jit(solution)/shard_map/ppermute | solution.py:228
  33.2 6.6 %collective-permute-start.13 = (bf16[16,1728]{1,0:T(8,128)(2,1)S(1)}, bf16[16,1728]{1,0:T(8,128)(2,1)S(1)}, u32[]{:S(2)}, u32[]{:S(2)}) collective-permute-start(bf16[16,1728]{1,0:T(8,128)(2,1)S(1)} %add_convert_fusion.5.refs_4_), channel_id=1, source_target_pairs={{0,16},{8,24},{16,0},{24,8},{1,17},{9,25},{17,1},{25,9},{2,18},{10... | collective-permute-start | bytes 165896 | tf_op jit(solution)/shard_map/ppermute | solution.py:228
  36.2 4.0 %collective-permute-start.10 = (bf16[8,2048]{1,0:T(8,128)(2,1)S(1)}, bf16[8,2048]{1,0:T(8,128)(2,1)S(1)}, u32[]{:S(2)}, u32[]{:S(2)}) collective-permute-start(bf16[8,2048]{1,0:T(8,128)(2,1)S(1)} %get-tuple-element.37), channel_id=1, source_target_pairs={{0,4},{1,5},{2,6},{3,7},{4,0},{5,1},{6,2},{7,3},{8,12},{9,13},{10,... | collective-permute-start | bytes 98312 | tf_op jit(solution)/shard_map/ppermute | solution.py:228
  37.2 4.8 %collective-permute-start.11 = (bf16[8,2048]{1,0:T(8,128)(2,1)S(1)}, bf16[8,2048]{1,0:T(8,128)(2,1)S(1)}, u32[]{:S(2)}, u32[]{:S(2)}) collective-permute-start(bf16[8,2048]{1,0:T(8,128)(2,1)S(1)} %get-tuple-element.36), channel_id=1, source_target_pairs={{0,6},{1,7},{2,4},{3,5},{4,2},{5,3},{6,0},{7,1},{8,14},{9,15},{10,... | collective-permute-start | bytes 98312 | tf_op jit(solution)/shard_map/ppermute | solution.py:228
  38.4 3.9 %collective-permute-start.9 = (bf16[8,2048]{1,0:T(8,128)(2,1)S(1)}, bf16[8,2048]{1,0:T(8,128)(2,1)S(1)}, u32[]{:S(2)}, u32[]{:S(2)}) collective-permute-start(bf16[8,2048]{1,0:T(8,128)(2,1)S(1)} %get-tuple-element.38), channel_id=1, source_target_pairs={{0,2},{1,3},{2,0},{3,1},{4,6},{5,7},{6,4},{7,5},{8,10},{9,11},{10,... | collective-permute-start | bytes 98312 | tf_op jit(solution)/shard_map/ppermute | solution.py:228

commit v11 on v9

--- a/solution.py
+++ b/solution.py
@@ -333,9 +333,9 @@
     ins = sum_over_chips(keep, got)
 
     second_got, *_ = lax.optimization_barrier((second_got, grad_first))
-    for bit in bits[::-1][:-1]:
+    for bit in bits[:-1]:
         grad_first = add(grad_first, swap(grad_first, "sample", bit))
-    first_got = swap(grad_first, "sample", bits[::-1][-1])
+    first_got = swap(grad_first, "sample", bits[-1])
     for bit in bits[1:]:
         grad_second = add(grad_second, second_got)
         second_got = swap(grad_second, "sample", bit)

time: 43 us -> 43.1 us (level)
  waiting for transfers between devices: 13.2 us -> 14.6 us
  starting transfers between devices: 19.8 us -> 18.5 us
    ppermute x16, waiting for transfers between devices: 13.2 us -> 14.6 us  [swap(): return lax.ppermute(value, axis, [(i, i ^ k) for i in range(n)])]
    ppermute x16, starting transfers between devices: 19.8 us -> 18.5 us  [swap(): return lax.ppermute(value, axis, [(i, i ^ k) for i in range(n)])]
where the time goes in v11:
time: 43.1 us; the launch traced here: 42.9 us
  starting transfers between devices  18.5 us (43%)
  waiting for transfers between devices  14.6 us (34%)
  Pallas kernels  5.89 us (14%)
  local copies, waits for them, and re-layouts  2.01 us (5%)
  other arithmetic  1.08 us (3%)
  between operations  0.76 us (2%)
    ppermute x16, starting transfers between devices, swap(): return lax.ppermute(value, axis, [(i, i ^ k) for i in range(n)])  18.5 us
    ppermute x16, waiting for transfers between devices, swap(): return lax.ppermute(value, axis, [(i, i ^ k) for i in range(n)])  14.6 us
    pallas_call x1, Pallas kernels, local(): call(functools.partial(forward_kernel, n_mp, c0), [sds((f2, cells), BF16)...  4.03 us
    unnamed x7, local copies, waits for them, and re-layouts  1.21 us
    pallas_call x1, Pallas kernels, local(): call(functools.partial(backward_kernel, n_mp), [sds((half, rows_in, cells...  0.98 us
    another operation x2, other arithmetic, local(): near = jnp.stack(near)  0.91 us
    pallas_call x1, Pallas kernels, local(): call(functools.partial(finish_kernel, scale, half), [sds((f2, cells), BF1...  0.88 us
  transfers between devices with their start and end apart: 16, of which 12 were waited for; matrix products, arithmetic and copies ran while one was open for 2% of the time, Pallas kernels for 2%

profile of v11, /device:TPU:0, one launch (start us, length us, event | category | flops | bytes accessed | tf_op | source)
XLA Modules:
  0.0 42.9 jit_solution(7363937977501792726)
XLA Ops:
  0.6 0.9 %fusion.10 = (bf16[1,24,2048]{2,1,0:T(8,128)(2,1)S(1)}, bf16[24,2048]{1,0:T(8,128)(2,1)S(1)}) fusion(bf16[8,2048]{1,0:T(8,128)(2,1)} %bitcast.46, bf16[16,1728]{1,0:T(8,128)(2,1)} %param.5), kind=kLoop, calls=%fused_computation.23 | loop fusion | flops 294912 | bytes 284672 | tf_op jit(solution)/shard_map/stack | solution.py:278
  1.5 3.0 %collective-permute-start = (bf16[24,2048]{1,0:T(8,128)(2,1)S(1)}, bf16[24,2048]{1,0:T(8,128)(2,1)S(1)}, u32[]{:S(2)}, u32[]{:S(2)}) collective-permute-start(bf16[24,2048]{1,0:T(8,128)(2,1)S(1)} %get-tuple-element.41), channel_id=1, source_target_pairs={{0,2},{1,3},{2,0},{3,1},{4,6},{5,7},{6,4},{7,5},{8,10},{9,11},{10,... | collective-permute-start | bytes 294920 | tf_op jit(solution)/shard_map/ppermute | solution.py:228
  4.5 1.5 %collective-permute-start.1 = (bf16[24,2048]{1,0:T(8,128)(2,1)S(1)}, bf16[24,2048]{1,0:T(8,128)(2,1)S(1)}, u32[]{:S(2)}, u32[]{:S(2)}) collective-permute-start(bf16[24,2048]{1,0:T(8,128)(2,1)S(1)} %get-tuple-element.41), channel_id=1, source_target_pairs={{0,4},{1,5},{2,6},{3,7},{4,0},{5,1},{6,2},{7,3},{8,12},{9,13},{10,... | collective-permute-start | bytes 294920 | tf_op jit(solution)/shard_map/ppermute | solution.py:228
  6.0 0.0 collective-permute-start.2
  6.0 1.5 %collective-permute-done = bf16[24,2048]{1,0:T(8,128)(2,1)S(1)} collective-permute-done((bf16[24,2048]{1,0:T(8,128)(2,1)S(1)}, bf16[24,2048]{1,0:T(8,128)(2,1)S(1)}, u32[]{:S(2)}, u32[]{:S(2)}) %collective-permute-start) | collective-permute-done | bytes 98336 | tf_op jit(solution)/shard_map/ppermute | solution.py:228
  7.5 2.6 %collective-permute-done.1 = bf16[24,2048]{1,0:T(8,128)(2,1)S(1)} collective-permute-done((bf16[24,2048]{1,0:T(8,128)(2,1)S(1)}, bf16[24,2048]{1,0:T(8,128)(2,1)S(1)}, u32[]{:S(2)}, u32[]{:S(2)}) %collective-permute-start.1) | collective-permute-done | bytes 98336 | tf_op jit(solution)/shard_map/ppermute | solution.py:228
  10.2 1.4 %collective-permute-done.2 = bf16[24,2048]{1,0:T(8,128)(2,1)S(1)} collective-permute-done((bf16[24,2048]{1,0:T(8,128)(2,1)S(1)}, bf16[24,2048]{1,0:T(8,128)(2,1)S(1)}, u32[]{:S(2)}, u32[]{:S(2)}) %collective-permute-start.2) | collective-permute-done | bytes 98336 | tf_op jit(solution)/shard_map/ppermute | solution.py:228
  11.5 0.0 copy-start.2
  11.5 0.1 pad_maximum_fusion.refs_0_
  11.6 0.1 collective-permute-start.3
  11.7 0.8 %copy-done.2 = bf16[32,3456]{1,0:T(8,128)(2,1)S(1)} copy-done((bf16[32,3456]{1,0:T(8,128)(2,1)S(1)}, bf16[32,3456]{1,0:T(8,128)(2,1)}, u32[]{:S(2)}) %copy-start.2) | copy-done | bytes 221208
  12.5 0.1 reshape.68
  12.6 0.1 copy.11
  12.8 0.1 copy.12
  12.8 0.0 copy-start
  12.8 0.2 copy.13.refs_3_
  13.0 0.4 collective-permute-done.3.refs_1_
  13.4 0.4 copy-done
  13.7 4.0 %shard_map.75 = (bf16[32,2048]{1,0:T(8,128)(2,1)S(1)}, f32[16,2048]{1,0:T(8,128)S(1)}, bf16[64,2048]{1,0:T(8,128)(2,1)S(1)}, bf16[4,16,2048]{2,1,0:T(8,128)(2,1)...) custom-call(bf16[4,24,2048]{2,1,0:T(8,128)(2,1)S(1)} %pad_maximum_fusion.refs_0_, ...), custom_call_target="tpu_custom_call" | custom-call | flops 2264924160 | bytes 4194304 | tf_op jit(solution)/shard_map/pallas_call | solution.py:288
  17.8 0.1 collective-permute-start.4
  17.9 2.7 %collective-permute-start.14 = (bf16[32,3456]{1,0:T(8,128)(2,1)S(1)}, bf16[32,3456]{1,0:T(8,128)(2,1)S(1)}, u32[]{:S(2)}, u32[]{:S(2)}) collective-permute-start(bf16[32,3456]{1,0:T(8,128)(2,1)S(1)} %get-tuple-element.25), channel_id=1, source_target_pairs={{0,16},{8,24},{16,0},{24,8},{1,17},{9,25},{17,1},{25,9},{2,18},{10... | collective-permute-start | bytes 663560 | tf_op jit(solution)/shard_map/ppermute | solution.py:228
  20.5 0.0 collective-permute-done.4
  20.5 0.0 copy-start.1
  20.5 0.1 fusion.5
  20.6 0.7 %collective-permute-start.5 = (bf16[16,2048]{1,0:T(8,128)(2,1)S(1)}, bf16[16,2048]{1,0:T(8,128)(2,1)S(1)}, u32[]{:S(2)}, u32[]{:S(2)}) collective-permute-start(bf16[16,2048]{1,0:T(8,128)(2,1)S(1)} %get-tuple-element.34), channel_id=1, source_target_pairs={{0,2},{1,3},{2,0},{3,1},{4,6},{5,7},{6,4},{7,5},{8,10},{9,11},{10,... | collective-permute-start | bytes 196616 | tf_op jit(solution)/shard_map/ppermute | solution.py:228
  21.3 1.0 %collective-permute-start.6 = (bf16[16,2048]{1,0:T(8,128)(2,1)S(1)}, bf16[16,2048]{1,0:T(8,128)(2,1)S(1)}, u32[]{:S(2)}, u32[]{:S(2)}) collective-permute-start(bf16[16,2048]{1,0:T(8,128)(2,1)S(1)} %get-tuple-element.33), channel_id=1, source_target_pairs={{0,4},{1,5},{2,6},{3,7},{4,0},{5,1},{6,2},{7,3},{8,12},{9,13},{10,... | collective-permute-start | bytes 196616 | tf_op jit(solution)/shard_map/ppermute | solution.py:228
  22.3 1.9 %collective-permute-start.7 = (bf16[16,2048]{1,0:T(8,128)(2,1)S(1)}, bf16[16,2048]{1,0:T(8,128)(2,1)S(1)}, u32[]{:S(2)}, u32[]{:S(2)}) collective-permute-start(bf16[16,2048]{1,0:T(8,128)(2,1)S(1)} %get-tuple-element.32), channel_id=1, source_target_pairs={{0,6},{1,7},{2,4},{3,5},{4,2},{5,3},{6,0},{7,1},{8,14},{9,15},{10,... | collective-permute-start | bytes 196616 | tf_op jit(solution)/shard_map/ppermute | solution.py:228
  24.1 0.0 copy-done.1
  24.1 0.2 reshape.72
  24.4 0.1 copy.15.refs_6_
  24.5 0.4 %collective-permute-done.5.refs_1_ = bf16[16,2048]{1,0:T(8,128)(2,1)S(1)} collective-permute-done((bf16[16,2048]{1,0:T(8,128)(2,1)S(1)}, bf16[16,2048]{1,0:T(8,128)(2,1)S(1)}, u32[]{:S(2)}, u32[]{:S(2)}) %collective-permute-start.5) | collective-permute-done | bytes 65568 | tf_op jit(solution)/shard_map/ppermute | solution.py:228
  24.9 1.4 %collective-permute-done.6.refs_2_ = bf16[16,2048]{1,0:T(8,128)(2,1)S(1)} collective-permute-done((bf16[16,2048]{1,0:T(8,128)(2,1)S(1)}, bf16[16,2048]{1,0:T(8,128)(2,1)S(1)}, u32[]{:S(2)}, u32[]{:S(2)}) %collective-permute-start.6) | collective-permute-done | bytes 65568 | tf_op jit(solution)/shard_map/ppermute | solution.py:228
  26.3 1.2 %collective-permute-done.7.refs_3_ = bf16[16,2048]{1,0:T(8,128)(2,1)S(1)} collective-permute-done((bf16[16,2048]{1,0:T(8,128)(2,1)S(1)}, bf16[16,2048]{1,0:T(8,128)(2,1)S(1)}, u32[]{:S(2)}, u32[]{:S(2)}) %collective-permute-start.7) | collective-permute-done | bytes 65568 | tf_op jit(solution)/shard_map/ppermute | solution.py:228
  27.4 1.0 %shard_map.76 = (bf16[4,8,2048]{2,1,0:T(8,128)(2,1)S(1)}, bf16[4,8,2048]{2,1,0:T(8,128)(2,1)S(1)}, bf16[16,1728]{1,0:T(8,128)(2,1)S(1)}) custom-call(bf16[16,2048]{1,0:T(8,128)(2,1)S(1)} %get-tuple-element.35.refs_0_, bf16[16,2048]{1,0:T(8,128)(2,1)S(1)} %collective-permute-done.5.refs_1_, bf16[16,2048]{1,0:T(8,128)(2,1)S(1)} %collective-permute-done.6.refs_2_, ...), custom_call_target="tpu_custom_call" | custom-call | flops 226492416 | bytes 1048576 | tf_op jit(solution)/shard_map/pallas_call | solution.py:317
  28.4 1.5 %collective-permute-start.12 = (bf16[16,1728]{1,0:T(8,128)(2,1)S(1)}, bf16[16,1728]{1,0:T(8,128)(2,1)S(1)}, u32[]{:S(2)}, u32[]{:S(2)}) collective-permute-start(bf16[16,1728]{1,0:T(8,128)(2,1)S(1)} %get-tuple-element.24), channel_id=1, source_target_pairs={{0,16},{8,24},{16,0},{24,8},{1,17},{9,25},{17,1},{25,9},{2,18},{10... | collective-permute-start | bytes 165896 | tf_op jit(solution)/shard_map/ppermute | solution.py:228
  29.9 1.9 %collective-permute-done.14 = bf16[32,3456]{1,0:T(8,128)(2,1)S(1)} collective-permute-done((bf16[32,3456]{1,0:T(8,128)(2,1)S(1)}, bf16[32,3456]{1,0:T(8,128)(2,1)S(1)}, u32[]{:S(2)}, u32[]{:S(2)}) %collective-permute-start.14) | collective-permute-done | bytes 221216 | tf_op jit(solution)/shard_map/ppermute | solution.py:228
  31.8 0.1 add_convert_fusion.refs_6_
  31.9 0.9 %collective-permute-start.15 = (bf16[32,3456]{1,0:T(8,128)(2,1)S(1)}, bf16[32,3456]{1,0:T(8,128)(2,1)S(1)}, u32[]{:S(2)}, u32[]{:S(2)}) collective-permute-start(bf16[32,3456]{1,0:T(8,128)(2,1)S(1)} %add_convert_fusion.refs_6_), channel_id=1, source_target_pairs={{0,8},{8,0},{16,24},{24,16},{1,9},{9,1},{17,25},{25,17},{2,10},{10... | collective-permute-start | bytes 663560 | tf_op jit(solution)/shard_map/ppermute | solution.py:228
  32.8 0.0 collective-permute-start.8
  32.8 0.7 %collective-permute-done.12 = bf16[16,1728]{1,0:T(8,128)(2,1)S(1)} collective-permute-done((bf16[16,1728]{1,0:T(8,128)(2,1)S(1)}, bf16[16,1728]{1,0:T(8,128)(2,1)S(1)}, u32[]{:S(2)}, u32[]{:S(2)}) %collective-permute-start.12) | collective-permute-done | bytes 55328 | tf_op jit(solution)/shard_map/ppermute | solution.py:228
  33.6 1.6 %collective-permute-start.13 = (bf16[16,1728]{1,0:T(8,128)(2,1)S(1)}, bf16[16,1728]{1,0:T(8,128)(2,1)S(1)}, u32[]{:S(2)}, u32[]{:S(2)}) collective-permute-start(bf16[16,1728]{1,0:T(8,128)(2,1)S(1)} %add_convert_fusion.5.refs_4_), channel_id=1, source_target_pairs={{0,8},{8,0},{16,24},{24,16},{1,9},{9,1},{17,25},{25,17},{2,10},{10... | collective-permute-start | bytes 165896 | tf_op jit(solution)/shard_map/ppermute | solution.py:228
  35.2 0.0 collective-permute-done.8
  35.3 1.1 %collective-permute-start.10 = (bf16[8,2048]{1,0:T(8,128)(2,1)S(1)}, bf16[8,2048]{1,0:T(8,128)(2,1)S(1)}, u32[]{:S(2)}, u32[]{:S(2)}) collective-permute-start(bf16[8,2048]{1,0:T(8,128)(2,1)S(1)} %get-tuple-element.37), channel_id=1, source_target_pairs={{0,4},{1,5},{2,6},{3,7},{4,0},{5,1},{6,2},{7,3},{8,12},{9,13},{10,... | collective-permute-start | bytes 98312 | tf_op jit(solution)/shard_map/ppermute | solution.py:228
  36.4 1.7 %collective-permute-start.11 = (bf16[8,2048]{1,0:T(8,128)(2,1)S(1)}, bf16[8,2048]{1,0:T(8,128)(2,1)S(1)}, u32[]{:S(2)}, u32[]{:S(2)}) collective-permute-start(bf16[8,2048]{1,0:T(8,128)(2,1)S(1)} %get-tuple-element.36), channel_id=1, source_target_pairs={{0,6},{1,7},{2,4},{3,5},{4,2},{5,3},{6,0},{7,1},{8,14},{9,15},{10,... | collective-permute-start | bytes 98312 | tf_op jit(solution)/shard_map/ppermute | solution.py:228
  38.1 0.7 %collective-permute-start.9 = (bf16[8,2048]{1,0:T(8,128)(2,1)S(1)}, bf16[8,2048]{1,0:T(8,128)(2,1)S(1)}, u32[]{:S(2)}, u32[]{:S(2)}) collective-permute-start(bf16[8,2048]{1,0:T(8,128)(2,1)S(1)} %get-tuple-element.38), channel_id=1, source_target_pairs={{0,2},{1,3},{2,0},{3,1},{4,6},{5,7},{6,4},{7,5},{8,10},{9,11},{10,... | collective-permute-start | bytes 98312 | tf_op jit(solution)/shard_map/ppermute | solution.py:228
  38.8 0.9 %collective-permute-done.13.refs_5_ = bf16[16,1728]{1,0:T(8,128)(2,1)S(1)} collective-permute-done((bf16[16,1728]{1,0:T(8,128)(2,1)S(1)}, bf16[16,1728]{1,0:T(8,128)(2,1)S(1)}, u32[]{:S(2)}, u32[]{:S(2)}) %collective-permute-start.13) | collective-permute-done | bytes 55328 | tf_op jit(solution)/shard_map/ppermute | solution.py:228
  39.7 0.0 collective-permute-done.10.refs_2_
  39.7 1.5 %collective-permute-done.11.refs_3_ = bf16[8,2048]{1,0:T(8,128)(2,1)S(1)} collective-permute-done((bf16[8,2048]{1,0:T(8,128)(2,1)S(1)}, bf16[8,2048]{1,0:T(8,128)(2,1)S(1)}, u32[]{:S(2)}, u32[]{:S(2)}) %collective-permute-start.11) | collective-permute-done | bytes 32800 | tf_op jit(solution)/shard_map/ppermute | solution.py:228
  41.2 0.8 %collective-permute-done.9.refs_1_ = bf16[8,2048]{1,0:T(8,128)(2,1)S(1)} collective-permute-done((bf16[8,2048]{1,0:T(8,128)(2,1)S(1)}, bf16[8,2048]{1,0:T(8,128)(2,1)S(1)}, u32[]{:S(2)}, u32[]{:S(2)}) %collective-permute-start.9) | collective-permute-done | bytes 32800 | tf_op jit(solution)/shard_map/ppermute | solution.py:228
  42.0 0.0 collective-permute-done.15.refs_7_
  42.0 0.9 %shard_map.77 = (bf16[32,2048]{1,0:T(8,128)(2,1)}, bf16[8,2048]{1,0:T(8,128)(2,1)}, f32[16,1728]{1,0:T(8,128)}, f32[32,3456]{1,0:T(8,128)}) custom-call(bf16[8,2048]{1,0:T(8,128)(2,1)S(1)} %get-tuple-element.39.refs_0_, bf16[8,2048]{1,0:T(8,128)(2,1)S(1)} %collective-permute-done.9.refs_1_, bf16[8,2048]{1,0:T(8,128)(2,1)S(1)} %collective-permute-done.10.refs_2_, ...), custom_call_target="tpu_custom_call" | custom-call | bytes 2097152 | tf_op jit(solution)/shard_map/pallas_call | solution.py:342
  (4 shorter events, 0.1 us)
Async XLA Ops:
  1.5 6.1 %collective-permute-start = (bf16[24,2048]{1,0:T(8,128)(2,1)S(1)}, bf16[24,2048]{1,0:T(8,128)(2,1)S(1)}, u32[]{:S(2)}, u32[]{:S(2)}) collective-permute-start(bf16[24,2048]{1,0:T(8,128)(2,1)S(1)} %get-tuple-element.41), channel_id=1, source_target_pairs={{0,2},{1,3},{2,0},{3,1},{4,6},{5,7},{6,4},{7,5},{8,10},{9,11},{10,... | collective-permute-start | bytes 294920 | tf_op jit(solution)/shard_map/ppermute | solution.py:228
  4.5 5.7 %collective-permute-start.1 = (bf16[24,2048]{1,0:T(8,128)(2,1)S(1)}, bf16[24,2048]{1,0:T(8,128)(2,1)S(1)}, u32[]{:S(2)}, u32[]{:S(2)}) collective-permute-start(bf16[24,2048]{1,0:T(8,128)(2,1)S(1)} %get-tuple-element.41), channel_id=1, source_target_pairs={{0,4},{1,5},{2,6},{3,7},{4,0},{5,1},{6,2},{7,3},{8,12},{9,13},{10,... | collective-permute-start | bytes 294920 | tf_op jit(solution)/shard_map/ppermute | solution.py:228
  6.0 5.5 %collective-permute-start.2 = (bf16[24,2048]{1,0:T(8,128)(2,1)S(1)}, bf16[24,2048]{1,0:T(8,128)(2,1)S(1)}, u32[]{:S(2)}, u32[]{:S(2)}) collective-permute-start(bf16[24,2048]{1,0:T(8,128)(2,1)S(1)} %get-tuple-element.41), channel_id=1, source_target_pairs={{0,6},{1,7},{2,4},{3,5},{4,2},{5,3},{6,0},{7,1},{8,14},{9,15},{10,... | collective-permute-start | bytes 294920 | tf_op jit(solution)/shard_map/ppermute | solution.py:228
  11.5 0.9 %copy-start.2 = (bf16[32,3456]{1,0:T(8,128)(2,1)S(1)}, bf16[32,3456]{1,0:T(8,128)(2,1)}, u32[]{:S(2)}) copy-start(bf16[32,3456]{1,0:T(8,128)(2,1)} %param.6) | copy-start | bytes 663556
  11.6 1.8 %collective-permute-start.3 = (bf16[4,24,2048]{2,1,0:T(8,128)(2,1)S(1)}, bf16[4,24,2048]{2,1,0:T(8,128)(2,1)S(1)}, u32[]{:S(2)}, u32[]{:S(2)}) collective-permute-start(bf16[4,24,2048]{2,1,0:T(8,128)(2,1)S(1)} %pad_maximum_fusion.refs_0_), channel_id=1, source_target_pairs={{0,1},{1,0},{2,3},{3,2},{4,5},{5,4},{6,7},{7,6},{8,9},{9,8},{10,11... | collective-permute-start | bytes 1179656 | tf_op jit(solution)/shard_map/ppermute | solution.py:228
  12.8 0.9 %copy-start = (bf16[32,1,2048]{2,0,1:T(8,128)(2,1)S(1)}, bf16[32,1,2048]{2,0,1:T(8,128)(2,1)}, u32[]{:S(2)}) copy-start(bf16[32,1,2048]{2,0,1:T(8,128)(2,1)} %param.7) | copy-start | bytes 393220
  17.8 2.7 %collective-permute-start.4 = (bf16[4,16,2048]{2,1,0:T(8,128)(2,1)S(1)}, bf16[4,16,2048]{2,1,0:T(8,128)(2,1)S(1)}, u32[]{:S(2)}, u32[]{:S(2)}) collective-permute-start(bf16[4,16,2048]{2,1,0:T(8,128)(2,1)S(1)} %get-tuple-element.19), channel_id=1, source_target_pairs={{0,1},{1,0},{2,3},{3,2},{4,5},{5,4},{6,7},{7,6},{8,9},{9,8},{10,11... | collective-permute-start | bytes 786440 | tf_op jit(solution)/shard_map/ppermute | solution.py:228
  17.9 13.9 %collective-permute-start.14 = (bf16[32,3456]{1,0:T(8,128)(2,1)S(1)}, bf16[32,3456]{1,0:T(8,128)(2,1)S(1)}, u32[]{:S(2)}, u32[]{:S(2)}) collective-permute-start(bf16[32,3456]{1,0:T(8,128)(2,1)S(1)} %get-tuple-element.25), channel_id=1, source_target_pairs={{0,16},{8,24},{16,0},{24,8},{1,17},{9,25},{17,1},{25,9},{2,18},{10... | collective-permute-start | bytes 663560 | tf_op jit(solution)/shard_map/ppermute | solution.py:228
  20.5 3.6 %copy-start.1 = (bf16[16,1728]{1,0:T(8,128)(2,1)S(1)}, bf16[16,1728]{1,0:T(8,128)(2,1)}, u32[]{:S(2)}) copy-start(bf16[16,1728]{1,0:T(8,128)(2,1)} %param.5) | copy-start | bytes 165892
  20.6 4.3 %collective-permute-start.5 = (bf16[16,2048]{1,0:T(8,128)(2,1)S(1)}, bf16[16,2048]{1,0:T(8,128)(2,1)S(1)}, u32[]{:S(2)}, u32[]{:S(2)}) collective-permute-start(bf16[16,2048]{1,0:T(8,128)(2,1)S(1)} %get-tuple-element.34), channel_id=1, source_target_pairs={{0,2},{1,3},{2,0},{3,1},{4,6},{5,7},{6,4},{7,5},{8,10},{9,11},{10,... | collective-permute-start | bytes 196616 | tf_op jit(solution)/shard_map/ppermute | solution.py:228
  21.3 5.0 %collective-permute-start.6 = (bf16[16,2048]{1,0:T(8,128)(2,1)S(1)}, bf16[16,2048]{1,0:T(8,128)(2,1)S(1)}, u32[]{:S(2)}, u32[]{:S(2)}) collective-permute-start(bf16[16,2048]{1,0:T(8,128)(2,1)S(1)} %get-tuple-element.33), channel_id=1, source_target_pairs={{0,4},{1,5},{2,6},{3,7},{4,0},{5,1},{6,2},{7,3},{8,12},{9,13},{10,... | collective-permute-start | bytes 196616 | tf_op jit(solution)/shard_map/ppermute | solution.py:228
  22.3 5.2 %collective-permute-start.7 = (bf16[16,2048]{1,0:T(8,128)(2,1)S(1)}, bf16[16,2048]{1,0:T(8,128)(2,1)S(1)}, u32[]{:S(2)}, u32[]{:S(2)}) collective-permute-start(bf16[16,2048]{1,0:T(8,128)(2,1)S(1)} %get-tuple-element.32), channel_id=1, source_target_pairs={{0,6},{1,7},{2,4},{3,5},{4,2},{5,3},{6,0},{7,1},{8,14},{9,15},{10,... | collective-permute-start | bytes 196616 | tf_op jit(solution)/shard_map/ppermute | solution.py:228
  28.4 5.1 %collective-permute-start.12 = (bf16[16,1728]{1,0:T(8,128)(2,1)S(1)}, bf16[16,1728]{1,0:T(8,128)(2,1)S(1)}, u32[]{:S(2)}, u32[]{:S(2)}) collective-permute-start(bf16[16,1728]{1,0:T(8,128)(2,1)S(1)} %get-tuple-element.24), channel_id=1, source_target_pairs={{0,16},{8,24},{16,0},{24,8},{1,17},{9,25},{17,1},{25,9},{2,18},{10... | collective-permute-start | bytes 165896 | tf_op jit(solution)/shard_map/ppermute | solution.py:228
  31.9 10.2 %collective-permute-start.15 = (bf16[32,3456]{1,0:T(8,128)(2,1)S(1)}, bf16[32,3456]{1,0:T(8,128)(2,1)S(1)}, u32[]{:S(2)}, u32[]{:S(2)}) collective-permute-start(bf16[32,3456]{1,0:T(8,128)(2,1)S(1)} %add_convert_fusion.refs_6_), channel_id=1, source_target_pairs={{0,8},{8,0},{16,24},{24,16},{1,9},{9,1},{17,25},{25,17},{2,10},{10... | collective-permute-start | bytes 663560 | tf_op jit(solution)/shard_map/ppermute | solution.py:228
  32.8 2.4 %collective-permute-start.8 = (bf16[4,8,2048]{2,1,0:T(8,128)(2,1)S(1)}, bf16[4,8,2048]{2,1,0:T(8,128)(2,1)S(1)}, u32[]{:S(2)}, u32[]{:S(2)}) collective-permute-start(bf16[4,8,2048]{2,1,0:T(8,128)(2,1)S(1)} %get-tuple-element.23), channel_id=1, source_target_pairs={{0,1},{1,0},{2,3},{3,2},{4,5},{5,4},{6,7},{7,6},{8,9},{9,8},{10,11... | collective-permute-start | bytes 393224 | tf_op jit(solution)/shard_map/ppermute | solution.py:228
  33.6 6.1 %collective-permute-start.13 = (bf16[16,1728]{1,0:T(8,128)(2,1)S(1)}, bf16[16,1728]{1,0:T(8,128)(2,1)S(1)}, u32[]{:S(2)}, u32[]{:S(2)}) collective-permute-start(bf16[16,1728]{1,0:T(8,128)(2,1)S(1)} %add_convert_fusion.5.refs_4_), channel_id=1, source_target_pairs={{0,8},{8,0},{16,24},{24,16},{1,9},{9,1},{17,25},{25,17},{2,10},{10... | collective-permute-start | bytes 165896 | tf_op jit(solution)/shard_map/ppermute | solution.py:228
  35.3 4.5 %collective-permute-start.10 = (bf16[8,2048]{1,0:T(8,128)(2,1)S(1)}, bf16[8,2048]{1,0:T(8,128)(2,1)S(1)}, u32[]{:S(2)}, u32[]{:S(2)}) collective-permute-start(bf16[8,2048]{1,0:T(8,128)(2,1)S(1)} %get-tuple-element.37), channel_id=1, source_target_pairs={{0,4},{1,5},{2,6},{3,7},{4,0},{5,1},{6,2},{7,3},{8,12},{9,13},{10,... | collective-permute-start | bytes 98312 | tf_op jit(solution)/shard_map/ppermute | solution.py:228
  36.4 4.8 %collective-permute-start.11 = (bf16[8,2048]{1,0:T(8,128)(2,1)S(1)}, bf16[8,2048]{1,0:T(8,128)(2,1)S(1)}, u32[]{:S(2)}, u32[]{:S(2)}) collective-permute-start(bf16[8,2048]{1,0:T(8,128)(2,1)S(1)} %get-tuple-element.36), channel_id=1, source_target_pairs={{0,6},{1,7},{2,4},{3,5},{4,2},{5,3},{6,0},{7,1},{8,14},{9,15},{10,... | collective-permute-start | bytes 98312 | tf_op jit(solution)/shard_map/ppermute | solution.py:228
  38.1 3.9 %collective-permute-start.9 = (bf16[8,2048]{1,0:T(8,128)(2,1)S(1)}, bf16[8,2048]{1,0:T(8,128)(2,1)S(1)}, u32[]{:S(2)}, u32[]{:S(2)}) collective-permute-start(bf16[8,2048]{1,0:T(8,128)(2,1)S(1)} %get-tuple-element.38), channel_id=1, source_target_pairs={{0,2},{1,3},{2,0},{3,1},{4,6},{5,7},{6,4},{7,5},{8,10},{9,11},{10,... | collective-permute-start | bytes 98312 | tf_op jit(solution)/shard_map/ppermute | solution.py:228

commit v12 on v11

--- a/solution.py
+++ b/solution.py
@@ -332,11 +332,11 @@
     got = swap(give, "mp", 1)
     ins = sum_over_chips(keep, got)
 
-    second_got, *_ = lax.optimization_barrier((second_got, grad_first))
-    for bit in bits[:-1]:
-        grad_first = add(grad_first, swap(grad_first, "sample", bit))
-    first_got = swap(grad_first, "sample", bits[-1])
+    first_got = swap(grad_first, "sample", bits[0])
+    second_got, first_got = lax.optimization_barrier((second_got, first_got))
     for bit in bits[1:]:
+        grad_first = add(grad_first, first_got)
+        first_got = swap(grad_first, "sample", bit)
         grad_second = add(grad_second, second_got)
         second_got = swap(grad_second, "sample", bit)
     features, input_grad, grad_first, grad_second = call(

time: 43.1 us -> 43.7 us (1.014)
  waiting for transfers between devices: 14.6 us -> 15.6 us
    ppermute x16, waiting for transfers between devices: 14.6 us -> 15.6 us  [swap(): return lax.ppermute(value, axis, [(i, i ^ k) for i in range(n)])]
where the time goes in v12:
time: 43.7 us; the launch traced here: 43.5 us
  starting transfers between devices  18.1 us (41%)
  waiting for transfers between devices  15.6 us (36%)
  Pallas kernels  5.89 us (13%)
  local copies, waits for them, and re-layouts  2.01 us (5%)
  other arithmetic  1.08 us (2%)
  between operations  0.76 us (2%)
    ppermute x16, starting transfers between devices, swap(): return lax.ppermute(value, axis, [(i, i ^ k) for i in range(n)])  18.1 us
    ppermute x16, waiting for transfers between devices, swap(): return lax.ppermute(value, axis, [(i, i ^ k) for i in range(n)])  15.6 us
    pallas_call x1, Pallas kernels, local(): call(functools.partial(forward_kernel, n_mp, c0), [sds((f2, cells), BF16)...  4.03 us
    unnamed x7, local copies, waits for them, and re-layouts  1.21 us
    pallas_call x1, Pallas kernels, local(): call(functools.partial(backward_kernel, n_mp), [sds((half, rows_in, cells...  0.98 us
    another operation x2, other arithmetic, local(): near = jnp.stack(near)  0.91 us
    pallas_call x1, Pallas kernels, local(): call(functools.partial(finish_kernel, scale, half), [sds((f2, cells), BF1...  0.88 us
  transfers between devices with their start and end apart: 16, of which 12 were waited for; matrix products, arithmetic and copies ran while one was open for 2% of the time, Pallas kernels for 2%

profile of v12, /device:TPU:0, one launch (start us, length us, event | category | flops | bytes accessed | tf_op | source)
XLA Modules:
  0.0 43.5 jit_solution(1700081553589058165)
XLA Ops:
  0.6 0.9 %fusion.10 = (bf16[1,24,2048]{2,1,0:T(8,128)(2,1)S(1)}, bf16[24,2048]{1,0:T(8,128)(2,1)S(1)}) fusion(bf16[8,2048]{1,0:T(8,128)(2,1)} %bitcast.46, bf16[16,1728]{1,0:T(8,128)(2,1)} %param.5), kind=kLoop, calls=%fused_computation.23 | loop fusion | flops 294912 | bytes 284672 | tf_op jit(solution)/shard_map/stack | solution.py:278
  1.5 3.0 %collective-permute-start = (bf16[24,2048]{1,0:T(8,128)(2,1)S(1)}, bf16[24,2048]{1,0:T(8,128)(2,1)S(1)}, u32[]{:S(2)}, u32[]{:S(2)}) collective-permute-start(bf16[24,2048]{1,0:T(8,128)(2,1)S(1)} %get-tuple-element.43), channel_id=1, source_target_pairs={{0,2},{1,3},{2,0},{3,1},{4,6},{5,7},{6,4},{7,5},{8,10},{9,11},{10,... | collective-permute-start | bytes 294920 | tf_op jit(solution)/shard_map/ppermute | solution.py:228
  4.5 1.5 %collective-permute-start.1 = (bf16[24,2048]{1,0:T(8,128)(2,1)S(1)}, bf16[24,2048]{1,0:T(8,128)(2,1)S(1)}, u32[]{:S(2)}, u32[]{:S(2)}) collective-permute-start(bf16[24,2048]{1,0:T(8,128)(2,1)S(1)} %get-tuple-element.43), channel_id=1, source_target_pairs={{0,4},{1,5},{2,6},{3,7},{4,0},{5,1},{6,2},{7,3},{8,12},{9,13},{10,... | collective-permute-start | bytes 294920 | tf_op jit(solution)/shard_map/ppermute | solution.py:228
  6.0 0.0 collective-permute-start.2
  6.0 1.5 %collective-permute-done = bf16[24,2048]{1,0:T(8,128)(2,1)S(1)} collective-permute-done((bf16[24,2048]{1,0:T(8,128)(2,1)S(1)}, bf16[24,2048]{1,0:T(8,128)(2,1)S(1)}, u32[]{:S(2)}, u32[]{:S(2)}) %collective-permute-start) | collective-permute-done | bytes 98336 | tf_op jit(solution)/shard_map/ppermute | solution.py:228
  7.5 2.6 %collective-permute-done.1 = bf16[24,2048]{1,0:T(8,128)(2,1)S(1)} collective-permute-done((bf16[24,2048]{1,0:T(8,128)(2,1)S(1)}, bf16[24,2048]{1,0:T(8,128)(2,1)S(1)}, u32[]{:S(2)}, u32[]{:S(2)}) %collective-permute-start.1) | collective-permute-done | bytes 98336 | tf_op jit(solution)/shard_map/ppermute | solution.py:228
  10.2 1.4 %collective-permute-done.2 = bf16[24,2048]{1,0:T(8,128)(2,1)S(1)} collective-permute-done((bf16[24,2048]{1,0:T(8,128)(2,1)S(1)}, bf16[24,2048]{1,0:T(8,128)(2,1)S(1)}, u32[]{:S(2)}, u32[]{:S(2)}) %collective-permute-start.2) | collective-permute-done | bytes 98336 | tf_op jit(solution)/shard_map/ppermute | solution.py:228
  11.5 0.0 copy-start.2
  11.5 0.1 pad_maximum_fusion.refs_0_
  11.6 0.1 collective-permute-start.3
  11.7 0.8 %copy-done.2 = bf16[32,3456]{1,0:T(8,128)(2,1)S(1)} copy-done((bf16[32,3456]{1,0:T(8,128)(2,1)S(1)}, bf16[32,3456]{1,0:T(8,128)(2,1)}, u32[]{:S(2)}) %copy-start.2) | copy-done | bytes 221208
  12.5 0.1 reshape.68
  12.6 0.1 copy.11
  12.8 0.1 copy.12
  12.8 0.0 copy-start
  12.8 0.2 copy.13.refs_3_
  13.0 0.4 collective-permute-done.3.refs_1_
  13.4 0.4 copy-done
  13.7 4.0 %shard_map.75 = (bf16[32,2048]{1,0:T(8,128)(2,1)S(1)}, f32[16,2048]{1,0:T(8,128)S(1)}, bf16[64,2048]{1,0:T(8,128)(2,1)S(1)}, bf16[4,16,2048]{2,1,0:T(8,128)(2,1)...) custom-call(bf16[4,24,2048]{2,1,0:T(8,128)(2,1)S(1)} %pad_maximum_fusion.refs_0_, ...), custom_call_target="tpu_custom_call" | custom-call | flops 2264924160 | bytes 4194304 | tf_op jit(solution)/shard_map/pallas_call | solution.py:288
  17.8 0.1 collective-permute-start.4
  17.9 2.7 %collective-permute-start.12 = (bf16[32,3456]{1,0:T(8,128)(2,1)S(1)}, bf16[32,3456]{1,0:T(8,128)(2,1)S(1)}, u32[]{:S(2)}, u32[]{:S(2)}) collective-permute-start(bf16[32,3456]{1,0:T(8,128)(2,1)S(1)} %get-tuple-element.26), channel_id=1, source_target_pairs={{0,16},{8,24},{16,0},{24,8},{1,17},{9,25},{17,1},{25,9},{2,18},{10... | collective-permute-start | bytes 663560 | tf_op jit(solution)/shard_map/ppermute | solution.py:228
  20.5 0.0 collective-permute-done.4
  20.5 0.0 copy-start.1
  20.5 0.1 fusion.5
  20.6 0.7 %collective-permute-start.5 = (bf16[16,2048]{1,0:T(8,128)(2,1)S(1)}, bf16[16,2048]{1,0:T(8,128)(2,1)S(1)}, u32[]{:S(2)}, u32[]{:S(2)}) collective-permute-start(bf16[16,2048]{1,0:T(8,128)(2,1)S(1)} %get-tuple-element.36), channel_id=1, source_target_pairs={{0,2},{1,3},{2,0},{3,1},{4,6},{5,7},{6,4},{7,5},{8,10},{9,11},{10,... | collective-permute-start | bytes 196616 | tf_op jit(solution)/shard_map/ppermute | solution.py:228
  21.3 1.0 %collective-permute-start.6 = (bf16[16,2048]{1,0:T(8,128)(2,1)S(1)}, bf16[16,2048]{1,0:T(8,128)(2,1)S(1)}, u32[]{:S(2)}, u32[]{:S(2)}) collective-permute-start(bf16[16,2048]{1,0:T(8,128)(2,1)S(1)} %get-tuple-element.35), channel_id=1, source_target_pairs={{0,4},{1,5},{2,6},{3,7},{4,0},{5,1},{6,2},{7,3},{8,12},{9,13},{10,... | collective-permute-start | bytes 196616 | tf_op jit(solution)/shard_map/ppermute | solution.py:228
  22.3 1.9 %collective-permute-start.7 = (bf16[16,2048]{1,0:T(8,128)(2,1)S(1)}, bf16[16,2048]{1,0:T(8,128)(2,1)S(1)}, u32[]{:S(2)}, u32[]{:S(2)}) collective-permute-start(bf16[16,2048]{1,0:T(8,128)(2,1)S(1)} %get-tuple-element.34), channel_id=1, source_target_pairs={{0,6},{1,7},{2,4},{3,5},{4,2},{5,3},{6,0},{7,1},{8,14},{9,15},{10,... | collective-permute-start | bytes 196616 | tf_op jit(solution)/shard_map/ppermute | solution.py:228
  24.1 0.0 copy-done.1
  24.1 0.2 reshape.72
  24.4 0.1 copy.15.refs_6_
  24.5 0.4 collective-permute-done.5.refs_1_
  24.9 1.4 %collective-permute-done.6.refs_2_ = bf16[16,2048]{1,0:T(8,128)(2,1)S(1)} collective-permute-done((bf16[16,2048]{1,0:T(8,128)(2,1)S(1)}, bf16[16,2048]{1,0:T(8,128)(2,1)S(1)}, u32[]{:S(2)}, u32[]{:S(2)}) %collective-permute-start.6) | collective-permute-done | bytes 65568 | tf_op jit(solution)/shard_map/ppermute | solution.py:228
  26.3 1.2 %collective-permute-done.7.refs_3_ = bf16[16,2048]{1,0:T(8,128)(2,1)S(1)} collective-permute-done((bf16[16,2048]{1,0:T(8,128)(2,1)S(1)}, bf16[16,2048]{1,0:T(8,128)(2,1)S(1)}, u32[]{:S(2)}, u32[]{:S(2)}) %collective-permute-start.7) | collective-permute-done | bytes 65568 | tf_op jit(solution)/shard_map/ppermute | solution.py:228
  27.4 1.0 %shard_map.76 = (bf16[4,8,2048]{2,1,0:T(8,128)(2,1)S(1)}, bf16[4,8,2048]{2,1,0:T(8,128)(2,1)S(1)}, bf16[16,1728]{1,0:T(8,128)(2,1)S(1)}) custom-call(bf16[16,2048]{1,0:T(8,128)(2,1)S(1)} %get-tuple-element.37.refs_0_, bf16[16,2048]{1,0:T(8,128)(2,1)S(1)} %collective-permute-done.5.refs_1_, bf16[16,2048]{1,0:T(8,128)(2,1)S(1)} %collective-permute-done.6.refs_2_, ...), custom_call_target="tpu_custom_call" | custom-call | flops 226492416 | bytes 1048576 | tf_op jit(solution)/shard_map/pallas_call | solution.py:317
  28.4 1.5 %collective-permute-start.13 = (bf16[16,1728]{1,0:T(8,128)(2,1)S(1)}, bf16[16,1728]{1,0:T(8,128)(2,1)S(1)}, u32[]{:S(2)}, u32[]{:S(2)}) collective-permute-start(bf16[16,1728]{1,0:T(8,128)(2,1)S(1)} %get-tuple-element.25), channel_id=1, source_target_pairs={{0,16},{8,24},{16,0},{24,8},{1,17},{9,25},{17,1},{25,9},{2,18},{10... | collective-permute-start | bytes 165896 | tf_op jit(solution)/shard_map/ppermute | solution.py:228
  29.9 0.0 collective-permute-start.8
  29.9 1.9 %collective-permute-done.12 = bf16[32,3456]{1,0:T(8,128)(2,1)S(1)} collective-permute-done((bf16[32,3456]{1,0:T(8,128)(2,1)S(1)}, bf16[32,3456]{1,0:T(8,128)(2,1)S(1)}, u32[]{:S(2)}, u32[]{:S(2)}) %collective-permute-start.12) | collective-permute-done | bytes 221216 | tf_op jit(solution)/shard_map/ppermute | solution.py:228
  31.8 1.7 %collective-permute-done.13 = bf16[16,1728]{1,0:T(8,128)(2,1)S(1)} collective-permute-done((bf16[16,1728]{1,0:T(8,128)(2,1)S(1)}, bf16[16,1728]{1,0:T(8,128)(2,1)S(1)}, u32[]{:S(2)}, u32[]{:S(2)}) %collective-permute-start.13) | collective-permute-done | bytes 55328 | tf_op jit(solution)/shard_map/ppermute | solution.py:228
  33.6 0.1 add_convert_fusion.refs_6_
  33.6 1.6 %collective-permute-start.15 = (bf16[32,3456]{1,0:T(8,128)(2,1)S(1)}, bf16[32,3456]{1,0:T(8,128)(2,1)S(1)}, u32[]{:S(2)}, u32[]{:S(2)}) collective-permute-start(bf16[32,3456]{1,0:T(8,128)(2,1)S(1)} %add_convert_fusion.refs_6_), channel_id=1, source_target_pairs={{0,8},{8,0},{16,24},{24,16},{1,9},{9,1},{17,25},{25,17},{2,10},{10... | collective-permute-start | bytes 663560 | tf_op jit(solution)/shard_map/ppermute | solution.py:228
  35.3 0.5 %collective-permute-start.14 = (bf16[16,1728]{1,0:T(8,128)(2,1)S(1)}, bf16[16,1728]{1,0:T(8,128)(2,1)S(1)}, u32[]{:S(2)}, u32[]{:S(2)}) collective-permute-start(bf16[16,1728]{1,0:T(8,128)(2,1)S(1)} %add_convert_fusion.5.refs_4_), channel_id=1, source_target_pairs={{0,8},{8,0},{16,24},{24,16},{1,9},{9,1},{17,25},{25,17},{2,10},{10... | collective-permute-start | bytes 165896 | tf_op jit(solution)/shard_map/ppermute | solution.py:228
  35.8 0.0 collective-permute-done.8
  35.8 1.1 %collective-permute-start.10 = (bf16[8,2048]{1,0:T(8,128)(2,1)S(1)}, bf16[8,2048]{1,0:T(8,128)(2,1)S(1)}, u32[]{:S(2)}, u32[]{:S(2)}) collective-permute-start(bf16[8,2048]{1,0:T(8,128)(2,1)S(1)} %get-tuple-element.39), channel_id=1, source_target_pairs={{0,4},{1,5},{2,6},{3,7},{4,0},{5,1},{6,2},{7,3},{8,12},{9,13},{10,... | collective-permute-start | bytes 98312 | tf_op jit(solution)/shard_map/ppermute | solution.py:228
  37.0 1.7 %collective-permute-start.11 = (bf16[8,2048]{1,0:T(8,128)(2,1)S(1)}, bf16[8,2048]{1,0:T(8,128)(2,1)S(1)}, u32[]{:S(2)}, u32[]{:S(2)}) collective-permute-start(bf16[8,2048]{1,0:T(8,128)(2,1)S(1)} %get-tuple-element.38), channel_id=1, source_target_pairs={{0,6},{1,7},{2,4},{3,5},{4,2},{5,3},{6,0},{7,1},{8,14},{9,15},{10,... | collective-permute-start | bytes 98312 | tf_op jit(solution)/shard_map/ppermute | solution.py:228
  38.7 0.7 %collective-permute-start.9 = (bf16[8,2048]{1,0:T(8,128)(2,1)S(1)}, bf16[8,2048]{1,0:T(8,128)(2,1)S(1)}, u32[]{:S(2)}, u32[]{:S(2)}) collective-permute-start(bf16[8,2048]{1,0:T(8,128)(2,1)S(1)} %get-tuple-element.40), channel_id=1, source_target_pairs={{0,2},{1,3},{2,0},{3,1},{4,6},{5,7},{6,4},{7,5},{8,10},{9,11},{10,... | collective-permute-start | bytes 98312 | tf_op jit(solution)/shard_map/ppermute | solution.py:228
  39.4 2.1 %collective-permute-done.14.refs_5_ = bf16[16,1728]{1,0:T(8,128)(2,1)S(1)} collective-permute-done((bf16[16,1728]{1,0:T(8,128)(2,1)S(1)}, bf16[16,1728]{1,0:T(8,128)(2,1)S(1)}, u32[]{:S(2)}, u32[]{:S(2)}) %collective-permute-start.14) | collective-permute-done | bytes 55328 | tf_op jit(solution)/shard_map/ppermute | solution.py:228
  41.5 0.0 collective-permute-done.10.refs_2_
  41.5 0.3 collective-permute-done.11.refs_3_
  41.8 0.8 %collective-permute-done.9.refs_1_ = bf16[8,2048]{1,0:T(8,128)(2,1)S(1)} collective-permute-done((bf16[8,2048]{1,0:T(8,128)(2,1)S(1)}, bf16[8,2048]{1,0:T(8,128)(2,1)S(1)}, u32[]{:S(2)}, u32[]{:S(2)}) %collective-permute-start.9) | collective-permute-done | bytes 32800 | tf_op jit(solution)/shard_map/ppermute | solution.py:228
  42.6 0.0 collective-permute-done.15.refs_7_
  42.6 0.9 %shard_map.77 = (bf16[32,2048]{1,0:T(8,128)(2,1)}, bf16[8,2048]{1,0:T(8,128)(2,1)}, f32[16,1728]{1,0:T(8,128)}, f32[32,3456]{1,0:T(8,128)}) custom-call(bf16[8,2048]{1,0:T(8,128)(2,1)S(1)} %get-tuple-element.41.refs_0_, bf16[8,2048]{1,0:T(8,128)(2,1)S(1)} %collective-permute-done.9.refs_1_, bf16[8,2048]{1,0:T(8,128)(2,1)S(1)} %collective-permute-done.10.refs_2_, ...), custom_call_target="tpu_custom_call" | custom-call | bytes 2097152 | tf_op jit(solution)/shard_map/pallas_call | solution.py:342
  (4 shorter events, 0.1 us)
Async XLA Ops:
  1.5 6.1 %collective-permute-start = (bf16[24,2048]{1,0:T(8,128)(2,1)S(1)}, bf16[24,2048]{1,0:T(8,128)(2,1)S(1)}, u32[]{:S(2)}, u32[]{:S(2)}) collective-permute-start(bf16[24,2048]{1,0:T(8,128)(2,1)S(1)} %get-tuple-element.43), channel_id=1, source_target_pairs={{0,2},{1,3},{2,0},{3,1},{4,6},{5,7},{6,4},{7,5},{8,10},{9,11},{10,... | collective-permute-start | bytes 294920 | tf_op jit(solution)/shard_map/ppermute | solution.py:228
  4.5 5.7 %collective-permute-start.1 = (bf16[24,2048]{1,0:T(8,128)(2,1)S(1)}, bf16[24,2048]{1,0:T(8,128)(2,1)S(1)}, u32[]{:S(2)}, u32[]{:S(2)}) collective-permute-start(bf16[24,2048]{1,0:T(8,128)(2,1)S(1)} %get-tuple-element.43), channel_id=1, source_target_pairs={{0,4},{1,5},{2,6},{3,7},{4,0},{5,1},{6,2},{7,3},{8,12},{9,13},{10,... | collective-permute-start | bytes 294920 | tf_op jit(solution)/shard_map/ppermute | solution.py:228
  6.0 5.5 %collective-permute-start.2 = (bf16[24,2048]{1,0:T(8,128)(2,1)S(1)}, bf16[24,2048]{1,0:T(8,128)(2,1)S(1)}, u32[]{:S(2)}, u32[]{:S(2)}) collective-permute-start(bf16[24,2048]{1,0:T(8,128)(2,1)S(1)} %get-tuple-element.43), channel_id=1, source_target_pairs={{0,6},{1,7},{2,4},{3,5},{4,2},{5,3},{6,0},{7,1},{8,14},{9,15},{10,... | collective-permute-start | bytes 294920 | tf_op jit(solution)/shard_map/ppermute | solution.py:228
  11.5 0.9 %copy-start.2 = (bf16[32,3456]{1,0:T(8,128)(2,1)S(1)}, bf16[32,3456]{1,0:T(8,128)(2,1)}, u32[]{:S(2)}) copy-start(bf16[32,3456]{1,0:T(8,128)(2,1)} %param.6) | copy-start | bytes 663556
  11.6 1.8 %collective-permute-start.3 = (bf16[4,24,2048]{2,1,0:T(8,128)(2,1)S(1)}, bf16[4,24,2048]{2,1,0:T(8,128)(2,1)S(1)}, u32[]{:S(2)}, u32[]{:S(2)}) collective-permute-start(bf16[4,24,2048]{2,1,0:T(8,128)(2,1)S(1)} %pad_maximum_fusion.refs_0_), channel_id=1, source_target_pairs={{0,1},{1,0},{2,3},{3,2},{4,5},{5,4},{6,7},{7,6},{8,9},{9,8},{10,11... | collective-permute-start | bytes 1179656 | tf_op jit(solution)/shard_map/ppermute | solution.py:228
  12.8 0.9 %copy-start = (bf16[32,1,2048]{2,0,1:T(8,128)(2,1)S(1)}, bf16[32,1,2048]{2,0,1:T(8,128)(2,1)}, u32[]{:S(2)}) copy-start(bf16[32,1,2048]{2,0,1:T(8,128)(2,1)} %param.7) | copy-start | bytes 393220
  17.8 2.7 %collective-permute-start.4 = (bf16[4,16,2048]{2,1,0:T(8,128)(2,1)S(1)}, bf16[4,16,2048]{2,1,0:T(8,128)(2,1)S(1)}, u32[]{:S(2)}, u32[]{:S(2)}) collective-permute-start(bf16[4,16,2048]{2,1,0:T(8,128)(2,1)S(1)} %get-tuple-element.20), channel_id=1, source_target_pairs={{0,1},{1,0},{2,3},{3,2},{4,5},{5,4},{6,7},{7,6},{8,9},{9,8},{10,11... | collective-permute-start | bytes 786440 | tf_op jit(solution)/shard_map/ppermute | solution.py:228
  17.9 13.9 %collective-permute-start.12 = (bf16[32,3456]{1,0:T(8,128)(2,1)S(1)}, bf16[32,3456]{1,0:T(8,128)(2,1)S(1)}, u32[]{:S(2)}, u32[]{:S(2)}) collective-permute-start(bf16[32,3456]{1,0:T(8,128)(2,1)S(1)} %get-tuple-element.26), channel_id=1, source_target_pairs={{0,16},{8,24},{16,0},{24,8},{1,17},{9,25},{17,1},{25,9},{2,18},{10... | collective-permute-start | bytes 663560 | tf_op jit(solution)/shard_map/ppermute | solution.py:228
  20.5 3.6 %copy-start.1 = (bf16[16,1728]{1,0:T(8,128)(2,1)S(1)}, bf16[16,1728]{1,0:T(8,128)(2,1)}, u32[]{:S(2)}) copy-start(bf16[16,1728]{1,0:T(8,128)(2,1)} %param.5) | copy-start | bytes 165892
  20.6 4.3 %collective-permute-start.5 = (bf16[16,2048]{1,0:T(8,128)(2,1)S(1)}, bf16[16,2048]{1,0:T(8,128)(2,1)S(1)}, u32[]{:S(2)}, u32[]{:S(2)}) collective-permute-start(bf16[16,2048]{1,0:T(8,128)(2,1)S(1)} %get-tuple-element.36), channel_id=1, source_target_pairs={{0,2},{1,3},{2,0},{3,1},{4,6},{5,7},{6,4},{7,5},{8,10},{9,11},{10,... | collective-permute-start | bytes 196616 | tf_op jit(solution)/shard_map/ppermute | solution.py:228
  21.3 5.0 %collective-permute-start.6 = (bf16[16,2048]{1,0:T(8,128)(2,1)S(1)}, bf16[16,2048]{1,0:T(8,128)(2,1)S(1)}, u32[]{:S(2)}, u32[]{:S(2)}) collective-permute-start(bf16[16,2048]{1,0:T(8,128)(2,1)S(1)} %get-tuple-element.35), channel_id=1, source_target_pairs={{0,4},{1,5},{2,6},{3,7},{4,0},{5,1},{6,2},{7,3},{8,12},{9,13},{10,... | collective-permute-start | bytes 196616 | tf_op jit(solution)/shard_map/ppermute | solution.py:228
  22.3 5.2 %collective-permute-start.7 = (bf16[16,2048]{1,0:T(8,128)(2,1)S(1)}, bf16[16,2048]{1,0:T(8,128)(2,1)S(1)}, u32[]{:S(2)}, u32[]{:S(2)}) collective-permute-start(bf16[16,2048]{1,0:T(8,128)(2,1)S(1)} %get-tuple-element.34), channel_id=1, source_target_pairs={{0,6},{1,7},{2,4},{3,5},{4,2},{5,3},{6,0},{7,1},{8,14},{9,15},{10,... | collective-permute-start | bytes 196616 | tf_op jit(solution)/shard_map/ppermute | solution.py:228
  28.4 5.1 %collective-permute-start.13 = (bf16[16,1728]{1,0:T(8,128)(2,1)S(1)}, bf16[16,1728]{1,0:T(8,128)(2,1)S(1)}, u32[]{:S(2)}, u32[]{:S(2)}) collective-permute-start(bf16[16,1728]{1,0:T(8,128)(2,1)S(1)} %get-tuple-element.25), channel_id=1, source_target_pairs={{0,16},{8,24},{16,0},{24,8},{1,17},{9,25},{17,1},{25,9},{2,18},{10... | collective-permute-start | bytes 165896 | tf_op jit(solution)/shard_map/ppermute | solution.py:228
  29.9 5.9 %collective-permute-start.8 = (bf16[4,8,2048]{2,1,0:T(8,128)(2,1)S(1)}, bf16[4,8,2048]{2,1,0:T(8,128)(2,1)S(1)}, u32[]{:S(2)}, u32[]{:S(2)}) collective-permute-start(bf16[4,8,2048]{2,1,0:T(8,128)(2,1)S(1)} %get-tuple-element.24), channel_id=1, source_target_pairs={{0,1},{1,0},{2,3},{3,2},{4,5},{5,4},{6,7},{7,6},{8,9},{9,8},{10,11... | collective-permute-start | bytes 393224 | tf_op jit(solution)/shard_map/ppermute | solution.py:228
  33.6 9.0 %collective-permute-start.15 = (bf16[32,3456]{1,0:T(8,128)(2,1)S(1)}, bf16[32,3456]{1,0:T(8,128)(2,1)S(1)}, u32[]{:S(2)}, u32[]{:S(2)}) collective-permute-start(bf16[32,3456]{1,0:T(8,128)(2,1)S(1)} %add_convert_fusion.refs_6_), channel_id=1, source_target_pairs={{0,8},{8,0},{16,24},{24,16},{1,9},{9,1},{17,25},{25,17},{2,10},{10... | collective-permute-start | bytes 663560 | tf_op jit(solution)/shard_map/ppermute | solution.py:228
  35.3 6.2 %collective-permute-start.14 = (bf16[16,1728]{1,0:T(8,128)(2,1)S(1)}, bf16[16,1728]{1,0:T(8,128)(2,1)S(1)}, u32[]{:S(2)}, u32[]{:S(2)}) collective-permute-start(bf16[16,1728]{1,0:T(8,128)(2,1)S(1)} %add_convert_fusion.5.refs_4_), channel_id=1, source_target_pairs={{0,8},{8,0},{16,24},{24,16},{1,9},{9,1},{17,25},{25,17},{2,10},{10... | collective-permute-start | bytes 165896 | tf_op jit(solution)/shard_map/ppermute | solution.py:228
  35.8 5.7 %collective-permute-start.10 = (bf16[8,2048]{1,0:T(8,128)(2,1)S(1)}, bf16[8,2048]{1,0:T(8,128)(2,1)S(1)}, u32[]{:S(2)}, u32[]{:S(2)}) collective-permute-start(bf16[8,2048]{1,0:T(8,128)(2,1)S(1)} %get-tuple-element.39), channel_id=1, source_target_pairs={{0,4},{1,5},{2,6},{3,7},{4,0},{5,1},{6,2},{7,3},{8,12},{9,13},{10,... | collective-permute-start | bytes 98312 | tf_op jit(solution)/shard_map/ppermute | solution.py:228
  37.0 4.8 %collective-permute-start.11 = (bf16[8,2048]{1,0:T(8,128)(2,1)S(1)}, bf16[8,2048]{1,0:T(8,128)(2,1)S(1)}, u32[]{:S(2)}, u32[]{:S(2)}) collective-permute-start(bf16[8,2048]{1,0:T(8,128)(2,1)S(1)} %get-tuple-element.38), channel_id=1, source_target_pairs={{0,6},{1,7},{2,4},{3,5},{4,2},{5,3},{6,0},{7,1},{8,14},{9,15},{10,... | collective-permute-start | bytes 98312 | tf_op jit(solution)/shard_map/ppermute | solution.py:228
  38.7 3.9 %collective-permute-start.9 = (bf16[8,2048]{1,0:T(8,128)(2,1)S(1)}, bf16[8,2048]{1,0:T(8,128)(2,1)S(1)}, u32[]{:S(2)}, u32[]{:S(2)}) collective-permute-start(bf16[8,2048]{1,0:T(8,128)(2,1)S(1)} %get-tuple-element.40), channel_id=1, source_target_pairs={{0,2},{1,3},{2,0},{3,1},{4,6},{5,7},{6,4},{7,5},{8,10},{9,11},{10,... | collective-permute-start | bytes 98312 | tf_op jit(solution)/shard_map/ppermute | solution.py:228

commit v13 on v11

--- a/solution.py
+++ b/solution.py
@@ -131,7 +131,7 @@
                 total = term if total is None else total + term
         s = sigmoid(total)
         feat_ref[:, base : base + chunk] = (total * s).astype(BF16)
-        cot = cot_ref[:, base : base + chunk].astype(F32)
+        cot = cot_ref[:, base : base + chunk]
         delta = (cot * (s * (1.0 + total * (1.0 - s)))).astype(BF16).astype(F32)
         for dy in range(3):
             for dx in range(3):
@@ -262,7 +262,7 @@
     pitch = pitch_of(c0)
     scale = 1.0 / math.sqrt(n_sample * volumes.shape[1] * cells)
     volumes = volumes.reshape(rows_in, cells)
-    cotangent = cotangent.reshape(f2, cells)
+    cotangent = cotangent.reshape(f2, cells).astype(F32)
     padded = cells + 2 * PLANE
 
     need = (8 * 3 * c0) // 128 * 128 + pitch

time: 43.1 us -> 42.8 us (level)
  waiting for transfers between devices: 14.6 us -> 15.4 us
  starting transfers between devices: 18.5 us -> 17.9 us
    ppermute x16, waiting for transfers between devices: 14.6 us -> 15.4 us  [swap(): return lax.ppermute(value, axis, [(i, i ^ k) for i in range(n)])]
    ppermute x16, starting transfers between devices: 18.5 us -> 17.9 us  [swap(): return lax.ppermute(value, axis, [(i, i ^ k) for i in range(n)])]
where the time goes in v13:
time: 42.8 us; the launch traced here: 42.7 us
  starting transfers between devices  17.9 us (42%)
  waiting for transfers between devices  15.4 us (36%)
  Pallas kernels  5.89 us (14%)
  local copies, waits for them, and re-layouts  1.61 us (4%)
  other arithmetic  1.14 us (3%)
  between operations  0.76 us (2%)
    ppermute x16, starting transfers between devices, swap(): return lax.ppermute(value, axis, [(i, i ^ k) for i in range(n)])  17.9 us
    ppermute x16, waiting for transfers between devices, swap(): return lax.ppermute(value, axis, [(i, i ^ k) for i in range(n)])  15.4 us
    pallas_call x1, Pallas kernels, local(): call(functools.partial(forward_kernel, n_mp, c0), [sds((f2, cells), BF16)...  4.04 us
    pallas_call x1, Pallas kernels, local(): call(functools.partial(backward_kernel, n_mp), [sds((half, rows_in, cells...  0.98 us
    another operation x2, other arithmetic, local(): near = jnp.stack(near)  0.94 us
    pallas_call x1, Pallas kernels, local(): call(functools.partial(finish_kernel, scale, half), [sds((f2, cells), BF1...  0.88 us
  transfers between devices with their start and end apart: 16, of which 12 were waited for; matrix products, arithmetic and copies ran while one was open for 2% of the time, Pallas kernels for 2%

profile of v13, /device:TPU:0, one launch (start us, length us, event | category | flops | bytes accessed | tf_op | source)
XLA Modules:
  0.0 42.7 jit_solution(658611963958628270)
XLA Ops:
  0.6 0.0 copy-start.1
  0.6 0.9 %fusion.10 = (bf16[1,24,2048]{2,1,0:T(8,128)(2,1)S(1)}, bf16[24,2048]{1,0:T(8,128)(2,1)S(1)}) fusion(bf16[8,2048]{1,0:T(8,128)(2,1)} %bitcast.47, bf16[16,1728]{1,0:T(8,128)(2,1)} %param.5), kind=kLoop, calls=%fused_computation.24 | loop fusion | flops 294912 | bytes 284672 | tf_op jit(solution)/shard_map/stack | solution.py:278
  1.5 3.0 %collective-permute-start = (bf16[24,2048]{1,0:T(8,128)(2,1)S(1)}, bf16[24,2048]{1,0:T(8,128)(2,1)S(1)}, u32[]{:S(2)}, u32[]{:S(2)}) collective-permute-start(bf16[24,2048]{1,0:T(8,128)(2,1)S(1)} %get-tuple-element.41), channel_id=1, source_target_pairs={{0,2},{1,3},{2,0},{3,1},{4,6},{5,7},{6,4},{7,5},{8,10},{9,11},{10,... | collective-permute-start | bytes 294920 | tf_op jit(solution)/shard_map/ppermute | solution.py:228
  4.5 1.5 %collective-permute-start.1 = (bf16[24,2048]{1,0:T(8,128)(2,1)S(1)}, bf16[24,2048]{1,0:T(8,128)(2,1)S(1)}, u32[]{:S(2)}, u32[]{:S(2)}) collective-permute-start(bf16[24,2048]{1,0:T(8,128)(2,1)S(1)} %get-tuple-element.41), channel_id=1, source_target_pairs={{0,4},{1,5},{2,6},{3,7},{4,0},{5,1},{6,2},{7,3},{8,12},{9,13},{10,... | collective-permute-start | bytes 294920 | tf_op jit(solution)/shard_map/ppermute | solution.py:228
  6.1 0.0 collective-permute-start.2
  6.1 0.0 copy-done.1
  6.1 0.1 reshape.68
  6.2 0.1 copy.11
  6.4 0.1 copy.12
  6.5 0.2 copy.13.refs_3_
  6.6 1.0 %collective-permute-done = bf16[24,2048]{1,0:T(8,128)(2,1)S(1)} collective-permute-done((bf16[24,2048]{1,0:T(8,128)(2,1)S(1)}, bf16[24,2048]{1,0:T(8,128)(2,1)S(1)}, u32[]{:S(2)}, u32[]{:S(2)}) %collective-permute-start) | collective-permute-done | bytes 98336 | tf_op jit(solution)/shard_map/ppermute | solution.py:228
  7.6 2.6 %collective-permute-done.1 = bf16[24,2048]{1,0:T(8,128)(2,1)S(1)} collective-permute-done((bf16[24,2048]{1,0:T(8,128)(2,1)S(1)}, bf16[24,2048]{1,0:T(8,128)(2,1)S(1)}, u32[]{:S(2)}, u32[]{:S(2)}) %collective-permute-start.1) | collective-permute-done | bytes 98336 | tf_op jit(solution)/shard_map/ppermute | solution.py:228
  10.2 1.4 %collective-permute-done.2 = bf16[24,2048]{1,0:T(8,128)(2,1)S(1)} collective-permute-done((bf16[24,2048]{1,0:T(8,128)(2,1)S(1)}, bf16[24,2048]{1,0:T(8,128)(2,1)S(1)}, u32[]{:S(2)}, u32[]{:S(2)}) %collective-permute-start.2) | collective-permute-done | bytes 98336 | tf_op jit(solution)/shard_map/ppermute | solution.py:228
  11.6 0.0 copy-start.2
  11.6 0.1 pad_maximum_fusion.refs_0_
  11.6 0.1 collective-permute-start.3
  11.7 0.8 %copy-done.2 = bf16[32,1,2048]{2,0,1:T(8,128)(2,1)S(1)} copy-done((bf16[32,1,2048]{2,0,1:T(8,128)(2,1)S(1)}, bf16[32,1,2048]{2,0,1:T(8,128)(2,1)}, u32[]{:S(2)}) %copy-start.2) | copy-done | bytes 131096
  12.5 0.9 %collective-permute-done.3.refs_1_ = bf16[4,24,2048]{2,1,0:T(8,128)(2,1)S(1)} collective-permute-done((bf16[4,24,2048]{2,1,0:T(8,128)(2,1)S(1)}, bf16[4,24,2048]{2,1,0:T(8,128)(2,1)S(1)}, u32[]{:S(2)}, u32[]{:S(2)}) %collective-permute-start.3) | collective-permute-done | bytes 393248 | tf_op jit(solution)/shard_map/ppermute | solution.py:228
  13.4 4.0 %shard_map.75 = (bf16[32,2048]{1,0:T(8,128)(2,1)S(1)}, f32[16,2048]{1,0:T(8,128)S(1)}, bf16[64,2048]{1,0:T(8,128)(2,1)S(1)}, bf16[4,16,2048]{2,1,0:T(8,128)(2,1)...) custom-call(bf16[4,24,2048]{2,1,0:T(8,128)(2,1)S(1)} %pad_maximum_fusion.refs_0_, ...), custom_call_target="tpu_custom_call" | custom-call | flops 2264924160 | bytes 4194304 | tf_op jit(solution)/shard_map/pallas_call | solution.py:288
  17.5 0.2 collective-permute-start.4
  17.7 2.6 %collective-permute-start.14 = (bf16[32,3456]{1,0:T(8,128)(2,1)S(1)}, bf16[32,3456]{1,0:T(8,128)(2,1)S(1)}, u32[]{:S(2)}, u32[]{:S(2)}) collective-permute-start(bf16[32,3456]{1,0:T(8,128)(2,1)S(1)} %get-tuple-element.25), channel_id=1, source_target_pairs={{0,16},{8,24},{16,0},{24,8},{1,17},{9,25},{17,1},{25,9},{2,18},{10... | collective-permute-start | bytes 663560 | tf_op jit(solution)/shard_map/ppermute | solution.py:228
  20.3 0.0 collective-permute-done.4
  20.3 0.0 copy-start
  20.3 0.1 fusion.5
  20.3 0.7 %collective-permute-start.5 = (bf16[16,2048]{1,0:T(8,128)(2,1)S(1)}, bf16[16,2048]{1,0:T(8,128)(2,1)S(1)}, u32[]{:S(2)}, u32[]{:S(2)}) collective-permute-start(bf16[16,2048]{1,0:T(8,128)(2,1)S(1)} %get-tuple-element.34), channel_id=1, source_target_pairs={{0,2},{1,3},{2,0},{3,1},{4,6},{5,7},{6,4},{7,5},{8,10},{9,11},{10,... | collective-permute-start | bytes 196616 | tf_op jit(solution)/shard_map/ppermute | solution.py:228
  21.1 1.0 %collective-permute-start.6 = (bf16[16,2048]{1,0:T(8,128)(2,1)S(1)}, bf16[16,2048]{1,0:T(8,128)(2,1)S(1)}, u32[]{:S(2)}, u32[]{:S(2)}) collective-permute-start(bf16[16,2048]{1,0:T(8,128)(2,1)S(1)} %get-tuple-element.33), channel_id=1, source_target_pairs={{0,4},{1,5},{2,6},{3,7},{4,0},{5,1},{6,2},{7,3},{8,12},{9,13},{10,... | collective-permute-start | bytes 196616 | tf_op jit(solution)/shard_map/ppermute | solution.py:228
  22.0 1.9 %collective-permute-start.7 = (bf16[16,2048]{1,0:T(8,128)(2,1)S(1)}, bf16[16,2048]{1,0:T(8,128)(2,1)S(1)}, u32[]{:S(2)}, u32[]{:S(2)}) collective-permute-start(bf16[16,2048]{1,0:T(8,128)(2,1)S(1)} %get-tuple-element.32), channel_id=1, source_target_pairs={{0,6},{1,7},{2,4},{3,5},{4,2},{5,3},{6,0},{7,1},{8,14},{9,15},{10,... | collective-permute-start | bytes 196616 | tf_op jit(solution)/shard_map/ppermute | solution.py:228
  23.9 0.0 copy-done
  23.9 0.2 reshape.71
  24.1 0.1 copy.15.refs_6_
  24.2 0.5 %collective-permute-done.5.refs_1_ = bf16[16,2048]{1,0:T(8,128)(2,1)S(1)} collective-permute-done((bf16[16,2048]{1,0:T(8,128)(2,1)S(1)}, bf16[16,2048]{1,0:T(8,128)(2,1)S(1)}, u32[]{:S(2)}, u32[]{:S(2)}) %collective-permute-start.5) | collective-permute-done | bytes 65568 | tf_op jit(solution)/shard_map/ppermute | solution.py:228
  24.8 1.3 %collective-permute-done.6.refs_2_ = bf16[16,2048]{1,0:T(8,128)(2,1)S(1)} collective-permute-done((bf16[16,2048]{1,0:T(8,128)(2,1)S(1)}, bf16[16,2048]{1,0:T(8,128)(2,1)S(1)}, u32[]{:S(2)}, u32[]{:S(2)}) %collective-permute-start.6) | collective-permute-done | bytes 65568 | tf_op jit(solution)/shard_map/ppermute | solution.py:228
  26.0 1.2 %collective-permute-done.7.refs_3_ = bf16[16,2048]{1,0:T(8,128)(2,1)S(1)} collective-permute-done((bf16[16,2048]{1,0:T(8,128)(2,1)S(1)}, bf16[16,2048]{1,0:T(8,128)(2,1)S(1)}, u32[]{:S(2)}, u32[]{:S(2)}) %collective-permute-start.7) | collective-permute-done | bytes 65568 | tf_op jit(solution)/shard_map/ppermute | solution.py:228
  27.2 1.0 %shard_map.76 = (bf16[4,8,2048]{2,1,0:T(8,128)(2,1)S(1)}, bf16[4,8,2048]{2,1,0:T(8,128)(2,1)S(1)}, bf16[16,1728]{1,0:T(8,128)(2,1)S(1)}) custom-call(bf16[16,2048]{1,0:T(8,128)(2,1)S(1)} %get-tuple-element.35.refs_0_, bf16[16,2048]{1,0:T(8,128)(2,1)S(1)} %collective-permute-done.5.refs_1_, bf16[16,2048]{1,0:T(8,128)(2,1)S(1)} %collective-permute-done.6.refs_2_, ...), custom_call_target="tpu_custom_call" | custom-call | flops 226492416 | bytes 1048576 | tf_op jit(solution)/shard_map/pallas_call | solution.py:317
  28.2 1.4 %collective-permute-start.12 = (bf16[16,1728]{1,0:T(8,128)(2,1)S(1)}, bf16[16,1728]{1,0:T(8,128)(2,1)S(1)}, u32[]{:S(2)}, u32[]{:S(2)}) collective-permute-start(bf16[16,1728]{1,0:T(8,128)(2,1)S(1)} %get-tuple-element.24), channel_id=1, source_target_pairs={{0,16},{8,24},{16,0},{24,8},{1,17},{9,25},{17,1},{25,9},{2,18},{10... | collective-permute-start | bytes 165896 | tf_op jit(solution)/shard_map/ppermute | solution.py:228
  29.6 2.6 %collective-permute-done.14 = bf16[32,3456]{1,0:T(8,128)(2,1)S(1)} collective-permute-done((bf16[32,3456]{1,0:T(8,128)(2,1)S(1)}, bf16[32,3456]{1,0:T(8,128)(2,1)S(1)}, u32[]{:S(2)}, u32[]{:S(2)}) %collective-permute-start.14) | collective-permute-done | bytes 221216 | tf_op jit(solution)/shard_map/ppermute | solution.py:228
  32.2 0.1 add_convert_fusion.refs_6_
  32.3 0.3 collective-permute-start.15
  32.5 0.0 collective-permute-start.8
  32.5 0.8 %collective-permute-done.12 = bf16[16,1728]{1,0:T(8,128)(2,1)S(1)} collective-permute-done((bf16[16,1728]{1,0:T(8,128)(2,1)S(1)}, bf16[16,1728]{1,0:T(8,128)(2,1)S(1)}, u32[]{:S(2)}, u32[]{:S(2)}) %collective-permute-start.12) | collective-permute-done | bytes 55328 | tf_op jit(solution)/shard_map/ppermute | solution.py:228
  33.3 1.6 %collective-permute-start.13 = (bf16[16,1728]{1,0:T(8,128)(2,1)S(1)}, bf16[16,1728]{1,0:T(8,128)(2,1)S(1)}, u32[]{:S(2)}, u32[]{:S(2)}) collective-permute-start(bf16[16,1728]{1,0:T(8,128)(2,1)S(1)} %add_convert_fusion.5.refs_4_), channel_id=1, source_target_pairs={{0,8},{8,0},{16,24},{24,16},{1,9},{9,1},{17,25},{25,17},{2,10},{10... | collective-permute-start | bytes 165896 | tf_op jit(solution)/shard_map/ppermute | solution.py:228
  35.0 0.0 collective-permute-done.8
  35.0 1.1 %collective-permute-start.10 = (bf16[8,2048]{1,0:T(8,128)(2,1)S(1)}, bf16[8,2048]{1,0:T(8,128)(2,1)S(1)}, u32[]{:S(2)}, u32[]{:S(2)}) collective-permute-start(bf16[8,2048]{1,0:T(8,128)(2,1)S(1)} %get-tuple-element.37), channel_id=1, source_target_pairs={{0,4},{1,5},{2,6},{3,7},{4,0},{5,1},{6,2},{7,3},{8,12},{9,13},{10,... | collective-permute-start | bytes 98312 | tf_op jit(solution)/shard_map/ppermute | solution.py:228
  36.1 1.7 %collective-permute-start.11 = (bf16[8,2048]{1,0:T(8,128)(2,1)S(1)}, bf16[8,2048]{1,0:T(8,128)(2,1)S(1)}, u32[]{:S(2)}, u32[]{:S(2)}) collective-permute-start(bf16[8,2048]{1,0:T(8,128)(2,1)S(1)} %get-tuple-element.36), channel_id=1, source_target_pairs={{0,6},{1,7},{2,4},{3,5},{4,2},{5,3},{6,0},{7,1},{8,14},{9,15},{10,... | collective-permute-start | bytes 98312 | tf_op jit(solution)/shard_map/ppermute | solution.py:228
  37.9 0.7 %collective-permute-start.9 = (bf16[8,2048]{1,0:T(8,128)(2,1)S(1)}, bf16[8,2048]{1,0:T(8,128)(2,1)S(1)}, u32[]{:S(2)}, u32[]{:S(2)}) collective-permute-start(bf16[8,2048]{1,0:T(8,128)(2,1)S(1)} %get-tuple-element.38), channel_id=1, source_target_pairs={{0,2},{1,3},{2,0},{3,1},{4,6},{5,7},{6,4},{7,5},{8,10},{9,11},{10,... | collective-permute-start | bytes 98312 | tf_op jit(solution)/shard_map/ppermute | solution.py:228
  38.6 0.8 %collective-permute-done.13.refs_5_ = bf16[16,1728]{1,0:T(8,128)(2,1)S(1)} collective-permute-done((bf16[16,1728]{1,0:T(8,128)(2,1)S(1)}, bf16[16,1728]{1,0:T(8,128)(2,1)S(1)}, u32[]{:S(2)}, u32[]{:S(2)}) %collective-permute-start.13) | collective-permute-done | bytes 55328 | tf_op jit(solution)/shard_map/ppermute | solution.py:228
  39.4 0.0 collective-permute-done.10.refs_2_
  39.4 1.6 %collective-permute-done.11.refs_3_ = bf16[8,2048]{1,0:T(8,128)(2,1)S(1)} collective-permute-done((bf16[8,2048]{1,0:T(8,128)(2,1)S(1)}, bf16[8,2048]{1,0:T(8,128)(2,1)S(1)}, u32[]{:S(2)}, u32[]{:S(2)}) %collective-permute-start.11) | collective-permute-done | bytes 32800 | tf_op jit(solution)/shard_map/ppermute | solution.py:228
  41.0 0.8 %collective-permute-done.9.refs_1_ = bf16[8,2048]{1,0:T(8,128)(2,1)S(1)} collective-permute-done((bf16[8,2048]{1,0:T(8,128)(2,1)S(1)}, bf16[8,2048]{1,0:T(8,128)(2,1)S(1)}, u32[]{:S(2)}, u32[]{:S(2)}) %collective-permute-start.9) | collective-permute-done | bytes 32800 | tf_op jit(solution)/shard_map/ppermute | solution.py:228
  41.8 0.0 collective-permute-done.15.refs_7_
  41.8 0.9 %shard_map.77 = (bf16[32,2048]{1,0:T(8,128)(2,1)}, bf16[8,2048]{1,0:T(8,128)(2,1)}, f32[16,1728]{1,0:T(8,128)}, f32[32,3456]{1,0:T(8,128)}) custom-call(bf16[8,2048]{1,0:T(8,128)(2,1)S(1)} %get-tuple-element.39.refs_0_, bf16[8,2048]{1,0:T(8,128)(2,1)S(1)} %collective-permute-done.9.refs_1_, bf16[8,2048]{1,0:T(8,128)(2,1)S(1)} %collective-permute-done.10.refs_2_, ...), custom_call_target="tpu_custom_call" | custom-call | bytes 2097152 | tf_op jit(solution)/shard_map/pallas_call | solution.py:342
  (5 shorter events, 0.2 us)
Async XLA Ops:
  0.6 5.5 %copy-start.1 = (bf16[32,3456]{1,0:T(8,128)(2,1)S(1)}, bf16[32,3456]{1,0:T(8,128)(2,1)}, u32[]{:S(2)}) copy-start(bf16[32,3456]{1,0:T(8,128)(2,1)} %param.6) | copy-start | bytes 663556
  1.5 6.1 %collective-permute-start = (bf16[24,2048]{1,0:T(8,128)(2,1)S(1)}, bf16[24,2048]{1,0:T(8,128)(2,1)S(1)}, u32[]{:S(2)}, u32[]{:S(2)}) collective-permute-start(bf16[24,2048]{1,0:T(8,128)(2,1)S(1)} %get-tuple-element.41), channel_id=1, source_target_pairs={{0,2},{1,3},{2,0},{3,1},{4,6},{5,7},{6,4},{7,5},{8,10},{9,11},{10,... | collective-permute-start | bytes 294920 | tf_op jit(solution)/shard_map/ppermute | solution.py:228
  4.5 5.7 %collective-permute-start.1 = (bf16[24,2048]{1,0:T(8,128)(2,1)S(1)}, bf16[24,2048]{1,0:T(8,128)(2,1)S(1)}, u32[]{:S(2)}, u32[]{:S(2)}) collective-permute-start(bf16[24,2048]{1,0:T(8,128)(2,1)S(1)} %get-tuple-element.41), channel_id=1, source_target_pairs={{0,4},{1,5},{2,6},{3,7},{4,0},{5,1},{6,2},{7,3},{8,12},{9,13},{10,... | collective-permute-start | bytes 294920 | tf_op jit(solution)/shard_map/ppermute | solution.py:228
  6.1 5.5 %collective-permute-start.2 = (bf16[24,2048]{1,0:T(8,128)(2,1)S(1)}, bf16[24,2048]{1,0:T(8,128)(2,1)S(1)}, u32[]{:S(2)}, u32[]{:S(2)}) collective-permute-start(bf16[24,2048]{1,0:T(8,128)(2,1)S(1)} %get-tuple-element.41), channel_id=1, source_target_pairs={{0,6},{1,7},{2,4},{3,5},{4,2},{5,3},{6,0},{7,1},{8,14},{9,15},{10,... | collective-permute-start | bytes 294920 | tf_op jit(solution)/shard_map/ppermute | solution.py:228
  11.6 0.9 %copy-start.2 = (bf16[32,1,2048]{2,0,1:T(8,128)(2,1)S(1)}, bf16[32,1,2048]{2,0,1:T(8,128)(2,1)}, u32[]{:S(2)}) copy-start(bf16[32,1,2048]{2,0,1:T(8,128)(2,1)} %param.7) | copy-start | bytes 393220
  11.6 1.8 %collective-permute-start.3 = (bf16[4,24,2048]{2,1,0:T(8,128)(2,1)S(1)}, bf16[4,24,2048]{2,1,0:T(8,128)(2,1)S(1)}, u32[]{:S(2)}, u32[]{:S(2)}) collective-permute-start(bf16[4,24,2048]{2,1,0:T(8,128)(2,1)S(1)} %pad_maximum_fusion.refs_0_), channel_id=1, source_target_pairs={{0,1},{1,0},{2,3},{3,2},{4,5},{5,4},{6,7},{7,6},{8,9},{9,8},{10,11... | collective-permute-start | bytes 1179656 | tf_op jit(solution)/shard_map/ppermute | solution.py:228
  17.5 2.8 %collective-permute-start.4 = (bf16[4,16,2048]{2,1,0:T(8,128)(2,1)S(1)}, bf16[4,16,2048]{2,1,0:T(8,128)(2,1)S(1)}, u32[]{:S(2)}, u32[]{:S(2)}) collective-permute-start(bf16[4,16,2048]{2,1,0:T(8,128)(2,1)S(1)} %get-tuple-element.19), channel_id=1, source_target_pairs={{0,1},{1,0},{2,3},{3,2},{4,5},{5,4},{6,7},{7,6},{8,9},{9,8},{10,11... | collective-permute-start | bytes 786440 | tf_op jit(solution)/shard_map/ppermute | solution.py:228
  17.7 14.5 %collective-permute-start.14 = (bf16[32,3456]{1,0:T(8,128)(2,1)S(1)}, bf16[32,3456]{1,0:T(8,128)(2,1)S(1)}, u32[]{:S(2)}, u32[]{:S(2)}) collective-permute-start(bf16[32,3456]{1,0:T(8,128)(2,1)S(1)} %get-tuple-element.25), channel_id=1, source_target_pairs={{0,16},{8,24},{16,0},{24,8},{1,17},{9,25},{17,1},{25,9},{2,18},{10... | collective-permute-start | bytes 663560 | tf_op jit(solution)/shard_map/ppermute | solution.py:228
  20.3 3.6 %copy-start = (bf16[16,1728]{1,0:T(8,128)(2,1)S(1)}, bf16[16,1728]{1,0:T(8,128)(2,1)}, u32[]{:S(2)}) copy-start(bf16[16,1728]{1,0:T(8,128)(2,1)} %param.5) | copy-start | bytes 165892
  20.3 4.4 %collective-permute-start.5 = (bf16[16,2048]{1,0:T(8,128)(2,1)S(1)}, bf16[16,2048]{1,0:T(8,128)(2,1)S(1)}, u32[]{:S(2)}, u32[]{:S(2)}) collective-permute-start(bf16[16,2048]{1,0:T(8,128)(2,1)S(1)} %get-tuple-element.34), channel_id=1, source_target_pairs={{0,2},{1,3},{2,0},{3,1},{4,6},{5,7},{6,4},{7,5},{8,10},{9,11},{10,... | collective-permute-start | bytes 196616 | tf_op jit(solution)/shard_map/ppermute | solution.py:228
  21.1 5.0 %collective-permute-start.6 = (bf16[16,2048]{1,0:T(8,128)(2,1)S(1)}, bf16[16,2048]{1,0:T(8,128)(2,1)S(1)}, u32[]{:S(2)}, u32[]{:S(2)}) collective-permute-start(bf16[16,2048]{1,0:T(8,128)(2,1)S(1)} %get-tuple-element.33), channel_id=1, source_target_pairs={{0,4},{1,5},{2,6},{3,7},{4,0},{5,1},{6,2},{7,3},{8,12},{9,13},{10,... | collective-permute-start | bytes 196616 | tf_op jit(solution)/shard_map/ppermute | solution.py:228
  22.0 5.2 %collective-permute-start.7 = (bf16[16,2048]{1,0:T(8,128)(2,1)S(1)}, bf16[16,2048]{1,0:T(8,128)(2,1)S(1)}, u32[]{:S(2)}, u32[]{:S(2)}) collective-permute-start(bf16[16,2048]{1,0:T(8,128)(2,1)S(1)} %get-tuple-element.32), channel_id=1, source_target_pairs={{0,6},{1,7},{2,4},{3,5},{4,2},{5,3},{6,0},{7,1},{8,14},{9,15},{10,... | collective-permute-start | bytes 196616 | tf_op jit(solution)/shard_map/ppermute | solution.py:228
  28.2 5.1 %collective-permute-start.12 = (bf16[16,1728]{1,0:T(8,128)(2,1)S(1)}, bf16[16,1728]{1,0:T(8,128)(2,1)S(1)}, u32[]{:S(2)}, u32[]{:S(2)}) collective-permute-start(bf16[16,1728]{1,0:T(8,128)(2,1)S(1)} %get-tuple-element.24), channel_id=1, source_target_pairs={{0,16},{8,24},{16,0},{24,8},{1,17},{9,25},{17,1},{25,9},{2,18},{10... | collective-permute-start | bytes 165896 | tf_op jit(solution)/shard_map/ppermute | solution.py:228
  32.3 9.5 %collective-permute-start.15 = (bf16[32,3456]{1,0:T(8,128)(2,1)S(1)}, bf16[32,3456]{1,0:T(8,128)(2,1)S(1)}, u32[]{:S(2)}, u32[]{:S(2)}) collective-permute-start(bf16[32,3456]{1,0:T(8,128)(2,1)S(1)} %add_convert_fusion.refs_6_), channel_id=1, source_target_pairs={{0,8},{8,0},{16,24},{24,16},{1,9},{9,1},{17,25},{25,17},{2,10},{10... | collective-permute-start | bytes 663560 | tf_op jit(solution)/shard_map/ppermute | solution.py:228
  32.5 2.5 %collective-permute-start.8 = (bf16[4,8,2048]{2,1,0:T(8,128)(2,1)S(1)}, bf16[4,8,2048]{2,1,0:T(8,128)(2,1)S(1)}, u32[]{:S(2)}, u32[]{:S(2)}) collective-permute-start(bf16[4,8,2048]{2,1,0:T(8,128)(2,1)S(1)} %get-tuple-element.23), channel_id=1, source_target_pairs={{0,1},{1,0},{2,3},{3,2},{4,5},{5,4},{6,7},{7,6},{8,9},{9,8},{10,11... | collective-permute-start | bytes 393224 | tf_op jit(solution)/shard_map/ppermute | solution.py:228
  33.3 6.1 %collective-permute-start.13 = (bf16[16,1728]{1,0:T(8,128)(2,1)S(1)}, bf16[16,1728]{1,0:T(8,128)(2,1)S(1)}, u32[]{:S(2)}, u32[]{:S(2)}) collective-permute-start(bf16[16,1728]{1,0:T(8,128)(2,1)S(1)} %add_convert_fusion.5.refs_4_), channel_id=1, source_target_pairs={{0,8},{8,0},{16,24},{24,16},{1,9},{9,1},{17,25},{25,17},{2,10},{10... | collective-permute-start | bytes 165896 | tf_op jit(solution)/shard_map/ppermute | solution.py:228
  35.0 4.4 %collective-permute-start.10 = (bf16[8,2048]{1,0:T(8,128)(2,1)S(1)}, bf16[8,2048]{1,0:T(8,128)(2,1)S(1)}, u32[]{:S(2)}, u32[]{:S(2)}) collective-permute-start(bf16[8,2048]{1,0:T(8,128)(2,1)S(1)} %get-tuple-element.37), channel_id=1, source_target_pairs={{0,4},{1,5},{2,6},{3,7},{4,0},{5,1},{6,2},{7,3},{8,12},{9,13},{10,... | collective-permute-start | bytes 98312 | tf_op jit(solution)/shard_map/ppermute | solution.py:228
  36.1 4.8 %collective-permute-start.11 = (bf16[8,2048]{1,0:T(8,128)(2,1)S(1)}, bf16[8,2048]{1,0:T(8,128)(2,1)S(1)}, u32[]{:S(2)}, u32[]{:S(2)}) collective-permute-start(bf16[8,2048]{1,0:T(8,128)(2,1)S(1)} %get-tuple-element.36), channel_id=1, source_target_pairs={{0,6},{1,7},{2,4},{3,5},{4,2},{5,3},{6,0},{7,1},{8,14},{9,15},{10,... | collective-permute-start | bytes 98312 | tf_op jit(solution)/shard_map/ppermute | solution.py:228
  37.9 3.9 %collective-permute-start.9 = (bf16[8,2048]{1,0:T(8,128)(2,1)S(1)}, bf16[8,2048]{1,0:T(8,128)(2,1)S(1)}, u32[]{:S(2)}, u32[]{:S(2)}) collective-permute-start(bf16[8,2048]{1,0:T(8,128)(2,1)S(1)} %get-tuple-element.38), channel_id=1, source_target_pairs={{0,2},{1,3},{2,0},{3,1},{4,6},{5,7},{6,4},{7,5},{8,10},{9,11},{10,... | collective-permute-start | bytes 98312 | tf_op jit(solution)/shard_map/ppermute | solution.py:228
